TPU v7x, 32 devices: a whole 2x2x4 slice. The times are simulated.
32 devices in a mesh: win: 8 (over y, x, core), tok: 4 (over z).
Axes of the slice: x: 2, y: 2, z: 4, core: 2. Of those that a mesh axis runs over, the one named last changes fastest.
Arguments:
- field_tokens: bfloat16 [8, 40, 40, 1280], P('win', 'tok'), may hold values from -60 to 60
- lon_shift: int32 [4], replicated, may hold values from 1 to 20, as said below
- norm_gain: float32 [1280], replicated, may hold values from 0.1 to 1.9
- qkv_weight: bfloat16 [1280, 1920], replicated, may hold values from -1 to 1
- out_weight: bfloat16 [640, 1280], replicated, may hold values from -0.25 to 0.25
Outputs:
- result: bfloat16 [8, 40, 40, 1280], P('win', 'tok')
Inputs may be any that keep to these rules, and one draw needn't show every extreme that they name: `lon_shift`: one entry is 20 and another is 1.
All inputs are finite; a program needn't handle non-finite values.
Results may differ from a plain program's by a relative error of at most 0.0046.
Values may be sent and summed in bfloat16 or wider, within the bound.
No kernel may reach another device: no remote copies, remote signals or barrier semaphores. Data moves between devices by JAX's collectives and lax.ppermute only.
A program may use at most 64 MiB of HBM per device.

v0:
```python
import jax
import jax.numpy as jnp
from jax import lax
from jax.sharding import PartitionSpec as P

HEADS = 8
HD = 80
LAT_WINDOWS = 4


def shifted(block, axis, distance):
    devices = range(lax.axis_size(axis))
    route = [((i - distance) % len(devices), i) for i in devices]
    return lax.ppermute(block, axis, route)


def attend(packed):
    queries = packed[:, 0, 0]
    key_rows = packed[:, 1, 0]
    value_rows = packed[:, 2, 0]
    count = queries.shape[0]
    local_heads = queries.shape[1]
    head_size = queries.shape[2]
    factor = head_size ** (-0.5)
    pieces = 2
    grouped = queries.reshape(pieces, count // pieces, local_heads, head_size)

    def one_block(query_block):
        scores = (
            jnp.einsum("qhd,khd->hqk", query_block, key_rows, preferred_element_type=jnp.float32)
            * factor
        )
        row_top = jnp.max(scores, axis=-1, keepdims=True)
        exponent = jnp.exp(scores - row_top)
        weights = (exponent / jnp.sum(exponent, axis=-1, keepdims=True)).astype(jnp.bfloat16)
        return jnp.einsum(
            "hqk,khd->qhd", weights, value_rows, preferred_element_type=jnp.float32
        ).astype(jnp.bfloat16)

    return lax.map(one_block, grouped).reshape(count, local_heads, head_size)


def shards(field_tokens, lon_shift, norm_gain, qkv_weight, out_weight):
    row_count = field_tokens.shape[1]
    column_count = field_tokens.shape[2]
    feature_count = field_tokens.shape[3]
    groups = lax.axis_size("tok")
    latitude = lax.axis_index("win") % LAT_WINDOWS
    offset = lax.dynamic_index_in_dim(lon_shift, latitude, 0, keepdims=False)
    outgoing = field_tokens[:, :, : column_count // 2]
    eastern = shifted(outgoing, "win", -LAT_WINDOWS)
    joined = jnp.concatenate([field_tokens, eastern], axis=2)
    moved = lax.dynamic_slice_in_dim(joined, offset, column_count, axis=2)
    tokens = moved.reshape(row_count * column_count, feature_count)
    values = tokens.astype(jnp.float32)
    factor = lax.rsqrt(jnp.mean(values * values, axis=-1, keepdims=True) + 1e-06)
    normed = (values * factor * norm_gain).astype(jnp.bfloat16)
    qkv = jnp.dot(normed, qkv_weight, preferred_element_type=jnp.float32).astype(jnp.bfloat16)
    qkv = qkv.reshape(row_count * column_count, 3, groups, HEADS // groups, HD)
    attended = attend(lax.all_to_all(qkv, "tok", split_axis=2, concat_axis=0, tiled=True))
    returned = lax.all_to_all(attended, "tok", split_axis=0, concat_axis=1, tiled=True)
    projected = jnp.dot(
        returned.reshape(row_count * column_count, HEADS * HD),
        out_weight,
        preferred_element_type=jnp.float32,
    )
    mixed = (
        (values + projected).astype(jnp.bfloat16).reshape(1, row_count, column_count, feature_count)
    )
    leaving = mixed[:, :, column_count - column_count // 2 :]
    western = shifted(leaving, "win", LAT_WINDOWS)
    combined = jnp.concatenate([western, mixed], axis=2)
    return lax.dynamic_slice_in_dim(combined, western.shape[2] - offset, column_count, axis=2)


def solution(mesh):
    placed = (P("win", "tok", None, None), P(), P(), P(), P())
    return jax.shard_map(
        shards, mesh=mesh, in_specs=placed, out_specs=P("win", "tok", None, None), check_vma=False
    )
```

profile of v0, /device:TPU:0, one launch (start us, length us, event | category | flops | bytes accessed | tf_op | source)
XLA Modules:
  0.0 169.5 jit_solution(11658042654718585793)
XLA Ops:
  0.0 0.0 copy-start
  0.0 1.2 slice.15
  1.2 0.0 copy-start.3
  1.3 3.0 %collective-permute-start = (bf16[1,10,20,1280]{3,2,1,0:T(8,128)(2,1)S(1)}, bf16[1,10,20,1280]{3,2,1,0:T(8,128)(2,1)S(1)}, u32[]{:S(2)}, u32[]{:S(2)}) collective-permute-start(bf16[1,10,20,1280]{3,2,1,0:T(8,128)(2,1)S(1)} %slice.15), channel_id=1, source_target_pairs={{16,0},{20,4},{24,8},{28,12},{0,16},{4,20},{8,24},{12,28},{17,1},{... | collective-permute-start | bytes 1536008 | tf_op jit(solution)/shard_map/ppermute | solution.py:14
  4.3 1.3 dynamic_slice.14
  7.7 10.4 %collective-permute-done = bf16[1,10,20,1280]{3,2,1,0:T(8,128)(2,1)S(1)} collective-permute-done((bf16[1,10,20,1280]{3,2,1,0:T(8,128)(2,1)S(1)}, bf16[1,10,20,1280]{3,2,1,0:T(8,128)(2,1)S(1)}, u32[]{:S(2)}, u32[]{:S(2)}) %collective-permute-start) | collective-permute-done | bytes 512032 | tf_op jit(solution)/shard_map/ppermute | solution.py:14
  18.1 3.3 %multiply_reduce_fusion.1 = (f32[10,40]{1,0:T(8,128)S(1)}, f32[1,10,40,1280]{3,2,1,0:T(8,128)}) fusion(s32[]{:T(128)S(6)} %select_n.19, bf16[1,10,20,1280]{3,2,1,0:T(8,128)(2,1)S(1)} %collective-permute-done, bf16[1,10,40,1280]{3,2,1,0:T(8,128)(2,1)} %param.7), kind=kLoop, calls=%fused_computation.25 | loop fusion | flops 3071600 | bytes 3585604 | tf_op jit(solution)/shard_map/reduce_sum | solution.py:56
  21.4 0.1 rsqrt.12
  21.5 0.0 copy-done.3
  21.5 1.8 %fusion.29 = bf16[400,1280]{1,0:T(8,128)(2,1)S(1)} fusion(f32[1,10,40,1280]{3,2,1,0:T(8,128)} %get-tuple-element.59, f32[1280]{0:T(1024)S(1)} %copy-done.3, f32[400]{0:T(512)S(1)} %rsqrt.12), kind=kLoop, calls=%fused_computation.24 | loop fusion | flops 1536000 | bytes 3078720 | tf_op jit(solution)/shard_map/convert_element_type | solution.py:57
  23.3 4.7 %convolution_convert_fusion = bf16[400,1920]{1,0:T(8,128)(2,1)S(1)} fusion(bf16[400,1280]{1,0:T(8,128)(2,1)S(1)} %fusion.29, bf16[1280,1920]{1,0:T(8,128)(2,1)} %param.10), kind=kOutput, calls=%fused_computation.21 | convolution fusion | flops 1966848000 | bytes 7475200 | tf_op jit(solution)/shard_map/dot_general | solution.py:58
  28.0 2.3 %copy.16 = bf16[400,1920]{0,1:T(8,128)(2,1)} copy(bf16[400,1920]{1,0:T(8,128)(2,1)S(1)} %convolution_convert_fusion) | data formatting | bytes 3072000 | tf_op jit(solution)/shard_map/convert_element_type | solution.py:58
  30.3 3.0 %copy.17 = bf16[400,3,4,2,80]{0,4,3,1,2:T(8,128)(2,1)} copy(bf16[400,3,4,2,80]{0,4,3,2,1:T(8,128)(2,1)} %bitcast.62) | data formatting | bytes 3072000 | tf_op jit(solution)/shard_map/reshape | solution.py:59
  33.3 5.1 %all-to-all-start = ((bf16[400,3,4,2,80]{0,4,3,1,2:T(8,128)(2,1)}), bf16[400,3,4,2,80]{0,4,3,1,2:T(8,128)(2,1)}, u32[]{:S(2)}, u32[]{:S(2)}) async-start(bf16[400,3,4,2,80]{0,4,3,1,2:T(8,128)(2,1)} %copy.17), calls=%async_computation | async-start | bytes 3932160 | tf_op jit(solution)/shard_map/all_to_all | solution.py:60
  38.4 44.6 %all-to-all-done = bf16[400,3,4,2,80]{0,4,3,1,2:T(8,128)(2,1)} async-done(((bf16[400,3,4,2,80]{0,4,3,1,2:T(8,128)(2,1)}), bf16[400,3,4,2,80]{0,4,3,1,2:T(8,128)(2,1)}, u32[]{:S(2)}, u32[]{:S(2)}) %all-to-all-start) | async-done | bytes 1536032 | tf_op jit(solution)/shard_map/all_to_all | solution.py:60
  83.0 4.3 %copy.18 = bf16[4,400,3,1,2,80]{1,0,5,4,2,3:T(4,128)(2,1)} copy(bf16[4,400,3,1,2,80]{1,5,4,2,0,3:T(8,128)(2,1)} %bitcast.7) | data formatting | bytes 3072000 | tf_op jit(solution)/shard_map/all_to_all | solution.py:60
  87.4 3.9 %all_to_all.27 = bf16[1600,3,1,2,80]{0,4,3,1,2:T(8,128)(2,1)S(1)} reshape(bf16[4,400,3,1,2,80]{1,0,5,4,2,3:T(4,128)(2,1)} %copy.18) | data formatting | bytes 3072000 | tf_op jit(solution)/shard_map/all_to_all | solution.py:60
  91.3 1.3 slice_bitcast_fusion
  92.5 0.0 copy-start.1
  92.6 2.2 %reshape_squeeze.3 = bf16[2,800,2,80]{1,0,3,2:T(2,128)(2,1)S(1)} reshape(bf16[1600,1,1,2,80]{0,4,3,1,2:T(8,128)(2,1)} %get-tuple-element.64) | data formatting | bytes 1024000 | tf_op jit(solution)/shard_map/reshape;squeeze | solution.py:26
  94.7 0.1 copy.19
  94.8 0.0 copy-done.1
  94.8 29.0 %while.10 = (s32[]{:T(128)}, bf16[2,800,2,80]{1,3,2,0:T(8,128)(2,1)S(1)}, bf16[2,800,2,80]{1,3,2,0:T(8,128)(2,1)S(1)}, bf16[1600,2,80]{0,2,1:T(8,128)(2,1)}, bf16[1600,2,80]{0,2,1:T(8,128)(2,1)}, /*index=5*/s32[]{:T(128)}) while((s32[]{:T(128)}, bf16[2,800,2,80]{1,3,2,0:T(8,128)(2,1)S(1)}, bf16[2,800,2,80]{1,3,2,0:T(8,128)(2,1)S(1)}, ...), condition=%wide.region_4.5_spmd, body=%wide.region_1.4_spmd.sunk | while | flops 832129600 | bytes 24159592 | solution.py:40
  94.8 0.0 copy-start.2
  94.8 8.6 %fusion.54 = (f32[2,800]{1,0:T(2,128)S(1)}, f32[2,800,1600]{2,1,0:T(8,128)}) fusion(bf16[1600,2,80]{0,2,1:T(8,128)(2,1)} %get-tuple-element.115, bf16[2,800,2,80]{1,3,2,0:T(8,128)(2,1)S(1)} %get-tuple-element.114, s32[]{:T(128)} %get-tuple-element.106), kind=kOutput, calls=%fused_computation.36.clone.1 | convolution fusion | flops 417281600 | bytes 11045124 | tf_op jit(solution)/shard_map/while/body/eval_jaxpr/sub | solution.py:34
  103.4 0.0 copy-done.2
  103.4 5.9 %fusion.55 = bf16[2,800,2,80]{1,3,2,0:T(8,128)(2,1)S(1)} fusion(bf16[2,800,2,80]{1,3,2,0:T(8,128)(2,1)S(1)} %get-tuple-element.107, s32[]{:T(128)} %get-tuple-element.106, bf16[1600,2,80]{0,2,1:T(8,128)(2,1)S(1)} %copy-done.2, f32[2,800,1600]{2,1,0:T(8,128)} %get-tuple-element.98, f32[2,800]{1,0:T(2,128)S(1)} %get-tuple-element.99), kind=kOutput, calls=%fused_computation.10.clone.1 | convolution fusion | flops 414848000 | bytes 11066372 | tf_op jit(solution)/shard_map/while/body/eval_jaxpr/hqk,khd->qhd/dot_general | solution.py:36
  109.3 0.0 copy-start.2
  109.3 8.6 %fusion.54 = (f32[2,800]{1,0:T(2,128)S(1)}, f32[2,800,1600]{2,1,0:T(8,128)}) fusion(bf16[1600,2,80]{0,2,1:T(8,128)(2,1)} %get-tuple-element.115, bf16[2,800,2,80]{1,3,2,0:T(8,128)(2,1)S(1)} %get-tuple-element.114, s32[]{:T(128)} %get-tuple-element.106), kind=kOutput, calls=%fused_computation.36.clone.1 | convolution fusion | flops 417281600 | bytes 11045124 | tf_op jit(solution)/shard_map/while/body/eval_jaxpr/sub | solution.py:34
  118.0 0.0 copy-done.2
  118.0 5.9 %fusion.55 = bf16[2,800,2,80]{1,3,2,0:T(8,128)(2,1)S(1)} fusion(bf16[2,800,2,80]{1,3,2,0:T(8,128)(2,1)S(1)} %get-tuple-element.107, s32[]{:T(128)} %get-tuple-element.106, bf16[1600,2,80]{0,2,1:T(8,128)(2,1)S(1)} %copy-done.2, f32[2,800,1600]{2,1,0:T(8,128)} %get-tuple-element.98, f32[2,800]{1,0:T(2,128)S(1)} %get-tuple-element.99), kind=kOutput, calls=%fused_computation.10.clone.1 | convolution fusion | flops 414848000 | bytes 11066372 | tf_op jit(solution)/shard_map/while/body/eval_jaxpr/hqk,khd->qhd/dot_general | solution.py:36
  123.8 1.4 copy.23
  125.2 22.7 %all_to_all.33 = bf16[1600,2,80]{2,1,0:T(2,128)(2,1)S(1)} all-to-all(bf16[1600,2,80]{2,1,0:T(2,128)(2,1)S(1)} %bitcast.63), channel_id=1, replica_groups=mesh['win'=8,'tok'=4] {'tok'}, dimensions={0} | all-to-all | bytes 1024000 | tf_op jit(solution)/shard_map/all_to_all | solution.py:61
  147.9 1.8 %copy.22 = bf16[4,400,2,80]{1,3,2,0:T(8,128)(2,1)} copy(bf16[4,400,2,80]{3,2,1,0:T(2,128)(2,1)S(1)} %bitcast.64) | data formatting | bytes 1024000 | tf_op jit(solution)/shard_map/all_to_all | solution.py:61
  149.8 0.0 copy-done
  149.8 2.8 %fusion.27 = bf16[400,1280]{1,0:T(8,128)(2,1)S(1)} fusion(f32[400,1280]{1,0:T(8,128)} %bitcast.61, bf16[400,640]{0,1:T(8,128)(2,1)} %bitcast.67, bf16[640,1280]{1,0:T(8,128)(2,1)S(1)} %copy-done), kind=kOutput, calls=%fused_computation.20 | convolution fusion | flops 656384000 | bytes 5222400 | tf_op jit(solution)/shard_map/dot_general | solution.py:62
  152.5 1.0 slice.23
  153.5 1.5 collective-permute-start.1
  156.4 11.6 %collective-permute-done.1 = bf16[1,10,20,1280]{3,2,1,0:T(8,128)(2,1)S(1)} collective-permute-done((bf16[1,10,20,1280]{3,2,1,0:T(8,128)(2,1)}, bf16[1,10,20,1280]{3,2,1,0:T(8,128)(2,1)S(1)}, u32[]{:S(2)}, u32[]{:S(2)}) %collective-permute-start.1) | collective-permute-done | bytes 512032 | tf_op jit(solution)/shard_map/ppermute | solution.py:14
  168.0 1.5 fusion.30
  (2 shorter events, 0.0 us)
Async XLA Ops:
  0.0 149.8 %copy-start = (bf16[640,1280]{1,0:T(8,128)(2,1)S(1)}, bf16[640,1280]{1,0:T(8,128)(2,1)}, u32[]{:S(2)}) copy-start(bf16[640,1280]{1,0:T(8,128)(2,1)} %param.11) | copy-start | bytes 4915204
  1.2 20.2 %copy-start.3 = (f32[1280]{0:T(1024)S(1)}, f32[1280]{0:T(1024)}, u32[]{:S(2)}) copy-start(f32[1280]{0:T(1024)} %param.9) | copy-start | bytes 15364
  1.3 16.9 %collective-permute-start = (bf16[1,10,20,1280]{3,2,1,0:T(8,128)(2,1)S(1)}, bf16[1,10,20,1280]{3,2,1,0:T(8,128)(2,1)S(1)}, u32[]{:S(2)}, u32[]{:S(2)}) collective-permute-start(bf16[1,10,20,1280]{3,2,1,0:T(8,128)(2,1)S(1)} %slice.15), channel_id=1, source_target_pairs={{16,0},{20,4},{24,8},{28,12},{0,16},{4,20},{8,24},{12,28},{17,1},{... | collective-permute-start | bytes 1536008 | tf_op jit(solution)/shard_map/ppermute | solution.py:14
  33.3 49.7 %all-to-all-start = ((bf16[400,3,4,2,80]{0,4,3,1,2:T(8,128)(2,1)}), bf16[400,3,4,2,80]{0,4,3,1,2:T(8,128)(2,1)}, u32[]{:S(2)}, u32[]{:S(2)}) async-start(bf16[400,3,4,2,80]{0,4,3,1,2:T(8,128)(2,1)} %copy.17), calls=%async_computation | async-start | bytes 3932160 | tf_op jit(solution)/shard_map/all_to_all | solution.py:60
  92.5 2.3 %copy-start.1 = (bf16[2,800,2,80]{1,3,2,0:T(8,128)(2,1)S(1)}, bf16[2,800,2,80]{1,3,2,0:T(8,128)(2,1)}, u32[]{:S(2)}) copy-start(bf16[2,800,2,80]{1,3,2,0:T(8,128)(2,1)} %custom-call) | copy-start | bytes 1536004
  94.8 8.6 %copy-start.2 = (bf16[1600,2,80]{0,2,1:T(8,128)(2,1)S(1)}, bf16[1600,2,80]{0,2,1:T(8,128)(2,1)}, u32[]{:S(2)}) copy-start(bf16[1600,2,80]{0,2,1:T(8,128)(2,1)} %get-tuple-element.116) | copy-start | bytes 1536004 | tf_op jit(solution)/shard_map/while
  109.3 8.6 %copy-start.2 = (bf16[1600,2,80]{0,2,1:T(8,128)(2,1)S(1)}, bf16[1600,2,80]{0,2,1:T(8,128)(2,1)}, u32[]{:S(2)}) copy-start(bf16[1600,2,80]{0,2,1:T(8,128)(2,1)} %get-tuple-element.116) | copy-start | bytes 1536004 | tf_op jit(solution)/shard_map/while
  153.5 14.5 %collective-permute-start.1 = (bf16[1,10,20,1280]{3,2,1,0:T(8,128)(2,1)}, bf16[1,10,20,1280]{3,2,1,0:T(8,128)(2,1)S(1)}, u32[]{:S(2)}, u32[]{:S(2)}) collective-permute-start(bf16[1,10,20,1280]{3,2,1,0:T(8,128)(2,1)} %slice.23), channel_id=1, source_target_pairs={{16,0},{20,4},{24,8},{28,12},{0,16},{4,20},{8,24},{12,28},{17,1},{... | collective-permute-start | bytes 1536008 | tf_op jit(solution)/shard_map/ppermute | solution.py:14
where the time goes:
time: 170 us
  waiting for transfers between devices  66.6 us (39%)
  matrix products  36.4 us (21%)
  local copies, waits for them, and re-layouts  23.9 us (14%)
  blocking collectives  22.7 us (13%)
  starting transfers between devices  9.64 us (6%)
  other arithmetic  6.59 us (4%)
  between operations  3.58 us (2%)
    all_to_all x1, waiting for transfers between devices, shards(): lax.all_to_all(qkv, 'tok', split_axis=2, concat_axis=0, tiled=True)  44.6 us
    all_to_all x1, blocking collectives, shards(): lax.all_to_all(attended, 'tok', split_axis=0, concat_axis=1, tiled=True)  22.7 us
    ppermute x2, waiting for transfers between devices, shifted(): return lax.ppermute(block, axis, route)  22 us
    sub x2, matrix products, one_block(): exponent = jnp.exp(scores - row_top)  17.2 us
    dot_general x2, matrix products, one_block(): jnp.einsum('hqk,khd->qhd', weights, value_rows, preferred_element_type=jn...  11.7 us
    all_to_all x2, local copies, waits for them, and re-layouts, shards(): lax.all_to_all(qkv, 'tok', split_axis=2, concat_axis=0, tiled=True)  8.23 us
    all_to_all x1, starting transfers between devices, shards(): lax.all_to_all(qkv, 'tok', split_axis=2, concat_axis=0, tiled=True)  5.09 us
    dot_general x1, matrix products, shards(): jnp.dot(normed, qkv_weight, preferred_element_type=jnp.float32)  4.71 us
  transfers between devices with their start and end apart: 3, of which 3 were waited for; matrix products, arithmetic and copies ran while one was open for 1% of the time, Pallas kernels for 0%

commit v1 on v0

v1 whole, which is shorter than its diff:
```python
import functools

import jax
import jax.numpy as jnp
from jax import lax
from jax.experimental import pallas as pl
from jax.experimental.pallas import tpu as pltpu
from jax.sharding import PartitionSpec as P

HEADS = 8
HD = 80
LAT_WINDOWS = 4
LANES = 128
SUBLANES = 8
VMEM_BYTES = 48 * 1024 * 1024


def round_up(value, unit):
    return -(-value // unit) * unit


def shifted(block, axis, distance):
    count = lax.axis_size(axis)
    return lax.ppermute(block, axis, [(i, (i + distance) % count) for i in range(count)])


def project(place, tokens, gain, weight, slots, outs, width):
    groups = len(outs)
    count = tokens.shape[0]
    factor = lax.rsqrt(jnp.mean(tokens * tokens, axis=-1, keepdims=True) + 1e-06)
    normed = (tokens * factor * gain[...]).astype(jnp.bfloat16)
    qkv = jnp.dot(normed, weight[...], preferred_element_type=jnp.float32)
    tail = jnp.ones((count, slots.shape[2] - 3 * width), jnp.float32)
    for group in range(groups):
        columns = [
            qkv[:, (kind * groups + group) * width : (kind * groups + group + 1) * width]
            for kind in range(3)
        ]
        slot = lax.rem(group - place[0] + groups, groups)
        slots[slot] = jnp.concatenate(columns + [tail], axis=1).astype(jnp.bfloat16)
    for slot in range(groups):
        outs[slot][...] = slots[slot]


def kept_kernel(split, width, place, field, gain, weight, *refs):
    *outs, slots = refs
    rows, columns, features = field.shape
    tokens = field[...].astype(jnp.float32)[:, split:]
    tokens = tokens.reshape(rows * (columns - split), features)
    project(place, tokens, gain, weight, slots, outs, width)


def mixed_kernel(split, width, place, field, eastern, gain, weight, *refs):
    *outs, slots = refs
    rows, _, features = field.shape
    own = field[...].astype(jnp.float32)[:, :split]
    column = lax.broadcasted_iota(jnp.int32, own.shape, 1)
    tokens = jnp.where(column < place[1], eastern[...].astype(jnp.float32), own)
    project(place, tokens.reshape(rows * split, features), gain, weight, slots, outs, width)


def folded_rows(count, fold):
    return round_up(-(-count // fold), SUBLANES)


def attention_kernel(width, blocks, *refs):
    ins, outs = refs[:blocks], refs[blocks : 2 * blocks]
    held, keys, attended = refs[2 * blocks :]
    start = 0
    for block in ins:
        held[start : start + block.shape[0]] = block[...]
        start += block.shape[0]
    total = start
    span = 2 * LANES
    key_at = width // LANES * LANES
    value_at = 2 * width // LANES * LANES
    keys[...] = held[:, key_at : key_at + span].T
    factor = HD ** (-0.5) * 1.4426950408889634
    step = attended.shape[0] // 10

    def one_step(index, carry):
        at = pl.multiple_of(index * step, 16)
        queries = held[pl.ds(at, step), :span]
        queries = pltpu.roll(queries.astype(jnp.float32), width - key_at, axis=1)
        lane = lax.broadcasted_iota(jnp.int32, queries.shape, 1)
        value_lane = lax.broadcasted_iota(jnp.int32, (step, span), 1)
        result = None
        for head in range(width // HD):
            first = width - key_at + head * HD
            inside = (lane >= first) & (lane < first + HD)
            chosen = jnp.where(inside, queries, 0.0).astype(jnp.bfloat16)
            scores = jnp.dot(chosen, keys[...], preferred_element_type=jnp.float32)
            top = jnp.max(scores, axis=-1, keepdims=True)
            weights = jnp.exp2((scores - top) * factor).astype(jnp.bfloat16)
            mixed = jnp.dot(
                weights, held[:, value_at : value_at + span], preferred_element_type=jnp.float32
            )
            ones_at = 3 * width - value_at
            scaled = mixed / mixed[:, ones_at : ones_at + 1]
            first = 2 * width - value_at + head * HD
            result = scaled if result is None else jnp.where(value_lane < first, result, scaled)
        attended[pl.ds(at, step)] = pltpu.roll(result, span - (2 * width - value_at), axis=1)
        return carry

    lax.fori_loop(0, attended.shape[0] // step, one_step, 0)

    rest = width - LANES
    fold = LANES // rest
    start = 0
    for block, out in zip(ins, outs):
        count = block.shape[0]
        part = folded_rows(count, fold)
        lane = lax.broadcasted_iota(jnp.int32, (part, LANES), 1)
        packed = jnp.zeros((part, LANES), jnp.float32)
        for index in range(fold):
            size = min(part, count - index * part)
            piece = attended[start + index * part : start + index * part + size, LANES:]
            if size < part:
                piece = jnp.concatenate([piece, jnp.zeros((part - size, LANES), jnp.float32)], axis=0)
            if index:
                piece = pltpu.roll(piece, index * rest, axis=1)
            packed = jnp.where(lane // rest == index, piece, packed)
        out[...] = jnp.concatenate(
            [attended[start : start + count, :LANES], packed], axis=0
        ).astype(jnp.bfloat16)
        start += count


def unpack(blocks, count, rest):
    fold = LANES // rest
    part = folded_rows(count, fold)
    mains = [block[:count] for block in blocks]
    lane = lax.broadcasted_iota(jnp.int32, (part, LANES), 1)
    rests = []
    for index in range(fold):
        row = jnp.zeros((part, LANES), jnp.float32)
        for group, block in enumerate(blocks):
            turn = ((group - index) * rest) % LANES
            piece = block[count : count + part]
            piece = pltpu.roll(piece, turn, axis=1) if turn else piece
            row = jnp.where(lane // rest == group, piece, row)
        rests.append(row[: min(part, count - index * part)])
    return jnp.concatenate(mains + [jnp.concatenate(rests, axis=0)], axis=1)


def output_kernel(split, width, groups, place, field, weight, *refs):
    kept, mixed, western = refs[:groups], refs[groups : 2 * groups], refs[2 * groups : 3 * groups]
    out, ordered = refs[3 * groups :]
    rows, columns, features = field.shape
    rest = width - LANES
    fold = LANES // rest
    for slot in range(groups):
        group = lax.rem(place[0] + slot, groups)
        at = pl.multiple_of(group * width, rest)
        ordered[slot * LANES : (slot + 1) * LANES] = weight[pl.ds(at, LANES)]
        at = pl.multiple_of(group * width + LANES, rest)
        first = groups * LANES + slot * rest
        ordered[first : first + rest] = weight[pl.ds(at, rest)]
    tokens = field[...].astype(jnp.float32)

    count = rows * (columns - split)
    blocks = [block[...].astype(jnp.float32) for block in kept]
    attended = unpack(blocks, count, rest).astype(jnp.bfloat16)
    projected = jnp.dot(attended, ordered[...], preferred_element_type=jnp.float32)
    right = tokens[:, split:] + projected.reshape(rows, columns - split, features)

    count = rows * split
    part = folded_rows(count, fold)
    shape = mixed[0].shape
    row = lax.broadcasted_iota(jnp.int32, shape, 0)
    lane = lax.broadcasted_iota(jnp.int32, shape, 1)
    token = jnp.where(row < count, row, row - count + lane // rest * part)
    taken = lax.rem(token, split) < place[1]
    blocks = [
        jnp.where(taken, west[...].astype(jnp.float32), own[...].astype(jnp.float32))
        for own, west in zip(mixed, western)
    ]
    attended = unpack(blocks, count, rest).astype(jnp.bfloat16)
    projected = jnp.dot(attended, ordered[...], preferred_element_type=jnp.float32)
    left = tokens[:, :split] + projected.reshape(rows, split, features)
    out[...] = jnp.concatenate([left, right], axis=1).astype(jnp.bfloat16)


def whole(count):
    return [pl.BlockSpec(memory_space=pltpu.VMEM)] * count


def shards(field_tokens, lon_shift, norm_gain, qkv_weight, out_weight):
    _, rows, columns, features = field_tokens.shape
    groups = lax.axis_size("tok")
    width = HEADS // groups * HD
    padded = round_up(3 * width + 1, LANES)
    split = round_up(columns // 2, SUBLANES)
    latitude = lax.axis_index("win") % LAT_WINDOWS
    offset = lax.dynamic_index_in_dim(lon_shift, latitude, 0, keepdims=False)
    place = jnp.stack([lax.axis_index("tok").astype(jnp.int32), offset])
    field = field_tokens[0]
    gain = norm_gain.reshape(1, features)
    smem = pl.BlockSpec(memory_space=pltpu.SMEM)
    params = pltpu.CompilerParams(vmem_limit_bytes=VMEM_BYTES)

    def projection(kernel, count, *operands):
        block = jax.ShapeDtypeStruct((count, padded), jnp.bfloat16)
        return pl.pallas_call(
            functools.partial(kernel, split, width),
            out_shape=[block] * groups,
            in_specs=[smem] + whole(len(operands) + 2),
            out_specs=whole(groups),
            scratch_shapes=[pltpu.VMEM((groups, count, padded), jnp.bfloat16)],
            compiler_params=params,
            cost_estimate=pl.CostEstimate(
                flops=2 * count * features * 3 * HEADS * HD,
                bytes_accessed=2 * features * (3 * HEADS * HD + 2 * count),
                transcendentals=0,
            ),
        )(place, *operands, gain, qkv_weight)

    def spread(blocks, sign):
        return [blocks[0]] + [
            shifted(blocks[distance], "tok", sign * distance) for distance in range(1, groups)
        ]

    eastern = shifted(field[:, :split], "win", -LAT_WINDOWS)
    kept_count, mixed_count = rows * (columns - split), rows * split
    kept = spread(projection(kept_kernel, kept_count, field), 1)
    mixed = spread(projection(mixed_kernel, mixed_count, field, eastern), 1)

    total = groups * rows * columns
    fold = LANES // (width - LANES)
    packed = [
        jax.ShapeDtypeStruct((count + folded_rows(count, fold), LANES), jnp.bfloat16)
        for count in (kept_count, mixed_count)
        for _ in range(groups)
    ]
    attended = pl.pallas_call(
        functools.partial(attention_kernel, width, 2 * groups),
        out_shape=packed,
        in_specs=whole(2 * groups),
        out_specs=whole(2 * groups),
        scratch_shapes=[
            pltpu.VMEM((total, padded), jnp.bfloat16),
            pltpu.VMEM((2 * LANES, total), jnp.bfloat16),
            pltpu.VMEM((total, 2 * LANES), jnp.float32),
        ],
        compiler_params=params,
        cost_estimate=pl.CostEstimate(
            flops=4 * total * total * width,
            bytes_accessed=2 * total * (padded + width),
            transcendentals=total * total * (width // HD),
        ),
    )(*kept, *mixed)
    mixed_back = spread(attended[groups:], -1)
    western = [shifted(block, "win", LAT_WINDOWS) for block in mixed_back]
    kept_back = spread(attended[:groups], -1)

    result = pl.pallas_call(
        functools.partial(output_kernel, split, width, groups),
        out_shape=jax.ShapeDtypeStruct(field.shape, jnp.bfloat16),
        in_specs=[smem] + whole(2 + 3 * groups),
        out_specs=pl.BlockSpec(memory_space=pltpu.VMEM),
        scratch_shapes=[pltpu.VMEM(out_weight.shape, jnp.bfloat16)],
        compiler_params=params,
        cost_estimate=pl.CostEstimate(
            flops=2 * rows * columns * HEADS * HD * features,
            bytes_accessed=2 * features * (HEADS * HD + 2 * rows * columns),
            transcendentals=0,
        ),
    )(place, field, out_weight, *kept_back, *mixed_back, *western)
    return result[None]


def solution(mesh):
    placed = (P("win", "tok", None, None), P(), P(), P(), P())
    return jax.shard_map(
        shards, mesh=mesh, in_specs=placed, out_specs=P("win", "tok", None, None), check_vma=False
    )
```

time: 170 us -> 95.1 us (0.56)
  matrix products: 36.4 us -> 0 us
  waiting for transfers between devices: 66.6 us -> 33.2 us
  Pallas kernels: 0 us -> 25.7 us
  blocking collectives: 22.7 us -> 0 us
  starting transfers between devices: 9.64 us -> 30.8 us
  local copies, waits for them, and re-layouts: 23.9 us -> 4.28 us
  other arithmetic: 6.59 us -> 0.72 us
  between operations: 3.58 us -> 0.09 us
    all_to_all x1 -> x0, waiting for transfers between devices: 44.6 us -> none  [shards(): lax.all_to_all(qkv, 'tok', split_axis=2, concat_axis=0, tiled=True)]
    ppermute x2 -> x17, starting transfers between devices: 4.55 us -> 30.8 us  [shifted(): lax.ppermute(block, axis, [(i, (i + distance) % count) for i in range(cou...]
    pallas_call x0 -> x4, Pallas kernels: none -> 25.7 us  [the longest x1 15.1 us: shards(): pl.pallas_call(functools.partial(attention_kernel, width, 2 * groups), ou...]
    all_to_all x1 -> x0, blocking collectives: 22.7 us -> none  [shards(): lax.all_to_all(attended, 'tok', split_axis=0, concat_axis=1, tiled=True)]
    dot_general x4 -> x0, matrix products: 19.2 us -> none  [the longest x2 11.7 us: one_block(): jnp.einsum('hqk,khd->qhd', weights, value_rows, preferred_element_type=jn...]
    sub x2 -> x0, matrix products: 17.2 us -> none  [one_block(): exponent = jnp.exp(scores - row_top)]
    ppermute x2 -> x17, waiting for transfers between devices: 22 us -> 33.2 us  [shifted(): lax.ppermute(block, axis, [(i, (i + distance) % count) for i in range(cou...]
    all_to_all x3 -> x0, local copies, waits for them, and re-layouts: 10.1 us -> none  [the longest x2 8.23 us: shards(): lax.all_to_all(qkv, 'tok', split_axis=2, concat_axis=0, tiled=True)]
  transfers between devices with their start and end apart: 3 -> 17, of which waited for: 3 -> 5; matrix products, arithmetic and copies ran while one was open for 1% -> 3% of each run, Pallas kernels for 0% -> 8%
where the time goes in v1:
time: 95.1 us; the launch traced here: 94.8 us
  waiting for transfers between devices  33.2 us (35%)
  starting transfers between devices  30.8 us (32%)
  Pallas kernels  25.7 us (27%)
  local copies, waits for them, and re-layouts  4.28 us (5%)
    ppermute x17, waiting for transfers between devices, shifted(): lax.ppermute(block, axis, [(i, (i + distance) % count) for i in range(cou...  33.2 us
    ppermute x17, starting transfers between devices, shifted(): lax.ppermute(block, axis, [(i, (i + distance) % count) for i in range(cou...  30.8 us
    pallas_call x1, Pallas kernels, shards(): pl.pallas_call(functools.partial(attention_kernel, width, 2 * groups), ou...  15.1 us
    pallas_call x2, Pallas kernels, projection(): pl.pallas_call(functools.partial(kernel, split, width), out_shape=[block]...  8.06 us
    pallas_call x1, Pallas kernels, shards(): pl.pallas_call(functools.partial(output_kernel, split, width, groups), ou...  2.55 us
  transfers between devices with their start and end apart: 17, of which 5 were waited for; matrix products, arithmetic and copies ran while one was open for 3% of the time, Pallas kernels for 8%

profile of v1, /device:TPU:0, one launch (start us, length us, event | category | flops | bytes accessed | tf_op | source)
XLA Modules:
  0.0 94.8 jit_solution(2190448157999989322)
XLA Ops:
  0.0 1.1 %slice.4 = bf16[10,24,1280]{2,1,0:T(8,128)(2,1)S(1)} slice(bf16[10,40,1280]{2,1,0:T(8,128)(2,1)} %bitcast.3), slice={[0:10], [0:24], [0:1280]} | slice | bytes 1228800 | tf_op jit(solution)/shard_map/slice | solution.py:223
  1.1 3.0 %collective-permute-start.3 = (bf16[10,24,1280]{2,1,0:T(8,128)(2,1)S(1)}, bf16[10,24,1280]{2,1,0:T(8,128)(2,1)S(1)}, u32[]{:S(2)}, u32[]{:S(2)}) collective-permute-start(bf16[10,24,1280]{2,1,0:T(8,128)(2,1)S(1)} %slice.4), channel_id=1, source_target_pairs={{0,16},{4,20},{8,24},{12,28},{16,0},{20,4},{24,8},{28,12},{1,17},{... | collective-permute-start | bytes 1843208 | tf_op jit(solution)/shard_map/ppermute | solution.py:24
  4.2 0.7 reshape.3.gain
  4.9 1.2 %dynamic_slice.4 = s32[1]{0:T(128)} dynamic-slice(s32[4]{0:T(128)} %param.6, s32[]{:T(128)S(6)} %select_n.12), dynamic_slice_sizes={1} | dynamic-slice | bytes 12 | tf_op jit(solution)/shard_map/jit(dynamic_index_in_dim)/dynamic_slice | solution.py:195
  6.1 0.7 pad_add_fusion.place
  6.8 0.0 copy-start
  6.8 1.2 %copy-done = bf16[1,10,40,1280]{3,2,1,0:T(8,128)(2,1)S(1)} copy-done((bf16[1,10,40,1280]{3,2,1,0:T(8,128)(2,1)S(1)}, bf16[1,10,40,1280]{3,2,1,0:T(8,128)(2,1)}, u32[]{:S(2)}) %copy-start) | copy-done | bytes 1024024
  8.0 3.7 %shard_map.55 = (bf16[160,512]{1,0:T(8,128)(2,1)S(1)}, bf16[160,512]{1,0:T(8,128)(2,1)S(1)}, bf16[160,512]{1,0:T(8,128)(2,1)S(1)}, bf16[160,512]{1,0:T(8,128)(2,1)S(1)}) custom-call(s32[2]{0:T(128)S(1)} %pad_add_fusion.place, bf16[10,40,1280]{2,1,0:T(8,128)(2,1)S(1)} %bitcast.4, f32[1,1280]{1,0:T(1,128)S(1)} %reshape.3.gain, bf16[1280,1920]{1,0:T(8,128)(2,1)} %weight.4), custom_call_target="tpu_custom_call" | custom-call | flops 786432000 | bytes 5734400 | tf_op jit(solution)/shard_map/pallas_call | solution.py:204
  11.7 1.6 %collective-permute-start = (bf16[160,512]{1,0:T(8,128)(2,1)S(1)}, bf16[160,512]{1,0:T(8,128)(2,1)S(1)}, u32[]{:S(2)}, u32[]{:S(2)}) collective-permute-start(bf16[160,512]{1,0:T(8,128)(2,1)S(1)} %get-tuple-element.22), channel_id=1, source_target_pairs={{0,1},{1,2},{2,3},{3,0},{4,5},{5,6},{6,7},{7,4},{8,9},{9,10},{10,1... | collective-permute-start | bytes 491528 | tf_op jit(solution)/shard_map/ppermute | solution.py:24
  13.4 4.6 %collective-permute-done.3.eastern = bf16[10,24,1280]{2,1,0:T(8,128)(2,1)S(1)} collective-permute-done((bf16[10,24,1280]{2,1,0:T(8,128)(2,1)S(1)}, bf16[10,24,1280]{2,1,0:T(8,128)(2,1)S(1)}, u32[]{:S(2)}, u32[]{:S(2)}) %collective-permute-start.3) | collective-permute-done | bytes 614432 | tf_op jit(solution)/shard_map/ppermute | solution.py:24
  18.0 4.4 %shard_map.56 = (bf16[240,512]{1,0:T(8,128)(2,1)S(1)}, bf16[240,512]{1,0:T(8,128)(2,1)S(1)}, bf16[240,512]{1,0:T(8,128)(2,1)S(1)}, bf16[240,512]{1,0:T(8,128)(2,1)S(1)}) custom-call(s32[2]{0:T(128)S(1)} %pad_add_fusion.place, bf16[10,40,1280]{2,1,0:T(8,128)(2,1)S(1)} %bitcast.5, bf16[10,24,1280]{2,1,0:T(8,128)(2,1)S(1)} %collective-permute-done.3.eastern, ...), custom_call_target="tpu_custom_call" | custom-call | flops 1179648000 | bytes 6144000 | tf_op jit(solution)/shard_map/pallas_call | solution.py:204
  22.4 0.0 copy-start.1
  22.4 0.0 copy-start.2
  22.4 1.8 %collective-permute-start.4 = (bf16[240,512]{1,0:T(8,128)(2,1)S(1)}, bf16[240,512]{1,0:T(8,128)(2,1)S(1)}, u32[]{:S(2)}, u32[]{:S(2)}) collective-permute-start(bf16[240,512]{1,0:T(8,128)(2,1)S(1)} %get-tuple-element.26), channel_id=1, source_target_pairs={{0,1},{1,2},{2,3},{3,0},{4,5},{5,6},{6,7},{7,4},{8,9},{9,10},{10,1... | collective-permute-start | bytes 737288 | tf_op jit(solution)/shard_map/ppermute | solution.py:24
  24.2 2.6 %collective-permute-start.5 = (bf16[240,512]{1,0:T(8,128)(2,1)S(1)}, bf16[240,512]{1,0:T(8,128)(2,1)S(1)}, u32[]{:S(2)}, u32[]{:S(2)}) collective-permute-start(bf16[240,512]{1,0:T(8,128)(2,1)S(1)} %get-tuple-element.27), channel_id=1, source_target_pairs={{0,2},{1,3},{2,0},{3,1},{4,6},{5,7},{6,4},{7,5},{8,10},{9,11},{10,... | collective-permute-start | bytes 737288 | tf_op jit(solution)/shard_map/ppermute | solution.py:24
  26.8 1.3 %collective-permute-start.6 = (bf16[240,512]{1,0:T(8,128)(2,1)S(1)}, bf16[240,512]{1,0:T(8,128)(2,1)S(1)}, u32[]{:S(2)}, u32[]{:S(2)}) collective-permute-start(bf16[240,512]{1,0:T(8,128)(2,1)S(1)} %get-tuple-element.28), channel_id=1, source_target_pairs={{0,3},{1,0},{2,1},{3,2},{4,7},{5,4},{6,5},{7,6},{8,11},{9,8},{10,9... | collective-permute-start | bytes 737288 | tf_op jit(solution)/shard_map/ppermute | solution.py:24
  28.2 0.2 collective-permute-start.1
  28.4 0.0 collective-permute-done.refs_1_
  28.4 2.8 %collective-permute-start.2 = (bf16[160,512]{1,0:T(8,128)(2,1)S(1)}, bf16[160,512]{1,0:T(8,128)(2,1)S(1)}, u32[]{:S(2)}, u32[]{:S(2)}) collective-permute-start(bf16[160,512]{1,0:T(8,128)(2,1)S(1)} %get-tuple-element.24), channel_id=1, source_target_pairs={{0,3},{1,0},{2,1},{3,2},{4,7},{5,4},{6,5},{7,6},{8,11},{9,8},{10,9... | collective-permute-start | bytes 491528 | tf_op jit(solution)/shard_map/ppermute | solution.py:24
  31.2 23.1 %collective-permute-done.1.refs_2_ = bf16[160,512]{1,0:T(8,128)(2,1)S(1)} collective-permute-done((bf16[160,512]{1,0:T(8,128)(2,1)S(1)}, bf16[160,512]{1,0:T(8,128)(2,1)S(1)}, u32[]{:S(2)}, u32[]{:S(2)}) %collective-permute-start.1) | collective-permute-done | bytes 163872 | tf_op jit(solution)/shard_map/ppermute | solution.py:24
  54.4 0.0 collective-permute-done.2.refs_3_
  54.4 0.0 collective-permute-done.4.refs_5_
  54.4 0.0 collective-permute-done.5.refs_6_
  54.4 0.0 collective-permute-done.6.refs_7_
  54.4 15.1 %shard_map.57 = (bf16[200,128]{1,0:T(8,128)(2,1)S(1)}, bf16[200,128]{1,0:T(8,128)(2,1)S(1)}, bf16[200,128]{1,0:T(8,128)(2,1)S(1)}, bf16[200,128]{1,0:T(8,128)(2,...) custom-call(bf16[160,512]{1,0:T(8,128)(2,1)S(1)} %get-tuple-element., ...), custom_call_target="tpu_custom_call" | custom-call | flops 1638400000 | bytes 2150400 | tf_op jit(solution)/shard_map/pallas_call | solution.py:235
  69.5 5.0 %collective-permute-start.10 = (bf16[304,128]{1,0:T(8,128)(2,1)S(1)}, bf16[304,128]{1,0:T(8,128)(2,1)S(1)}, u32[]{:S(2)}, u32[]{:S(2)}) collective-permute-start(bf16[304,128]{1,0:T(8,128)(2,1)S(1)} %get-tuple-element.34), channel_id=1, source_target_pairs={{0,3},{1,0},{2,1},{3,2},{4,7},{5,4},{6,5},{7,6},{8,11},{9,8},{10,9... | collective-permute-start | bytes 233480 | tf_op jit(solution)/shard_map/ppermute | solution.py:24
  74.5 0.5 collective-permute-start.11
  75.0 0.2 collective-permute-start.12
  75.1 3.7 %collective-permute-start.7 = (bf16[200,128]{1,0:T(8,128)(2,1)S(1)}, bf16[200,128]{1,0:T(8,128)(2,1)S(1)}, u32[]{:S(2)}, u32[]{:S(2)}) collective-permute-start(bf16[200,128]{1,0:T(8,128)(2,1)S(1)} %get-tuple-element.30), channel_id=1, source_target_pairs={{0,3},{1,0},{2,1},{3,2},{4,7},{5,4},{6,5},{7,6},{8,11},{9,8},{10,9... | collective-permute-start | bytes 153608 | tf_op jit(solution)/shard_map/ppermute | solution.py:24
  78.8 0.6 collective-permute-start.8
  79.4 1.2 %collective-permute-done.7.refs_1_ = bf16[200,128]{1,0:T(8,128)(2,1)S(1)} collective-permute-done((bf16[200,128]{1,0:T(8,128)(2,1)S(1)}, bf16[200,128]{1,0:T(8,128)(2,1)S(1)}, u32[]{:S(2)}, u32[]{:S(2)}) %collective-permute-start.7) | collective-permute-done | bytes 51232 | tf_op jit(solution)/shard_map/ppermute | solution.py:24
  80.7 1.5 %collective-permute-start.13 = (bf16[304,128]{1,0:T(8,128)(2,1)S(1)}, bf16[304,128]{1,0:T(8,128)(2,1)S(1)}, u32[]{:S(2)}, u32[]{:S(2)}) collective-permute-start(bf16[304,128]{1,0:T(8,128)(2,1)S(1)} %get-tuple-element.33.refs_4_), channel_id=1, source_target_pairs={{0,16},{4,20},{8,24},{12,28},{16,0},{20,4},{24,8},{28,12},{1,17},{... | collective-permute-start | bytes 233480 | tf_op jit(solution)/shard_map/ppermute | solution.py:24
  82.2 0.0 collective-permute-done.10.refs_5_
  82.2 0.5 collective-permute-start.14
  82.7 1.6 %collective-permute-done.11.refs_6_ = bf16[304,128]{1,0:T(8,128)(2,1)S(1)} collective-permute-done((bf16[304,128]{1,0:T(8,128)(2,1)S(1)}, bf16[304,128]{1,0:T(8,128)(2,1)S(1)}, u32[]{:S(2)}, u32[]{:S(2)}) %collective-permute-start.11) | collective-permute-done | bytes 77856 | tf_op jit(solution)/shard_map/ppermute | solution.py:24
  84.3 1.5 %collective-permute-start.15 = (bf16[304,128]{1,0:T(8,128)(2,1)S(1)}, bf16[304,128]{1,0:T(8,128)(2,1)S(1)}, u32[]{:S(2)}, u32[]{:S(2)}) collective-permute-start(bf16[304,128]{1,0:T(8,128)(2,1)S(1)} %collective-permute-done.11.refs_6_), channel_id=1, source_target_pairs={{0,16},{4,20},{8,24},{12,28},{16,0},{20,4},{24,8},{28,12},{1,17},{... | collective-permute-start | bytes 233480 | tf_op jit(solution)/shard_map/ppermute | solution.py:24
  85.8 0.0 collective-permute-done.12.refs_7_
  85.8 0.5 collective-permute-start.16
  86.3 0.0 collective-permute-done.8.refs_2_
  86.3 3.3 %collective-permute-start.9 = (bf16[200,128]{1,0:T(8,128)(2,1)S(1)}, bf16[200,128]{1,0:T(8,128)(2,1)S(1)}, u32[]{:S(2)}, u32[]{:S(2)}) collective-permute-start(bf16[200,128]{1,0:T(8,128)(2,1)S(1)} %get-tuple-element.32), channel_id=1, source_target_pairs={{0,1},{1,2},{2,3},{3,0},{4,5},{5,6},{6,7},{7,4},{8,9},{9,10},{10,1... | collective-permute-start | bytes 153608 | tf_op jit(solution)/shard_map/ppermute | solution.py:24
  89.6 2.6 %collective-permute-done.9.refs_3_ = bf16[200,128]{1,0:T(8,128)(2,1)S(1)} collective-permute-done((bf16[200,128]{1,0:T(8,128)(2,1)S(1)}, bf16[200,128]{1,0:T(8,128)(2,1)S(1)}, u32[]{:S(2)}, u32[]{:S(2)}) %collective-permute-start.9) | collective-permute-done | bytes 51232 | tf_op jit(solution)/shard_map/ppermute | solution.py:24
  92.2 0.0 collective-permute-done.13.refs_8_
  92.2 0.0 collective-permute-done.14.refs_9_
  92.2 0.0 collective-permute-done.15.refs_10_
  92.2 0.0 collective-permute-done.16.refs_11_
  92.2 0.0 copy-done.1
  92.2 0.0 copy-done.2
  92.3 2.5 %shard_map.58 = bf16[10,40,1280]{2,1,0:T(8,128)(2,1)} custom-call(s32[2]{0:T(128)S(1)} %pad_add_fusion.place, bf16[10,40,1280]{2,1,0:T(8,128)(2,1)S(1)} %bitcast.6, bf16[640,1280]{1,0:T(8,128)(2,1)S(1)} %copy-done.2, bf16[200,128]{1,0:T(8,128)(2,1)S(1)} %get-tuple-element.29.refs_0_, bf16[200,128]{1,0:T(8,128)(2,1)S(1)} %collective-permute-done.7.refs_1_, ...), custom_call_target="tpu_custom_call" | custom-call | flops 655360000 | bytes 3686400 | tf_op jit(solution)/shard_map/pallas_call | solution.py:256
Async XLA Ops:
  1.1 16.9 %collective-permute-start.3 = (bf16[10,24,1280]{2,1,0:T(8,128)(2,1)S(1)}, bf16[10,24,1280]{2,1,0:T(8,128)(2,1)S(1)}, u32[]{:S(2)}, u32[]{:S(2)}) collective-permute-start(bf16[10,24,1280]{2,1,0:T(8,128)(2,1)S(1)} %slice.4), channel_id=1, source_target_pairs={{0,16},{4,20},{8,24},{12,28},{16,0},{20,4},{24,8},{28,12},{1,17},{... | collective-permute-start | bytes 1843208 | tf_op jit(solution)/shard_map/ppermute | solution.py:24
  6.8 1.2 %copy-start = (bf16[1,10,40,1280]{3,2,1,0:T(8,128)(2,1)S(1)}, bf16[1,10,40,1280]{3,2,1,0:T(8,128)(2,1)}, u32[]{:S(2)}) copy-start(bf16[1,10,40,1280]{3,2,1,0:T(8,128)(2,1)} %param.5) | copy-start | bytes 3072004
  11.7 16.7 %collective-permute-start = (bf16[160,512]{1,0:T(8,128)(2,1)S(1)}, bf16[160,512]{1,0:T(8,128)(2,1)S(1)}, u32[]{:S(2)}, u32[]{:S(2)}) collective-permute-start(bf16[160,512]{1,0:T(8,128)(2,1)S(1)} %get-tuple-element.22), channel_id=1, source_target_pairs={{0,1},{1,2},{2,3},{3,0},{4,5},{5,6},{6,7},{7,4},{8,9},{9,10},{10,1... | collective-permute-start | bytes 491528 | tf_op jit(solution)/shard_map/ppermute | solution.py:24
  22.4 69.9 %copy-start.1 = (bf16[1,10,40,1280]{3,2,1,0:T(8,128)(2,1)S(1)}, bf16[1,10,40,1280]{3,2,1,0:T(8,128)(2,1)}, u32[]{:S(2)}) copy-start(bf16[1,10,40,1280]{3,2,1,0:T(8,128)(2,1)} %param.5) | copy-start | bytes 3072004
  22.4 69.9 %copy-start.2 = (bf16[640,1280]{1,0:T(8,128)(2,1)S(1)}, bf16[640,1280]{1,0:T(8,128)(2,1)}, u32[]{:S(2)}) copy-start(bf16[640,1280]{1,0:T(8,128)(2,1)} %weight.5) | copy-start | bytes 4915204
  22.4 32.0 %collective-permute-start.4 = (bf16[240,512]{1,0:T(8,128)(2,1)S(1)}, bf16[240,512]{1,0:T(8,128)(2,1)S(1)}, u32[]{:S(2)}, u32[]{:S(2)}) collective-permute-start(bf16[240,512]{1,0:T(8,128)(2,1)S(1)} %get-tuple-element.26), channel_id=1, source_target_pairs={{0,1},{1,2},{2,3},{3,0},{4,5},{5,6},{6,7},{7,4},{8,9},{9,10},{10,1... | collective-permute-start | bytes 737288 | tf_op jit(solution)/shard_map/ppermute | solution.py:24
  24.2 30.2 %collective-permute-start.5 = (bf16[240,512]{1,0:T(8,128)(2,1)S(1)}, bf16[240,512]{1,0:T(8,128)(2,1)S(1)}, u32[]{:S(2)}, u32[]{:S(2)}) collective-permute-start(bf16[240,512]{1,0:T(8,128)(2,1)S(1)} %get-tuple-element.27), channel_id=1, source_target_pairs={{0,2},{1,3},{2,0},{3,1},{4,6},{5,7},{6,4},{7,5},{8,10},{9,11},{10,... | collective-permute-start | bytes 737288 | tf_op jit(solution)/shard_map/ppermute | solution.py:24
  26.8 27.6 %collective-permute-start.6 = (bf16[240,512]{1,0:T(8,128)(2,1)S(1)}, bf16[240,512]{1,0:T(8,128)(2,1)S(1)}, u32[]{:S(2)}, u32[]{:S(2)}) collective-permute-start(bf16[240,512]{1,0:T(8,128)(2,1)S(1)} %get-tuple-element.28), channel_id=1, source_target_pairs={{0,3},{1,0},{2,1},{3,2},{4,7},{5,4},{6,5},{7,6},{8,11},{9,8},{10,9... | collective-permute-start | bytes 737288 | tf_op jit(solution)/shard_map/ppermute | solution.py:24
  28.2 26.2 %collective-permute-start.1 = (bf16[160,512]{1,0:T(8,128)(2,1)S(1)}, bf16[160,512]{1,0:T(8,128)(2,1)S(1)}, u32[]{:S(2)}, u32[]{:S(2)}) collective-permute-start(bf16[160,512]{1,0:T(8,128)(2,1)S(1)} %get-tuple-element.23), channel_id=1, source_target_pairs={{0,2},{1,3},{2,0},{3,1},{4,6},{5,7},{6,4},{7,5},{8,10},{9,11},{10,... | collective-permute-start | bytes 491528 | tf_op jit(solution)/shard_map/ppermute | solution.py:24
  28.4 26.0 %collective-permute-start.2 = (bf16[160,512]{1,0:T(8,128)(2,1)S(1)}, bf16[160,512]{1,0:T(8,128)(2,1)S(1)}, u32[]{:S(2)}, u32[]{:S(2)}) collective-permute-start(bf16[160,512]{1,0:T(8,128)(2,1)S(1)} %get-tuple-element.24), channel_id=1, source_target_pairs={{0,3},{1,0},{2,1},{3,2},{4,7},{5,4},{6,5},{7,6},{8,11},{9,8},{10,9... | collective-permute-start | bytes 491528 | tf_op jit(solution)/shard_map/ppermute | solution.py:24
  69.5 12.7 %collective-permute-start.10 = (bf16[304,128]{1,0:T(8,128)(2,1)S(1)}, bf16[304,128]{1,0:T(8,128)(2,1)S(1)}, u32[]{:S(2)}, u32[]{:S(2)}) collective-permute-start(bf16[304,128]{1,0:T(8,128)(2,1)S(1)} %get-tuple-element.34), channel_id=1, source_target_pairs={{0,3},{1,0},{2,1},{3,2},{4,7},{5,4},{6,5},{7,6},{8,11},{9,8},{10,9... | collective-permute-start | bytes 233480 | tf_op jit(solution)/shard_map/ppermute | solution.py:24
  74.5 9.8 %collective-permute-start.11 = (bf16[304,128]{1,0:T(8,128)(2,1)S(1)}, bf16[304,128]{1,0:T(8,128)(2,1)S(1)}, u32[]{:S(2)}, u32[]{:S(2)}) collective-permute-start(bf16[304,128]{1,0:T(8,128)(2,1)S(1)} %get-tuple-element.35), channel_id=1, source_target_pairs={{0,2},{1,3},{2,0},{3,1},{4,6},{5,7},{6,4},{7,5},{8,10},{9,11},{10,... | collective-permute-start | bytes 233480 | tf_op jit(solution)/shard_map/ppermute | solution.py:24
  75.0 10.8 %collective-permute-start.12 = (bf16[304,128]{1,0:T(8,128)(2,1)S(1)}, bf16[304,128]{1,0:T(8,128)(2,1)S(1)}, u32[]{:S(2)}, u32[]{:S(2)}) collective-permute-start(bf16[304,128]{1,0:T(8,128)(2,1)S(1)} %get-tuple-element.36), channel_id=1, source_target_pairs={{0,1},{1,2},{2,3},{3,0},{4,5},{5,6},{6,7},{7,4},{8,9},{9,10},{10,1... | collective-permute-start | bytes 233480 | tf_op jit(solution)/shard_map/ppermute | solution.py:24
  75.1 5.5 %collective-permute-start.7 = (bf16[200,128]{1,0:T(8,128)(2,1)S(1)}, bf16[200,128]{1,0:T(8,128)(2,1)S(1)}, u32[]{:S(2)}, u32[]{:S(2)}) collective-permute-start(bf16[200,128]{1,0:T(8,128)(2,1)S(1)} %get-tuple-element.30), channel_id=1, source_target_pairs={{0,3},{1,0},{2,1},{3,2},{4,7},{5,4},{6,5},{7,6},{8,11},{9,8},{10,9... | collective-permute-start | bytes 153608 | tf_op jit(solution)/shard_map/ppermute | solution.py:24
  78.8 7.5 %collective-permute-start.8 = (bf16[200,128]{1,0:T(8,128)(2,1)S(1)}, bf16[200,128]{1,0:T(8,128)(2,1)S(1)}, u32[]{:S(2)}, u32[]{:S(2)}) collective-permute-start(bf16[200,128]{1,0:T(8,128)(2,1)S(1)} %get-tuple-element.31), channel_id=1, source_target_pairs={{0,2},{1,3},{2,0},{3,1},{4,6},{5,7},{6,4},{7,5},{8,10},{9,11},{10,... | collective-permute-start | bytes 153608 | tf_op jit(solution)/shard_map/ppermute | solution.py:24
  80.7 11.5 %collective-permute-start.13 = (bf16[304,128]{1,0:T(8,128)(2,1)S(1)}, bf16[304,128]{1,0:T(8,128)(2,1)S(1)}, u32[]{:S(2)}, u32[]{:S(2)}) collective-permute-start(bf16[304,128]{1,0:T(8,128)(2,1)S(1)} %get-tuple-element.33.refs_4_), channel_id=1, source_target_pairs={{0,16},{4,20},{8,24},{12,28},{16,0},{20,4},{24,8},{28,12},{1,17},{... | collective-permute-start | bytes 233480 | tf_op jit(solution)/shard_map/ppermute | solution.py:24
  82.2 10.0 %collective-permute-start.14 = (bf16[304,128]{1,0:T(8,128)(2,1)S(1)}, bf16[304,128]{1,0:T(8,128)(2,1)S(1)}, u32[]{:S(2)}, u32[]{:S(2)}) collective-permute-start(bf16[304,128]{1,0:T(8,128)(2,1)S(1)} %collective-permute-done.10.refs_5_), channel_id=1, source_target_pairs={{0,16},{4,20},{8,24},{12,28},{16,0},{20,4},{24,8},{28,12},{1,17},{... | collective-permute-start | bytes 233480 | tf_op jit(solution)/shard_map/ppermute | solution.py:24
  84.3 8.0 %collective-permute-start.15 = (bf16[304,128]{1,0:T(8,128)(2,1)S(1)}, bf16[304,128]{1,0:T(8,128)(2,1)S(1)}, u32[]{:S(2)}, u32[]{:S(2)}) collective-permute-start(bf16[304,128]{1,0:T(8,128)(2,1)S(1)} %collective-permute-done.11.refs_6_), channel_id=1, source_target_pairs={{0,16},{4,20},{8,24},{12,28},{16,0},{20,4},{24,8},{28,12},{1,17},{... | collective-permute-start | bytes 233480 | tf_op jit(solution)/shard_map/ppermute | solution.py:24
  85.8 6.5 %collective-permute-start.16 = (bf16[304,128]{1,0:T(8,128)(2,1)S(1)}, bf16[304,128]{1,0:T(8,128)(2,1)S(1)}, u32[]{:S(2)}, u32[]{:S(2)}) collective-permute-start(bf16[304,128]{1,0:T(8,128)(2,1)S(1)} %collective-permute-done.12.refs_7_), channel_id=1, source_target_pairs={{0,16},{4,20},{8,24},{12,28},{16,0},{20,4},{24,8},{28,12},{1,17},{... | collective-permute-start | bytes 233480 | tf_op jit(solution)/shard_map/ppermute | solution.py:24
  86.3 5.9 %collective-permute-start.9 = (bf16[200,128]{1,0:T(8,128)(2,1)S(1)}, bf16[200,128]{1,0:T(8,128)(2,1)S(1)}, u32[]{:S(2)}, u32[]{:S(2)}) collective-permute-start(bf16[200,128]{1,0:T(8,128)(2,1)S(1)} %get-tuple-element.32), channel_id=1, source_target_pairs={{0,1},{1,2},{2,3},{3,0},{4,5},{5,6},{6,7},{7,4},{8,9},{9,10},{10,1... | collective-permute-start | bytes 153608 | tf_op jit(solution)/shard_map/ppermute | solution.py:24

commit v2 on v1

v2 whole, which is shorter than its diff:
```python
import functools

import jax
import jax.numpy as jnp
from jax import lax
from jax.experimental import pallas as pl
from jax.experimental.pallas import tpu as pltpu
from jax.sharding import PartitionSpec as P

HEADS = 8
HD = 80
LAT_WINDOWS = 4
LANES = 128
SUBLANES = 8
VMEM_BYTES = 48 * 1024 * 1024


def round_up(value, unit):
    return -(-value // unit) * unit


def shifted(block, axis, distance):
    count = lax.axis_size(axis)
    return lax.ppermute(block, axis, [(i, (i + distance) % count) for i in range(count)])


def column_offset(lon_shift):
    return lon_shift[lax.rem(lax.axis_index("win"), LAT_WINDOWS)]


def project(tokens, gain, weight, slots, outs):
    local = HEADS // slots.shape[0]
    groups = slots.shape[0]
    count, features = tokens.shape
    span = slots.shape[2] // local
    factor = lax.rsqrt(jnp.mean(tokens * tokens, axis=-1, keepdims=True) + 1e-06)
    normed = (tokens * factor * gain[...].reshape(1, features)).astype(jnp.bfloat16)
    qkv = jnp.dot(normed, weight[...], preferred_element_type=jnp.float32)
    tail = jnp.ones((count, span - 3 * HD), jnp.float32)
    place = lax.axis_index("tok")
    for group in range(groups):
        slot = lax.rem(group - place + groups, groups)
        columns = []
        for head in range(group * local, (group + 1) * local):
            columns += [
                qkv[:, (kind * HEADS + head) * HD : (kind * HEADS + head + 1) * HD]
                for kind in range(3)
            ] + [tail]
        slots[slot] = jnp.concatenate(columns, axis=1).astype(jnp.bfloat16)
    parts = len(outs) // groups
    for index, out in enumerate(outs):
        first = index // groups * out.shape[1]
        out[...] = slots[index % groups, :, first : first + out.shape[1]]


def kept_kernel(split, field, gain, weight, *refs):
    *outs, slots = refs
    rows, columns, features = field.shape
    tokens = field[...].astype(jnp.float32)[:, split:]
    project(tokens.reshape(rows * (columns - split), features), gain, weight, slots, outs)


def mixed_kernel(split, lon_shift, field, eastern, gain, weight, *refs):
    *outs, slots = refs
    rows, _, features = field.shape
    own = field[...].astype(jnp.float32)[:, :split]
    column = lax.broadcasted_iota(jnp.int32, own.shape, 1)
    tokens = jnp.where(column < column_offset(lon_shift), eastern[...].astype(jnp.float32), own)
    project(tokens.reshape(rows * split, features), gain, weight, slots, outs)


def folded_rows(count, fold):
    return round_up(-(-count // fold), SUBLANES)


def attend(head, kept, mixed, held, keys, scores, weights, attended):
    span = held.shape[1]
    start = 0
    for block in kept:
        held[start : start + block.shape[0]] = block[:, head * span : (head + 1) * span]
        start += block.shape[0]
    for block in mixed:
        held[start : start + block.shape[0]] = block[...]
        start += block.shape[0]
    keys[...] = held[...].T
    factor = HD ** (-0.5) * 1.4426950408889634
    step = scores[0].shape[0]
    chunk = 16

    def score(index, out):
        queries = held[index * step : (index + 1) * step].astype(jnp.float32)
        queries = pltpu.roll(queries, HD, axis=1)
        lane = lax.broadcasted_iota(jnp.int32, queries.shape, 1)
        queries = jnp.where((lane >= HD) & (lane < 2 * HD), queries, 0.0).astype(jnp.bfloat16)
        out[...] = jnp.dot(queries, keys[...], preferred_element_type=jnp.float32)

    steps = start // step
    score(0, scores[0])
    for index in range(steps):
        if index + 1 < steps:
            score(index + 1, scores[(index + 1) % 2])
        now, out = scores[index % 2], weights[index % 2]
        for first in range(0, step, chunk):
            part = now[first : first + chunk]
            top = jnp.max(part, axis=-1, keepdims=True)
            out[first : first + chunk] = jnp.exp2((part - top) * factor).astype(jnp.bfloat16)
        mixed_values = jnp.dot(out[...], held[...], preferred_element_type=jnp.float32)
        scaled = mixed_values / mixed_values[:, 3 * HD : 3 * HD + 1]
        attended[index * step : (index + 1) * step] = pltpu.roll(scaled, span - 2 * HD, axis=1)[
            :, :LANES
        ]


def first_head_kernel(groups, *refs):
    kept, mixed, out = refs[:groups], refs[groups : 2 * groups], refs[2 * groups]
    held, keys, *rest = refs[2 * groups + 1 :]
    attend(0, kept, mixed, held, keys, rest[:2], rest[2:4], rest[4])
    out[...] = rest[4][...].astype(jnp.bfloat16)


def second_head_kernel(groups, width, *refs):
    kept, mixed, other = refs[:groups], refs[groups : 2 * groups], refs[2 * groups]
    outs = refs[2 * groups + 1 : 4 * groups + 1]
    held, keys, *scratch = refs[4 * groups + 1 :]
    attended = scratch[4]
    attend(1, kept, mixed, held, keys, scratch[:2], scratch[2:4], attended)
    rest = width - LANES
    fold = LANES // rest
    start = 0
    for block, out in zip((*kept, *mixed), outs):
        count = block.shape[0]
        part = folded_rows(count, fold)
        lane = lax.broadcasted_iota(jnp.int32, (count, LANES), 1)
        second = pltpu.roll(attended[start : start + count], HD, axis=1)
        main = jnp.where(lane < HD, other[start : start + count].astype(jnp.float32), second)
        ends = attended[start : start + count]
        lane = lax.broadcasted_iota(jnp.int32, (part, LANES), 1)
        packed = jnp.zeros((part, LANES), jnp.float32)
        for index in range(fold):
            size = min(part, count - index * part)
            piece = ends[index * part : index * part + size]
            if size < part:
                piece = jnp.concatenate([piece, jnp.zeros((part - size, LANES), jnp.float32)], axis=0)
            piece = pltpu.roll(piece, (index * rest + HD) % LANES, axis=1)
            packed = jnp.where(lane // rest == index, piece, packed)
        out[...] = jnp.concatenate([main, packed], axis=0).astype(jnp.bfloat16)
        start += count


def unpack(blocks, count, rest):
    fold = LANES // rest
    part = folded_rows(count, fold)
    mains = [block[:count] for block in blocks]
    lane = lax.broadcasted_iota(jnp.int32, (part, LANES), 1)
    rests = []
    for index in range(fold):
        row = jnp.zeros((part, LANES), jnp.float32)
        for group, block in enumerate(blocks):
            turn = ((group - index) * rest) % LANES
            piece = block[count : count + part]
            piece = pltpu.roll(piece, turn, axis=1) if turn else piece
            row = jnp.where(lane // rest == group, piece, row)
        rests.append(row[: min(part, count - index * part)])
    return jnp.concatenate(mains + [jnp.concatenate(rests, axis=0)], axis=1)


def output_kernel(split, width, groups, lon_shift, field, weight, *refs):
    kept, mixed, western = refs[:groups], refs[groups : 2 * groups], refs[2 * groups : 3 * groups]
    out, ordered = refs[3 * groups :]
    rows, columns, features = field.shape
    rest = width - LANES
    fold = LANES // rest
    for slot in range(groups):
        group = lax.rem(lax.axis_index("tok") + slot, groups)
        at = pl.multiple_of(group * width, rest)
        ordered[slot * LANES : (slot + 1) * LANES] = weight[pl.ds(at, LANES)]
        at = pl.multiple_of(group * width + LANES, rest)
        first = groups * LANES + slot * rest
        ordered[first : first + rest] = weight[pl.ds(at, rest)]
    tokens = field[...].astype(jnp.float32)

    count = rows * (columns - split)
    blocks = [block[...].astype(jnp.float32) for block in kept]
    attended = unpack(blocks, count, rest).astype(jnp.bfloat16)
    projected = jnp.dot(attended, ordered[...], preferred_element_type=jnp.float32)
    right = tokens[:, split:] + projected.reshape(rows, columns - split, features)

    count = rows * split
    part = folded_rows(count, fold)
    shape = mixed[0].shape
    row = lax.broadcasted_iota(jnp.int32, shape, 0)
    lane = lax.broadcasted_iota(jnp.int32, shape, 1)
    token = jnp.where(row < count, row, row - count + lane // rest * part)
    taken = lax.rem(token, split) < column_offset(lon_shift)
    blocks = [
        jnp.where(taken, west[...].astype(jnp.float32), own[...].astype(jnp.float32))
        for own, west in zip(mixed, western)
    ]
    attended = unpack(blocks, count, rest).astype(jnp.bfloat16)
    projected = jnp.dot(attended, ordered[...], preferred_element_type=jnp.float32)
    left = tokens[:, :split] + projected.reshape(rows, split, features)
    out[...] = jnp.concatenate([left, right], axis=1).astype(jnp.bfloat16)


def whole(count):
    return [pl.BlockSpec(memory_space=pltpu.VMEM)] * count


def shards(field_tokens, lon_shift, norm_gain, qkv_weight, out_weight):
    _, rows, columns, features = field_tokens.shape
    groups = lax.axis_size("tok")
    local = HEADS // groups
    width = local * HD
    span = round_up(3 * HD + 1, LANES)
    split = round_up(columns // 2, SUBLANES)
    field = field_tokens[0]
    smem = pl.BlockSpec(memory_space=pltpu.SMEM)
    params = pltpu.CompilerParams(vmem_limit_bytes=VMEM_BYTES)
    kept_count, mixed_count = rows * (columns - split), rows * split

    def projection(kernel, count, parts, scalars, operands):
        block = jax.ShapeDtypeStruct((count, local * span // parts), jnp.bfloat16)
        return pl.pallas_call(
            functools.partial(kernel, split),
            out_shape=[block] * (parts * groups),
            in_specs=[smem] * len(scalars) + whole(len(operands) + 2),
            out_specs=whole(parts * groups),
            scratch_shapes=[pltpu.VMEM((groups, count, local * span), jnp.bfloat16)],
            compiler_params=params,
            cost_estimate=pl.CostEstimate(
                flops=2 * count * features * 3 * HEADS * HD,
                bytes_accessed=2 * features * (3 * HEADS * HD + 2 * count),
                transcendentals=0,
            ),
        )(*scalars, *operands, norm_gain, qkv_weight)

    def spread(blocks, sign):
        return [blocks[0]] + [
            shifted(blocks[distance], "tok", sign * distance) for distance in range(1, groups)
        ]

    eastern = shifted(field[:, :split], "win", -LAT_WINDOWS)
    kept = spread(projection(kept_kernel, kept_count, 1, [], [field]), 1)
    mixed = projection(mixed_kernel, mixed_count, local, [lon_shift], [field, eastern])
    first_mixed, second_mixed = spread(mixed[:groups], 1), spread(mixed[groups:], 1)

    total = groups * rows * columns
    step = total // 5
    fold = LANES // (width - LANES)
    packed = [
        jax.ShapeDtypeStruct((count + folded_rows(count, fold), LANES), jnp.bfloat16)
        for count in (kept_count, mixed_count)
        for _ in range(groups)
    ]

    def attention(kernel, out_shape, *operands):
        return pl.pallas_call(
            kernel,
            out_shape=out_shape,
            in_specs=whole(len(operands)),
            out_specs=whole(len(out_shape)),
            scratch_shapes=[
                pltpu.VMEM((total, span), jnp.bfloat16),
                pltpu.VMEM((span, total), jnp.bfloat16),
                pltpu.VMEM((step, total), jnp.float32),
                pltpu.VMEM((step, total), jnp.float32),
                pltpu.VMEM((step, total), jnp.bfloat16),
                pltpu.VMEM((step, total), jnp.bfloat16),
                pltpu.VMEM((total, LANES), jnp.float32),
            ],
            compiler_params=params,
            cost_estimate=pl.CostEstimate(
                flops=4 * total * total * span,
                bytes_accessed=2 * total * (span + LANES),
                transcendentals=total * total,
            ),
        )(*operands)

    (other,) = attention(
        functools.partial(first_head_kernel, groups),
        [jax.ShapeDtypeStruct((total, LANES), jnp.bfloat16)],
        *kept,
        *first_mixed,
    )
    attended = attention(
        functools.partial(second_head_kernel, groups, width), packed, *kept, *second_mixed, other
    )
    mixed_back = spread(attended[groups:], -1)
    western = [shifted(block, "win", LAT_WINDOWS) for block in mixed_back]
    kept_back = spread(attended[:groups], -1)

    result = pl.pallas_call(
        functools.partial(output_kernel, split, width, groups),
        out_shape=jax.ShapeDtypeStruct(field.shape, jnp.bfloat16),
        in_specs=[smem] + whole(2 + 3 * groups),
        out_specs=pl.BlockSpec(memory_space=pltpu.VMEM),
        scratch_shapes=[pltpu.VMEM(out_weight.shape, jnp.bfloat16)],
        compiler_params=params,
        cost_estimate=pl.CostEstimate(
            flops=2 * rows * columns * HEADS * HD * features,
            bytes_accessed=2 * features * (HEADS * HD + 2 * rows * columns),
            transcendentals=0,
        ),
    )(lon_shift, field, out_weight, *kept_back, *mixed_back, *western)
    return result[None]


def solution(mesh):
    placed = (P("win", "tok", None, None), P(), P(), P(), P())
    return jax.shard_map(
        shards, mesh=mesh, in_specs=placed, out_specs=P("win", "tok", None, None), check_vma=False
    )
```

time: 95.1 us -> 75.5 us (0.79)
  waiting for transfers between devices: 33.2 us -> 12.8 us
  starting transfers between devices: 30.8 us -> 40.2 us
  Pallas kernels: 25.7 us -> 19.2 us
  local copies, waits for them, and re-layouts: 4.28 us -> 3.05 us
    ppermute x17 -> x20, waiting for transfers between devices: 33.2 us -> 12.8 us  [shifted(): lax.ppermute(block, axis, [(i, (i + distance) % count) for i in range(cou...]
    ppermute x17 -> x20, starting transfers between devices: 30.8 us -> 40.2 us  [shifted(): lax.ppermute(block, axis, [(i, (i + distance) % count) for i in range(cou...]
    pallas_call x3 -> x4, Pallas kernels: 23.1 us -> 16.6 us  [the longest x2 8.47 us: attention(): pl.pallas_call(kernel, out_shape=out_shape, in_specs=whole(len(operands))...]
    dynamic_slice x1 -> x0, local copies, waits for them, and re-layouts: 1.24 us -> none  [shards(): offset = lax.dynamic_index_in_dim(lon_shift, latitude, 0, keepdims=False)]
    unnamed x6 -> x10, local copies, waits for them, and re-layouts: 1.23 us -> 1.92 us
  transfers between devices with their start and end apart: 17 -> 20, of which waited for: 5 -> 6; matrix products, arithmetic and copies ran while one was open for 3% -> 0% of each run, Pallas kernels for 8% -> 16%
where the time goes in v2:
time: 75.5 us; the launch traced here: 75.2 us
  starting transfers between devices  40.2 us (53%)
  Pallas kernels  19.2 us (25%)
  waiting for transfers between devices  12.8 us (17%)
  local copies, waits for them, and re-layouts  3.05 us (4%)
    ppermute x20, starting transfers between devices, shifted(): lax.ppermute(block, axis, [(i, (i + distance) % count) for i in range(cou...  40.2 us
    ppermute x20, waiting for transfers between devices, shifted(): lax.ppermute(block, axis, [(i, (i + distance) % count) for i in range(cou...  12.8 us
    pallas_call x2, Pallas kernels, attention(): pl.pallas_call(kernel, out_shape=out_shape, in_specs=whole(len(operands))...  8.47 us
    pallas_call x2, Pallas kernels, projection(): pl.pallas_call(functools.partial(kernel, split), out_shape=[block] * (par...  8.14 us
    pallas_call x1, Pallas kernels, shards(): pl.pallas_call(functools.partial(output_kernel, split, width, groups), ou...  2.55 us
    unnamed x10, local copies, waits for them, and re-layouts  1.92 us
  transfers between devices with their start and end apart: 20, of which 6 were waited for; matrix products, arithmetic and copies ran while one was open for 0% of the time, Pallas kernels for 16%

profile of v2, /device:TPU:0, one launch (start us, length us, event | category | flops | bytes accessed | tf_op | source)
XLA Modules:
  0.0 75.2 jit_solution(1649346470879351827)
XLA Ops:
  0.0 0.0 copy-start.4
  0.0 1.1 %slice.4 = bf16[10,24,1280]{2,1,0:T(8,128)(2,1)S(1)} slice(bf16[10,40,1280]{2,1,0:T(8,128)(2,1)} %bitcast.2), slice={[0:10], [0:24], [0:1280]} | slice | bytes 1228800 | tf_op jit(solution)/shard_map/slice | solution.py:242
  1.1 3.0 %collective-permute-start.3 = (bf16[10,24,1280]{2,1,0:T(8,128)(2,1)S(1)}, bf16[10,24,1280]{2,1,0:T(8,128)(2,1)S(1)}, u32[]{:S(2)}, u32[]{:S(2)}) collective-permute-start(bf16[10,24,1280]{2,1,0:T(8,128)(2,1)S(1)} %slice.4), channel_id=1, source_target_pairs={{0,16},{4,20},{8,24},{12,28},{16,0},{20,4},{24,8},{28,12},{1,17},{... | collective-permute-start | bytes 1843208 | tf_op jit(solution)/shard_map/ppermute | solution.py:24
  4.2 0.0 copy-start
  4.2 1.2 %copy-done = bf16[1,10,40,1280]{3,2,1,0:T(8,128)(2,1)S(1)} copy-done((bf16[1,10,40,1280]{3,2,1,0:T(8,128)(2,1)S(1)}, bf16[1,10,40,1280]{3,2,1,0:T(8,128)(2,1)}, u32[]{:S(2)}) %copy-start) | copy-done | bytes 1024024
  5.4 0.0 copy-start.3
  5.4 0.7 copy-done.3
  6.1 3.7 %shard_map.55 = (bf16[160,512]{1,0:T(8,128)(2,1)S(1)}, bf16[160,512]{1,0:T(8,128)(2,1)S(1)}, bf16[160,512]{1,0:T(8,128)(2,1)S(1)}, bf16[160,512]{1,0:T(8,128)(2,1)S(1)}) custom-call(bf16[10,40,1280]{2,1,0:T(8,128)(2,1)S(1)} %bitcast.3, f32[1280]{0:T(1024)S(1)} %copy-done.3, bf16[1280,1920]{1,0:T(8,128)(2,1)} %weight.4), custom_call_target="tpu_custom_call" | custom-call | flops 786432000 | bytes 5734400 | tf_op jit(solution)/shard_map/pallas_call | solution.py:223
  9.8 1.6 %collective-permute-start = (bf16[160,512]{1,0:T(8,128)(2,1)S(1)}, bf16[160,512]{1,0:T(8,128)(2,1)S(1)}, u32[]{:S(2)}, u32[]{:S(2)}) collective-permute-start(bf16[160,512]{1,0:T(8,128)(2,1)S(1)} %get-tuple-element.26), channel_id=1, source_target_pairs={{0,1},{1,2},{2,3},{3,0},{4,5},{5,6},{6,7},{7,4},{8,9},{9,10},{10,1... | collective-permute-start | bytes 491528 | tf_op jit(solution)/shard_map/ppermute | solution.py:24
  11.4 2.6 %collective-permute-start.1 = (bf16[160,512]{1,0:T(8,128)(2,1)S(1)}, bf16[160,512]{1,0:T(8,128)(2,1)S(1)}, u32[]{:S(2)}, u32[]{:S(2)}) collective-permute-start(bf16[160,512]{1,0:T(8,128)(2,1)S(1)} %get-tuple-element.27), channel_id=1, source_target_pairs={{0,2},{1,3},{2,0},{3,1},{4,6},{5,7},{6,4},{7,5},{8,10},{9,11},{10,... | collective-permute-start | bytes 491528 | tf_op jit(solution)/shard_map/ppermute | solution.py:24
  14.0 1.3 %collective-permute-start.2 = (bf16[160,512]{1,0:T(8,128)(2,1)S(1)}, bf16[160,512]{1,0:T(8,128)(2,1)S(1)}, u32[]{:S(2)}, u32[]{:S(2)}) collective-permute-start(bf16[160,512]{1,0:T(8,128)(2,1)S(1)} %get-tuple-element.28), channel_id=1, source_target_pairs={{0,3},{1,0},{2,1},{3,2},{4,7},{5,4},{6,5},{7,6},{8,11},{9,8},{10,9... | collective-permute-start | bytes 491528 | tf_op jit(solution)/shard_map/ppermute | solution.py:24
  15.4 2.6 %collective-permute-done.3.eastern = bf16[10,24,1280]{2,1,0:T(8,128)(2,1)S(1)} collective-permute-done((bf16[10,24,1280]{2,1,0:T(8,128)(2,1)S(1)}, bf16[10,24,1280]{2,1,0:T(8,128)(2,1)S(1)}, u32[]{:S(2)}, u32[]{:S(2)}) %collective-permute-start.3) | collective-permute-done | bytes 614432 | tf_op jit(solution)/shard_map/ppermute | solution.py:24
  18.0 0.0 copy-done.4
  18.0 4.4 %shard_map.56 = (bf16[240,256]{1,0:T(8,128)(2,1)S(1)}, bf16[240,256]{1,0:T(8,128)(2,1)S(1)}, bf16[240,256]{1,0:T(8,128)(2,1)S(1)}, bf16[240,256]{1,0:T(8,128)(2,...) custom-call(s32[4]{0:T(128)S(1)} %copy-done.4, ...), custom_call_target="tpu_custom_call" | custom-call | flops 1179648000 | bytes 6144000 | tf_op jit(solution)/shard_map/pallas_call | solution.py:223
  22.4 1.9 %collective-permute-start.7 = (bf16[240,256]{1,0:T(8,128)(2,1)S(1)}, bf16[240,256]{1,0:T(8,128)(2,1)S(1)}, u32[]{:S(2)}, u32[]{:S(2)}) collective-permute-start(bf16[240,256]{1,0:T(8,128)(2,1)S(1)} %get-tuple-element.34), channel_id=1, source_target_pairs={{0,1},{1,2},{2,3},{3,0},{4,5},{5,6},{6,7},{7,4},{8,9},{9,10},{10,1... | collective-permute-start | bytes 368648 | tf_op jit(solution)/shard_map/ppermute | solution.py:24
  24.3 2.6 %collective-permute-start.8 = (bf16[240,256]{1,0:T(8,128)(2,1)S(1)}, bf16[240,256]{1,0:T(8,128)(2,1)S(1)}, u32[]{:S(2)}, u32[]{:S(2)}) collective-permute-start(bf16[240,256]{1,0:T(8,128)(2,1)S(1)} %get-tuple-element.35), channel_id=1, source_target_pairs={{0,2},{1,3},{2,0},{3,1},{4,6},{5,7},{6,4},{7,5},{8,10},{9,11},{10,... | collective-permute-start | bytes 368648 | tf_op jit(solution)/shard_map/ppermute | solution.py:24
  26.9 0.0 collective-permute-done.refs_1_
  26.9 1.3 %collective-permute-start.9 = (bf16[240,256]{1,0:T(8,128)(2,1)S(1)}, bf16[240,256]{1,0:T(8,128)(2,1)S(1)}, u32[]{:S(2)}, u32[]{:S(2)}) collective-permute-start(bf16[240,256]{1,0:T(8,128)(2,1)S(1)} %get-tuple-element.36), channel_id=1, source_target_pairs={{0,3},{1,0},{2,1},{3,2},{4,7},{5,4},{6,5},{7,6},{8,11},{9,8},{10,9... | collective-permute-start | bytes 368648 | tf_op jit(solution)/shard_map/ppermute | solution.py:24
  28.2 0.0 collective-permute-done.1.refs_2_
  28.2 0.7 collective-permute-start.4
  28.9 0.0 collective-permute-done.2.refs_3_
  28.9 4.5 %collective-permute-start.5 = (bf16[240,256]{1,0:T(8,128)(2,1)S(1)}, bf16[240,256]{1,0:T(8,128)(2,1)S(1)}, u32[]{:S(2)}, u32[]{:S(2)}) collective-permute-start(bf16[240,256]{1,0:T(8,128)(2,1)S(1)} %get-tuple-element.31), channel_id=1, source_target_pairs={{0,2},{1,3},{2,0},{3,1},{4,6},{5,7},{6,4},{7,5},{8,10},{9,11},{10,... | collective-permute-start | bytes 368648 | tf_op jit(solution)/shard_map/ppermute | solution.py:24
  33.4 0.0 collective-permute-done.7.refs_5_
  33.4 3.7 %collective-permute-start.6 = (bf16[240,256]{1,0:T(8,128)(2,1)S(1)}, bf16[240,256]{1,0:T(8,128)(2,1)S(1)}, u32[]{:S(2)}, u32[]{:S(2)}) collective-permute-start(bf16[240,256]{1,0:T(8,128)(2,1)S(1)} %get-tuple-element.32), channel_id=1, source_target_pairs={{0,3},{1,0},{2,1},{3,2},{4,7},{5,4},{6,5},{7,6},{8,11},{9,8},{10,9... | collective-permute-start | bytes 368648 | tf_op jit(solution)/shard_map/ppermute | solution.py:24
  37.1 4.0 %collective-permute-done.8.refs_6_ = bf16[240,256]{1,0:T(8,128)(2,1)S(1)} collective-permute-done((bf16[240,256]{1,0:T(8,128)(2,1)S(1)}, bf16[240,256]{1,0:T(8,128)(2,1)S(1)}, u32[]{:S(2)}, u32[]{:S(2)}) %collective-permute-start.8) | collective-permute-done | bytes 122912 | tf_op jit(solution)/shard_map/ppermute | solution.py:24
  41.2 0.0 collective-permute-done.9.refs_7_
  41.2 4.2 %shard_map.57.refs_8_ = bf16[1600,128]{1,0:T(8,128)(2,1)S(1)} custom-call(bf16[160,512]{1,0:T(8,128)(2,1)S(1)} %get-tuple-element.25.refs_0_, bf16[160,512]{1,0:T(8,128)(2,1)S(1)} %collective-permute-done.refs_1_, bf16[160,512]{1,0:T(8,128)(2,1)S(1)} %collective-permute-done.1.refs_2_, bf16[160,512]{1,0:T(8,128)(2,1)S(1)} %collective-permute-done.2.refs_3_, ...), custom_call_target="tpu_custom_call" | custom-call | flops 2621440000 | bytes 1228800 | tf_op jit(solution)/shard_map/pallas_call | solution.py:257
  45.3 0.0 copy-start.1
  45.3 0.0 copy-start.2
  45.3 0.0 collective-permute-done.4.refs_5_
  45.4 1.1 %collective-permute-done.5.refs_6_ = bf16[240,256]{1,0:T(8,128)(2,1)S(1)} collective-permute-done((bf16[240,256]{1,0:T(8,128)(2,1)S(1)}, bf16[240,256]{1,0:T(8,128)(2,1)S(1)}, u32[]{:S(2)}, u32[]{:S(2)}) %collective-permute-start.5) | collective-permute-done | bytes 122912 | tf_op jit(solution)/shard_map/ppermute | solution.py:24
  46.5 0.0 collective-permute-done.6.refs_7_
  46.5 4.3 %shard_map.58 = (bf16[200,128]{1,0:T(8,128)(2,1)S(1)}, bf16[200,128]{1,0:T(8,128)(2,1)S(1)}, bf16[200,128]{1,0:T(8,128)(2,1)S(1)}, bf16[200,128]{1,0:T(8,128)(2,...) custom-call(bf16[160,512]{1,0:T(8,128)(2,1)S(1)} %get-tuple-element., ...), custom_call_target="tpu_custom_call" | custom-call | flops 2621440000 | bytes 1228800 | tf_op jit(solution)/shard_map/pallas_call | solution.py:257
  50.8 4.6 %collective-permute-start.13 = (bf16[304,128]{1,0:T(8,128)(2,1)S(1)}, bf16[304,128]{1,0:T(8,128)(2,1)S(1)}, u32[]{:S(2)}, u32[]{:S(2)}) collective-permute-start(bf16[304,128]{1,0:T(8,128)(2,1)S(1)} %get-tuple-element.42), channel_id=1, source_target_pairs={{0,3},{1,0},{2,1},{3,2},{4,7},{5,4},{6,5},{7,6},{8,11},{9,8},{10,9... | collective-permute-start | bytes 233480 | tf_op jit(solution)/shard_map/ppermute | solution.py:24
  55.4 0.0 collective-permute-start.14
  55.4 0.6 collective-permute-start.15
  56.0 3.2 %collective-permute-start.10 = (bf16[200,128]{1,0:T(8,128)(2,1)S(1)}, bf16[200,128]{1,0:T(8,128)(2,1)S(1)}, u32[]{:S(2)}, u32[]{:S(2)}) collective-permute-start(bf16[200,128]{1,0:T(8,128)(2,1)S(1)} %get-tuple-element.38), channel_id=1, source_target_pairs={{0,3},{1,0},{2,1},{3,2},{4,7},{5,4},{6,5},{7,6},{8,11},{9,8},{10,9... | collective-permute-start | bytes 153608 | tf_op jit(solution)/shard_map/ppermute | solution.py:24
  59.2 1.1 %collective-permute-start.11 = (bf16[200,128]{1,0:T(8,128)(2,1)S(1)}, bf16[200,128]{1,0:T(8,128)(2,1)S(1)}, u32[]{:S(2)}, u32[]{:S(2)}) collective-permute-start(bf16[200,128]{1,0:T(8,128)(2,1)S(1)} %get-tuple-element.39), channel_id=1, source_target_pairs={{0,2},{1,3},{2,0},{3,1},{4,6},{5,7},{6,4},{7,5},{8,10},{9,11},{10,... | collective-permute-start | bytes 153608 | tf_op jit(solution)/shard_map/ppermute | solution.py:24
  60.4 1.1 %collective-permute-done.10.refs_1_ = bf16[200,128]{1,0:T(8,128)(2,1)S(1)} collective-permute-done((bf16[200,128]{1,0:T(8,128)(2,1)S(1)}, bf16[200,128]{1,0:T(8,128)(2,1)S(1)}, u32[]{:S(2)}, u32[]{:S(2)}) %collective-permute-start.10) | collective-permute-done | bytes 51232 | tf_op jit(solution)/shard_map/ppermute | solution.py:24
  61.5 0.3 collective-permute-start.16
  61.8 0.0 collective-permute-done.13.refs_5_
  61.8 1.7 %collective-permute-start.17 = (bf16[304,128]{1,0:T(8,128)(2,1)S(1)}, bf16[304,128]{1,0:T(8,128)(2,1)S(1)}, u32[]{:S(2)}, u32[]{:S(2)}) collective-permute-start(bf16[304,128]{1,0:T(8,128)(2,1)S(1)} %collective-permute-done.13.refs_5_), channel_id=1, source_target_pairs={{0,16},{4,20},{8,24},{12,28},{16,0},{20,4},{24,8},{28,12},{1,17},{... | collective-permute-start | bytes 233480 | tf_op jit(solution)/shard_map/ppermute | solution.py:24
  63.5 1.2 %collective-permute-done.14.refs_6_ = bf16[304,128]{1,0:T(8,128)(2,1)S(1)} collective-permute-done((bf16[304,128]{1,0:T(8,128)(2,1)S(1)}, bf16[304,128]{1,0:T(8,128)(2,1)S(1)}, u32[]{:S(2)}, u32[]{:S(2)}) %collective-permute-start.14) | collective-permute-done | bytes 77856 | tf_op jit(solution)/shard_map/ppermute | solution.py:24
  64.7 0.4 collective-permute-start.18
  65.1 0.0 collective-permute-done.15.refs_7_
  65.1 1.6 %collective-permute-start.19 = (bf16[304,128]{1,0:T(8,128)(2,1)S(1)}, bf16[304,128]{1,0:T(8,128)(2,1)S(1)}, u32[]{:S(2)}, u32[]{:S(2)}) collective-permute-start(bf16[304,128]{1,0:T(8,128)(2,1)S(1)} %collective-permute-done.15.refs_7_), channel_id=1, source_target_pairs={{0,16},{4,20},{8,24},{12,28},{16,0},{20,4},{24,8},{28,12},{1,17},{... | collective-permute-start | bytes 233480 | tf_op jit(solution)/shard_map/ppermute | solution.py:24
  66.7 0.0 collective-permute-done.11.refs_2_
  66.7 3.3 %collective-permute-start.12 = (bf16[200,128]{1,0:T(8,128)(2,1)S(1)}, bf16[200,128]{1,0:T(8,128)(2,1)S(1)}, u32[]{:S(2)}, u32[]{:S(2)}) collective-permute-start(bf16[200,128]{1,0:T(8,128)(2,1)S(1)} %get-tuple-element.40), channel_id=1, source_target_pairs={{0,1},{1,2},{2,3},{3,0},{4,5},{5,6},{6,7},{7,4},{8,9},{9,10},{10,1... | collective-permute-start | bytes 153608 | tf_op jit(solution)/shard_map/ppermute | solution.py:24
  70.0 2.6 %collective-permute-done.12.refs_3_ = bf16[200,128]{1,0:T(8,128)(2,1)S(1)} collective-permute-done((bf16[200,128]{1,0:T(8,128)(2,1)S(1)}, bf16[200,128]{1,0:T(8,128)(2,1)S(1)}, u32[]{:S(2)}, u32[]{:S(2)}) %collective-permute-start.12) | collective-permute-done | bytes 51232 | tf_op jit(solution)/shard_map/ppermute | solution.py:24
  72.6 0.0 collective-permute-done.16.refs_8_
  72.7 0.0 collective-permute-done.17.refs_9_
  72.7 0.0 collective-permute-done.18.refs_10_
  72.7 0.0 collective-permute-done.19.refs_11_
  72.7 0.0 copy-done.1
  72.7 0.0 copy-done.2
  72.7 2.5 %shard_map.59 = bf16[10,40,1280]{2,1,0:T(8,128)(2,1)} custom-call(s32[4]{0:T(128)S(1)} %copy-done.4, bf16[10,40,1280]{2,1,0:T(8,128)(2,1)S(1)} %bitcast.5, bf16[640,1280]{1,0:T(8,128)(2,1)S(1)} %copy-done.2, bf16[200,128]{1,0:T(8,128)(2,1)S(1)} %get-tuple-element.37.refs_0_, bf16[200,128]{1,0:T(8,128)(2,1)S(1)} %collective-permute-done.10.refs_1_, ...), custom_call_target="tpu_custom_call" | custom-call | flops 655360000 | bytes 3686400 | tf_op jit(solution)/shard_map/pallas_call | solution.py:292
Async XLA Ops:
  0.0 18.0 %copy-start.4 = (s32[4]{0:T(128)S(1)}, s32[4]{0:T(128)}, u32[]{:S(2)}) copy-start(s32[4]{0:T(128)} %lon_shift.3) | copy-start | bytes 52
  1.1 16.9 %collective-permute-start.3 = (bf16[10,24,1280]{2,1,0:T(8,128)(2,1)S(1)}, bf16[10,24,1280]{2,1,0:T(8,128)(2,1)S(1)}, u32[]{:S(2)}, u32[]{:S(2)}) collective-permute-start(bf16[10,24,1280]{2,1,0:T(8,128)(2,1)S(1)} %slice.4), channel_id=1, source_target_pairs={{0,16},{4,20},{8,24},{12,28},{16,0},{20,4},{24,8},{28,12},{1,17},{... | collective-permute-start | bytes 1843208 | tf_op jit(solution)/shard_map/ppermute | solution.py:24
  4.2 1.2 %copy-start = (bf16[1,10,40,1280]{3,2,1,0:T(8,128)(2,1)S(1)}, bf16[1,10,40,1280]{3,2,1,0:T(8,128)(2,1)}, u32[]{:S(2)}) copy-start(bf16[1,10,40,1280]{3,2,1,0:T(8,128)(2,1)} %param.5) | copy-start | bytes 3072004
  5.4 0.7 copy-start.3
  9.8 17.1 %collective-permute-start = (bf16[160,512]{1,0:T(8,128)(2,1)S(1)}, bf16[160,512]{1,0:T(8,128)(2,1)S(1)}, u32[]{:S(2)}, u32[]{:S(2)}) collective-permute-start(bf16[160,512]{1,0:T(8,128)(2,1)S(1)} %get-tuple-element.26), channel_id=1, source_target_pairs={{0,1},{1,2},{2,3},{3,0},{4,5},{5,6},{6,7},{7,4},{8,9},{9,10},{10,1... | collective-permute-start | bytes 491528 | tf_op jit(solution)/shard_map/ppermute | solution.py:24
  11.4 16.8 %collective-permute-start.1 = (bf16[160,512]{1,0:T(8,128)(2,1)S(1)}, bf16[160,512]{1,0:T(8,128)(2,1)S(1)}, u32[]{:S(2)}, u32[]{:S(2)}) collective-permute-start(bf16[160,512]{1,0:T(8,128)(2,1)S(1)} %get-tuple-element.27), channel_id=1, source_target_pairs={{0,2},{1,3},{2,0},{3,1},{4,6},{5,7},{6,4},{7,5},{8,10},{9,11},{10,... | collective-permute-start | bytes 491528 | tf_op jit(solution)/shard_map/ppermute | solution.py:24
  14.0 14.9 %collective-permute-start.2 = (bf16[160,512]{1,0:T(8,128)(2,1)S(1)}, bf16[160,512]{1,0:T(8,128)(2,1)S(1)}, u32[]{:S(2)}, u32[]{:S(2)}) collective-permute-start(bf16[160,512]{1,0:T(8,128)(2,1)S(1)} %get-tuple-element.28), channel_id=1, source_target_pairs={{0,3},{1,0},{2,1},{3,2},{4,7},{5,4},{6,5},{7,6},{8,11},{9,8},{10,9... | collective-permute-start | bytes 491528 | tf_op jit(solution)/shard_map/ppermute | solution.py:24
  22.4 11.0 %collective-permute-start.7 = (bf16[240,256]{1,0:T(8,128)(2,1)S(1)}, bf16[240,256]{1,0:T(8,128)(2,1)S(1)}, u32[]{:S(2)}, u32[]{:S(2)}) collective-permute-start(bf16[240,256]{1,0:T(8,128)(2,1)S(1)} %get-tuple-element.34), channel_id=1, source_target_pairs={{0,1},{1,2},{2,3},{3,0},{4,5},{5,6},{6,7},{7,4},{8,9},{9,10},{10,1... | collective-permute-start | bytes 368648 | tf_op jit(solution)/shard_map/ppermute | solution.py:24
  24.3 16.9 %collective-permute-start.8 = (bf16[240,256]{1,0:T(8,128)(2,1)S(1)}, bf16[240,256]{1,0:T(8,128)(2,1)S(1)}, u32[]{:S(2)}, u32[]{:S(2)}) collective-permute-start(bf16[240,256]{1,0:T(8,128)(2,1)S(1)} %get-tuple-element.35), channel_id=1, source_target_pairs={{0,2},{1,3},{2,0},{3,1},{4,6},{5,7},{6,4},{7,5},{8,10},{9,11},{10,... | collective-permute-start | bytes 368648 | tf_op jit(solution)/shard_map/ppermute | solution.py:24
  26.9 14.3 %collective-permute-start.9 = (bf16[240,256]{1,0:T(8,128)(2,1)S(1)}, bf16[240,256]{1,0:T(8,128)(2,1)S(1)}, u32[]{:S(2)}, u32[]{:S(2)}) collective-permute-start(bf16[240,256]{1,0:T(8,128)(2,1)S(1)} %get-tuple-element.36), channel_id=1, source_target_pairs={{0,3},{1,0},{2,1},{3,2},{4,7},{5,4},{6,5},{7,6},{8,11},{9,8},{10,9... | collective-permute-start | bytes 368648 | tf_op jit(solution)/shard_map/ppermute | solution.py:24
  28.2 17.1 %collective-permute-start.4 = (bf16[240,256]{1,0:T(8,128)(2,1)S(1)}, bf16[240,256]{1,0:T(8,128)(2,1)S(1)}, u32[]{:S(2)}, u32[]{:S(2)}) collective-permute-start(bf16[240,256]{1,0:T(8,128)(2,1)S(1)} %get-tuple-element.30), channel_id=1, source_target_pairs={{0,1},{1,2},{2,3},{3,0},{4,5},{5,6},{6,7},{7,4},{8,9},{9,10},{10,1... | collective-permute-start | bytes 368648 | tf_op jit(solution)/shard_map/ppermute | solution.py:24
  28.9 17.6 %collective-permute-start.5 = (bf16[240,256]{1,0:T(8,128)(2,1)S(1)}, bf16[240,256]{1,0:T(8,128)(2,1)S(1)}, u32[]{:S(2)}, u32[]{:S(2)}) collective-permute-start(bf16[240,256]{1,0:T(8,128)(2,1)S(1)} %get-tuple-element.31), channel_id=1, source_target_pairs={{0,2},{1,3},{2,0},{3,1},{4,6},{5,7},{6,4},{7,5},{8,10},{9,11},{10,... | collective-permute-start | bytes 368648 | tf_op jit(solution)/shard_map/ppermute | solution.py:24
  33.4 13.1 %collective-permute-start.6 = (bf16[240,256]{1,0:T(8,128)(2,1)S(1)}, bf16[240,256]{1,0:T(8,128)(2,1)S(1)}, u32[]{:S(2)}, u32[]{:S(2)}) collective-permute-start(bf16[240,256]{1,0:T(8,128)(2,1)S(1)} %get-tuple-element.32), channel_id=1, source_target_pairs={{0,3},{1,0},{2,1},{3,2},{4,7},{5,4},{6,5},{7,6},{8,11},{9,8},{10,9... | collective-permute-start | bytes 368648 | tf_op jit(solution)/shard_map/ppermute | solution.py:24
  45.3 27.3 %copy-start.1 = (bf16[1,10,40,1280]{3,2,1,0:T(8,128)(2,1)S(1)}, bf16[1,10,40,1280]{3,2,1,0:T(8,128)(2,1)}, u32[]{:S(2)}) copy-start(bf16[1,10,40,1280]{3,2,1,0:T(8,128)(2,1)} %param.5) | copy-start | bytes 3072004
  45.3 27.3 %copy-start.2 = (bf16[640,1280]{1,0:T(8,128)(2,1)S(1)}, bf16[640,1280]{1,0:T(8,128)(2,1)}, u32[]{:S(2)}) copy-start(bf16[640,1280]{1,0:T(8,128)(2,1)} %weight.5) | copy-start | bytes 4915204
  50.8 11.0 %collective-permute-start.13 = (bf16[304,128]{1,0:T(8,128)(2,1)S(1)}, bf16[304,128]{1,0:T(8,128)(2,1)S(1)}, u32[]{:S(2)}, u32[]{:S(2)}) collective-permute-start(bf16[304,128]{1,0:T(8,128)(2,1)S(1)} %get-tuple-element.42), channel_id=1, source_target_pairs={{0,3},{1,0},{2,1},{3,2},{4,7},{5,4},{6,5},{7,6},{8,11},{9,8},{10,9... | collective-permute-start | bytes 233480 | tf_op jit(solution)/shard_map/ppermute | solution.py:24
  55.4 9.3 %collective-permute-start.14 = (bf16[304,128]{1,0:T(8,128)(2,1)S(1)}, bf16[304,128]{1,0:T(8,128)(2,1)S(1)}, u32[]{:S(2)}, u32[]{:S(2)}) collective-permute-start(bf16[304,128]{1,0:T(8,128)(2,1)S(1)} %get-tuple-element.43), channel_id=1, source_target_pairs={{0,2},{1,3},{2,0},{3,1},{4,6},{5,7},{6,4},{7,5},{8,10},{9,11},{10,... | collective-permute-start | bytes 233480 | tf_op jit(solution)/shard_map/ppermute | solution.py:24
  55.4 9.7 %collective-permute-start.15 = (bf16[304,128]{1,0:T(8,128)(2,1)S(1)}, bf16[304,128]{1,0:T(8,128)(2,1)S(1)}, u32[]{:S(2)}, u32[]{:S(2)}) collective-permute-start(bf16[304,128]{1,0:T(8,128)(2,1)S(1)} %get-tuple-element.44), channel_id=1, source_target_pairs={{0,1},{1,2},{2,3},{3,0},{4,5},{5,6},{6,7},{7,4},{8,9},{9,10},{10,1... | collective-permute-start | bytes 233480 | tf_op jit(solution)/shard_map/ppermute | solution.py:24
  56.0 5.4 %collective-permute-start.10 = (bf16[200,128]{1,0:T(8,128)(2,1)S(1)}, bf16[200,128]{1,0:T(8,128)(2,1)S(1)}, u32[]{:S(2)}, u32[]{:S(2)}) collective-permute-start(bf16[200,128]{1,0:T(8,128)(2,1)S(1)} %get-tuple-element.38), channel_id=1, source_target_pairs={{0,3},{1,0},{2,1},{3,2},{4,7},{5,4},{6,5},{7,6},{8,11},{9,8},{10,9... | collective-permute-start | bytes 153608 | tf_op jit(solution)/shard_map/ppermute | solution.py:24
  59.2 7.5 %collective-permute-start.11 = (bf16[200,128]{1,0:T(8,128)(2,1)S(1)}, bf16[200,128]{1,0:T(8,128)(2,1)S(1)}, u32[]{:S(2)}, u32[]{:S(2)}) collective-permute-start(bf16[200,128]{1,0:T(8,128)(2,1)S(1)} %get-tuple-element.39), channel_id=1, source_target_pairs={{0,2},{1,3},{2,0},{3,1},{4,6},{5,7},{6,4},{7,5},{8,10},{9,11},{10,... | collective-permute-start | bytes 153608 | tf_op jit(solution)/shard_map/ppermute | solution.py:24
  61.5 11.2 %collective-permute-start.16 = (bf16[304,128]{1,0:T(8,128)(2,1)S(1)}, bf16[304,128]{1,0:T(8,128)(2,1)S(1)}, u32[]{:S(2)}, u32[]{:S(2)}) collective-permute-start(bf16[304,128]{1,0:T(8,128)(2,1)S(1)} %get-tuple-element.41.refs_4_), channel_id=1, source_target_pairs={{0,16},{4,20},{8,24},{12,28},{16,0},{20,4},{24,8},{28,12},{1,17},{... | collective-permute-start | bytes 233480 | tf_op jit(solution)/shard_map/ppermute | solution.py:24
  61.8 10.9 %collective-permute-start.17 = (bf16[304,128]{1,0:T(8,128)(2,1)S(1)}, bf16[304,128]{1,0:T(8,128)(2,1)S(1)}, u32[]{:S(2)}, u32[]{:S(2)}) collective-permute-start(bf16[304,128]{1,0:T(8,128)(2,1)S(1)} %collective-permute-done.13.refs_5_), channel_id=1, source_target_pairs={{0,16},{4,20},{8,24},{12,28},{16,0},{20,4},{24,8},{28,12},{1,17},{... | collective-permute-start | bytes 233480 | tf_op jit(solution)/shard_map/ppermute | solution.py:24
  64.7 8.0 %collective-permute-start.18 = (bf16[304,128]{1,0:T(8,128)(2,1)S(1)}, bf16[304,128]{1,0:T(8,128)(2,1)S(1)}, u32[]{:S(2)}, u32[]{:S(2)}) collective-permute-start(bf16[304,128]{1,0:T(8,128)(2,1)S(1)} %collective-permute-done.14.refs_6_), channel_id=1, source_target_pairs={{0,16},{4,20},{8,24},{12,28},{16,0},{20,4},{24,8},{28,12},{1,17},{... | collective-permute-start | bytes 233480 | tf_op jit(solution)/shard_map/ppermute | solution.py:24
  65.1 7.5 %collective-permute-start.19 = (bf16[304,128]{1,0:T(8,128)(2,1)S(1)}, bf16[304,128]{1,0:T(8,128)(2,1)S(1)}, u32[]{:S(2)}, u32[]{:S(2)}) collective-permute-start(bf16[304,128]{1,0:T(8,128)(2,1)S(1)} %collective-permute-done.15.refs_7_), channel_id=1, source_target_pairs={{0,16},{4,20},{8,24},{12,28},{16,0},{20,4},{24,8},{28,12},{1,17},{... | collective-permute-start | bytes 233480 | tf_op jit(solution)/shard_map/ppermute | solution.py:24
  66.7 5.9 %collective-permute-start.12 = (bf16[200,128]{1,0:T(8,128)(2,1)S(1)}, bf16[200,128]{1,0:T(8,128)(2,1)S(1)}, u32[]{:S(2)}, u32[]{:S(2)}) collective-permute-start(bf16[200,128]{1,0:T(8,128)(2,1)S(1)} %get-tuple-element.40), channel_id=1, source_target_pairs={{0,1},{1,2},{2,3},{3,0},{4,5},{5,6},{6,7},{7,4},{8,9},{9,10},{10,1... | collective-permute-start | bytes 153608 | tf_op jit(solution)/shard_map/ppermute | solution.py:24

commit v3 on v2

v3 whole, which is shorter than its diff:
```python
import functools

import jax
import jax.numpy as jnp
from jax import lax
from jax.experimental import pallas as pl
from jax.experimental.pallas import tpu as pltpu
from jax.sharding import PartitionSpec as P

HEADS = 8
HD = 80
LAT_WINDOWS = 4
LANES = 128
SUBLANES = 8
VMEM_BYTES = 48 * 1024 * 1024


def round_up(value, unit):
    return -(-value // unit) * unit


def shifted(block, axis, distance):
    count = lax.axis_size(axis)
    return lax.ppermute(block, axis, [(i, (i + distance) % count) for i in range(count)])


def after(blocks, arrived):
    return [blocks[0]] + [
        lax.optimization_barrier(pair)[0] for pair in zip(blocks[1:], arrived[1:])
    ]


def column_offset(lon_shift):
    return lon_shift[lax.rem(lax.axis_index("win"), LAT_WINDOWS)]


def project(tokens, gain, weight, slots, outs):
    local = HEADS // slots.shape[0]
    groups = slots.shape[0]
    count, features = tokens.shape
    span = slots.shape[2] // local
    factor = lax.rsqrt(jnp.mean(tokens * tokens, axis=-1, keepdims=True) + 1e-06)
    normed = (tokens * factor * gain[...].reshape(1, features)).astype(jnp.bfloat16)
    qkv = jnp.dot(normed, weight[...], preferred_element_type=jnp.float32)
    tail = jnp.ones((count, span - 3 * HD), jnp.float32)
    place = lax.axis_index("tok")
    for group in range(groups):
        slot = lax.rem(group - place + groups, groups)
        columns = []
        for head in range(group * local, (group + 1) * local):
            columns += [
                qkv[:, (kind * HEADS + head) * HD : (kind * HEADS + head + 1) * HD]
                for kind in range(3)
            ] + [tail]
        slots[slot] = jnp.concatenate(columns, axis=1).astype(jnp.bfloat16)
    parts = len(outs) // groups
    for index, out in enumerate(outs):
        first = index // groups * out.shape[1]
        out[...] = slots[index % groups, :, first : first + out.shape[1]]


def kept_kernel(split, field, gain, weight, *refs):
    *outs, slots = refs
    rows, columns, features = field.shape
    tokens = field[...].astype(jnp.float32)[:, split:]
    project(tokens.reshape(rows * (columns - split), features), gain, weight, slots, outs)


def mixed_kernel(split, lon_shift, field, eastern, gain, weight, *refs):
    *outs, slots = refs
    rows, _, features = field.shape
    own = field[...].astype(jnp.float32)[:, :split]
    column = lax.broadcasted_iota(jnp.int32, own.shape, 1)
    tokens = jnp.where(column < column_offset(lon_shift), eastern[...].astype(jnp.float32), own)
    project(tokens.reshape(rows * split, features), gain, weight, slots, outs)


def attention_kernel(head, groups, *refs):
    kept, mixed = refs[:groups], refs[groups : 2 * groups]
    kept_out, mixed_out, held, keys = refs[2 * groups : 2 * groups + 4]
    scores, weights = refs[2 * groups + 4 : 2 * groups + 6], refs[2 * groups + 6 :]
    span = held.shape[1]
    start = 0
    for block in kept:
        held[start : start + block.shape[0]] = block[:, head * span : (head + 1) * span]
        start += block.shape[0]
    for block in mixed:
        held[start : start + block.shape[0]] = block[...]
        start += block.shape[0]
    keys[...] = held[...].T
    factor = HD ** (-0.5) * 1.4426950408889634
    step = scores[0].shape[0]
    chunk = 16

    def score(index, out):
        queries = held[index * step : (index + 1) * step].astype(jnp.float32)
        queries = pltpu.roll(queries, HD, axis=1)
        lane = lax.broadcasted_iota(jnp.int32, queries.shape, 1)
        queries = jnp.where((lane >= HD) & (lane < 2 * HD), queries, 0.0).astype(jnp.bfloat16)
        out[...] = jnp.dot(queries, keys[...], preferred_element_type=jnp.float32)

    steps = start // step
    score(0, scores[0])
    for index in range(steps):
        if index + 1 < steps:
            score(index + 1, scores[(index + 1) % 2])
        now, out = scores[index % 2], weights[index % 2]
        for first in range(0, step, chunk):
            part = now[first : first + chunk]
            top = jnp.max(part, axis=-1, keepdims=True)
            out[first : first + chunk] = jnp.exp2((part - top) * factor).astype(jnp.bfloat16)
        mixed_values = jnp.dot(out[...], held[...], preferred_element_type=jnp.float32)
        scaled = mixed_values / mixed_values[:, 3 * HD : 3 * HD + 1]
        values = pltpu.roll(scaled, span - 2 * HD, axis=1)[:, :LANES].astype(jnp.bfloat16)
        first = index * step
        if first < kept_out.shape[0]:
            kept_out[first : first + step] = values
        else:
            first -= kept_out.shape[0]
            mixed_out[first : first + step] = values


def pack_kernel(split, lon_shift, kept, mixed, western, *outs):
    groups = len(outs)
    half = LANES // 2
    rest = HD - half
    fold = LANES // rest
    kept_count, mixed_count = kept.shape[0] // groups, mixed.shape[0] // groups
    count = kept_count + mixed_count
    part = round_up(-(-count // fold), SUBLANES)
    shape = (mixed_count // split, split, LANES)
    taken = lax.broadcasted_iota(jnp.int32, shape, 1) < column_offset(lon_shift)
    for group, out in enumerate(outs):
        rows = slice(group * mixed_count, (group + 1) * mixed_count)
        own, west = mixed[rows].astype(jnp.float32), western[rows].astype(jnp.float32)
        chosen = jnp.where(taken, west.reshape(shape), own.reshape(shape)).reshape(own.shape)
        rows = kept[group * kept_count : (group + 1) * kept_count].astype(jnp.float32)
        rows = jnp.concatenate([rows, chosen], axis=0)
        lane = lax.broadcasted_iota(jnp.int32, (count // 2, LANES), 1)
        main = jnp.where(lane < half, rows[: count // 2], pltpu.roll(rows[count // 2 :], half, axis=1))
        lane = lax.broadcasted_iota(jnp.int32, (part, LANES), 1)
        rests = jnp.zeros((part, LANES), jnp.float32)
        for index in range(fold):
            piece = rows[index * part : (index + 1) * part]
            if piece.shape[0] < part:
                empty = jnp.zeros((part - piece.shape[0], LANES), jnp.float32)
                piece = jnp.concatenate([piece, empty], axis=0)
            piece = pltpu.roll(piece, (index * rest + half) % LANES, axis=1)
            rests = jnp.where(lane // rest == index, piece, rests)
        out[...] = jnp.concatenate([main, rests], axis=0).astype(jnp.bfloat16)


def unpack(blocks, count):
    half = LANES // 2
    rest = HD - half
    fold = LANES // rest
    part = round_up(-(-count // fold), SUBLANES)
    columns = []
    for block in blocks:
        block = block[...].astype(jnp.float32)
        main, rests = block[: count // 2], block[count // 2 :]
        main = jnp.concatenate([main, pltpu.roll(main, half, axis=1)], axis=0)
        pieces = []
        for index in range(fold):
            turn = (half - index * rest) % LANES
            piece = pltpu.roll(rests, turn, axis=1) if turn else rests
            pieces.append(piece[: min(part, count - index * part)])
        lane = lax.broadcasted_iota(jnp.int32, main.shape, 1)
        columns.append(jnp.where(lane < half, main, jnp.concatenate(pieces, axis=0)))
    return jnp.concatenate(columns, axis=1).astype(jnp.bfloat16)


def by_column(projected, rows, columns, split):
    kept_count = rows * (columns - split)
    right = projected[:kept_count].reshape(rows, columns - split, -1)
    left = projected[kept_count:].reshape(rows, split, -1)
    return jnp.concatenate([left, right], axis=1)


def first_output_kernel(split, groups, field, weight, *refs):
    blocks, (out, second, first) = refs[:groups], refs[groups:]
    rows, columns, features = field.shape
    for slot in range(groups):
        group = lax.rem(lax.axis_index("tok") + slot, groups)
        for head, ordered in enumerate((first, second)):
            at = pl.multiple_of((group * HEADS // groups + head) * HD, 16)
            ordered[slot * LANES : slot * LANES + HD] = weight[pl.ds(at, HD)]
            ordered[slot * LANES + HD : (slot + 1) * LANES] = jnp.zeros(
                (LANES - HD, features), jnp.bfloat16
            )
    attended = unpack(blocks, rows * columns)
    projected = jnp.dot(attended, first[...], preferred_element_type=jnp.float32)
    out[...] = field[...].astype(jnp.float32) + by_column(projected, rows, columns, split)


def second_output_kernel(split, partial, weight, *refs):
    *blocks, out = refs
    rows, columns, _ = partial.shape
    attended = unpack(blocks, rows * columns)
    projected = jnp.dot(attended, weight[...], preferred_element_type=jnp.float32)
    out[...] = (partial[...] + by_column(projected, rows, columns, split)).astype(jnp.bfloat16)


def whole(count):
    return [pl.BlockSpec(memory_space=pltpu.VMEM)] * count


def shards(field_tokens, lon_shift, norm_gain, qkv_weight, out_weight):
    _, rows, columns, features = field_tokens.shape
    groups = lax.axis_size("tok")
    local = HEADS // groups
    width = local * HD
    span = round_up(3 * HD + 1, LANES)
    split = round_up(columns // 2, SUBLANES)
    field = field_tokens[0]
    smem = pl.BlockSpec(memory_space=pltpu.SMEM)
    params = pltpu.CompilerParams(vmem_limit_bytes=VMEM_BYTES)
    kept_count, mixed_count = rows * (columns - split), rows * split

    def projection(kernel, count, parts, scalars, operands):
        block = jax.ShapeDtypeStruct((count, local * span // parts), jnp.bfloat16)
        return pl.pallas_call(
            functools.partial(kernel, split),
            out_shape=[block] * (parts * groups),
            in_specs=[smem] * len(scalars) + whole(len(operands) + 2),
            out_specs=whole(parts * groups),
            scratch_shapes=[pltpu.VMEM((groups, count, local * span), jnp.bfloat16)],
            compiler_params=params,
            cost_estimate=pl.CostEstimate(
                flops=2 * count * features * 3 * HEADS * HD,
                bytes_accessed=2 * features * (3 * HEADS * HD + 2 * count),
                transcendentals=0,
            ),
        )(*scalars, *operands, norm_gain, qkv_weight)

    def spread(blocks, sign):
        return [blocks[0]] + [
            shifted(blocks[distance], "tok", sign * distance) for distance in range(1, groups)
        ]

    eastern = shifted(field[:, :split], "win", -LAT_WINDOWS)
    kept = spread(projection(kept_kernel, kept_count, 1, [], [field]), 1)
    mixed = projection(mixed_kernel, mixed_count, local, [lon_shift], [field, eastern])
    first_mixed = spread(after(mixed[:groups], kept), 1)
    second_mixed = spread(after(mixed[groups:], first_mixed), 1)

    total = groups * rows * columns
    step = total // 5
    packed_rows = round_up(rows * columns // 2 + -(-rows * columns * (HD - LANES // 2) // LANES), 16)

    def attention(head, blocks):
        return pl.pallas_call(
            functools.partial(attention_kernel, head, groups),
            out_shape=[
                jax.ShapeDtypeStruct((groups * count, LANES), jnp.bfloat16)
                for count in (kept_count, mixed_count)
            ],
            in_specs=whole(len(blocks)),
            out_specs=whole(2),
            scratch_shapes=[
                pltpu.VMEM((total, span), jnp.bfloat16),
                pltpu.VMEM((span, total), jnp.bfloat16),
                pltpu.VMEM((step, total), jnp.float32),
                pltpu.VMEM((step, total), jnp.float32),
                pltpu.VMEM((step, total), jnp.bfloat16),
                pltpu.VMEM((step, total), jnp.bfloat16),
            ],
            compiler_params=params,
            cost_estimate=pl.CostEstimate(
                flops=4 * total * total * span,
                bytes_accessed=2 * total * (span + LANES),
                transcendentals=total * total,
            ),
        )(*blocks)

    def back(kept_values, mixed_values):
        western = shifted(mixed_values, "win", LAT_WINDOWS)
        packed = pl.pallas_call(
            functools.partial(pack_kernel, split),
            out_shape=[jax.ShapeDtypeStruct((packed_rows, LANES), jnp.bfloat16)] * groups,
            in_specs=[smem] + whole(3),
            out_specs=whole(groups),
            compiler_params=params,
            cost_estimate=pl.CostEstimate(
                flops=total * LANES * 20, bytes_accessed=8 * total * LANES, transcendentals=0
            ),
        )(lon_shift, kept_values, mixed_values, western)
        return spread(packed, -1)

    first = back(*attention(0, [*kept, *first_mixed]))
    second = back(*attention(1, [*kept, *second_mixed]))

    cost = pl.CostEstimate(
        flops=2 * rows * columns * groups * LANES * features,
        bytes_accessed=features * (HEADS * HD + 6 * rows * columns),
        transcendentals=0,
    )
    ordered = (groups * LANES, features)
    partial, weight = pl.pallas_call(
        functools.partial(first_output_kernel, split, groups),
        out_shape=[
            jax.ShapeDtypeStruct(field.shape, jnp.float32),
            jax.ShapeDtypeStruct(ordered, jnp.bfloat16),
        ],
        in_specs=whole(2 + groups),
        out_specs=whole(2),
        scratch_shapes=[pltpu.VMEM(ordered, jnp.bfloat16)],
        compiler_params=params,
        cost_estimate=cost,
    )(field, out_weight, *first)
    result = pl.pallas_call(
        functools.partial(second_output_kernel, split),
        out_shape=jax.ShapeDtypeStruct(field.shape, jnp.bfloat16),
        in_specs=whole(2 + groups),
        out_specs=pl.BlockSpec(memory_space=pltpu.VMEM),
        compiler_params=params,
        cost_estimate=cost,
    )(partial, weight, *second)
    return result[None]


def solution(mesh):
    placed = (P("win", "tok", None, None), P(), P(), P(), P())
    return jax.shard_map(
        shards, mesh=mesh, in_specs=placed, out_specs=P("win", "tok", None, None), check_vma=False
    )
```

time: 75.5 us -> 73.6 us (0.975)
  waiting for transfers between devices: 12.8 us -> 9.24 us
  starting transfers between devices: 40.2 us -> 37.4 us
  Pallas kernels: 19.2 us -> 22 us
  local copies, waits for them, and re-layouts: 3.05 us -> 4.61 us
    ppermute x20 -> x18, waiting for transfers between devices: 12.8 us -> 9.24 us  [shifted(): lax.ppermute(block, axis, [(i, (i + distance) % count) for i in range(cou...]
    pallas_call x3 -> x6, Pallas kernels: 11 us -> 13.8 us  [the longest x2 8.35 us: attention(): pl.pallas_call(functools.partial(attention_kernel, head, groups), out_sha...]
    ppermute x20 -> x18, starting transfers between devices: 40.2 us -> 37.4 us  [shifted(): lax.ppermute(block, axis, [(i, (i + distance) % count) for i in range(cou...]
    unnamed x10 -> x12, local copies, waits for them, and re-layouts: 1.92 us -> 3.5 us
  transfers between devices with their start and end apart: 20 -> 18, of which waited for: 6 -> 6; matrix products, arithmetic and copies ran while one was open for 0% -> 0% of each run, Pallas kernels for 16% -> 28%
where the time goes in v3:
time: 73.6 us; the launch traced here: 73.3 us
  starting transfers between devices  37.4 us (51%)
  Pallas kernels  22 us (30%)
  waiting for transfers between devices  9.24 us (13%)
  local copies, waits for them, and re-layouts  4.61 us (6%)
    ppermute x18, starting transfers between devices, shifted(): lax.ppermute(block, axis, [(i, (i + distance) % count) for i in range(cou...  37.4 us
    ppermute x18, waiting for transfers between devices, shifted(): lax.ppermute(block, axis, [(i, (i + distance) % count) for i in range(cou...  9.24 us
    pallas_call x2, Pallas kernels, attention(): pl.pallas_call(functools.partial(attention_kernel, head, groups), out_sha...  8.35 us
    pallas_call x2, Pallas kernels, projection(): pl.pallas_call(functools.partial(kernel, split), out_shape=[block] * (par...  8.16 us
    unnamed x12, local copies, waits for them, and re-layouts  3.5 us
    pallas_call x1, Pallas kernels, shards(): pl.pallas_call(functools.partial(first_output_kernel, split, groups), out...  2.16 us
    pallas_call x1, Pallas kernels, shards(): pl.pallas_call(functools.partial(second_output_kernel, split), out_shape=...  1.76 us
    pallas_call x2, Pallas kernels, back(): pl.pallas_call(functools.partial(pack_kernel, split), out_shape=[jax.Shap...  1.55 us
  transfers between devices with their start and end apart: 18, of which 6 were waited for; matrix products, arithmetic and copies ran while one was open for 0% of the time, Pallas kernels for 28%

profile of v3, /device:TPU:0, one launch (start us, length us, event | category | flops | bytes accessed | tf_op | source)
XLA Modules:
  0.0 73.3 jit_solution(10183642592604834132)
XLA Ops:
  0.0 1.1 %slice.4 = bf16[10,24,1280]{2,1,0:T(8,128)(2,1)S(1)} slice(bf16[10,40,1280]{2,1,0:T(8,128)(2,1)} %bitcast.2), slice={[0:10], [0:24], [0:1280]} | slice | bytes 1228800 | tf_op jit(solution)/shard_map/slice | solution.py:241
  1.1 3.0 %collective-permute-start.3 = (bf16[10,24,1280]{2,1,0:T(8,128)(2,1)S(1)}, bf16[10,24,1280]{2,1,0:T(8,128)(2,1)S(1)}, u32[]{:S(2)}, u32[]{:S(2)}) collective-permute-start(bf16[10,24,1280]{2,1,0:T(8,128)(2,1)S(1)} %slice.4), channel_id=1, source_target_pairs={{0,16},{4,20},{8,24},{12,28},{16,0},{20,4},{24,8},{28,12},{1,17},{... | collective-permute-start | bytes 1843208 | tf_op jit(solution)/shard_map/ppermute | solution.py:24
  4.2 0.0 copy-start
  4.2 1.2 %copy-done = bf16[1,10,40,1280]{3,2,1,0:T(8,128)(2,1)S(1)} copy-done((bf16[1,10,40,1280]{3,2,1,0:T(8,128)(2,1)S(1)}, bf16[1,10,40,1280]{3,2,1,0:T(8,128)(2,1)}, u32[]{:S(2)}) %copy-start) | copy-done | bytes 1024024
  5.4 0.0 copy-start.4
  5.4 0.7 copy-done.4
  6.1 0.0 copy-start.5
  6.1 3.7 %shard_map.55 = (bf16[160,512]{1,0:T(8,128)(2,1)S(1)}, bf16[160,512]{1,0:T(8,128)(2,1)S(1)}, bf16[160,512]{1,0:T(8,128)(2,1)S(1)}, bf16[160,512]{1,0:T(8,128)(2,1)S(1)}) custom-call(bf16[10,40,1280]{2,1,0:T(8,128)(2,1)S(1)} %bitcast.3, f32[1280]{0:T(1024)S(1)} %copy-done.4, bf16[1280,1920]{1,0:T(8,128)(2,1)} %weight.4), custom_call_target="tpu_custom_call" | custom-call | flops 786432000 | bytes 5734400 | tf_op jit(solution)/shard_map/pallas_call | solution.py:222
  9.8 1.6 %collective-permute-start = (bf16[160,512]{1,0:T(8,128)(2,1)S(1)}, bf16[160,512]{1,0:T(8,128)(2,1)S(1)}, u32[]{:S(2)}, u32[]{:S(2)}) collective-permute-start(bf16[160,512]{1,0:T(8,128)(2,1)S(1)} %get-tuple-element.38), channel_id=1, source_target_pairs={{0,1},{1,2},{2,3},{3,0},{4,5},{5,6},{6,7},{7,4},{8,9},{9,10},{10,1... | collective-permute-start | bytes 491528 | tf_op jit(solution)/shard_map/ppermute | solution.py:24
  11.4 2.6 %collective-permute-start.1 = (bf16[160,512]{1,0:T(8,128)(2,1)S(1)}, bf16[160,512]{1,0:T(8,128)(2,1)S(1)}, u32[]{:S(2)}, u32[]{:S(2)}) collective-permute-start(bf16[160,512]{1,0:T(8,128)(2,1)S(1)} %get-tuple-element.39), channel_id=1, source_target_pairs={{0,2},{1,3},{2,0},{3,1},{4,6},{5,7},{6,4},{7,5},{8,10},{9,11},{10,... | collective-permute-start | bytes 491528 | tf_op jit(solution)/shard_map/ppermute | solution.py:24
  14.0 1.3 %collective-permute-start.2 = (bf16[160,512]{1,0:T(8,128)(2,1)S(1)}, bf16[160,512]{1,0:T(8,128)(2,1)S(1)}, u32[]{:S(2)}, u32[]{:S(2)}) collective-permute-start(bf16[160,512]{1,0:T(8,128)(2,1)S(1)} %get-tuple-element.40), channel_id=1, source_target_pairs={{0,3},{1,0},{2,1},{3,2},{4,7},{5,4},{6,5},{7,6},{8,11},{9,8},{10,9... | collective-permute-start | bytes 491528 | tf_op jit(solution)/shard_map/ppermute | solution.py:24
  15.4 2.6 %collective-permute-done.3.eastern = bf16[10,24,1280]{2,1,0:T(8,128)(2,1)S(1)} collective-permute-done((bf16[10,24,1280]{2,1,0:T(8,128)(2,1)S(1)}, bf16[10,24,1280]{2,1,0:T(8,128)(2,1)S(1)}, u32[]{:S(2)}, u32[]{:S(2)}) %collective-permute-start.3) | collective-permute-done | bytes 614432 | tf_op jit(solution)/shard_map/ppermute | solution.py:24
  18.0 0.0 copy-done.5
  18.0 4.4 %shard_map.56 = (bf16[240,256]{1,0:T(8,128)(2,1)S(1)}, bf16[240,256]{1,0:T(8,128)(2,1)S(1)}, bf16[240,256]{1,0:T(8,128)(2,1)S(1)}, bf16[240,256]{1,0:T(8,128)(2,...) custom-call(s32[4]{0:T(128)S(1)} %copy-done.5, ...), custom_call_target="tpu_custom_call" | custom-call | flops 1179648000 | bytes 6144000 | tf_op jit(solution)/shard_map/pallas_call | solution.py:222
  22.4 0.0 collective-permute-done.refs_1_
  22.4 2.3 %collective-permute-start.4 = (bf16[240,256]{1,0:T(8,128)(2,1)S(1)}, bf16[240,256]{1,0:T(8,128)(2,1)S(1)}, u32[]{:S(2)}, u32[]{:S(2)}) collective-permute-start(bf16[240,256]{1,0:T(8,128)(2,1)S(1)} %get-tuple-element.43), channel_id=1, source_target_pairs={{0,1},{1,2},{2,3},{3,0},{4,5},{5,6},{6,7},{7,4},{8,9},{9,10},{10,1... | collective-permute-start | bytes 368648 | tf_op jit(solution)/shard_map/ppermute | solution.py:24
  24.7 0.0 collective-permute-done.1.refs_2_
  24.7 2.2 %collective-permute-start.5 = (bf16[240,256]{1,0:T(8,128)(2,1)S(1)}, bf16[240,256]{1,0:T(8,128)(2,1)S(1)}, u32[]{:S(2)}, u32[]{:S(2)}) collective-permute-start(bf16[240,256]{1,0:T(8,128)(2,1)S(1)} %get-tuple-element.45), channel_id=1, source_target_pairs={{0,2},{1,3},{2,0},{3,1},{4,6},{5,7},{6,4},{7,5},{8,10},{9,11},{10,... | collective-permute-start | bytes 368648 | tf_op jit(solution)/shard_map/ppermute | solution.py:24
  26.9 0.0 collective-permute-done.2.refs_3_
  26.9 5.0 %collective-permute-start.6 = (bf16[240,256]{1,0:T(8,128)(2,1)S(1)}, bf16[240,256]{1,0:T(8,128)(2,1)S(1)}, u32[]{:S(2)}, u32[]{:S(2)}) collective-permute-start(bf16[240,256]{1,0:T(8,128)(2,1)S(1)} %get-tuple-element.47), channel_id=1, source_target_pairs={{0,3},{1,0},{2,1},{3,2},{4,7},{5,4},{6,5},{7,6},{8,11},{9,8},{10,9... | collective-permute-start | bytes 368648 | tf_op jit(solution)/shard_map/ppermute | solution.py:24
  31.9 0.0 collective-permute-done.4.refs_5_
  31.9 2.8 %collective-permute-start.11 = (bf16[240,256]{1,0:T(8,128)(2,1)S(1)}, bf16[240,256]{1,0:T(8,128)(2,1)S(1)}, u32[]{:S(2)}, u32[]{:S(2)}) collective-permute-start(bf16[240,256]{1,0:T(8,128)(2,1)S(1)} %get-tuple-element.58), channel_id=1, source_target_pairs={{0,1},{1,2},{2,3},{3,0},{4,5},{5,6},{6,7},{7,4},{8,9},{9,10},{10,1... | collective-permute-start | bytes 368648 | tf_op jit(solution)/shard_map/ppermute | solution.py:24
  34.7 1.1 %collective-permute-done.5.refs_6_ = bf16[240,256]{1,0:T(8,128)(2,1)S(1)} collective-permute-done((bf16[240,256]{1,0:T(8,128)(2,1)S(1)}, bf16[240,256]{1,0:T(8,128)(2,1)S(1)}, u32[]{:S(2)}, u32[]{:S(2)}) %collective-permute-start.5) | collective-permute-done | bytes 122912 | tf_op jit(solution)/shard_map/ppermute | solution.py:24
  35.8 1.1 %collective-permute-start.12 = (bf16[240,256]{1,0:T(8,128)(2,1)S(1)}, bf16[240,256]{1,0:T(8,128)(2,1)S(1)}, u32[]{:S(2)}, u32[]{:S(2)}) collective-permute-start(bf16[240,256]{1,0:T(8,128)(2,1)S(1)} %get-tuple-element.60), channel_id=1, source_target_pairs={{0,2},{1,3},{2,0},{3,1},{4,6},{5,7},{6,4},{7,5},{8,10},{9,11},{10,... | collective-permute-start | bytes 368648 | tf_op jit(solution)/shard_map/ppermute | solution.py:24
  36.9 1.3 %collective-permute-done.6.refs_7_ = bf16[240,256]{1,0:T(8,128)(2,1)S(1)} collective-permute-done((bf16[240,256]{1,0:T(8,128)(2,1)S(1)}, bf16[240,256]{1,0:T(8,128)(2,1)S(1)}, u32[]{:S(2)}, u32[]{:S(2)}) %collective-permute-start.6) | collective-permute-done | bytes 122912 | tf_op jit(solution)/shard_map/ppermute | solution.py:24
  38.2 4.4 %collective-permute-start.13 = (bf16[240,256]{1,0:T(8,128)(2,1)S(1)}, bf16[240,256]{1,0:T(8,128)(2,1)S(1)}, u32[]{:S(2)}, u32[]{:S(2)}) collective-permute-start(bf16[240,256]{1,0:T(8,128)(2,1)S(1)} %get-tuple-element.62), channel_id=1, source_target_pairs={{0,3},{1,0},{2,1},{3,2},{4,7},{5,4},{6,5},{7,6},{8,11},{9,8},{10,9... | collective-permute-start | bytes 368648 | tf_op jit(solution)/shard_map/ppermute | solution.py:24
  42.6 4.2 %shard_map.57 = (bf16[640,128]{1,0:T(8,128)(2,1)S(1)}, bf16[960,128]{1,0:T(8,128)(2,1)S(1)}) custom-call(bf16[160,512]{1,0:T(8,128)(2,1)S(1)} %get-tuple-element.37.refs_0_, bf16[160,512]{1,0:T(8,128)(2,1)S(1)} %collective-permute-done.refs_1_, bf16[160,512]{1,0:T(8,128)(2,1)S(1)} %collective-permute-done.1.refs_2_, ...), custom_call_target="tpu_custom_call" | custom-call | flops 2621440000 | bytes 1228800 | tf_op jit(solution)/shard_map/pallas_call | solution.py:252
  46.8 0.1 collective-permute-start.7
  46.9 0.0 collective-permute-done.11.refs_5_
  46.9 0.0 collective-permute-done.12.refs_6_
  46.9 0.8 %collective-permute-done.13.refs_7_ = bf16[240,256]{1,0:T(8,128)(2,1)S(1)} collective-permute-done((bf16[240,256]{1,0:T(8,128)(2,1)S(1)}, bf16[240,256]{1,0:T(8,128)(2,1)S(1)}, u32[]{:S(2)}, u32[]{:S(2)}) %collective-permute-start.13) | collective-permute-done | bytes 122912 | tf_op jit(solution)/shard_map/ppermute | solution.py:24
  47.7 0.0 copy-start.1
  47.7 0.0 copy-start.3
  47.7 4.2 %shard_map.60 = (bf16[640,128]{1,0:T(8,128)(2,1)S(1)}, bf16[960,128]{1,0:T(8,128)(2,1)S(1)}) custom-call(bf16[160,512]{1,0:T(8,128)(2,1)S(1)} %get-tuple-element.37.refs_0_, bf16[160,512]{1,0:T(8,128)(2,1)S(1)} %collective-permute-done.refs_1_, bf16[160,512]{1,0:T(8,128)(2,1)S(1)} %collective-permute-done.1.refs_2_, ...), custom_call_target="tpu_custom_call" | custom-call | flops 2621440000 | bytes 1228800 | tf_op jit(solution)/shard_map/pallas_call | solution.py:252
  51.9 1.5 %collective-permute-start.14 = (bf16[960,128]{1,0:T(8,128)(2,1)S(1)}, bf16[960,128]{1,0:T(8,128)(2,1)S(1)}, u32[]{:S(2)}, u32[]{:S(2)}) collective-permute-start(bf16[960,128]{1,0:T(8,128)(2,1)S(1)} %get-tuple-element.64.mixed), channel_id=1, source_target_pairs={{0,16},{4,20},{8,24},{12,28},{16,0},{20,4},{24,8},{28,12},{1,17},{... | collective-permute-start | bytes 737288 | tf_op jit(solution)/shard_map/ppermute | solution.py:24
  53.4 0.0 collective-permute-done.7.western
  53.4 0.8 %shard_map.58 = (bf16[256,128]{1,0:T(8,128)(2,1)S(1)}, bf16[256,128]{1,0:T(8,128)(2,1)S(1)}, bf16[256,128]{1,0:T(8,128)(2,1)S(1)}, bf16[256,128]{1,0:T(8,128)(2,1)S(1)}) custom-call(s32[4]{0:T(128)S(1)} %copy-done.5, bf16[640,128]{1,0:T(8,128)(2,1)S(1)} %get-tuple-element.48.kept, bf16[960,128]{1,0:T(8,128)(2,1)S(1)} %get-tuple-element.49.mixed, ...), custom_call_target="tpu_custom_call" | custom-call | flops 4096000 | bytes 1638400 | tf_op jit(solution)/shard_map/pallas_call | solution.py:278
  54.1 2.6 %collective-permute-start.8 = (bf16[256,128]{1,0:T(8,128)(2,1)S(1)}, bf16[256,128]{1,0:T(8,128)(2,1)S(1)}, u32[]{:S(2)}, u32[]{:S(2)}) collective-permute-start(bf16[256,128]{1,0:T(8,128)(2,1)S(1)} %get-tuple-element.51), channel_id=1, source_target_pairs={{0,3},{1,0},{2,1},{3,2},{4,7},{5,4},{6,5},{7,6},{8,11},{9,8},{10,9... | collective-permute-start | bytes 196616 | tf_op jit(solution)/shard_map/ppermute | solution.py:24
  56.8 1.1 %collective-permute-start.9 = (bf16[256,128]{1,0:T(8,128)(2,1)S(1)}, bf16[256,128]{1,0:T(8,128)(2,1)S(1)}, u32[]{:S(2)}, u32[]{:S(2)}) collective-permute-start(bf16[256,128]{1,0:T(8,128)(2,1)S(1)} %get-tuple-element.52), channel_id=1, source_target_pairs={{0,2},{1,3},{2,0},{3,1},{4,6},{5,7},{6,4},{7,5},{8,10},{9,11},{10,... | collective-permute-start | bytes 196616 | tf_op jit(solution)/shard_map/ppermute | solution.py:24
  57.9 1.9 %collective-permute-start.10 = (bf16[256,128]{1,0:T(8,128)(2,1)S(1)}, bf16[256,128]{1,0:T(8,128)(2,1)S(1)}, u32[]{:S(2)}, u32[]{:S(2)}) collective-permute-start(bf16[256,128]{1,0:T(8,128)(2,1)S(1)} %get-tuple-element.53), channel_id=1, source_target_pairs={{0,1},{1,2},{2,3},{3,0},{4,5},{5,6},{6,7},{7,4},{8,9},{9,10},{10,1... | collective-permute-start | bytes 196616 | tf_op jit(solution)/shard_map/ppermute | solution.py:24
  59.8 0.0 collective-permute-done.14.western
  59.8 0.8 %shard_map.61 = (bf16[256,128]{1,0:T(8,128)(2,1)S(1)}, bf16[256,128]{1,0:T(8,128)(2,1)S(1)}, bf16[256,128]{1,0:T(8,128)(2,1)S(1)}, bf16[256,128]{1,0:T(8,128)(2,1)S(1)}) custom-call(s32[4]{0:T(128)S(1)} %copy-done.5, bf16[640,128]{1,0:T(8,128)(2,1)S(1)} %get-tuple-element.63.kept, bf16[960,128]{1,0:T(8,128)(2,1)S(1)} %get-tuple-element.64.mixed, ...), custom_call_target="tpu_custom_call" | custom-call | flops 4096000 | bytes 1638400 | tf_op jit(solution)/shard_map/pallas_call | solution.py:278
  60.6 1.9 %collective-permute-start.15 = (bf16[256,128]{1,0:T(8,128)(2,1)S(1)}, bf16[256,128]{1,0:T(8,128)(2,1)S(1)}, u32[]{:S(2)}, u32[]{:S(2)}) collective-permute-start(bf16[256,128]{1,0:T(8,128)(2,1)S(1)} %get-tuple-element.66), channel_id=1, source_target_pairs={{0,3},{1,0},{2,1},{3,2},{4,7},{5,4},{6,5},{7,6},{8,11},{9,8},{10,9... | collective-permute-start | bytes 196616 | tf_op jit(solution)/shard_map/ppermute | solution.py:24
  62.5 1.4 %collective-permute-start.16 = (bf16[256,128]{1,0:T(8,128)(2,1)S(1)}, bf16[256,128]{1,0:T(8,128)(2,1)S(1)}, u32[]{:S(2)}, u32[]{:S(2)}) collective-permute-start(bf16[256,128]{1,0:T(8,128)(2,1)S(1)} %get-tuple-element.67), channel_id=1, source_target_pairs={{0,2},{1,3},{2,0},{3,1},{4,6},{5,7},{6,4},{7,5},{8,10},{9,11},{10,... | collective-permute-start | bytes 196616 | tf_op jit(solution)/shard_map/ppermute | solution.py:24
  63.9 0.0 collective-permute-done.8.refs_1_
  63.9 0.5 collective-permute-start.17
  64.4 0.0 collective-permute-done.9.refs_2_
  64.4 0.0 collective-permute-done.10.refs_3_
  64.4 0.0 copy-done.1
  64.4 0.0 copy-done.3
  64.4 2.2 %shard_map.59 = (f32[10,40,1280]{2,1,0:T(8,128)}, bf16[512,1280]{1,0:T(8,128)(2,1)S(1)}) custom-call(bf16[10,40,1280]{2,1,0:T(8,128)(2,1)S(1)} %bitcast.5, bf16[640,1280]{1,0:T(8,128)(2,1)S(1)} %copy-done.3, bf16[256,128]{1,0:T(8,128)(2,1)S(1)} %get-tuple-element.50.refs_0_, bf16[256,128]{1,0:T(8,128)(2,1)S(1)} %collective-permute-done.8.refs_1_, ...), custom_call_target="tpu_custom_call" | custom-call | flops 524288000 | bytes 3891200 | tf_op jit(solution)/shard_map/pallas_call | solution.py:299
  66.6 0.0 collective-permute-done.15.refs_1_
  66.6 2.3 %collective-permute-done.16.refs_2_ = bf16[256,128]{1,0:T(8,128)(2,1)S(1)} collective-permute-done((bf16[256,128]{1,0:T(8,128)(2,1)S(1)}, bf16[256,128]{1,0:T(8,128)(2,1)S(1)}, u32[]{:S(2)}, u32[]{:S(2)}) %collective-permute-start.16) | collective-permute-done | bytes 65568 | tf_op jit(solution)/shard_map/ppermute | solution.py:24
  68.9 1.1 %collective-permute-done.17.refs_3_ = bf16[256,128]{1,0:T(8,128)(2,1)S(1)} collective-permute-done((bf16[256,128]{1,0:T(8,128)(2,1)S(1)}, bf16[256,128]{1,0:T(8,128)(2,1)S(1)}, u32[]{:S(2)}, u32[]{:S(2)}) %collective-permute-start.17) | collective-permute-done | bytes 65568 | tf_op jit(solution)/shard_map/ppermute | solution.py:24
  70.0 0.0 copy-start.2
  70.0 1.6 %copy-done.2 = f32[10,40,1280]{2,1,0:T(8,128)S(1)} copy-done((f32[10,40,1280]{2,1,0:T(8,128)S(1)}, f32[10,40,1280]{2,1,0:T(8,128)}, u32[]{:S(2)}) %copy-start.2) | copy-done | bytes 2048024
  71.5 1.8 %shard_map.62 = bf16[10,40,1280]{2,1,0:T(8,128)(2,1)} custom-call(f32[10,40,1280]{2,1,0:T(8,128)S(1)} %copy-done.2, bf16[512,1280]{1,0:T(8,128)(2,1)S(1)} %get-tuple-element.55.weight, bf16[256,128]{1,0:T(8,128)(2,1)S(1)} %get-tuple-element.65.refs_0_, bf16[256,128]{1,0:T(8,128)(2,1)S(1)} %collective-permute-done.15.refs_1_, ...), custom_call_target="tpu_custom_call" | custom-call | flops 524288000 | bytes 3891200 | tf_op jit(solution)/shard_map/pallas_call | solution.py:311
Async XLA Ops:
  1.1 16.9 %collective-permute-start.3 = (bf16[10,24,1280]{2,1,0:T(8,128)(2,1)S(1)}, bf16[10,24,1280]{2,1,0:T(8,128)(2,1)S(1)}, u32[]{:S(2)}, u32[]{:S(2)}) collective-permute-start(bf16[10,24,1280]{2,1,0:T(8,128)(2,1)S(1)} %slice.4), channel_id=1, source_target_pairs={{0,16},{4,20},{8,24},{12,28},{16,0},{20,4},{24,8},{28,12},{1,17},{... | collective-permute-start | bytes 1843208 | tf_op jit(solution)/shard_map/ppermute | solution.py:24
  4.2 1.2 %copy-start = (bf16[1,10,40,1280]{3,2,1,0:T(8,128)(2,1)S(1)}, bf16[1,10,40,1280]{3,2,1,0:T(8,128)(2,1)}, u32[]{:S(2)}) copy-start(bf16[1,10,40,1280]{3,2,1,0:T(8,128)(2,1)} %param.5) | copy-start | bytes 3072004
  5.4 0.7 copy-start.4
  6.1 11.9 %copy-start.5 = (s32[4]{0:T(128)S(1)}, s32[4]{0:T(128)}, u32[]{:S(2)}) copy-start(s32[4]{0:T(128)} %lon_shift.5) | copy-start | bytes 52
  9.8 12.6 %collective-permute-start = (bf16[160,512]{1,0:T(8,128)(2,1)S(1)}, bf16[160,512]{1,0:T(8,128)(2,1)S(1)}, u32[]{:S(2)}, u32[]{:S(2)}) collective-permute-start(bf16[160,512]{1,0:T(8,128)(2,1)S(1)} %get-tuple-element.38), channel_id=1, source_target_pairs={{0,1},{1,2},{2,3},{3,0},{4,5},{5,6},{6,7},{7,4},{8,9},{9,10},{10,1... | collective-permute-start | bytes 491528 | tf_op jit(solution)/shard_map/ppermute | solution.py:24
  11.4 13.2 %collective-permute-start.1 = (bf16[160,512]{1,0:T(8,128)(2,1)S(1)}, bf16[160,512]{1,0:T(8,128)(2,1)S(1)}, u32[]{:S(2)}, u32[]{:S(2)}) collective-permute-start(bf16[160,512]{1,0:T(8,128)(2,1)S(1)} %get-tuple-element.39), channel_id=1, source_target_pairs={{0,2},{1,3},{2,0},{3,1},{4,6},{5,7},{6,4},{7,5},{8,10},{9,11},{10,... | collective-permute-start | bytes 491528 | tf_op jit(solution)/shard_map/ppermute | solution.py:24
  14.0 12.9 %collective-permute-start.2 = (bf16[160,512]{1,0:T(8,128)(2,1)S(1)}, bf16[160,512]{1,0:T(8,128)(2,1)S(1)}, u32[]{:S(2)}, u32[]{:S(2)}) collective-permute-start(bf16[160,512]{1,0:T(8,128)(2,1)S(1)} %get-tuple-element.40), channel_id=1, source_target_pairs={{0,3},{1,0},{2,1},{3,2},{4,7},{5,4},{6,5},{7,6},{8,11},{9,8},{10,9... | collective-permute-start | bytes 491528 | tf_op jit(solution)/shard_map/ppermute | solution.py:24
  22.4 9.5 %collective-permute-start.4 = (bf16[240,256]{1,0:T(8,128)(2,1)S(1)}, bf16[240,256]{1,0:T(8,128)(2,1)S(1)}, u32[]{:S(2)}, u32[]{:S(2)}) collective-permute-start(bf16[240,256]{1,0:T(8,128)(2,1)S(1)} %get-tuple-element.43), channel_id=1, source_target_pairs={{0,1},{1,2},{2,3},{3,0},{4,5},{5,6},{6,7},{7,4},{8,9},{9,10},{10,1... | collective-permute-start | bytes 368648 | tf_op jit(solution)/shard_map/ppermute | solution.py:24
  24.7 11.1 %collective-permute-start.5 = (bf16[240,256]{1,0:T(8,128)(2,1)S(1)}, bf16[240,256]{1,0:T(8,128)(2,1)S(1)}, u32[]{:S(2)}, u32[]{:S(2)}) collective-permute-start(bf16[240,256]{1,0:T(8,128)(2,1)S(1)} %get-tuple-element.45), channel_id=1, source_target_pairs={{0,2},{1,3},{2,0},{3,1},{4,6},{5,7},{6,4},{7,5},{8,10},{9,11},{10,... | collective-permute-start | bytes 368648 | tf_op jit(solution)/shard_map/ppermute | solution.py:24
  26.9 11.3 %collective-permute-start.6 = (bf16[240,256]{1,0:T(8,128)(2,1)S(1)}, bf16[240,256]{1,0:T(8,128)(2,1)S(1)}, u32[]{:S(2)}, u32[]{:S(2)}) collective-permute-start(bf16[240,256]{1,0:T(8,128)(2,1)S(1)} %get-tuple-element.47), channel_id=1, source_target_pairs={{0,3},{1,0},{2,1},{3,2},{4,7},{5,4},{6,5},{7,6},{8,11},{9,8},{10,9... | collective-permute-start | bytes 368648 | tf_op jit(solution)/shard_map/ppermute | solution.py:24
  31.9 14.9 %collective-permute-start.11 = (bf16[240,256]{1,0:T(8,128)(2,1)S(1)}, bf16[240,256]{1,0:T(8,128)(2,1)S(1)}, u32[]{:S(2)}, u32[]{:S(2)}) collective-permute-start(bf16[240,256]{1,0:T(8,128)(2,1)S(1)} %get-tuple-element.58), channel_id=1, source_target_pairs={{0,1},{1,2},{2,3},{3,0},{4,5},{5,6},{6,7},{7,4},{8,9},{9,10},{10,1... | collective-permute-start | bytes 368648 | tf_op jit(solution)/shard_map/ppermute | solution.py:24
  35.8 11.1 %collective-permute-start.12 = (bf16[240,256]{1,0:T(8,128)(2,1)S(1)}, bf16[240,256]{1,0:T(8,128)(2,1)S(1)}, u32[]{:S(2)}, u32[]{:S(2)}) collective-permute-start(bf16[240,256]{1,0:T(8,128)(2,1)S(1)} %get-tuple-element.60), channel_id=1, source_target_pairs={{0,2},{1,3},{2,0},{3,1},{4,6},{5,7},{6,4},{7,5},{8,10},{9,11},{10,... | collective-permute-start | bytes 368648 | tf_op jit(solution)/shard_map/ppermute | solution.py:24
  38.2 9.5 %collective-permute-start.13 = (bf16[240,256]{1,0:T(8,128)(2,1)S(1)}, bf16[240,256]{1,0:T(8,128)(2,1)S(1)}, u32[]{:S(2)}, u32[]{:S(2)}) collective-permute-start(bf16[240,256]{1,0:T(8,128)(2,1)S(1)} %get-tuple-element.62), channel_id=1, source_target_pairs={{0,3},{1,0},{2,1},{3,2},{4,7},{5,4},{6,5},{7,6},{8,11},{9,8},{10,9... | collective-permute-start | bytes 368648 | tf_op jit(solution)/shard_map/ppermute | solution.py:24
  46.8 6.6 %collective-permute-start.7 = (bf16[960,128]{1,0:T(8,128)(2,1)S(1)}, bf16[960,128]{1,0:T(8,128)(2,1)S(1)}, u32[]{:S(2)}, u32[]{:S(2)}) collective-permute-start(bf16[960,128]{1,0:T(8,128)(2,1)S(1)} %get-tuple-element.49.mixed), channel_id=1, source_target_pairs={{0,16},{4,20},{8,24},{12,28},{16,0},{20,4},{24,8},{28,12},{1,17},{... | collective-permute-start | bytes 737288 | tf_op jit(solution)/shard_map/ppermute | solution.py:24
  47.7 16.7 %copy-start.1 = (bf16[1,10,40,1280]{3,2,1,0:T(8,128)(2,1)S(1)}, bf16[1,10,40,1280]{3,2,1,0:T(8,128)(2,1)}, u32[]{:S(2)}) copy-start(bf16[1,10,40,1280]{3,2,1,0:T(8,128)(2,1)} %param.5) | copy-start | bytes 3072004
  47.7 16.7 %copy-start.3 = (bf16[640,1280]{1,0:T(8,128)(2,1)S(1)}, bf16[640,1280]{1,0:T(8,128)(2,1)}, u32[]{:S(2)}) copy-start(bf16[640,1280]{1,0:T(8,128)(2,1)} %weight.5) | copy-start | bytes 4915204
  51.9 8.0 %collective-permute-start.14 = (bf16[960,128]{1,0:T(8,128)(2,1)S(1)}, bf16[960,128]{1,0:T(8,128)(2,1)S(1)}, u32[]{:S(2)}, u32[]{:S(2)}) collective-permute-start(bf16[960,128]{1,0:T(8,128)(2,1)S(1)} %get-tuple-element.64.mixed), channel_id=1, source_target_pairs={{0,16},{4,20},{8,24},{12,28},{16,0},{20,4},{24,8},{28,12},{1,17},{... | collective-permute-start | bytes 737288 | tf_op jit(solution)/shard_map/ppermute | solution.py:24
  54.1 9.7 %collective-permute-start.8 = (bf16[256,128]{1,0:T(8,128)(2,1)S(1)}, bf16[256,128]{1,0:T(8,128)(2,1)S(1)}, u32[]{:S(2)}, u32[]{:S(2)}) collective-permute-start(bf16[256,128]{1,0:T(8,128)(2,1)S(1)} %get-tuple-element.51), channel_id=1, source_target_pairs={{0,3},{1,0},{2,1},{3,2},{4,7},{5,4},{6,5},{7,6},{8,11},{9,8},{10,9... | collective-permute-start | bytes 196616 | tf_op jit(solution)/shard_map/ppermute | solution.py:24
  56.8 7.6 %collective-permute-start.9 = (bf16[256,128]{1,0:T(8,128)(2,1)S(1)}, bf16[256,128]{1,0:T(8,128)(2,1)S(1)}, u32[]{:S(2)}, u32[]{:S(2)}) collective-permute-start(bf16[256,128]{1,0:T(8,128)(2,1)S(1)} %get-tuple-element.52), channel_id=1, source_target_pairs={{0,2},{1,3},{2,0},{3,1},{4,6},{5,7},{6,4},{7,5},{8,10},{9,11},{10,... | collective-permute-start | bytes 196616 | tf_op jit(solution)/shard_map/ppermute | solution.py:24
  57.9 6.5 %collective-permute-start.10 = (bf16[256,128]{1,0:T(8,128)(2,1)S(1)}, bf16[256,128]{1,0:T(8,128)(2,1)S(1)}, u32[]{:S(2)}, u32[]{:S(2)}) collective-permute-start(bf16[256,128]{1,0:T(8,128)(2,1)S(1)} %get-tuple-element.53), channel_id=1, source_target_pairs={{0,1},{1,2},{2,3},{3,0},{4,5},{5,6},{6,7},{7,4},{8,9},{9,10},{10,1... | collective-permute-start | bytes 196616 | tf_op jit(solution)/shard_map/ppermute | solution.py:24
  60.6 6.0 %collective-permute-start.15 = (bf16[256,128]{1,0:T(8,128)(2,1)S(1)}, bf16[256,128]{1,0:T(8,128)(2,1)S(1)}, u32[]{:S(2)}, u32[]{:S(2)}) collective-permute-start(bf16[256,128]{1,0:T(8,128)(2,1)S(1)} %get-tuple-element.66), channel_id=1, source_target_pairs={{0,3},{1,0},{2,1},{3,2},{4,7},{5,4},{6,5},{7,6},{8,11},{9,8},{10,9... | collective-permute-start | bytes 196616 | tf_op jit(solution)/shard_map/ppermute | solution.py:24
  62.5 6.3 %collective-permute-start.16 = (bf16[256,128]{1,0:T(8,128)(2,1)S(1)}, bf16[256,128]{1,0:T(8,128)(2,1)S(1)}, u32[]{:S(2)}, u32[]{:S(2)}) collective-permute-start(bf16[256,128]{1,0:T(8,128)(2,1)S(1)} %get-tuple-element.67), channel_id=1, source_target_pairs={{0,2},{1,3},{2,0},{3,1},{4,6},{5,7},{6,4},{7,5},{8,10},{9,11},{10,... | collective-permute-start | bytes 196616 | tf_op jit(solution)/shard_map/ppermute | solution.py:24
  63.9 6.1 %collective-permute-start.17 = (bf16[256,128]{1,0:T(8,128)(2,1)S(1)}, bf16[256,128]{1,0:T(8,128)(2,1)S(1)}, u32[]{:S(2)}, u32[]{:S(2)}) collective-permute-start(bf16[256,128]{1,0:T(8,128)(2,1)S(1)} %get-tuple-element.68), channel_id=1, source_target_pairs={{0,1},{1,2},{2,3},{3,0},{4,5},{5,6},{6,7},{7,4},{8,9},{9,10},{10,1... | collective-permute-start | bytes 196616 | tf_op jit(solution)/shard_map/ppermute | solution.py:24
  70.0 1.6 %copy-start.2 = (f32[10,40,1280]{2,1,0:T(8,128)S(1)}, f32[10,40,1280]{2,1,0:T(8,128)}, u32[]{:S(2)}) copy-start(f32[10,40,1280]{2,1,0:T(8,128)} %get-tuple-element.54.partial) | copy-start | bytes 6144004

commit v4 on v3

--- a/solution.py
+++ b/solution.py
@@ -24,69 +24,60 @@
     return lax.ppermute(block, axis, [(i, (i + distance) % count) for i in range(count)])
 
 
-def after(blocks, arrived):
-    return [blocks[0]] + [
-        lax.optimization_barrier(pair)[0] for pair in zip(blocks[1:], arrived[1:])
-    ]
+def exchanged(blocks):
+    return lax.all_to_all(blocks, "tok", split_axis=0, concat_axis=0, tiled=True)
 
 
 def column_offset(lon_shift):
     return lon_shift[lax.rem(lax.axis_index("win"), LAT_WINDOWS)]
 
 
-def project(tokens, gain, weight, slots, outs):
-    local = HEADS // slots.shape[0]
-    groups = slots.shape[0]
+def project(tokens, gain, weight, outs):
+    groups = outs[0].shape[0]
+    local = HEADS // groups
     count, features = tokens.shape
-    span = slots.shape[2] // local
+    span = outs[0].shape[2] * len(outs) // local
     factor = lax.rsqrt(jnp.mean(tokens * tokens, axis=-1, keepdims=True) + 1e-06)
     normed = (tokens * factor * gain[...].reshape(1, features)).astype(jnp.bfloat16)
     qkv = jnp.dot(normed, weight[...], preferred_element_type=jnp.float32)
     tail = jnp.ones((count, span - 3 * HD), jnp.float32)
-    place = lax.axis_index("tok")
-    for group in range(groups):
-        slot = lax.rem(group - place + groups, groups)
-        columns = []
-        for head in range(group * local, (group + 1) * local):
-            columns += [
-                qkv[:, (kind * HEADS + head) * HD : (kind * HEADS + head + 1) * HD]
-                for kind in range(3)
-            ] + [tail]
-        slots[slot] = jnp.concatenate(columns, axis=1).astype(jnp.bfloat16)
-    parts = len(outs) // groups
-    for index, out in enumerate(outs):
-        first = index // groups * out.shape[1]
-        out[...] = slots[index % groups, :, first : first + out.shape[1]]
-
-
-def kept_kernel(split, field, gain, weight, *refs):
-    *outs, slots = refs
+    for index in range(HEADS):
+        group, head = index // local, index % local
+        columns = [
+            qkv[:, (kind * HEADS + index) * HD : (kind * HEADS + index + 1) * HD]
+            for kind in range(3)
+        ]
+        block = jnp.concatenate(columns + [tail], axis=1).astype(jnp.bfloat16)
+        if len(outs) == 1:
+            outs[0][group, :, head * span : (head + 1) * span] = block
+        else:
+            outs[head][group] = block
+
+
+def kept_kernel(split, field, gain, weight, *outs):
     rows, columns, features = field.shape
     tokens = field[...].astype(jnp.float32)[:, split:]
-    project(tokens.reshape(rows * (columns - split), features), gain, weight, slots, outs)
-
-
-def mixed_kernel(split, lon_shift, field, eastern, gain, weight, *refs):
-    *outs, slots = refs
+    project(tokens.reshape(rows * (columns - split), features), gain, weight, outs)
+
+
+def mixed_kernel(split, lon_shift, field, eastern, gain, weight, *outs):
     rows, _, features = field.shape
     own = field[...].astype(jnp.float32)[:, :split]
     column = lax.broadcasted_iota(jnp.int32, own.shape, 1)
     tokens = jnp.where(column < column_offset(lon_shift), eastern[...].astype(jnp.float32), own)
-    project(tokens.reshape(rows * split, features), gain, weight, slots, outs)
-
-
-def attention_kernel(head, groups, *refs):
-    kept, mixed = refs[:groups], refs[groups : 2 * groups]
-    kept_out, mixed_out, held, keys = refs[2 * groups : 2 * groups + 4]
-    scores, weights = refs[2 * groups + 4 : 2 * groups + 6], refs[2 * groups + 6 :]
+    project(tokens.reshape(rows * split, features), gain, weight, outs)
+
+
+def attention_kernel(head, kept, mixed, kept_out, mixed_out, held, keys, *refs):
+    scores, weights = refs[:2], refs[2:]
     span = held.shape[1]
     start = 0
-    for block in kept:
-        held[start : start + block.shape[0]] = block[:, head * span : (head + 1) * span]
-        start += block.shape[0]
-    for block in mixed:
-        held[start : start + block.shape[0]] = block[...]
-        start += block.shape[0]
+    for group in range(kept.shape[0]):
+        held[start : start + kept.shape[1]] = kept[group, :, head * span : (head + 1) * span]
+        start += kept.shape[1]
+    for group in range(mixed.shape[0]):
+        held[start : start + mixed.shape[1]] = mixed[group]
+        start += mixed.shape[1]
     keys[...] = held[...].T
     factor = HD ** (-0.5) * 1.4426950408889634
     step = scores[0].shape[0]
@@ -120,8 +111,8 @@
             mixed_out[first : first + step] = values
 
 
-def pack_kernel(split, lon_shift, kept, mixed, western, *outs):
-    groups = len(outs)
+def pack_kernel(split, lon_shift, kept, mixed, western, out):
+    groups = out.shape[0]
     half = LANES // 2
     rest = HD - half
     fold = LANES // rest
@@ -130,7 +121,7 @@
     part = round_up(-(-count // fold), SUBLANES)
     shape = (mixed_count // split, split, LANES)
     taken = lax.broadcasted_iota(jnp.int32, shape, 1) < column_offset(lon_shift)
-    for group, out in enumerate(outs):
+    for group in range(groups):
         rows = slice(group * mixed_count, (group + 1) * mixed_count)
         own, west = mixed[rows].astype(jnp.float32), western[rows].astype(jnp.float32)
         chosen = jnp.where(taken, west.reshape(shape), own.reshape(shape)).reshape(own.shape)
@@ -147,7 +138,7 @@
                 piece = jnp.concatenate([piece, empty], axis=0)
             piece = pltpu.roll(piece, (index * rest + half) % LANES, axis=1)
             rests = jnp.where(lane // rest == index, piece, rests)
-        out[...] = jnp.concatenate([main, rests], axis=0).astype(jnp.bfloat16)
+        out[group] = jnp.concatenate([main, rests], axis=0).astype(jnp.bfloat16)
 
 
 def unpack(blocks, count):
@@ -156,8 +147,8 @@
     fold = LANES // rest
     part = round_up(-(-count // fold), SUBLANES)
     columns = []
-    for block in blocks:
-        block = block[...].astype(jnp.float32)
+    for group in range(blocks.shape[0]):
+        block = blocks[group].astype(jnp.float32)
         main, rests = block[: count // 2], block[count // 2 :]
         main = jnp.concatenate([main, pltpu.roll(main, half, axis=1)], axis=0)
         pieces = []
@@ -177,15 +168,13 @@
     return jnp.concatenate([left, right], axis=1)
 
 
-def first_output_kernel(split, groups, field, weight, *refs):
-    blocks, (out, second, first) = refs[:groups], refs[groups:]
+def first_output_kernel(split, groups, field, weight, blocks, out, second, first):
     rows, columns, features = field.shape
-    for slot in range(groups):
-        group = lax.rem(lax.axis_index("tok") + slot, groups)
+    for group in range(groups):
         for head, ordered in enumerate((first, second)):
-            at = pl.multiple_of((group * HEADS // groups + head) * HD, 16)
-            ordered[slot * LANES : slot * LANES + HD] = weight[pl.ds(at, HD)]
-            ordered[slot * LANES + HD : (slot + 1) * LANES] = jnp.zeros(
+            at = (group * HEADS // groups + head) * HD
+            ordered[group * LANES : group * LANES + HD] = weight[at : at + HD]
+            ordered[group * LANES + HD : (group + 1) * LANES] = jnp.zeros(
                 (LANES - HD, features), jnp.bfloat16
             )
     attended = unpack(blocks, rows * columns)
@@ -193,8 +182,7 @@
     out[...] = field[...].astype(jnp.float32) + by_column(projected, rows, columns, split)
 
 
-def second_output_kernel(split, partial, weight, *refs):
-    *blocks, out = refs
+def second_output_kernel(split, partial, weight, blocks, out):
     rows, columns, _ = partial.shape
     attended = unpack(blocks, rows * columns)
     projected = jnp.dot(attended, weight[...], preferred_element_type=jnp.float32)
@@ -218,13 +206,12 @@
     kept_count, mixed_count = rows * (columns - split), rows * split
 
     def projection(kernel, count, parts, scalars, operands):
-        block = jax.ShapeDtypeStruct((count, local * span // parts), jnp.bfloat16)
+        block = jax.ShapeDtypeStruct((groups, count, local * span // parts), jnp.bfloat16)
         return pl.pallas_call(
             functools.partial(kernel, split),
-            out_shape=[block] * (parts * groups),
+            out_shape=[block] * parts,
             in_specs=[smem] * len(scalars) + whole(len(operands) + 2),
-            out_specs=whole(parts * groups),
-            scratch_shapes=[pltpu.VMEM((groups, count, local * span), jnp.bfloat16)],
+            out_specs=whole(parts),
             compiler_params=params,
             cost_estimate=pl.CostEstimate(
                 flops=2 * count * features * 3 * HEADS * HD,
@@ -233,24 +220,17 @@
             ),
         )(*scalars, *operands, norm_gain, qkv_weight)
 
-    def spread(blocks, sign):
-        return [blocks[0]] + [
-            shifted(blocks[distance], "tok", sign * distance) for distance in range(1, groups)
-        ]
-
     eastern = shifted(field[:, :split], "win", -LAT_WINDOWS)
-    kept = spread(projection(kept_kernel, kept_count, 1, [], [field]), 1)
+    kept = exchanged(projection(kept_kernel, kept_count, 1, [], [field])[0])
     mixed = projection(mixed_kernel, mixed_count, local, [lon_shift], [field, eastern])
-    first_mixed = spread(after(mixed[:groups], kept), 1)
-    second_mixed = spread(after(mixed[groups:], first_mixed), 1)
 
     total = groups * rows * columns
     step = total // 5
     packed_rows = round_up(rows * columns // 2 + -(-rows * columns * (HD - LANES // 2) // LANES), 16)
 
-    def attention(head, blocks):
+    def attention(head, *blocks):
         return pl.pallas_call(
-            functools.partial(attention_kernel, head, groups),
+            functools.partial(attention_kernel, head),
             out_shape=[
                 jax.ShapeDtypeStruct((groups * count, LANES), jnp.bfloat16)
                 for count in (kept_count, mixed_count)
@@ -277,18 +257,18 @@
         western = shifted(mixed_values, "win", LAT_WINDOWS)
         packed = pl.pallas_call(
             functools.partial(pack_kernel, split),
-            out_shape=[jax.ShapeDtypeStruct((packed_rows, LANES), jnp.bfloat16)] * groups,
+            out_shape=jax.ShapeDtypeStruct((groups, packed_rows, LANES), jnp.bfloat16),
             in_specs=[smem] + whole(3),
-            out_specs=whole(groups),
+            out_specs=pl.BlockSpec(memory_space=pltpu.VMEM),
             compiler_params=params,
             cost_estimate=pl.CostEstimate(
                 flops=total * LANES * 20, bytes_accessed=8 * total * LANES, transcendentals=0
             ),
         )(lon_shift, kept_values, mixed_values, western)
-        return spread(packed, -1)
-
-    first = back(*attention(0, [*kept, *first_mixed]))
-    second = back(*attention(1, [*kept, *second_mixed]))
+        return exchanged(packed)
+
+    first = back(*attention(0, kept, exchanged(mixed[0])))
+    second = back(*attention(1, kept, exchanged(mixed[1])))
 
     cost = pl.CostEstimate(
         flops=2 * rows * columns * groups * LANES * features,
@@ -302,20 +282,20 @@
             jax.ShapeDtypeStruct(field.shape, jnp.float32),
             jax.ShapeDtypeStruct(ordered, jnp.bfloat16),
         ],
-        in_specs=whole(2 + groups),
+        in_specs=whole(3),
         out_specs=whole(2),
         scratch_shapes=[pltpu.VMEM(ordered, jnp.bfloat16)],
         compiler_params=params,
         cost_estimate=cost,
-    )(field, out_weight, *first)
+    )(field, out_weight, first)
     result = pl.pallas_call(
         functools.partial(second_output_kernel, split),
         out_shape=jax.ShapeDtypeStruct(field.shape, jnp.bfloat16),
-        in_specs=whole(2 + groups),
+        in_specs=whole(3),
         out_specs=pl.BlockSpec(memory_space=pltpu.VMEM),
         compiler_params=params,
         cost_estimate=cost,
-    )(partial, weight, *second)
+    )(partial, weight, second)
     return result[None]
 
 

time: 73.6 us -> 101 us (1.37)
  waiting for transfers between devices: 9.24 us -> 27.1 us
  blocking collectives: 0 us -> 16.9 us
  starting transfers between devices: 37.4 us -> 24.4 us
  Pallas kernels: 22 us -> 24.8 us
  local copies, waits for them, and re-layouts: 4.61 us -> 7.02 us
    ppermute x18 -> x3, starting transfers between devices: 37.4 us -> 4.74 us  [shifted(): lax.ppermute(block, axis, [(i, (i + distance) % count) for i in range(cou...]
    all_to_all x0 -> x4, starting transfers between devices: none -> 19.6 us  [exchanged(): lax.all_to_all(blocks, 'tok', split_axis=0, concat_axis=0, tiled=True)]
    all_to_all x0 -> x1, blocking collectives: none -> 16.9 us  [exchanged(): lax.all_to_all(blocks, 'tok', split_axis=0, concat_axis=0, tiled=True)]
    ppermute x18 -> x3, waiting for transfers between devices: 9.24 us -> 23.1 us  [shifted(): lax.ppermute(block, axis, [(i, (i + distance) % count) for i in range(cou...]
    all_to_all x0 -> x4, waiting for transfers between devices: none -> 3.96 us  [exchanged(): lax.all_to_all(blocks, 'tok', split_axis=0, concat_axis=0, tiled=True)]
    unnamed x12 -> x22, local copies, waits for them, and re-layouts: 3.5 us -> 6.98 us
    pallas_call x6, Pallas kernels: 18.1 us -> 20.9 us  [the longest x2 9.61 us: projection(): pl.pallas_call(functools.partial(kernel, split), out_shape=[block] * part...]
    slice x1, local copies, waits for them, and re-layouts: 1.11 us -> 0.04 us  [shards(): eastern = shifted(field[:, :split], 'win', -LAT_WINDOWS)]
  transfers between devices with their start and end apart: 18 -> 7, of which waited for: 6 -> 5; matrix products, arithmetic and copies ran while one was open for 0% -> 0% of each run, Pallas kernels for 28% -> 18%
where the time goes in v4:
time: 101 us; the launch traced here: 100 us
  waiting for transfers between devices  27.1 us (27%)
  Pallas kernels  24.8 us (25%)
  starting transfers between devices  24.4 us (24%)
  blocking collectives  16.9 us (17%)
  local copies, waits for them, and re-layouts  7.02 us (7%)
    ppermute x3, waiting for transfers between devices, shifted(): lax.ppermute(block, axis, [(i, (i + distance) % count) for i in range(cou...  23.1 us
    all_to_all x4, starting transfers between devices, exchanged(): lax.all_to_all(blocks, 'tok', split_axis=0, concat_axis=0, tiled=True)  19.6 us
    all_to_all x1, blocking collectives, exchanged(): lax.all_to_all(blocks, 'tok', split_axis=0, concat_axis=0, tiled=True)  16.9 us
    pallas_call x2, Pallas kernels, projection(): pl.pallas_call(functools.partial(kernel, split), out_shape=[block] * part...  9.61 us
    pallas_call x2, Pallas kernels, attention(): pl.pallas_call(functools.partial(attention_kernel, head), out_shape=[jax....  8.36 us
    unnamed x22, local copies, waits for them, and re-layouts  6.98 us
    ppermute x3, starting transfers between devices, shifted(): lax.ppermute(block, axis, [(i, (i + distance) % count) for i in range(cou...  4.74 us
    all_to_all x4, waiting for transfers between devices, exchanged(): lax.all_to_all(blocks, 'tok', split_axis=0, concat_axis=0, tiled=True)  3.96 us
  transfers between devices with their start and end apart: 7, of which 5 were waited for; matrix products, arithmetic and copies ran while one was open for 0% of the time, Pallas kernels for 18%

profile of v4, /device:TPU:0, one launch (start us, length us, event | category | flops | bytes accessed | tf_op | source)
XLA Modules:
  0.0 100.3 jit_solution(11212955157447100407)
XLA Ops:
  0.0 0.0 copy-start
  0.0 1.2 %copy-done = bf16[1,10,40,1280]{3,2,1,0:T(8,128)(2,1)S(1)} copy-done((bf16[1,10,40,1280]{3,2,1,0:T(8,128)(2,1)S(1)}, bf16[1,10,40,1280]{3,2,1,0:T(8,128)(2,1)}, u32[]{:S(2)}) %copy-start) | copy-done | bytes 1024024
  1.2 0.0 copy-start.8
  1.2 0.7 copy-done.8
  1.9 0.0 copy-start.1
  1.9 4.6 %shard_map.55 = bf16[4,160,512]{2,1,0:T(8,128)(2,1)} custom-call(bf16[10,40,1280]{2,1,0:T(8,128)(2,1)S(1)} %bitcast.2, f32[1280]{0:T(1024)S(1)} %copy-done.8, bf16[1280,1920]{1,0:T(8,128)(2,1)} %weight.4), custom_call_target="tpu_custom_call" | custom-call | flops 786432000 | bytes 5734400 | tf_op jit(solution)/shard_map/pallas_call | solution.py:210
  6.5 0.0 copy-start.9
  6.5 0.0 copy-start.10
  6.5 6.5 %all-to-all-start = ((bf16[4,160,512]{2,1,0:T(8,128)(2,1)}), bf16[4,160,512]{2,1,0:T(8,128)(2,1)S(1)}, u32[]{:S(2)}, u32[]{:S(2)}) async-start(bf16[4,160,512]{2,1,0:T(8,128)(2,1)} %shard_map.55), calls=%async_computation | async-start | bytes 1310720 | tf_op jit(solution)/shard_map/all_to_all | solution.py:28
  12.9 0.0 copy-done.1
  13.0 1.6 %collective-permute-start = (bf16[10,24,1280]{2,1,0:T(8,128)(2,1)S(1)}, bf16[10,24,1280]{2,1,0:T(8,128)(2,1)S(1)}, u32[]{:S(2)}, u32[]{:S(2)}) collective-permute-start(bf16[10,24,1280]{2,1,0:T(8,128)(2,1)S(1)} %slice.4), channel_id=1, source_target_pairs={{0,16},{4,20},{8,24},{12,28},{16,0},{20,4},{24,8},{28,12},{1,17},{... | collective-permute-start | bytes 1843208 | tf_op jit(solution)/shard_map/ppermute | solution.py:24
  14.6 13.8 %collective-permute-done.eastern = bf16[10,24,1280]{2,1,0:T(8,128)(2,1)S(1)} collective-permute-done((bf16[10,24,1280]{2,1,0:T(8,128)(2,1)S(1)}, bf16[10,24,1280]{2,1,0:T(8,128)(2,1)S(1)}, u32[]{:S(2)}, u32[]{:S(2)}) %collective-permute-start) | collective-permute-done | bytes 614432 | tf_op jit(solution)/shard_map/ppermute | solution.py:24
  28.4 0.0 copy-done.9
  28.4 0.0 copy-done.10
  28.4 5.0 %shard_map.56 = (bf16[4,240,256]{2,1,0:T(8,128)(2,1)S(1)}, bf16[4,240,256]{2,1,0:T(8,128)(2,1)}) custom-call(s32[4]{0:T(128)S(1)} %copy-done.10, bf16[10,40,1280]{2,1,0:T(8,128)(2,1)S(1)} %bitcast.4, bf16[10,24,1280]{2,1,0:T(8,128)(2,1)S(1)} %collective-permute-done.eastern, f32[1280]{0:T(1024)S(1)} %copy-done.9, bf16[1280,1920]{1,0:T(8,128)(2,1)} %weight.4), custom_call_target="tpu_custom_call" | custom-call | flops 1179648000 | bytes 6144000 | tf_op jit(solution)/shard_map/pallas_call | solution.py:210
  33.4 0.0 all-to-all-done.kept
  33.4 0.0 copy-start.6
  33.4 16.9 %all_to_all.25.mixed = bf16[4,240,256]{2,1,0:T(8,128)(2,1)S(1)} all-to-all(bf16[4,240,256]{2,1,0:T(8,128)(2,1)S(1)} %get-tuple-element.13), channel_id=1, replica_groups=mesh['win'=8,'tok'=4] {'tok'}, dimensions={0} | all-to-all | bytes 983040 | tf_op jit(solution)/shard_map/all_to_all | solution.py:28
  50.3 3.5 %all-to-all-start.3 = ((bf16[4,240,256]{2,1,0:T(8,128)(2,1)}), bf16[4,240,256]{2,1,0:T(8,128)(2,1)S(1)}, u32[]{:S(2)}, u32[]{:S(2)}) async-start(bf16[4,240,256]{2,1,0:T(8,128)(2,1)} %get-tuple-element.18), calls=%async_computation.3 | async-start | bytes 983040 | tf_op jit(solution)/shard_map/all_to_all | solution.py:28
  53.8 4.2 %shard_map.57 = (bf16[640,128]{1,0:T(8,128)(2,1)S(1)}, bf16[960,128]{1,0:T(8,128)(2,1)S(1)}) custom-call(bf16[4,160,512]{2,1,0:T(8,128)(2,1)S(1)} %all-to-all-done.kept, bf16[4,240,256]{2,1,0:T(8,128)(2,1)S(1)} %all_to_all.25.mixed), custom_call_target="tpu_custom_call" | custom-call | flops 2621440000 | bytes 1228800 | tf_op jit(solution)/shard_map/pallas_call | solution.py:232
  58.0 0.0 copy-done.6
  58.0 1.6 %collective-permute-start.1 = (bf16[960,128]{1,0:T(8,128)(2,1)S(1)}, bf16[960,128]{1,0:T(8,128)(2,1)S(1)}, u32[]{:S(2)}, u32[]{:S(2)}) collective-permute-start(bf16[960,128]{1,0:T(8,128)(2,1)S(1)} %get-tuple-element.15.mixed), channel_id=1, source_target_pairs={{0,16},{4,20},{8,24},{12,28},{16,0},{20,4},{24,8},{28,12},{1,17},{... | collective-permute-start | bytes 737288 | tf_op jit(solution)/shard_map/ppermute | solution.py:24
  59.6 4.7 %collective-permute-done.1.western = bf16[960,128]{1,0:T(8,128)(2,1)S(1)} collective-permute-done((bf16[960,128]{1,0:T(8,128)(2,1)S(1)}, bf16[960,128]{1,0:T(8,128)(2,1)S(1)}, u32[]{:S(2)}, u32[]{:S(2)}) %collective-permute-start.1) | collective-permute-done | bytes 245792 | tf_op jit(solution)/shard_map/ppermute | solution.py:24
  64.2 1.5 %shard_map.58 = bf16[4,256,128]{2,1,0:T(8,128)(2,1)} custom-call(s32[4]{0:T(128)S(1)} %copy-done.10, bf16[640,128]{1,0:T(8,128)(2,1)S(1)} %get-tuple-element.14.kept, bf16[960,128]{1,0:T(8,128)(2,1)S(1)} %get-tuple-element.15.mixed, bf16[960,128]{1,0:T(8,128)(2,1)S(1)} %collective-permute-done.1.western), custom_call_target="tpu_custom_call" | custom-call | flops 4096000 | bytes 1638400 | tf_op jit(solution)/shard_map/pallas_call | solution.py:258
  65.7 0.4 all-to-all-done.3.mixed
  66.1 4.6 %all-to-all-start.2 = ((bf16[4,256,128]{2,1,0:T(8,128)(2,1)}), bf16[4,256,128]{2,1,0:T(8,128)(2,1)S(1)}, u32[]{:S(2)}, u32[]{:S(2)}) async-start(bf16[4,256,128]{2,1,0:T(8,128)(2,1)} %shard_map.58), calls=%async_computation.2 | async-start | bytes 524288 | tf_op jit(solution)/shard_map/all_to_all | solution.py:28
  70.8 0.0 copy-start.7
  70.8 1.1 %copy-done.7 = bf16[4,160,512]{2,1,0:T(8,128)(2,1)S(1)} copy-done((bf16[4,160,512]{2,1,0:T(8,128)(2,1)S(1)}, bf16[4,160,512]{2,1,0:T(8,128)(2,1)}, u32[]{:S(2)}) %copy-start.7) | copy-done | bytes 655384
  71.9 0.0 copy-start.3
  71.9 4.2 %shard_map.60 = (bf16[640,128]{1,0:T(8,128)(2,1)S(1)}, bf16[960,128]{1,0:T(8,128)(2,1)S(1)}) custom-call(bf16[4,160,512]{2,1,0:T(8,128)(2,1)S(1)} %copy-done.7, bf16[4,240,256]{2,1,0:T(8,128)(2,1)S(1)} %all-to-all-done.3.mixed), custom_call_target="tpu_custom_call" | custom-call | flops 2621440000 | bytes 1228800 | tf_op jit(solution)/shard_map/pallas_call | solution.py:232
  76.0 1.6 %collective-permute-start.2 = (bf16[960,128]{1,0:T(8,128)(2,1)S(1)}, bf16[960,128]{1,0:T(8,128)(2,1)S(1)}, u32[]{:S(2)}, u32[]{:S(2)}) collective-permute-start(bf16[960,128]{1,0:T(8,128)(2,1)S(1)} %get-tuple-element.20.mixed), channel_id=1, source_target_pairs={{0,16},{4,20},{8,24},{12,28},{16,0},{20,4},{24,8},{28,12},{1,17},{... | collective-permute-start | bytes 737288 | tf_op jit(solution)/shard_map/ppermute | solution.py:24
  77.6 4.7 %collective-permute-done.2.western = bf16[960,128]{1,0:T(8,128)(2,1)S(1)} collective-permute-done((bf16[960,128]{1,0:T(8,128)(2,1)S(1)}, bf16[960,128]{1,0:T(8,128)(2,1)S(1)}, u32[]{:S(2)}, u32[]{:S(2)}) %collective-permute-start.2) | collective-permute-done | bytes 245792 | tf_op jit(solution)/shard_map/ppermute | solution.py:24
  82.3 1.5 %shard_map.61 = bf16[4,256,128]{2,1,0:T(8,128)(2,1)} custom-call(s32[4]{0:T(128)S(1)} %copy-done.10, bf16[640,128]{1,0:T(8,128)(2,1)S(1)} %get-tuple-element.19.kept, bf16[960,128]{1,0:T(8,128)(2,1)S(1)} %get-tuple-element.20.mixed, bf16[960,128]{1,0:T(8,128)(2,1)S(1)} %collective-permute-done.2.western), custom_call_target="tpu_custom_call" | custom-call | flops 4096000 | bytes 1638400 | tf_op jit(solution)/shard_map/pallas_call | solution.py:258
  83.8 0.0 all-to-all-done.2.blocks
  83.8 5.1 %all-to-all-start.4 = ((bf16[4,256,128]{2,1,0:T(8,128)(2,1)}), bf16[4,256,128]{2,1,0:T(8,128)(2,1)S(1)}, u32[]{:S(2)}, u32[]{:S(2)}) async-start(bf16[4,256,128]{2,1,0:T(8,128)(2,1)} %shard_map.61), calls=%async_computation.4 | async-start | bytes 524288 | tf_op jit(solution)/shard_map/all_to_all | solution.py:28
  88.9 0.0 copy-done.3
  88.9 2.2 %shard_map.59 = (f32[10,40,1280]{2,1,0:T(8,128)}, bf16[512,1280]{1,0:T(8,128)(2,1)S(1)}) custom-call(bf16[10,40,1280]{2,1,0:T(8,128)(2,1)S(1)} %bitcast.5, bf16[640,1280]{1,0:T(8,128)(2,1)S(1)} %copy-done.3, bf16[4,256,128]{2,1,0:T(8,128)(2,1)S(1)} %all-to-all-done.2.blocks), custom_call_target="tpu_custom_call" | custom-call | flops 524288000 | bytes 3891200 | tf_op jit(solution)/shard_map/pallas_call | solution.py:279
  91.0 0.0 copy-start.4
  91.0 1.1 %copy-done.4 = bf16[512,1280]{1,0:T(8,128)(2,1)} copy-done((bf16[512,1280]{1,0:T(8,128)(2,1)}, bf16[512,1280]{1,0:T(8,128)(2,1)S(1)}, u32[]{:S(2)}) %copy-start.4) | copy-done | bytes 1310744
  92.1 3.5 %all-to-all-done.4.blocks = bf16[4,256,128]{2,1,0:T(8,128)(2,1)S(1)} async-done(((bf16[4,256,128]{2,1,0:T(8,128)(2,1)}), bf16[4,256,128]{2,1,0:T(8,128)(2,1)S(1)}, u32[]{:S(2)}, u32[]{:S(2)}) %all-to-all-start.4) | async-done | bytes 262176 | tf_op jit(solution)/shard_map/all_to_all | solution.py:28
  95.6 0.0 copy-start.2
  95.6 1.6 %copy-done.2 = f32[10,40,1280]{2,1,0:T(8,128)S(1)} copy-done((f32[10,40,1280]{2,1,0:T(8,128)S(1)}, f32[10,40,1280]{2,1,0:T(8,128)}, u32[]{:S(2)}) %copy-start.2) | copy-done | bytes 2048024
  97.2 0.0 copy-start.5
  97.2 1.3 %copy-done.5 = bf16[512,1280]{1,0:T(8,128)(2,1)S(1)} copy-done((bf16[512,1280]{1,0:T(8,128)(2,1)S(1)}, bf16[512,1280]{1,0:T(8,128)(2,1)}, u32[]{:S(2)}) %copy-start.5) | copy-done | bytes 1310744
  98.5 1.8 %shard_map.62 = bf16[10,40,1280]{2,1,0:T(8,128)(2,1)} custom-call(f32[10,40,1280]{2,1,0:T(8,128)S(1)} %copy-done.2, bf16[512,1280]{1,0:T(8,128)(2,1)S(1)} %copy-done.5, bf16[4,256,128]{2,1,0:T(8,128)(2,1)S(1)} %all-to-all-done.4.blocks), custom_call_target="tpu_custom_call" | custom-call | flops 524288000 | bytes 3891200 | tf_op jit(solution)/shard_map/pallas_call | solution.py:291
  (1 shorter events, 0.0 us)
Async XLA Ops:
  0.0 1.2 %copy-start = (bf16[1,10,40,1280]{3,2,1,0:T(8,128)(2,1)S(1)}, bf16[1,10,40,1280]{3,2,1,0:T(8,128)(2,1)}, u32[]{:S(2)}) copy-start(bf16[1,10,40,1280]{3,2,1,0:T(8,128)(2,1)} %param.5) | copy-start | bytes 3072004
  1.2 0.7 copy-start.8
  1.9 11.0 %copy-start.1 = (bf16[1,10,40,1280]{3,2,1,0:T(8,128)(2,1)S(1)}, bf16[1,10,40,1280]{3,2,1,0:T(8,128)(2,1)}, u32[]{:S(2)}) copy-start(bf16[1,10,40,1280]{3,2,1,0:T(8,128)(2,1)} %param.5) | copy-start | bytes 3072004
  6.5 21.9 %copy-start.9 = (f32[1280]{0:T(1024)S(1)}, f32[1280]{0:T(1024)}, u32[]{:S(2)}) copy-start(f32[1280]{0:T(1024)} %gain.3) | copy-start | bytes 15364
  6.5 21.9 %copy-start.10 = (s32[4]{0:T(128)S(1)}, s32[4]{0:T(128)}, u32[]{:S(2)}) copy-start(s32[4]{0:T(128)} %lon_shift.5) | copy-start | bytes 52
  6.5 26.9 %all-to-all-start = ((bf16[4,160,512]{2,1,0:T(8,128)(2,1)}), bf16[4,160,512]{2,1,0:T(8,128)(2,1)S(1)}, u32[]{:S(2)}, u32[]{:S(2)}) async-start(bf16[4,160,512]{2,1,0:T(8,128)(2,1)} %shard_map.55), calls=%async_computation | async-start | bytes 1310720 | tf_op jit(solution)/shard_map/all_to_all | solution.py:28
  13.0 15.4 %collective-permute-start = (bf16[10,24,1280]{2,1,0:T(8,128)(2,1)S(1)}, bf16[10,24,1280]{2,1,0:T(8,128)(2,1)S(1)}, u32[]{:S(2)}, u32[]{:S(2)}) collective-permute-start(bf16[10,24,1280]{2,1,0:T(8,128)(2,1)S(1)} %slice.4), channel_id=1, source_target_pairs={{0,16},{4,20},{8,24},{12,28},{16,0},{20,4},{24,8},{28,12},{1,17},{... | collective-permute-start | bytes 1843208 | tf_op jit(solution)/shard_map/ppermute | solution.py:24
  33.4 24.6 %copy-start.6 = (bf16[4,160,512]{2,1,0:T(8,128)(2,1)}, bf16[4,160,512]{2,1,0:T(8,128)(2,1)S(1)}, u32[]{:S(2)}) copy-start(bf16[4,160,512]{2,1,0:T(8,128)(2,1)S(1)} %all-to-all-done.kept) | copy-start | bytes 1966084
  50.3 15.8 %all-to-all-start.3 = ((bf16[4,240,256]{2,1,0:T(8,128)(2,1)}), bf16[4,240,256]{2,1,0:T(8,128)(2,1)S(1)}, u32[]{:S(2)}, u32[]{:S(2)}) async-start(bf16[4,240,256]{2,1,0:T(8,128)(2,1)} %get-tuple-element.18), calls=%async_computation.3 | async-start | bytes 983040 | tf_op jit(solution)/shard_map/all_to_all | solution.py:28
  58.0 6.3 %collective-permute-start.1 = (bf16[960,128]{1,0:T(8,128)(2,1)S(1)}, bf16[960,128]{1,0:T(8,128)(2,1)S(1)}, u32[]{:S(2)}, u32[]{:S(2)}) collective-permute-start(bf16[960,128]{1,0:T(8,128)(2,1)S(1)} %get-tuple-element.15.mixed), channel_id=1, source_target_pairs={{0,16},{4,20},{8,24},{12,28},{16,0},{20,4},{24,8},{28,12},{1,17},{... | collective-permute-start | bytes 737288 | tf_op jit(solution)/shard_map/ppermute | solution.py:24
  66.1 17.6 %all-to-all-start.2 = ((bf16[4,256,128]{2,1,0:T(8,128)(2,1)}), bf16[4,256,128]{2,1,0:T(8,128)(2,1)S(1)}, u32[]{:S(2)}, u32[]{:S(2)}) async-start(bf16[4,256,128]{2,1,0:T(8,128)(2,1)} %shard_map.58), calls=%async_computation.2 | async-start | bytes 524288 | tf_op jit(solution)/shard_map/all_to_all | solution.py:28
  70.8 1.1 %copy-start.7 = (bf16[4,160,512]{2,1,0:T(8,128)(2,1)S(1)}, bf16[4,160,512]{2,1,0:T(8,128)(2,1)}, u32[]{:S(2)}) copy-start(bf16[4,160,512]{2,1,0:T(8,128)(2,1)} %copy-done.6) | copy-start | bytes 1966084
  71.9 17.0 %copy-start.3 = (bf16[640,1280]{1,0:T(8,128)(2,1)S(1)}, bf16[640,1280]{1,0:T(8,128)(2,1)}, u32[]{:S(2)}) copy-start(bf16[640,1280]{1,0:T(8,128)(2,1)} %weight.5) | copy-start | bytes 4915204
  76.0 6.2 %collective-permute-start.2 = (bf16[960,128]{1,0:T(8,128)(2,1)S(1)}, bf16[960,128]{1,0:T(8,128)(2,1)S(1)}, u32[]{:S(2)}, u32[]{:S(2)}) collective-permute-start(bf16[960,128]{1,0:T(8,128)(2,1)S(1)} %get-tuple-element.20.mixed), channel_id=1, source_target_pairs={{0,16},{4,20},{8,24},{12,28},{16,0},{20,4},{24,8},{28,12},{1,17},{... | collective-permute-start | bytes 737288 | tf_op jit(solution)/shard_map/ppermute | solution.py:24
  83.8 11.9 %all-to-all-start.4 = ((bf16[4,256,128]{2,1,0:T(8,128)(2,1)}), bf16[4,256,128]{2,1,0:T(8,128)(2,1)S(1)}, u32[]{:S(2)}, u32[]{:S(2)}) async-start(bf16[4,256,128]{2,1,0:T(8,128)(2,1)} %shard_map.61), calls=%async_computation.4 | async-start | bytes 524288 | tf_op jit(solution)/shard_map/all_to_all | solution.py:28
  91.0 1.1 %copy-start.4 = (bf16[512,1280]{1,0:T(8,128)(2,1)}, bf16[512,1280]{1,0:T(8,128)(2,1)S(1)}, u32[]{:S(2)}) copy-start(bf16[512,1280]{1,0:T(8,128)(2,1)S(1)} %get-tuple-element.17.weight) | copy-start | bytes 3932164
  95.6 1.6 %copy-start.2 = (f32[10,40,1280]{2,1,0:T(8,128)S(1)}, f32[10,40,1280]{2,1,0:T(8,128)}, u32[]{:S(2)}) copy-start(f32[10,40,1280]{2,1,0:T(8,128)} %get-tuple-element.16.partial) | copy-start | bytes 6144004
  97.2 1.3 %copy-start.5 = (bf16[512,1280]{1,0:T(8,128)(2,1)S(1)}, bf16[512,1280]{1,0:T(8,128)(2,1)}, u32[]{:S(2)}) copy-start(bf16[512,1280]{1,0:T(8,128)(2,1)} %copy-done.4) | copy-start | bytes 3932164

commit v5 on v3

--- a/solution.py
+++ b/solution.py
@@ -12,7 +12,8 @@
 LAT_WINDOWS = 4
 LANES = 128
 SUBLANES = 8
-VMEM_BYTES = 48 * 1024 * 1024
+MIB = 1024 * 1024
+CHUNKS = 5
 
 
 def round_up(value, unit):
@@ -34,14 +35,18 @@
     return lon_shift[lax.rem(lax.axis_index("win"), LAT_WINDOWS)]
 
 
-def project(tokens, gain, weight, slots, outs):
-    local = HEADS // slots.shape[0]
+def project(tokens, gain, weight, copies, qkv, slots, outs):
     groups = slots.shape[0]
+    local = HEADS // groups
     count, features = tokens.shape
     span = slots.shape[2] // local
     factor = lax.rsqrt(jnp.mean(tokens * tokens, axis=-1, keepdims=True) + 1e-06)
     normed = (tokens * factor * gain[...].reshape(1, features)).astype(jnp.bfloat16)
-    qkv = jnp.dot(normed, weight[...], preferred_element_type=jnp.float32)
+    chunk = weight.shape[1] // CHUNKS
+    for index in range(CHUNKS):
+        copies[index].wait()
+        columns = slice(index * chunk, (index + 1) * chunk)
+        qkv[:, columns] = jnp.dot(normed, weight[:, columns], preferred_element_type=jnp.float32)
     tail = jnp.ones((count, span - 3 * HD), jnp.float32)
     place = lax.axis_index("tok")
     for group in range(groups):
@@ -53,32 +58,49 @@
                 for kind in range(3)
             ] + [tail]
         slots[slot] = jnp.concatenate(columns, axis=1).astype(jnp.bfloat16)
-    parts = len(outs) // groups
     for index, out in enumerate(outs):
         first = index // groups * out.shape[1]
         out[...] = slots[index % groups, :, first : first + out.shape[1]]
 
 
+def fetch(weight, held, sems):
+    chunk = weight.shape[1] // CHUNKS
+    copies = []
+    for index in range(CHUNKS):
+        columns = pl.ds(index * chunk, chunk)
+        copies.append(
+            pltpu.make_async_copy(weight.at[:, columns], held.at[:, columns], sems.at[index])
+        )
+        copies[-1].start()
+    return copies
+
+
 def kept_kernel(split, field, gain, weight, *refs):
-    *outs, slots = refs
+    *outs, qkv, slots, held_weight, sems, held_field, held_gain = refs
+    first = pltpu.make_async_copy(field, held_field, sems.at[CHUNKS])
+    second = pltpu.make_async_copy(gain, held_gain, sems.at[CHUNKS + 1])
+    first.start()
+    second.start()
+    copies = fetch(weight, held_weight, sems)
+    first.wait()
+    second.wait()
     rows, columns, features = field.shape
-    tokens = field[...].astype(jnp.float32)[:, split:]
-    project(tokens.reshape(rows * (columns - split), features), gain, weight, slots, outs)
-
-
-def mixed_kernel(split, lon_shift, field, eastern, gain, weight, *refs):
-    *outs, slots = refs
+    tokens = held_field[...].astype(jnp.float32)[:, split:]
+    tokens = tokens.reshape(rows * (columns - split), features)
+    project(tokens, held_gain, held_weight, copies, qkv, slots, outs)
+
+
+def mixed_kernel(split, field, gain, weight, lon_shift, eastern, *refs):
+    *outs, qkv, slots, held_weight, sems = refs
+    copies = fetch(weight, held_weight, sems)
     rows, _, features = field.shape
     own = field[...].astype(jnp.float32)[:, :split]
     column = lax.broadcasted_iota(jnp.int32, own.shape, 1)
     tokens = jnp.where(column < column_offset(lon_shift), eastern[...].astype(jnp.float32), own)
-    project(tokens.reshape(rows * split, features), gain, weight, slots, outs)
-
-
-def attention_kernel(head, groups, *refs):
-    kept, mixed = refs[:groups], refs[groups : 2 * groups]
-    kept_out, mixed_out, held, keys = refs[2 * groups : 2 * groups + 4]
-    scores, weights = refs[2 * groups + 4 : 2 * groups + 6], refs[2 * groups + 6 :]
+    project(tokens.reshape(rows * split, features), gain, held_weight, copies, qkv, slots, outs)
+
+
+def gather(head, kept, mixed, held, keys):
     span = held.shape[1]
     start = 0
     for block in kept:
@@ -88,21 +110,29 @@
         held[start : start + block.shape[0]] = block[...]
         start += block.shape[0]
     keys[...] = held[...].T
+
+
+def attend(held, keys, ranges, scores, weights):
+    span = held.shape[1]
     factor = HD ** (-0.5) * 1.4426950408889634
     step = scores[0].shape[0]
     chunk = 16
+    pieces = [
+        (first + offset, out, offset)
+        for first, count, out in ranges
+        for offset in range(0, count, step)
+    ]
 
     def score(index, out):
-        queries = held[index * step : (index + 1) * step].astype(jnp.float32)
-        queries = pltpu.roll(queries, HD, axis=1)
+        first = pieces[index][0]
+        queries = pltpu.roll(held[first : first + step].astype(jnp.float32), HD, axis=1)
         lane = lax.broadcasted_iota(jnp.int32, queries.shape, 1)
         queries = jnp.where((lane >= HD) & (lane < 2 * HD), queries, 0.0).astype(jnp.bfloat16)
         out[...] = jnp.dot(queries, keys[...], preferred_element_type=jnp.float32)
 
-    steps = start // step
     score(0, scores[0])
-    for index in range(steps):
-        if index + 1 < steps:
+    for index, (_, target, offset) in enumerate(pieces):
+        if index + 1 < len(pieces):
             score(index + 1, scores[(index + 1) % 2])
         now, out = scores[index % 2], weights[index % 2]
         for first in range(0, step, chunk):
@@ -111,13 +141,29 @@
             out[first : first + chunk] = jnp.exp2((part - top) * factor).astype(jnp.bfloat16)
         mixed_values = jnp.dot(out[...], held[...], preferred_element_type=jnp.float32)
         scaled = mixed_values / mixed_values[:, 3 * HD : 3 * HD + 1]
-        values = pltpu.roll(scaled, span - 2 * HD, axis=1)[:, :LANES].astype(jnp.bfloat16)
-        first = index * step
-        if first < kept_out.shape[0]:
-            kept_out[first : first + step] = values
-        else:
-            first -= kept_out.shape[0]
-            mixed_out[first : first + step] = values
+        values = pltpu.roll(scaled, span - 2 * HD, axis=1)[:, :LANES]
+        target[offset : offset + step] = values.astype(jnp.bfloat16)
+
+
+def first_head_kernel(groups, *refs):
+    kept, mixed = refs[:groups], refs[groups : 2 * groups]
+    kept_out, mixed_out, held, keys, *rest = refs[2 * groups :]
+    gather(0, kept, mixed, held, keys)
+    kept_count = kept_out.shape[0]
+    ranges = [(0, kept_count, kept_out), (kept_count, mixed_out.shape[0], mixed_out)]
+    attend(held, keys, ranges, rest[:2], rest[2:])
+
+
+def second_mixed_kernel(groups, *refs):
+    kept, mixed = refs[:groups], refs[groups : 2 * groups]
+    mixed_out, held, keys, *rest = refs[2 * groups :]
+    gather(1, kept, mixed, held, keys)
+    count = mixed_out.shape[0]
+    attend(held, keys, [(held.shape[0] - count, count, mixed_out)], rest[:2], rest[2:])
+
+
+def second_kept_kernel(held, keys, kept_out, *rest):
+    attend(held, keys, [(0, kept_out.shape[0], kept_out)], rest[:2], rest[2:])
 
 
 def pack_kernel(split, lon_shift, kept, mixed, western, *outs):
@@ -214,24 +260,30 @@
     split = round_up(columns // 2, SUBLANES)
     field = field_tokens[0]
     smem = pl.BlockSpec(memory_space=pltpu.SMEM)
-    params = pltpu.CompilerParams(vmem_limit_bytes=VMEM_BYTES)
     kept_count, mixed_count = rows * (columns - split), rows * split
 
-    def projection(kernel, count, parts, scalars, operands):
+    def limit(size):
+        return pltpu.CompilerParams(vmem_limit_bytes=size * MIB)
+
+    def projection(kernel, count, parts, specs, held, params, *operands):
         block = jax.ShapeDtypeStruct((count, local * span // parts), jnp.bfloat16)
         return pl.pallas_call(
             functools.partial(kernel, split),
             out_shape=[block] * (parts * groups),
-            in_specs=[smem] * len(scalars) + whole(len(operands) + 2),
+            in_specs=specs,
             out_specs=whole(parts * groups),
-            scratch_shapes=[pltpu.VMEM((groups, count, local * span), jnp.bfloat16)],
+            scratch_shapes=[
+                pltpu.VMEM((count, qkv_weight.shape[1]), jnp.float32),
+                pltpu.VMEM((groups, count, local * span), jnp.bfloat16),
+                *held,
+            ],
             compiler_params=params,
             cost_estimate=pl.CostEstimate(
                 flops=2 * count * features * 3 * HEADS * HD,
                 bytes_accessed=2 * features * (3 * HEADS * HD + 2 * count),
                 transcendentals=0,
             ),
-        )(*scalars, *operands, norm_gain, qkv_weight)
+        )(*operands)
 
     def spread(blocks, sign):
         return [blocks[0]] + [
@@ -239,56 +291,85 @@
         ]
 
     eastern = shifted(field[:, :split], "win", -LAT_WINDOWS)
-    kept = spread(projection(kept_kernel, kept_count, 1, [], [field]), 1)
-    mixed = projection(mixed_kernel, mixed_count, local, [lon_shift], [field, eastern])
+    hbm = pl.BlockSpec(memory_space=pltpu.HBM)
+    operands = (field, norm_gain, qkv_weight)
+    held = [
+        pltpu.VMEM(qkv_weight.shape, qkv_weight.dtype),
+        pltpu.SemaphoreType.DMA((CHUNKS + 2,)),
+        pltpu.VMEM(field.shape, field.dtype),
+        pltpu.VMEM(norm_gain.shape, norm_gain.dtype),
+    ]
+    kept = spread(projection(kept_kernel, kept_count, 1, [hbm] * 3, held, limit(60), *operands), 1)
+    specs = [*whole(2), hbm, smem, *whole(1)]
+    operands += (lon_shift, eastern)
+    mixed = projection(mixed_kernel, mixed_count, local, specs, held[:2], limit(52), *operands)
     first_mixed = spread(after(mixed[:groups], kept), 1)
-    second_mixed = spread(after(mixed[groups:], first_mixed), 1)
 
     total = groups * rows * columns
     step = total // 5
     packed_rows = round_up(rows * columns // 2 + -(-rows * columns * (HD - LANES // 2) // LANES), 16)
-
-    def attention(head, blocks):
+    kept_values = jax.ShapeDtypeStruct((groups * kept_count, LANES), jnp.bfloat16)
+    mixed_values = jax.ShapeDtypeStruct((groups * mixed_count, LANES), jnp.bfloat16)
+    gathered = [
+        jax.ShapeDtypeStruct((total, span), jnp.bfloat16),
+        jax.ShapeDtypeStruct((span, total), jnp.bfloat16),
+    ]
+
+    def attention(kernel, count, out_shape, held, *operands):
         return pl.pallas_call(
-            functools.partial(attention_kernel, head, groups),
-            out_shape=[
-                jax.ShapeDtypeStruct((groups * count, LANES), jnp.bfloat16)
-                for count in (kept_count, mixed_count)
-            ],
-            in_specs=whole(len(blocks)),
-            out_specs=whole(2),
-            scratch_shapes=[
-                pltpu.VMEM((total, span), jnp.bfloat16),
-                pltpu.VMEM((span, total), jnp.bfloat16),
-                pltpu.VMEM((step, total), jnp.float32),
-                pltpu.VMEM((step, total), jnp.float32),
-                pltpu.VMEM((step, total), jnp.bfloat16),
-                pltpu.VMEM((step, total), jnp.bfloat16),
-            ],
-            compiler_params=params,
+            kernel,
+            out_shape=out_shape,
+            in_specs=whole(len(operands)),
+            out_specs=whole(len(out_shape)),
+            scratch_shapes=[pltpu.VMEM(leaf.shape, leaf.dtype) for leaf in held]
+            + [pltpu.VMEM((step, total), jnp.float32)] * 2
+            + [pltpu.VMEM((step, total), jnp.bfloat16)] * 2,
+            compiler_params=limit(32),
             cost_estimate=pl.CostEstimate(
-                flops=4 * total * total * span,
+                flops=4 * count * total * span,
                 bytes_accessed=2 * total * (span + LANES),
-                transcendentals=total * total,
+                transcendentals=count * total,
             ),
-        )(*blocks)
-
-    def back(kept_values, mixed_values):
-        western = shifted(mixed_values, "win", LAT_WINDOWS)
+        )(*operands)
+
+    def back(kept_values, mixed_values, western):
         packed = pl.pallas_call(
             functools.partial(pack_kernel, split),
             out_shape=[jax.ShapeDtypeStruct((packed_rows, LANES), jnp.bfloat16)] * groups,
             in_specs=[smem] + whole(3),
             out_specs=whole(groups),
-            compiler_params=params,
+            compiler_params=limit(16),
             cost_estimate=pl.CostEstimate(
                 flops=total * LANES * 20, bytes_accessed=8 * total * LANES, transcendentals=0
             ),
         )(lon_shift, kept_values, mixed_values, western)
         return spread(packed, -1)
 
-    first = back(*attention(0, [*kept, *first_mixed]))
-    second = back(*attention(1, [*kept, *second_mixed]))
+    first_kept_values, first_mixed_values = attention(
+        functools.partial(first_head_kernel, groups),
+        total,
+        [kept_values, mixed_values],
+        gathered,
+        *kept,
+        *first_mixed,
+    )
+    first_western = shifted(first_mixed_values, "win", LAT_WINDOWS)
+    ready = first_mixed[:-1] + [first_mixed_values]
+    second_mixed = spread(after(mixed[groups:], ready), 1)
+    second_mixed_values, *second_gathered = attention(
+        functools.partial(second_mixed_kernel, groups),
+        groups * mixed_count,
+        [mixed_values, *gathered],
+        [],
+        *kept,
+        *second_mixed,
+    )
+    second_western = shifted(second_mixed_values, "win", LAT_WINDOWS)
+    (second_kept_values,) = attention(
+        second_kept_kernel, groups * kept_count, [kept_values], [], *second_gathered
+    )
+    first = back(first_kept_values, first_mixed_values, first_western)
+    second = back(second_kept_values, second_mixed_values, second_western)
 
     cost = pl.CostEstimate(
         flops=2 * rows * columns * groups * LANES * features,
@@ -305,7 +386,7 @@
         in_specs=whole(2 + groups),
         out_specs=whole(2),
         scratch_shapes=[pltpu.VMEM(ordered, jnp.bfloat16)],
-        compiler_params=params,
+        compiler_params=limit(24),
         cost_estimate=cost,
     )(field, out_weight, *first)
     result = pl.pallas_call(
@@ -313,7 +394,7 @@
         out_shape=jax.ShapeDtypeStruct(field.shape, jnp.bfloat16),
         in_specs=whole(2 + groups),
         out_specs=pl.BlockSpec(memory_space=pltpu.VMEM),
-        compiler_params=params,
+        compiler_params=limit(24),
         cost_estimate=cost,
     )(partial, weight, *second)
     return result[None]

time: 73.6 us -> 73.4 us (level)
  waiting for transfers between devices: 9.24 us -> 15.1 us
  local copies, waits for them, and re-layouts: 4.61 us -> 1.14 us
  starting transfers between devices: 37.4 us -> 34 us
  Pallas kernels: 22 us -> 22.9 us
    ppermute x18, waiting for transfers between devices: 9.24 us -> 15.1 us  [shifted(): lax.ppermute(block, axis, [(i, (i + distance) % count) for i in range(cou...]
    unnamed x12 -> x10, local copies, waits for them, and re-layouts: 3.5 us -> 0.02 us
    ppermute x18, starting transfers between devices: 37.4 us -> 34 us  [shifted(): lax.ppermute(block, axis, [(i, (i + distance) % count) for i in range(cou...]
    pallas_call x2, Pallas kernels: 8.16 us -> 9.76 us  [projection(): pl.pallas_call(functools.partial(kernel, split), out_shape=[block] * (par...]
    pallas_call x1, Pallas kernels: 2.16 us -> 0.83 us  [shards(): pl.pallas_call(functools.partial(first_output_kernel, split, groups), out...]
    pallas_call x2 -> x3, Pallas kernels: 8.35 us -> 8.97 us  [attention(): pl.pallas_call(kernel, out_shape=out_shape, in_specs=whole(len(operands))...]
  transfers between devices with their start and end apart: 18 -> 18, of which waited for: 6 -> 7; matrix products, arithmetic and copies ran while one was open for 0% -> 0% of each run, Pallas kernels for 28% -> 29%
where the time goes in v5:
time: 73.4 us; the launch traced here: 73.2 us
  starting transfers between devices  34 us (46%)
  Pallas kernels  22.9 us (31%)
  waiting for transfers between devices  15.1 us (21%)
  local copies, waits for them, and re-layouts  1.14 us (2%)
    ppermute x18, starting transfers between devices, shifted(): lax.ppermute(block, axis, [(i, (i + distance) % count) for i in range(cou...  34 us
    ppermute x18, waiting for transfers between devices, shifted(): lax.ppermute(block, axis, [(i, (i + distance) % count) for i in range(cou...  15.1 us
    pallas_call x2, Pallas kernels, projection(): pl.pallas_call(functools.partial(kernel, split), out_shape=[block] * (par...  9.76 us
    pallas_call x3, Pallas kernels, attention(): pl.pallas_call(kernel, out_shape=out_shape, in_specs=whole(len(operands))...  8.97 us
    pallas_call x1, Pallas kernels, shards(): pl.pallas_call(functools.partial(second_output_kernel, split), out_shape=...  1.76 us
    pallas_call x2, Pallas kernels, back(): pl.pallas_call(functools.partial(pack_kernel, split), out_shape=[jax.Shap...  1.55 us
  transfers between devices with their start and end apart: 18, of which 7 were waited for; matrix products, arithmetic and copies ran while one was open for 0% of the time, Pallas kernels for 29%

profile of v5, /device:TPU:0, one launch (start us, length us, event | category | flops | bytes accessed | tf_op | source)
XLA Modules:
  0.0 73.2 jit_solution(7297398969110664604)
XLA Ops:
  0.0 1.1 %slice.4 = bf16[10,24,1280]{2,1,0:T(8,128)(2,1)S(1)} slice(bf16[10,40,1280]{2,1,0:T(8,128)(2,1)} %bitcast.2), slice={[0:10], [0:24], [0:1280]} | slice | bytes 1228800 | tf_op jit(solution)/shard_map/slice | solution.py:293
  1.1 0.0 copy-start.2
  1.1 0.0 copy-start.3
  1.1 3.0 %collective-permute-start.3 = (bf16[10,24,1280]{2,1,0:T(8,128)(2,1)S(1)}, bf16[10,24,1280]{2,1,0:T(8,128)(2,1)S(1)}, u32[]{:S(2)}, u32[]{:S(2)}) collective-permute-start(bf16[10,24,1280]{2,1,0:T(8,128)(2,1)S(1)} %slice.4), channel_id=1, source_target_pairs={{0,16},{4,20},{8,24},{12,28},{16,0},{20,4},{24,8},{28,12},{1,17},{... | collective-permute-start | bytes 1843208 | tf_op jit(solution)/shard_map/ppermute | solution.py:25
  4.2 4.5 %shard_map.55 = (bf16[160,512]{1,0:T(8,128)(2,1)}, bf16[160,512]{1,0:T(8,128)(2,1)}, bf16[160,512]{1,0:T(8,128)(2,1)}, bf16[160,512]{1,0:T(8,128)(2,1)}) custom-call(bf16[10,40,1280]{2,1,0:T(8,128)(2,1)} %bitcast.3, f32[1280]{0:T(1024)} %gain.3, bf16[1280,1920]{1,0:T(8,128)(2,1)} %weight.4), custom_call_target="tpu_custom_call" | custom-call | flops 786432000 | bytes 5734400 | tf_op jit(solution)/shard_map/pallas_call | solution.py:270
  8.7 1.6 %collective-permute-start = (bf16[160,512]{1,0:T(8,128)(2,1)}, bf16[160,512]{1,0:T(8,128)(2,1)S(1)}, u32[]{:S(2)}, u32[]{:S(2)}) collective-permute-start(bf16[160,512]{1,0:T(8,128)(2,1)} %get-tuple-element.39), channel_id=1, source_target_pairs={{0,1},{1,2},{2,3},{3,0},{4,5},{5,6},{6,7},{7,4},{8,9},{9,10},{10,1... | collective-permute-start | bytes 491528 | tf_op jit(solution)/shard_map/ppermute | solution.py:25
  10.3 2.6 %collective-permute-start.1 = (bf16[160,512]{1,0:T(8,128)(2,1)}, bf16[160,512]{1,0:T(8,128)(2,1)S(1)}, u32[]{:S(2)}, u32[]{:S(2)}) collective-permute-start(bf16[160,512]{1,0:T(8,128)(2,1)} %get-tuple-element.40), channel_id=1, source_target_pairs={{0,2},{1,3},{2,0},{3,1},{4,6},{5,7},{6,4},{7,5},{8,10},{9,11},{10,... | collective-permute-start | bytes 491528 | tf_op jit(solution)/shard_map/ppermute | solution.py:25
  12.9 0.0 copy-start.4
  12.9 1.3 %collective-permute-start.2 = (bf16[160,512]{1,0:T(8,128)(2,1)}, bf16[160,512]{1,0:T(8,128)(2,1)S(1)}, u32[]{:S(2)}, u32[]{:S(2)}) collective-permute-start(bf16[160,512]{1,0:T(8,128)(2,1)} %get-tuple-element.41), channel_id=1, source_target_pairs={{0,3},{1,0},{2,1},{3,2},{4,7},{5,4},{6,5},{7,6},{8,11},{9,8},{10,9... | collective-permute-start | bytes 491528 | tf_op jit(solution)/shard_map/ppermute | solution.py:25
  14.3 3.8 %collective-permute-done.3.eastern = bf16[10,24,1280]{2,1,0:T(8,128)(2,1)S(1)} collective-permute-done((bf16[10,24,1280]{2,1,0:T(8,128)(2,1)S(1)}, bf16[10,24,1280]{2,1,0:T(8,128)(2,1)S(1)}, u32[]{:S(2)}, u32[]{:S(2)}) %collective-permute-start.3) | collective-permute-done | bytes 614432 | tf_op jit(solution)/shard_map/ppermute | solution.py:25
  18.0 0.0 copy-done.2
  18.0 0.0 copy-done.3
  18.0 5.3 %shard_map.56 = (bf16[240,256]{1,0:T(8,128)(2,1)S(1)}, bf16[240,256]{1,0:T(8,128)(2,1)S(1)}, bf16[240,256]{1,0:T(8,128)(2,1)S(1)}, bf16[240,256]{1,0:T(8,128)(2,...) custom-call(bf16[10,40,1280]{2,1,0:T(8,128)(2,1)} %bitcast.4, ...), custom_call_target="tpu_custom_call" | custom-call | flops 1179648000 | bytes 6144000 | tf_op jit(solution)/shard_map/pallas_call | solution.py:270
  23.3 0.0 collective-permute-done.refs_1_
  23.3 1.8 %collective-permute-start.4 = (bf16[240,256]{1,0:T(8,128)(2,1)S(1)}, bf16[240,256]{1,0:T(8,128)(2,1)S(1)}, u32[]{:S(2)}, u32[]{:S(2)}) collective-permute-start(bf16[240,256]{1,0:T(8,128)(2,1)S(1)} %get-tuple-element.44), channel_id=1, source_target_pairs={{0,1},{1,2},{2,3},{3,0},{4,5},{5,6},{6,7},{7,4},{8,9},{9,10},{10,1... | collective-permute-start | bytes 368648 | tf_op jit(solution)/shard_map/ppermute | solution.py:25
  25.2 0.0 collective-permute-done.1.refs_2_
  25.2 2.6 %collective-permute-start.5 = (bf16[240,256]{1,0:T(8,128)(2,1)S(1)}, bf16[240,256]{1,0:T(8,128)(2,1)S(1)}, u32[]{:S(2)}, u32[]{:S(2)}) collective-permute-start(bf16[240,256]{1,0:T(8,128)(2,1)S(1)} %get-tuple-element.46), channel_id=1, source_target_pairs={{0,2},{1,3},{2,0},{3,1},{4,6},{5,7},{6,4},{7,5},{8,10},{9,11},{10,... | collective-permute-start | bytes 368648 | tf_op jit(solution)/shard_map/ppermute | solution.py:25
  27.8 0.0 collective-permute-done.2.refs_3_
  27.8 1.3 %collective-permute-start.6 = (bf16[240,256]{1,0:T(8,128)(2,1)S(1)}, bf16[240,256]{1,0:T(8,128)(2,1)S(1)}, u32[]{:S(2)}, u32[]{:S(2)}) collective-permute-start(bf16[240,256]{1,0:T(8,128)(2,1)S(1)} %get-tuple-element.48), channel_id=1, source_target_pairs={{0,3},{1,0},{2,1},{3,2},{4,7},{5,4},{6,5},{7,6},{8,11},{9,8},{10,9... | collective-permute-start | bytes 368648 | tf_op jit(solution)/shard_map/ppermute | solution.py:25
  29.1 2.3 %collective-permute-done.4.refs_5_ = bf16[240,256]{1,0:T(8,128)(2,1)S(1)} collective-permute-done((bf16[240,256]{1,0:T(8,128)(2,1)S(1)}, bf16[240,256]{1,0:T(8,128)(2,1)S(1)}, u32[]{:S(2)}, u32[]{:S(2)}) %collective-permute-start.4) | collective-permute-done | bytes 122912 | tf_op jit(solution)/shard_map/ppermute | solution.py:25
  31.4 3.6 %collective-permute-start.11 = (bf16[240,256]{1,0:T(8,128)(2,1)S(1)}, bf16[240,256]{1,0:T(8,128)(2,1)S(1)}, u32[]{:S(2)}, u32[]{:S(2)}) collective-permute-start(bf16[240,256]{1,0:T(8,128)(2,1)S(1)} %get-tuple-element.59), channel_id=1, source_target_pairs={{0,1},{1,2},{2,3},{3,0},{4,5},{5,6},{6,7},{7,4},{8,9},{9,10},{10,1... | collective-permute-start | bytes 368648 | tf_op jit(solution)/shard_map/ppermute | solution.py:25
  35.0 1.4 %collective-permute-done.5.refs_6_ = bf16[240,256]{1,0:T(8,128)(2,1)S(1)} collective-permute-done((bf16[240,256]{1,0:T(8,128)(2,1)S(1)}, bf16[240,256]{1,0:T(8,128)(2,1)S(1)}, u32[]{:S(2)}, u32[]{:S(2)}) %collective-permute-start.5) | collective-permute-done | bytes 122912 | tf_op jit(solution)/shard_map/ppermute | solution.py:25
  36.3 1.0 %collective-permute-start.12 = (bf16[240,256]{1,0:T(8,128)(2,1)S(1)}, bf16[240,256]{1,0:T(8,128)(2,1)S(1)}, u32[]{:S(2)}, u32[]{:S(2)}) collective-permute-start(bf16[240,256]{1,0:T(8,128)(2,1)S(1)} %get-tuple-element.61), channel_id=1, source_target_pairs={{0,2},{1,3},{2,0},{3,1},{4,6},{5,7},{6,4},{7,5},{8,10},{9,11},{10,... | collective-permute-start | bytes 368648 | tf_op jit(solution)/shard_map/ppermute | solution.py:25
  37.4 0.0 collective-permute-done.6.refs_7_
  37.4 0.0 copy-done.4
  37.4 4.2 %shard_map.57 = (bf16[640,128]{1,0:T(8,128)(2,1)S(1)}, bf16[960,128]{1,0:T(8,128)(2,1)S(1)}) custom-call(bf16[160,512]{1,0:T(8,128)(2,1)S(1)} %copy-done.4, bf16[160,512]{1,0:T(8,128)(2,1)S(1)} %collective-permute-done.refs_1_, bf16[160,512]{1,0:T(8,128)(2,1)S(1)} %collective-permute-done.1.refs_2_, bf16[160,512]{1,0:T(8,128)(2,1)S(1)} %collective-permute-done.2.refs_3_, ...), custom_call_target="tpu_custom_call" | custom-call | flops 2621440000 | bytes 1228800 | tf_op jit(solution)/shard_map/pallas_call | solution.py:319
  41.6 3.9 %collective-permute-start.13 = (bf16[240,256]{1,0:T(8,128)(2,1)S(1)}, bf16[240,256]{1,0:T(8,128)(2,1)S(1)}, u32[]{:S(2)}, u32[]{:S(2)}) collective-permute-start(bf16[240,256]{1,0:T(8,128)(2,1)S(1)} %get-tuple-element.63), channel_id=1, source_target_pairs={{0,3},{1,0},{2,1},{3,2},{4,7},{5,4},{6,5},{7,6},{8,11},{9,8},{10,9... | collective-permute-start | bytes 368648 | tf_op jit(solution)/shard_map/ppermute | solution.py:25
  45.4 1.8 %collective-permute-start.7 = (bf16[960,128]{1,0:T(8,128)(2,1)S(1)}, bf16[960,128]{1,0:T(8,128)(2,1)S(1)}, u32[]{:S(2)}, u32[]{:S(2)}) collective-permute-start(bf16[960,128]{1,0:T(8,128)(2,1)S(1)} %get-tuple-element.50.mixed), channel_id=1, source_target_pairs={{0,16},{4,20},{8,24},{12,28},{16,0},{20,4},{24,8},{28,12},{1,17},{... | collective-permute-start | bytes 737288 | tf_op jit(solution)/shard_map/ppermute | solution.py:25
  47.2 0.0 collective-permute-done.11.refs_5_
  47.2 0.0 collective-permute-done.12.refs_6_
  47.2 2.8 %collective-permute-done.13.refs_7_ = bf16[240,256]{1,0:T(8,128)(2,1)S(1)} collective-permute-done((bf16[240,256]{1,0:T(8,128)(2,1)S(1)}, bf16[240,256]{1,0:T(8,128)(2,1)S(1)}, u32[]{:S(2)}, u32[]{:S(2)}) %collective-permute-start.13) | collective-permute-done | bytes 122912 | tf_op jit(solution)/shard_map/ppermute | solution.py:25
  50.0 2.8 %shard_map.60 = (bf16[960,128]{1,0:T(8,128)(2,1)S(1)}, bf16[1600,256]{1,0:T(8,128)(2,1)S(1)}, bf16[256,1600]{1,0:T(8,128)(2,1)S(1)}) custom-call(bf16[160,512]{1,0:T(8,128)(2,1)S(1)} %copy-done.4, bf16[160,512]{1,0:T(8,128)(2,1)S(1)} %collective-permute-done.refs_1_, bf16[160,512]{1,0:T(8,128)(2,1)S(1)} %collective-permute-done.1.refs_2_, ...), custom_call_target="tpu_custom_call" | custom-call | flops 1572864000 | bytes 1228800 | tf_op jit(solution)/shard_map/pallas_call | solution.py:319
  52.8 1.5 %collective-permute-start.14 = (bf16[960,128]{1,0:T(8,128)(2,1)S(1)}, bf16[960,128]{1,0:T(8,128)(2,1)S(1)}, u32[]{:S(2)}, u32[]{:S(2)}) collective-permute-start(bf16[960,128]{1,0:T(8,128)(2,1)S(1)} %get-tuple-element.66.mixed), channel_id=1, source_target_pairs={{0,16},{4,20},{8,24},{12,28},{16,0},{20,4},{24,8},{28,12},{1,17},{... | collective-permute-start | bytes 737288 | tf_op jit(solution)/shard_map/ppermute | solution.py:25
  54.4 0.0 collective-permute-done.7.western
  54.4 0.8 %shard_map.58 = (bf16[256,128]{1,0:T(8,128)(2,1)S(1)}, bf16[256,128]{1,0:T(8,128)(2,1)S(1)}, bf16[256,128]{1,0:T(8,128)(2,1)S(1)}, bf16[256,128]{1,0:T(8,128)(2,1)S(1)}) custom-call(s32[4]{0:T(128)S(1)} %copy-done.3, bf16[640,128]{1,0:T(8,128)(2,1)S(1)} %get-tuple-element.49.kept, bf16[960,128]{1,0:T(8,128)(2,1)S(1)} %get-tuple-element.50.mixed, ...), custom_call_target="tpu_custom_call" | custom-call | flops 4096000 | bytes 1638400 | tf_op jit(solution)/shard_map/pallas_call | solution.py:336
  55.1 2.5 %collective-permute-start.8 = (bf16[256,128]{1,0:T(8,128)(2,1)S(1)}, bf16[256,128]{1,0:T(8,128)(2,1)S(1)}, u32[]{:S(2)}, u32[]{:S(2)}) collective-permute-start(bf16[256,128]{1,0:T(8,128)(2,1)S(1)} %get-tuple-element.52), channel_id=1, source_target_pairs={{0,3},{1,0},{2,1},{3,2},{4,7},{5,4},{6,5},{7,6},{8,11},{9,8},{10,9... | collective-permute-start | bytes 196616 | tf_op jit(solution)/shard_map/ppermute | solution.py:25
  57.6 0.8 %collective-permute-start.9 = (bf16[256,128]{1,0:T(8,128)(2,1)S(1)}, bf16[256,128]{1,0:T(8,128)(2,1)S(1)}, u32[]{:S(2)}, u32[]{:S(2)}) collective-permute-start(bf16[256,128]{1,0:T(8,128)(2,1)S(1)} %get-tuple-element.53), channel_id=1, source_target_pairs={{0,2},{1,3},{2,0},{3,1},{4,6},{5,7},{6,4},{7,5},{8,10},{9,11},{10,... | collective-permute-start | bytes 196616 | tf_op jit(solution)/shard_map/ppermute | solution.py:25
  58.4 0.2 collective-permute-start.10
  58.6 0.0 copy-start
  58.6 0.0 copy-start.1
  58.6 2.0 %shard_map.61.kept = bf16[640,128]{1,0:T(8,128)(2,1)S(1)} custom-call(bf16[1600,256]{1,0:T(8,128)(2,1)S(1)} %get-tuple-element.64.held, bf16[256,1600]{1,0:T(8,128)(2,1)S(1)} %get-tuple-element.65.keys), custom_call_target="tpu_custom_call" | custom-call | flops 1048576000 | bytes 1228800 | tf_op jit(solution)/shard_map/pallas_call | solution.py:319
  60.6 0.0 collective-permute-done.14.western
  60.6 0.8 %shard_map.62 = (bf16[256,128]{1,0:T(8,128)(2,1)S(1)}, bf16[256,128]{1,0:T(8,128)(2,1)S(1)}, bf16[256,128]{1,0:T(8,128)(2,1)S(1)}, bf16[256,128]{1,0:T(8,128)(2,1)S(1)}) custom-call(s32[4]{0:T(128)S(1)} %copy-done.3, bf16[640,128]{1,0:T(8,128)(2,1)S(1)} %shard_map.61.kept, bf16[960,128]{1,0:T(8,128)(2,1)S(1)} %get-tuple-element.66.mixed, ...), custom_call_target="tpu_custom_call" | custom-call | flops 4096000 | bytes 1638400 | tf_op jit(solution)/shard_map/pallas_call | solution.py:336
  61.4 3.7 %collective-permute-start.15 = (bf16[256,128]{1,0:T(8,128)(2,1)S(1)}, bf16[256,128]{1,0:T(8,128)(2,1)S(1)}, u32[]{:S(2)}, u32[]{:S(2)}) collective-permute-start(bf16[256,128]{1,0:T(8,128)(2,1)S(1)} %get-tuple-element.68), channel_id=1, source_target_pairs={{0,3},{1,0},{2,1},{3,2},{4,7},{5,4},{6,5},{7,6},{8,11},{9,8},{10,9... | collective-permute-start | bytes 196616 | tf_op jit(solution)/shard_map/ppermute | solution.py:25
  65.0 0.3 collective-permute-start.16
  65.4 0.0 collective-permute-done.8.refs_1_
  65.4 0.3 collective-permute-start.17
  65.7 0.0 collective-permute-done.9.refs_2_
  65.7 0.0 collective-permute-done.10.refs_3_
  65.7 0.0 copy-done
  65.7 0.0 copy-done.1
  65.7 0.8 %shard_map.59 = (f32[10,40,1280]{2,1,0:T(8,128)S(1)}, bf16[512,1280]{1,0:T(8,128)(2,1)S(1)}) custom-call(bf16[10,40,1280]{2,1,0:T(8,128)(2,1)S(1)} %bitcast.5, bf16[640,1280]{1,0:T(8,128)(2,1)S(1)} %copy-done.1, bf16[256,128]{1,0:T(8,128)(2,1)S(1)} %get-tuple-element.51.refs_0_, bf16[256,128]{1,0:T(8,128)(2,1)S(1)} %collective-permute-done.8.refs_1_, ...), custom_call_target="tpu_custom_call" | custom-call | flops 524288000 | bytes 3891200 | tf_op jit(solution)/shard_map/pallas_call | solution.py:380
  66.5 0.4 collective-permute-done.15.refs_1_
  66.9 3.3 %collective-permute-done.16.refs_2_ = bf16[256,128]{1,0:T(8,128)(2,1)S(1)} collective-permute-done((bf16[256,128]{1,0:T(8,128)(2,1)S(1)}, bf16[256,128]{1,0:T(8,128)(2,1)S(1)}, u32[]{:S(2)}, u32[]{:S(2)}) %collective-permute-start.16) | collective-permute-done | bytes 65568 | tf_op jit(solution)/shard_map/ppermute | solution.py:25
  70.2 1.2 %collective-permute-done.17.refs_3_ = bf16[256,128]{1,0:T(8,128)(2,1)S(1)} collective-permute-done((bf16[256,128]{1,0:T(8,128)(2,1)S(1)}, bf16[256,128]{1,0:T(8,128)(2,1)S(1)}, u32[]{:S(2)}, u32[]{:S(2)}) %collective-permute-start.17) | collective-permute-done | bytes 65568 | tf_op jit(solution)/shard_map/ppermute | solution.py:25
  71.4 1.8 %shard_map.63 = bf16[10,40,1280]{2,1,0:T(8,128)(2,1)} custom-call(f32[10,40,1280]{2,1,0:T(8,128)S(1)} %get-tuple-element.55.partial, bf16[512,1280]{1,0:T(8,128)(2,1)S(1)} %get-tuple-element.56.weight, bf16[256,128]{1,0:T(8,128)(2,1)S(1)} %get-tuple-element.67.refs_0_, bf16[256,128]{1,0:T(8,128)(2,1)S(1)} %collective-permute-done.15.refs_1_, ...), custom_call_target="tpu_custom_call" | custom-call | flops 524288000 | bytes 3891200 | tf_op jit(solution)/shard_map/pallas_call | solution.py:392
Async XLA Ops:
  1.1 16.9 %copy-start.2 = (f32[1280]{0:T(1024)S(1)}, f32[1280]{0:T(1024)}, u32[]{:S(2)}) copy-start(f32[1280]{0:T(1024)} %gain.3) | copy-start | bytes 15364
  1.1 16.9 %copy-start.3 = (s32[4]{0:T(128)S(1)}, s32[4]{0:T(128)}, u32[]{:S(2)}) copy-start(s32[4]{0:T(128)} %lon_shift.5) | copy-start | bytes 52
  1.1 16.9 %collective-permute-start.3 = (bf16[10,24,1280]{2,1,0:T(8,128)(2,1)S(1)}, bf16[10,24,1280]{2,1,0:T(8,128)(2,1)S(1)}, u32[]{:S(2)}, u32[]{:S(2)}) collective-permute-start(bf16[10,24,1280]{2,1,0:T(8,128)(2,1)S(1)} %slice.4), channel_id=1, source_target_pairs={{0,16},{4,20},{8,24},{12,28},{16,0},{20,4},{24,8},{28,12},{1,17},{... | collective-permute-start | bytes 1843208 | tf_op jit(solution)/shard_map/ppermute | solution.py:25
  8.7 14.6 %collective-permute-start = (bf16[160,512]{1,0:T(8,128)(2,1)}, bf16[160,512]{1,0:T(8,128)(2,1)S(1)}, u32[]{:S(2)}, u32[]{:S(2)}) collective-permute-start(bf16[160,512]{1,0:T(8,128)(2,1)} %get-tuple-element.39), channel_id=1, source_target_pairs={{0,1},{1,2},{2,3},{3,0},{4,5},{5,6},{6,7},{7,4},{8,9},{9,10},{10,1... | collective-permute-start | bytes 491528 | tf_op jit(solution)/shard_map/ppermute | solution.py:25
  10.3 14.8 %collective-permute-start.1 = (bf16[160,512]{1,0:T(8,128)(2,1)}, bf16[160,512]{1,0:T(8,128)(2,1)S(1)}, u32[]{:S(2)}, u32[]{:S(2)}) collective-permute-start(bf16[160,512]{1,0:T(8,128)(2,1)} %get-tuple-element.40), channel_id=1, source_target_pairs={{0,2},{1,3},{2,0},{3,1},{4,6},{5,7},{6,4},{7,5},{8,10},{9,11},{10,... | collective-permute-start | bytes 491528 | tf_op jit(solution)/shard_map/ppermute | solution.py:25
  12.9 24.5 %copy-start.4 = (bf16[160,512]{1,0:T(8,128)(2,1)S(1)}, bf16[160,512]{1,0:T(8,128)(2,1)}, u32[]{:S(2)}) copy-start(bf16[160,512]{1,0:T(8,128)(2,1)} %get-tuple-element.38.refs_0_) | copy-start | bytes 491524
  12.9 14.8 %collective-permute-start.2 = (bf16[160,512]{1,0:T(8,128)(2,1)}, bf16[160,512]{1,0:T(8,128)(2,1)S(1)}, u32[]{:S(2)}, u32[]{:S(2)}) collective-permute-start(bf16[160,512]{1,0:T(8,128)(2,1)} %get-tuple-element.41), channel_id=1, source_target_pairs={{0,3},{1,0},{2,1},{3,2},{4,7},{5,4},{6,5},{7,6},{8,11},{9,8},{10,9... | collective-permute-start | bytes 491528 | tf_op jit(solution)/shard_map/ppermute | solution.py:25
  23.3 8.1 %collective-permute-start.4 = (bf16[240,256]{1,0:T(8,128)(2,1)S(1)}, bf16[240,256]{1,0:T(8,128)(2,1)S(1)}, u32[]{:S(2)}, u32[]{:S(2)}) collective-permute-start(bf16[240,256]{1,0:T(8,128)(2,1)S(1)} %get-tuple-element.44), channel_id=1, source_target_pairs={{0,1},{1,2},{2,3},{3,0},{4,5},{5,6},{6,7},{7,4},{8,9},{9,10},{10,1... | collective-permute-start | bytes 368648 | tf_op jit(solution)/shard_map/ppermute | solution.py:25
  25.2 11.2 %collective-permute-start.5 = (bf16[240,256]{1,0:T(8,128)(2,1)S(1)}, bf16[240,256]{1,0:T(8,128)(2,1)S(1)}, u32[]{:S(2)}, u32[]{:S(2)}) collective-permute-start(bf16[240,256]{1,0:T(8,128)(2,1)S(1)} %get-tuple-element.46), channel_id=1, source_target_pairs={{0,2},{1,3},{2,0},{3,1},{4,6},{5,7},{6,4},{7,5},{8,10},{9,11},{10,... | collective-permute-start | bytes 368648 | tf_op jit(solution)/shard_map/ppermute | solution.py:25
  27.8 9.6 %collective-permute-start.6 = (bf16[240,256]{1,0:T(8,128)(2,1)S(1)}, bf16[240,256]{1,0:T(8,128)(2,1)S(1)}, u32[]{:S(2)}, u32[]{:S(2)}) collective-permute-start(bf16[240,256]{1,0:T(8,128)(2,1)S(1)} %get-tuple-element.48), channel_id=1, source_target_pairs={{0,3},{1,0},{2,1},{3,2},{4,7},{5,4},{6,5},{7,6},{8,11},{9,8},{10,9... | collective-permute-start | bytes 368648 | tf_op jit(solution)/shard_map/ppermute | solution.py:25
  31.4 15.8 %collective-permute-start.11 = (bf16[240,256]{1,0:T(8,128)(2,1)S(1)}, bf16[240,256]{1,0:T(8,128)(2,1)S(1)}, u32[]{:S(2)}, u32[]{:S(2)}) collective-permute-start(bf16[240,256]{1,0:T(8,128)(2,1)S(1)} %get-tuple-element.59), channel_id=1, source_target_pairs={{0,1},{1,2},{2,3},{3,0},{4,5},{5,6},{6,7},{7,4},{8,9},{9,10},{10,1... | collective-permute-start | bytes 368648 | tf_op jit(solution)/shard_map/ppermute | solution.py:25
  36.3 10.9 %collective-permute-start.12 = (bf16[240,256]{1,0:T(8,128)(2,1)S(1)}, bf16[240,256]{1,0:T(8,128)(2,1)S(1)}, u32[]{:S(2)}, u32[]{:S(2)}) collective-permute-start(bf16[240,256]{1,0:T(8,128)(2,1)S(1)} %get-tuple-element.61), channel_id=1, source_target_pairs={{0,2},{1,3},{2,0},{3,1},{4,6},{5,7},{6,4},{7,5},{8,10},{9,11},{10,... | collective-permute-start | bytes 368648 | tf_op jit(solution)/shard_map/ppermute | solution.py:25
  41.6 8.4 %collective-permute-start.13 = (bf16[240,256]{1,0:T(8,128)(2,1)S(1)}, bf16[240,256]{1,0:T(8,128)(2,1)S(1)}, u32[]{:S(2)}, u32[]{:S(2)}) collective-permute-start(bf16[240,256]{1,0:T(8,128)(2,1)S(1)} %get-tuple-element.63), channel_id=1, source_target_pairs={{0,3},{1,0},{2,1},{3,2},{4,7},{5,4},{6,5},{7,6},{8,11},{9,8},{10,9... | collective-permute-start | bytes 368648 | tf_op jit(solution)/shard_map/ppermute | solution.py:25
  45.4 8.9 %collective-permute-start.7 = (bf16[960,128]{1,0:T(8,128)(2,1)S(1)}, bf16[960,128]{1,0:T(8,128)(2,1)S(1)}, u32[]{:S(2)}, u32[]{:S(2)}) collective-permute-start(bf16[960,128]{1,0:T(8,128)(2,1)S(1)} %get-tuple-element.50.mixed), channel_id=1, source_target_pairs={{0,16},{4,20},{8,24},{12,28},{16,0},{20,4},{24,8},{28,12},{1,17},{... | collective-permute-start | bytes 737288 | tf_op jit(solution)/shard_map/ppermute | solution.py:25
  52.8 7.8 %collective-permute-start.14 = (bf16[960,128]{1,0:T(8,128)(2,1)S(1)}, bf16[960,128]{1,0:T(8,128)(2,1)S(1)}, u32[]{:S(2)}, u32[]{:S(2)}) collective-permute-start(bf16[960,128]{1,0:T(8,128)(2,1)S(1)} %get-tuple-element.66.mixed), channel_id=1, source_target_pairs={{0,16},{4,20},{8,24},{12,28},{16,0},{20,4},{24,8},{28,12},{1,17},{... | collective-permute-start | bytes 737288 | tf_op jit(solution)/shard_map/ppermute | solution.py:25
  55.1 10.2 %collective-permute-start.8 = (bf16[256,128]{1,0:T(8,128)(2,1)S(1)}, bf16[256,128]{1,0:T(8,128)(2,1)S(1)}, u32[]{:S(2)}, u32[]{:S(2)}) collective-permute-start(bf16[256,128]{1,0:T(8,128)(2,1)S(1)} %get-tuple-element.52), channel_id=1, source_target_pairs={{0,3},{1,0},{2,1},{3,2},{4,7},{5,4},{6,5},{7,6},{8,11},{9,8},{10,9... | collective-permute-start | bytes 196616 | tf_op jit(solution)/shard_map/ppermute | solution.py:25
  57.6 8.1 %collective-permute-start.9 = (bf16[256,128]{1,0:T(8,128)(2,1)S(1)}, bf16[256,128]{1,0:T(8,128)(2,1)S(1)}, u32[]{:S(2)}, u32[]{:S(2)}) collective-permute-start(bf16[256,128]{1,0:T(8,128)(2,1)S(1)} %get-tuple-element.53), channel_id=1, source_target_pairs={{0,2},{1,3},{2,0},{3,1},{4,6},{5,7},{6,4},{7,5},{8,10},{9,11},{10,... | collective-permute-start | bytes 196616 | tf_op jit(solution)/shard_map/ppermute | solution.py:25
  58.4 7.3 %collective-permute-start.10 = (bf16[256,128]{1,0:T(8,128)(2,1)S(1)}, bf16[256,128]{1,0:T(8,128)(2,1)S(1)}, u32[]{:S(2)}, u32[]{:S(2)}) collective-permute-start(bf16[256,128]{1,0:T(8,128)(2,1)S(1)} %get-tuple-element.54), channel_id=1, source_target_pairs={{0,1},{1,2},{2,3},{3,0},{4,5},{5,6},{6,7},{7,4},{8,9},{9,10},{10,1... | collective-permute-start | bytes 196616 | tf_op jit(solution)/shard_map/ppermute | solution.py:25
  58.6 7.1 %copy-start = (bf16[1,10,40,1280]{3,2,1,0:T(8,128)(2,1)S(1)}, bf16[1,10,40,1280]{3,2,1,0:T(8,128)(2,1)}, u32[]{:S(2)}) copy-start(bf16[1,10,40,1280]{3,2,1,0:T(8,128)(2,1)} %param.5) | copy-start | bytes 3072004
  58.6 7.1 %copy-start.1 = (bf16[640,1280]{1,0:T(8,128)(2,1)S(1)}, bf16[640,1280]{1,0:T(8,128)(2,1)}, u32[]{:S(2)}) copy-start(bf16[640,1280]{1,0:T(8,128)(2,1)} %weight.5) | copy-start | bytes 4915204
  61.4 5.6 %collective-permute-start.15 = (bf16[256,128]{1,0:T(8,128)(2,1)S(1)}, bf16[256,128]{1,0:T(8,128)(2,1)S(1)}, u32[]{:S(2)}, u32[]{:S(2)}) collective-permute-start(bf16[256,128]{1,0:T(8,128)(2,1)S(1)} %get-tuple-element.68), channel_id=1, source_target_pairs={{0,3},{1,0},{2,1},{3,2},{4,7},{5,4},{6,5},{7,6},{8,11},{9,8},{10,9... | collective-permute-start | bytes 196616 | tf_op jit(solution)/shard_map/ppermute | solution.py:25
  65.0 5.2 %collective-permute-start.16 = (bf16[256,128]{1,0:T(8,128)(2,1)S(1)}, bf16[256,128]{1,0:T(8,128)(2,1)S(1)}, u32[]{:S(2)}, u32[]{:S(2)}) collective-permute-start(bf16[256,128]{1,0:T(8,128)(2,1)S(1)} %get-tuple-element.69), channel_id=1, source_target_pairs={{0,2},{1,3},{2,0},{3,1},{4,6},{5,7},{6,4},{7,5},{8,10},{9,11},{10,... | collective-permute-start | bytes 196616 | tf_op jit(solution)/shard_map/ppermute | solution.py:25
  65.4 6.1 %collective-permute-start.17 = (bf16[256,128]{1,0:T(8,128)(2,1)S(1)}, bf16[256,128]{1,0:T(8,128)(2,1)S(1)}, u32[]{:S(2)}, u32[]{:S(2)}) collective-permute-start(bf16[256,128]{1,0:T(8,128)(2,1)S(1)} %get-tuple-element.70), channel_id=1, source_target_pairs={{0,1},{1,2},{2,3},{3,0},{4,5},{5,6},{6,7},{7,4},{8,9},{9,10},{10,1... | collective-permute-start | bytes 196616 | tf_op jit(solution)/shard_map/ppermute | solution.py:25

commit v6 on v5

--- a/solution.py
+++ b/solution.py
@@ -26,8 +26,9 @@
 
 
 def after(blocks, arrived):
-    return [blocks[0]] + [
-        lax.optimization_barrier(pair)[0] for pair in zip(blocks[1:], arrived[1:])
+    return [
+        block if other is None else lax.optimization_barrier((block, other))[0]
+        for block, other in zip(blocks, arrived)
     ]
 
 
@@ -42,11 +43,12 @@
     span = slots.shape[2] // local
     factor = lax.rsqrt(jnp.mean(tokens * tokens, axis=-1, keepdims=True) + 1e-06)
     normed = (tokens * factor * gain[...].reshape(1, features)).astype(jnp.bfloat16)
-    chunk = weight.shape[1] // CHUNKS
+    chunk = features // CHUNKS
     for index in range(CHUNKS):
         copies[index].wait()
-        columns = slice(index * chunk, (index + 1) * chunk)
-        qkv[:, columns] = jnp.dot(normed, weight[:, columns], preferred_element_type=jnp.float32)
+        inner = slice(index * chunk, (index + 1) * chunk)
+        share = jnp.dot(normed[:, inner], weight[inner], preferred_element_type=jnp.float32)
+        qkv[...] = qkv[...] + share if index else share
     tail = jnp.ones((count, span - 3 * HD), jnp.float32)
     place = lax.axis_index("tok")
     for group in range(groups):
@@ -64,13 +66,11 @@
 
 
 def fetch(weight, held, sems):
-    chunk = weight.shape[1] // CHUNKS
+    chunk = weight.shape[0] // CHUNKS
     copies = []
     for index in range(CHUNKS):
-        columns = pl.ds(index * chunk, chunk)
-        copies.append(
-            pltpu.make_async_copy(weight.at[:, columns], held.at[:, columns], sems.at[index])
-        )
+        inner = pl.ds(index * chunk, chunk)
+        copies.append(pltpu.make_async_copy(weight.at[inner], held.at[inner], sems.at[index]))
         copies[-1].start()
     return copies
 
@@ -90,13 +90,27 @@
     project(tokens, held_gain, held_weight, copies, qkv, slots, outs)
 
 
+def leaving_kernel(field, out):
+    rows, columns, _ = field.shape
+    tokens = field[...].astype(jnp.float32)
+    pieces = [tokens[row, : columns // 2] for row in range(rows)]
+    out[...] = jnp.concatenate(pieces, axis=0).astype(jnp.bfloat16)
+
+
 def mixed_kernel(split, field, gain, weight, lon_shift, eastern, *refs):
     *outs, qkv, slots, held_weight, sems = refs
     copies = fetch(weight, held_weight, sems)
-    rows, _, features = field.shape
+    rows, columns, features = field.shape
+    count = columns // 2
     own = field[...].astype(jnp.float32)[:, :split]
+    arrived = eastern[...].astype(jnp.float32)
+    filler = jnp.zeros((split - count, features), jnp.float32)
+    pieces = []
+    for row in range(rows):
+        pieces += [arrived[row * count : (row + 1) * count], filler]
+    arrived = jnp.concatenate(pieces, axis=0).reshape(own.shape)
     column = lax.broadcasted_iota(jnp.int32, own.shape, 1)
-    tokens = jnp.where(column < column_offset(lon_shift), eastern[...].astype(jnp.float32), own)
+    tokens = jnp.where(column < column_offset(lon_shift), arrived, own)
     project(tokens.reshape(rows * split, features), gain, held_weight, copies, qkv, slots, outs)
 
 
@@ -290,7 +304,17 @@
             shifted(blocks[distance], "tok", sign * distance) for distance in range(1, groups)
         ]
 
-    eastern = shifted(field[:, :split], "win", -LAT_WINDOWS)
+    leaving = pl.pallas_call(
+        leaving_kernel,
+        out_shape=jax.ShapeDtypeStruct((rows * (columns // 2), features), jnp.bfloat16),
+        in_specs=whole(1),
+        out_specs=pl.BlockSpec(memory_space=pltpu.VMEM),
+        compiler_params=limit(62),
+        cost_estimate=pl.CostEstimate(
+            flops=0, bytes_accessed=3 * rows * columns * features, transcendentals=0
+        ),
+    )(field)
+    eastern = shifted(leaving, "win", -LAT_WINDOWS)
     hbm = pl.BlockSpec(memory_space=pltpu.HBM)
     operands = (field, norm_gain, qkv_weight)
     held = [
@@ -303,7 +327,8 @@
     specs = [*whole(2), hbm, smem, *whole(1)]
     operands += (lon_shift, eastern)
     mixed = projection(mixed_kernel, mixed_count, local, specs, held[:2], limit(52), *operands)
-    first_mixed = spread(after(mixed[:groups], kept), 1)
+    ahead = [None] * (groups - 1)
+    first_mixed = spread(after(mixed[:groups], [*ahead, kept[1]]), 1)
 
     total = groups * rows * columns
     step = total // 5
@@ -354,8 +379,7 @@
         *first_mixed,
     )
     first_western = shifted(first_mixed_values, "win", LAT_WINDOWS)
-    ready = first_mixed[:-1] + [first_mixed_values]
-    second_mixed = spread(after(mixed[groups:], ready), 1)
+    second_mixed = spread(after(mixed[groups:], [None, *kept[2:], first_mixed[1]]), 1)
     second_mixed_values, *second_gathered = attention(
         functools.partial(second_mixed_kernel, groups),
         groups * mixed_count,

time: 73.4 us -> 76.3 us (1.040)
  starting transfers between devices: 34 us -> 36.8 us
  Pallas kernels: 22.9 us -> 24.8 us
  local copies, waits for them, and re-layouts: 1.14 us -> 0.02 us
    ppermute x18, starting transfers between devices: 34 us -> 36.8 us  [shifted(): lax.ppermute(block, axis, [(i, (i + distance) % count) for i in range(cou...]
    pallas_call x0 -> x1, Pallas kernels: none -> 2.08 us  [shards(): pl.pallas_call(leaving_kernel, out_shape=jax.ShapeDtypeStruct((rows * (co...]
    slice x1 -> x0, local copies, waits for them, and re-layouts: 1.11 us -> none  [shards(): eastern = shifted(field[:, :split], 'win', -LAT_WINDOWS)]
  transfers between devices with their start and end apart: 18 -> 18, of which waited for: 7 -> 6; matrix products, arithmetic and copies ran while one was open for 0% -> 0% of each run, Pallas kernels for 29% -> 28%
where the time goes in v6:
time: 76.3 us; the launch traced here: 76.1 us
  starting transfers between devices  36.8 us (48%)
  Pallas kernels  24.8 us (33%)
  waiting for transfers between devices  14.4 us (19%)
    ppermute x18, starting transfers between devices, shifted(): lax.ppermute(block, axis, [(i, (i + distance) % count) for i in range(cou...  36.8 us
    ppermute x18, waiting for transfers between devices, shifted(): lax.ppermute(block, axis, [(i, (i + distance) % count) for i in range(cou...  14.4 us
    pallas_call x2, Pallas kernels, projection(): pl.pallas_call(functools.partial(kernel, split), out_shape=[block] * (par...  9.49 us
    pallas_call x3, Pallas kernels, attention(): pl.pallas_call(kernel, out_shape=out_shape, in_specs=whole(len(operands))...  9.06 us
    pallas_call x1, Pallas kernels, shards(): pl.pallas_call(leaving_kernel, out_shape=jax.ShapeDtypeStruct((rows * (co...  2.08 us
    pallas_call x1, Pallas kernels, shards(): pl.pallas_call(functools.partial(second_output_kernel, split), out_shape=...  1.77 us
    pallas_call x2, Pallas kernels, back(): pl.pallas_call(functools.partial(pack_kernel, split), out_shape=[jax.Shap...  1.55 us
  transfers between devices with their start and end apart: 18, of which 6 were waited for; matrix products, arithmetic and copies ran while one was open for 0% of the time, Pallas kernels for 28%

profile of v6, /device:TPU:0, one launch (start us, length us, event | category | flops | bytes accessed | tf_op | source)
XLA Modules:
  0.0 76.1 jit_solution(7322540775083296574)
XLA Ops:
  0.0 2.1 %shard_map.56 = bf16[200,1280]{1,0:T(8,128)(2,1)} custom-call(bf16[10,40,1280]{2,1,0:T(8,128)(2,1)} %bitcast.2), custom_call_target="tpu_custom_call" | custom-call | bytes 1536000 | tf_op jit(solution)/shard_map/pallas_call | solution.py:307
  2.1 0.0 copy-start.2
  2.1 0.0 copy-start.3
  2.1 3.0 %collective-permute-start.3 = (bf16[200,1280]{1,0:T(8,128)(2,1)}, bf16[200,1280]{1,0:T(8,128)(2,1)S(1)}, u32[]{:S(2)}, u32[]{:S(2)}) collective-permute-start(bf16[200,1280]{1,0:T(8,128)(2,1)} %shard_map.56), channel_id=1, source_target_pairs={{0,16},{4,20},{8,24},{12,28},{16,0},{20,4},{24,8},{28,12},{1,17},{... | collective-permute-start | bytes 1536008 | tf_op jit(solution)/shard_map/ppermute | solution.py:25
  5.1 4.4 %shard_map.55 = (bf16[160,512]{1,0:T(8,128)(2,1)}, bf16[160,512]{1,0:T(8,128)(2,1)}, bf16[160,512]{1,0:T(8,128)(2,1)}, bf16[160,512]{1,0:T(8,128)(2,1)}) custom-call(bf16[10,40,1280]{2,1,0:T(8,128)(2,1)} %bitcast.3, f32[1280]{0:T(1024)} %gain.3, bf16[1280,1920]{1,0:T(8,128)(2,1)} %weight.4), custom_call_target="tpu_custom_call" | custom-call | flops 786432000 | bytes 5734400 | tf_op jit(solution)/shard_map/pallas_call | solution.py:284
  9.5 1.6 %collective-permute-start = (bf16[160,512]{1,0:T(8,128)(2,1)}, bf16[160,512]{1,0:T(8,128)(2,1)S(1)}, u32[]{:S(2)}, u32[]{:S(2)}) collective-permute-start(bf16[160,512]{1,0:T(8,128)(2,1)} %get-tuple-element.37), channel_id=1, source_target_pairs={{0,1},{1,2},{2,3},{3,0},{4,5},{5,6},{6,7},{7,4},{8,9},{9,10},{10,1... | collective-permute-start | bytes 491528 | tf_op jit(solution)/shard_map/ppermute | solution.py:25
  11.1 2.6 %collective-permute-start.1 = (bf16[160,512]{1,0:T(8,128)(2,1)}, bf16[160,512]{1,0:T(8,128)(2,1)S(1)}, u32[]{:S(2)}, u32[]{:S(2)}) collective-permute-start(bf16[160,512]{1,0:T(8,128)(2,1)} %get-tuple-element.38), channel_id=1, source_target_pairs={{0,2},{1,3},{2,0},{3,1},{4,6},{5,7},{6,4},{7,5},{8,10},{9,11},{10,... | collective-permute-start | bytes 491528 | tf_op jit(solution)/shard_map/ppermute | solution.py:25
  13.7 0.0 copy-start.4
  13.7 1.3 %collective-permute-start.2 = (bf16[160,512]{1,0:T(8,128)(2,1)}, bf16[160,512]{1,0:T(8,128)(2,1)S(1)}, u32[]{:S(2)}, u32[]{:S(2)}) collective-permute-start(bf16[160,512]{1,0:T(8,128)(2,1)} %get-tuple-element.39), channel_id=1, source_target_pairs={{0,3},{1,0},{2,1},{3,2},{4,7},{5,4},{6,5},{7,6},{8,11},{9,8},{10,9... | collective-permute-start | bytes 491528 | tf_op jit(solution)/shard_map/ppermute | solution.py:25
  15.1 1.9 %collective-permute-done.3.eastern = bf16[200,1280]{1,0:T(8,128)(2,1)S(1)} collective-permute-done((bf16[200,1280]{1,0:T(8,128)(2,1)}, bf16[200,1280]{1,0:T(8,128)(2,1)S(1)}, u32[]{:S(2)}, u32[]{:S(2)}) %collective-permute-start.3) | collective-permute-done | bytes 512032 | tf_op jit(solution)/shard_map/ppermute | solution.py:25
  16.9 0.0 copy-done.2
  16.9 0.0 copy-done.3
  16.9 5.1 %shard_map.57 = (bf16[240,256]{1,0:T(8,128)(2,1)S(1)}, bf16[240,256]{1,0:T(8,128)(2,1)S(1)}, bf16[240,256]{1,0:T(8,128)(2,1)S(1)}, bf16[240,256]{1,0:T(8,128)(2,...) custom-call(bf16[10,40,1280]{2,1,0:T(8,128)(2,1)} %bitcast.4, ...), custom_call_target="tpu_custom_call" | custom-call | flops 1179648000 | bytes 6144000 | tf_op jit(solution)/shard_map/pallas_call | solution.py:284
  22.0 1.9 %collective-permute-start.4 = (bf16[240,256]{1,0:T(8,128)(2,1)S(1)}, bf16[240,256]{1,0:T(8,128)(2,1)S(1)}, u32[]{:S(2)}, u32[]{:S(2)}) collective-permute-start(bf16[240,256]{1,0:T(8,128)(2,1)S(1)} %get-tuple-element.41), channel_id=1, source_target_pairs={{0,1},{1,2},{2,3},{3,0},{4,5},{5,6},{6,7},{7,4},{8,9},{9,10},{10,1... | collective-permute-start | bytes 368648 | tf_op jit(solution)/shard_map/ppermute | solution.py:25
  23.9 2.6 %collective-permute-start.5 = (bf16[240,256]{1,0:T(8,128)(2,1)S(1)}, bf16[240,256]{1,0:T(8,128)(2,1)S(1)}, u32[]{:S(2)}, u32[]{:S(2)}) collective-permute-start(bf16[240,256]{1,0:T(8,128)(2,1)S(1)} %get-tuple-element.42), channel_id=1, source_target_pairs={{0,2},{1,3},{2,0},{3,1},{4,6},{5,7},{6,4},{7,5},{8,10},{9,11},{10,... | collective-permute-start | bytes 368648 | tf_op jit(solution)/shard_map/ppermute | solution.py:25
  26.4 0.0 collective-permute-done.refs_1_
  26.4 1.3 %collective-permute-start.6 = (bf16[240,256]{1,0:T(8,128)(2,1)S(1)}, bf16[240,256]{1,0:T(8,128)(2,1)S(1)}, u32[]{:S(2)}, u32[]{:S(2)}) collective-permute-start(bf16[240,256]{1,0:T(8,128)(2,1)S(1)} %get-tuple-element.44), channel_id=1, source_target_pairs={{0,3},{1,0},{2,1},{3,2},{4,7},{5,4},{6,5},{7,6},{8,11},{9,8},{10,9... | collective-permute-start | bytes 368648 | tf_op jit(solution)/shard_map/ppermute | solution.py:25
  27.8 0.0 collective-permute-done.1.refs_2_
  27.8 1.3 %collective-permute-start.11 = (bf16[240,256]{1,0:T(8,128)(2,1)S(1)}, bf16[240,256]{1,0:T(8,128)(2,1)S(1)}, u32[]{:S(2)}, u32[]{:S(2)}) collective-permute-start(bf16[240,256]{1,0:T(8,128)(2,1)S(1)} %get-tuple-element.55), channel_id=1, source_target_pairs={{0,1},{1,2},{2,3},{3,0},{4,5},{5,6},{6,7},{7,4},{8,9},{9,10},{10,1... | collective-permute-start | bytes 368648 | tf_op jit(solution)/shard_map/ppermute | solution.py:25
  29.1 0.0 collective-permute-done.2.refs_3_
  29.1 6.7 %collective-permute-start.12 = (bf16[240,256]{1,0:T(8,128)(2,1)S(1)}, bf16[240,256]{1,0:T(8,128)(2,1)S(1)}, u32[]{:S(2)}, u32[]{:S(2)}) collective-permute-start(bf16[240,256]{1,0:T(8,128)(2,1)S(1)} %get-tuple-element.57), channel_id=1, source_target_pairs={{0,2},{1,3},{2,0},{3,1},{4,6},{5,7},{6,4},{7,5},{8,10},{9,11},{10,... | collective-permute-start | bytes 368648 | tf_op jit(solution)/shard_map/ppermute | solution.py:25
  35.7 0.0 collective-permute-done.4.refs_5_
  35.7 1.6 %collective-permute-start.13 = (bf16[240,256]{1,0:T(8,128)(2,1)S(1)}, bf16[240,256]{1,0:T(8,128)(2,1)S(1)}, u32[]{:S(2)}, u32[]{:S(2)}) collective-permute-start(bf16[240,256]{1,0:T(8,128)(2,1)S(1)} %get-tuple-element.59), channel_id=1, source_target_pairs={{0,3},{1,0},{2,1},{3,2},{4,7},{5,4},{6,5},{7,6},{8,11},{9,8},{10,9... | collective-permute-start | bytes 368648 | tf_op jit(solution)/shard_map/ppermute | solution.py:25
  37.3 3.4 %collective-permute-done.5.refs_6_ = bf16[240,256]{1,0:T(8,128)(2,1)S(1)} collective-permute-done((bf16[240,256]{1,0:T(8,128)(2,1)S(1)}, bf16[240,256]{1,0:T(8,128)(2,1)S(1)}, u32[]{:S(2)}, u32[]{:S(2)}) %collective-permute-start.5) | collective-permute-done | bytes 122912 | tf_op jit(solution)/shard_map/ppermute | solution.py:25
  40.7 0.0 collective-permute-done.6.refs_7_
  40.7 0.0 copy-done.4
  40.7 4.2 %shard_map.58 = (bf16[640,128]{1,0:T(8,128)(2,1)S(1)}, bf16[960,128]{1,0:T(8,128)(2,1)S(1)}) custom-call(bf16[160,512]{1,0:T(8,128)(2,1)S(1)} %copy-done.4, bf16[160,512]{1,0:T(8,128)(2,1)S(1)} %collective-permute-done.refs_1_, bf16[160,512]{1,0:T(8,128)(2,1)S(1)} %collective-permute-done.1.refs_2_, bf16[160,512]{1,0:T(8,128)(2,1)S(1)} %collective-permute-done.2.refs_3_, ...), custom_call_target="tpu_custom_call" | custom-call | flops 2621440000 | bytes 1228800 | tf_op jit(solution)/shard_map/pallas_call | solution.py:344
  44.9 0.7 collective-permute-start.7
  45.6 0.0 collective-permute-done.11.refs_5_
  45.6 0.8 %collective-permute-done.12.refs_6_ = bf16[240,256]{1,0:T(8,128)(2,1)S(1)} collective-permute-done((bf16[240,256]{1,0:T(8,128)(2,1)S(1)}, bf16[240,256]{1,0:T(8,128)(2,1)S(1)}, u32[]{:S(2)}, u32[]{:S(2)}) %collective-permute-start.12) | collective-permute-done | bytes 122912 | tf_op jit(solution)/shard_map/ppermute | solution.py:25
  46.4 0.0 collective-permute-done.13.refs_7_
  46.4 2.9 %shard_map.61 = (bf16[960,128]{1,0:T(8,128)(2,1)S(1)}, bf16[1600,256]{1,0:T(8,128)(2,1)S(1)}, bf16[256,1600]{1,0:T(8,128)(2,1)S(1)}) custom-call(bf16[160,512]{1,0:T(8,128)(2,1)S(1)} %copy-done.4, bf16[160,512]{1,0:T(8,128)(2,1)S(1)} %collective-permute-done.refs_1_, bf16[160,512]{1,0:T(8,128)(2,1)S(1)} %collective-permute-done.1.refs_2_, ...), custom_call_target="tpu_custom_call" | custom-call | flops 1572864000 | bytes 1228800 | tf_op jit(solution)/shard_map/pallas_call | solution.py:344
  49.3 0.7 collective-permute-start.14
  49.9 3.2 %collective-permute-done.7.western = bf16[960,128]{1,0:T(8,128)(2,1)S(1)} collective-permute-done((bf16[960,128]{1,0:T(8,128)(2,1)S(1)}, bf16[960,128]{1,0:T(8,128)(2,1)S(1)}, u32[]{:S(2)}, u32[]{:S(2)}) %collective-permute-start.7) | collective-permute-done | bytes 245792 | tf_op jit(solution)/shard_map/ppermute | solution.py:25
  53.2 0.8 %shard_map.59 = (bf16[256,128]{1,0:T(8,128)(2,1)S(1)}, bf16[256,128]{1,0:T(8,128)(2,1)S(1)}, bf16[256,128]{1,0:T(8,128)(2,1)S(1)}, bf16[256,128]{1,0:T(8,128)(2,1)S(1)}) custom-call(s32[4]{0:T(128)S(1)} %copy-done.3, bf16[640,128]{1,0:T(8,128)(2,1)S(1)} %get-tuple-element.45.kept, bf16[960,128]{1,0:T(8,128)(2,1)S(1)} %get-tuple-element.46.mixed, ...), custom_call_target="tpu_custom_call" | custom-call | flops 4096000 | bytes 1638400 | tf_op jit(solution)/shard_map/pallas_call | solution.py:361
  53.9 6.5 %collective-permute-start.8 = (bf16[256,128]{1,0:T(8,128)(2,1)S(1)}, bf16[256,128]{1,0:T(8,128)(2,1)S(1)}, u32[]{:S(2)}, u32[]{:S(2)}) collective-permute-start(bf16[256,128]{1,0:T(8,128)(2,1)S(1)} %get-tuple-element.48), channel_id=1, source_target_pairs={{0,3},{1,0},{2,1},{3,2},{4,7},{5,4},{6,5},{7,6},{8,11},{9,8},{10,9... | collective-permute-start | bytes 196616 | tf_op jit(solution)/shard_map/ppermute | solution.py:25
  60.5 0.0 collective-permute-start.9
  60.5 0.6 collective-permute-start.10
  61.1 0.0 copy-start
  61.1 0.0 copy-start.1
  61.1 2.0 %shard_map.62.kept = bf16[640,128]{1,0:T(8,128)(2,1)S(1)} custom-call(bf16[1600,256]{1,0:T(8,128)(2,1)S(1)} %get-tuple-element.60.held, bf16[256,1600]{1,0:T(8,128)(2,1)S(1)} %get-tuple-element.61.keys), custom_call_target="tpu_custom_call" | custom-call | flops 1048576000 | bytes 1228800 | tf_op jit(solution)/shard_map/pallas_call | solution.py:344
  63.1 0.0 collective-permute-done.14.western
  63.1 0.8 %shard_map.63 = (bf16[256,128]{1,0:T(8,128)(2,1)S(1)}, bf16[256,128]{1,0:T(8,128)(2,1)S(1)}, bf16[256,128]{1,0:T(8,128)(2,1)S(1)}, bf16[256,128]{1,0:T(8,128)(2,1)S(1)}) custom-call(s32[4]{0:T(128)S(1)} %copy-done.3, bf16[640,128]{1,0:T(8,128)(2,1)S(1)} %shard_map.62.kept, bf16[960,128]{1,0:T(8,128)(2,1)S(1)} %get-tuple-element.62.mixed, ...), custom_call_target="tpu_custom_call" | custom-call | flops 4096000 | bytes 1638400 | tf_op jit(solution)/shard_map/pallas_call | solution.py:361
  63.9 3.2 %collective-permute-start.15 = (bf16[256,128]{1,0:T(8,128)(2,1)S(1)}, bf16[256,128]{1,0:T(8,128)(2,1)S(1)}, u32[]{:S(2)}, u32[]{:S(2)}) collective-permute-start(bf16[256,128]{1,0:T(8,128)(2,1)S(1)} %get-tuple-element.64), channel_id=1, source_target_pairs={{0,3},{1,0},{2,1},{3,2},{4,7},{5,4},{6,5},{7,6},{8,11},{9,8},{10,9... | collective-permute-start | bytes 196616 | tf_op jit(solution)/shard_map/ppermute | solution.py:25
  67.1 1.1 %collective-permute-start.16 = (bf16[256,128]{1,0:T(8,128)(2,1)S(1)}, bf16[256,128]{1,0:T(8,128)(2,1)S(1)}, u32[]{:S(2)}, u32[]{:S(2)}) collective-permute-start(bf16[256,128]{1,0:T(8,128)(2,1)S(1)} %get-tuple-element.65), channel_id=1, source_target_pairs={{0,2},{1,3},{2,0},{3,1},{4,6},{5,7},{6,4},{7,5},{8,10},{9,11},{10,... | collective-permute-start | bytes 196616 | tf_op jit(solution)/shard_map/ppermute | solution.py:25
  68.3 0.0 collective-permute-done.8.refs_1_
  68.3 0.0 collective-permute-start.17
  68.3 0.0 collective-permute-done.9.refs_2_
  68.3 0.0 collective-permute-done.10.refs_3_
  68.3 0.0 copy-done
  68.3 0.0 copy-done.1
  68.3 0.8 %shard_map.60 = (f32[10,40,1280]{2,1,0:T(8,128)S(1)}, bf16[512,1280]{1,0:T(8,128)(2,1)S(1)}) custom-call(bf16[10,40,1280]{2,1,0:T(8,128)(2,1)S(1)} %bitcast.5, bf16[640,1280]{1,0:T(8,128)(2,1)S(1)} %copy-done.1, bf16[256,128]{1,0:T(8,128)(2,1)S(1)} %get-tuple-element.47.refs_0_, bf16[256,128]{1,0:T(8,128)(2,1)S(1)} %collective-permute-done.8.refs_1_, ...), custom_call_target="tpu_custom_call" | custom-call | flops 524288000 | bytes 3891200 | tf_op jit(solution)/shard_map/pallas_call | solution.py:404
  69.2 0.0 collective-permute-done.15.refs_1_
  69.2 3.1 %collective-permute-done.16.refs_2_ = bf16[256,128]{1,0:T(8,128)(2,1)S(1)} collective-permute-done((bf16[256,128]{1,0:T(8,128)(2,1)S(1)}, bf16[256,128]{1,0:T(8,128)(2,1)S(1)}, u32[]{:S(2)}, u32[]{:S(2)}) %collective-permute-start.16) | collective-permute-done | bytes 65568 | tf_op jit(solution)/shard_map/ppermute | solution.py:25
  72.3 2.0 %collective-permute-done.17.refs_3_ = bf16[256,128]{1,0:T(8,128)(2,1)S(1)} collective-permute-done((bf16[256,128]{1,0:T(8,128)(2,1)S(1)}, bf16[256,128]{1,0:T(8,128)(2,1)S(1)}, u32[]{:S(2)}, u32[]{:S(2)}) %collective-permute-start.17) | collective-permute-done | bytes 65568 | tf_op jit(solution)/shard_map/ppermute | solution.py:25
  74.3 1.8 %shard_map.64 = bf16[10,40,1280]{2,1,0:T(8,128)(2,1)} custom-call(f32[10,40,1280]{2,1,0:T(8,128)S(1)} %get-tuple-element.51.partial, bf16[512,1280]{1,0:T(8,128)(2,1)S(1)} %get-tuple-element.52.weight, bf16[256,128]{1,0:T(8,128)(2,1)S(1)} %get-tuple-element.63.refs_0_, bf16[256,128]{1,0:T(8,128)(2,1)S(1)} %collective-permute-done.15.refs_1_, ...), custom_call_target="tpu_custom_call" | custom-call | flops 524288000 | bytes 3891200 | tf_op jit(solution)/shard_map/pallas_call | solution.py:416
Async XLA Ops:
  2.1 14.8 %copy-start.2 = (f32[1280]{0:T(1024)S(1)}, f32[1280]{0:T(1024)}, u32[]{:S(2)}) copy-start(f32[1280]{0:T(1024)} %gain.3) | copy-start | bytes 15364
  2.1 14.8 %copy-start.3 = (s32[4]{0:T(128)S(1)}, s32[4]{0:T(128)}, u32[]{:S(2)}) copy-start(s32[4]{0:T(128)} %lon_shift.5) | copy-start | bytes 52
  2.1 14.8 %collective-permute-start.3 = (bf16[200,1280]{1,0:T(8,128)(2,1)}, bf16[200,1280]{1,0:T(8,128)(2,1)S(1)}, u32[]{:S(2)}, u32[]{:S(2)}) collective-permute-start(bf16[200,1280]{1,0:T(8,128)(2,1)} %shard_map.56), channel_id=1, source_target_pairs={{0,16},{4,20},{8,24},{12,28},{16,0},{20,4},{24,8},{28,12},{1,17},{... | collective-permute-start | bytes 1536008 | tf_op jit(solution)/shard_map/ppermute | solution.py:25
  9.5 16.9 %collective-permute-start = (bf16[160,512]{1,0:T(8,128)(2,1)}, bf16[160,512]{1,0:T(8,128)(2,1)S(1)}, u32[]{:S(2)}, u32[]{:S(2)}) collective-permute-start(bf16[160,512]{1,0:T(8,128)(2,1)} %get-tuple-element.37), channel_id=1, source_target_pairs={{0,1},{1,2},{2,3},{3,0},{4,5},{5,6},{6,7},{7,4},{8,9},{9,10},{10,1... | collective-permute-start | bytes 491528 | tf_op jit(solution)/shard_map/ppermute | solution.py:25
  11.1 16.7 %collective-permute-start.1 = (bf16[160,512]{1,0:T(8,128)(2,1)}, bf16[160,512]{1,0:T(8,128)(2,1)S(1)}, u32[]{:S(2)}, u32[]{:S(2)}) collective-permute-start(bf16[160,512]{1,0:T(8,128)(2,1)} %get-tuple-element.38), channel_id=1, source_target_pairs={{0,2},{1,3},{2,0},{3,1},{4,6},{5,7},{6,4},{7,5},{8,10},{9,11},{10,... | collective-permute-start | bytes 491528 | tf_op jit(solution)/shard_map/ppermute | solution.py:25
  13.7 27.0 %copy-start.4 = (bf16[160,512]{1,0:T(8,128)(2,1)S(1)}, bf16[160,512]{1,0:T(8,128)(2,1)}, u32[]{:S(2)}) copy-start(bf16[160,512]{1,0:T(8,128)(2,1)} %get-tuple-element.36.refs_0_) | copy-start | bytes 491524
  13.7 15.4 %collective-permute-start.2 = (bf16[160,512]{1,0:T(8,128)(2,1)}, bf16[160,512]{1,0:T(8,128)(2,1)S(1)}, u32[]{:S(2)}, u32[]{:S(2)}) collective-permute-start(bf16[160,512]{1,0:T(8,128)(2,1)} %get-tuple-element.39), channel_id=1, source_target_pairs={{0,3},{1,0},{2,1},{3,2},{4,7},{5,4},{6,5},{7,6},{8,11},{9,8},{10,9... | collective-permute-start | bytes 491528 | tf_op jit(solution)/shard_map/ppermute | solution.py:25
  22.0 13.7 %collective-permute-start.4 = (bf16[240,256]{1,0:T(8,128)(2,1)S(1)}, bf16[240,256]{1,0:T(8,128)(2,1)S(1)}, u32[]{:S(2)}, u32[]{:S(2)}) collective-permute-start(bf16[240,256]{1,0:T(8,128)(2,1)S(1)} %get-tuple-element.41), channel_id=1, source_target_pairs={{0,1},{1,2},{2,3},{3,0},{4,5},{5,6},{6,7},{7,4},{8,9},{9,10},{10,1... | collective-permute-start | bytes 368648 | tf_op jit(solution)/shard_map/ppermute | solution.py:25
  23.9 16.8 %collective-permute-start.5 = (bf16[240,256]{1,0:T(8,128)(2,1)S(1)}, bf16[240,256]{1,0:T(8,128)(2,1)S(1)}, u32[]{:S(2)}, u32[]{:S(2)}) collective-permute-start(bf16[240,256]{1,0:T(8,128)(2,1)S(1)} %get-tuple-element.42), channel_id=1, source_target_pairs={{0,2},{1,3},{2,0},{3,1},{4,6},{5,7},{6,4},{7,5},{8,10},{9,11},{10,... | collective-permute-start | bytes 368648 | tf_op jit(solution)/shard_map/ppermute | solution.py:25
  26.4 14.3 %collective-permute-start.6 = (bf16[240,256]{1,0:T(8,128)(2,1)S(1)}, bf16[240,256]{1,0:T(8,128)(2,1)S(1)}, u32[]{:S(2)}, u32[]{:S(2)}) collective-permute-start(bf16[240,256]{1,0:T(8,128)(2,1)S(1)} %get-tuple-element.44), channel_id=1, source_target_pairs={{0,3},{1,0},{2,1},{3,2},{4,7},{5,4},{6,5},{7,6},{8,11},{9,8},{10,9... | collective-permute-start | bytes 368648 | tf_op jit(solution)/shard_map/ppermute | solution.py:25
  27.8 17.8 %collective-permute-start.11 = (bf16[240,256]{1,0:T(8,128)(2,1)S(1)}, bf16[240,256]{1,0:T(8,128)(2,1)S(1)}, u32[]{:S(2)}, u32[]{:S(2)}) collective-permute-start(bf16[240,256]{1,0:T(8,128)(2,1)S(1)} %get-tuple-element.55), channel_id=1, source_target_pairs={{0,1},{1,2},{2,3},{3,0},{4,5},{5,6},{6,7},{7,4},{8,9},{9,10},{10,1... | collective-permute-start | bytes 368648 | tf_op jit(solution)/shard_map/ppermute | solution.py:25
  29.1 17.3 %collective-permute-start.12 = (bf16[240,256]{1,0:T(8,128)(2,1)S(1)}, bf16[240,256]{1,0:T(8,128)(2,1)S(1)}, u32[]{:S(2)}, u32[]{:S(2)}) collective-permute-start(bf16[240,256]{1,0:T(8,128)(2,1)S(1)} %get-tuple-element.57), channel_id=1, source_target_pairs={{0,2},{1,3},{2,0},{3,1},{4,6},{5,7},{6,4},{7,5},{8,10},{9,11},{10,... | collective-permute-start | bytes 368648 | tf_op jit(solution)/shard_map/ppermute | solution.py:25
  35.7 10.6 %collective-permute-start.13 = (bf16[240,256]{1,0:T(8,128)(2,1)S(1)}, bf16[240,256]{1,0:T(8,128)(2,1)S(1)}, u32[]{:S(2)}, u32[]{:S(2)}) collective-permute-start(bf16[240,256]{1,0:T(8,128)(2,1)S(1)} %get-tuple-element.59), channel_id=1, source_target_pairs={{0,3},{1,0},{2,1},{3,2},{4,7},{5,4},{6,5},{7,6},{8,11},{9,8},{10,9... | collective-permute-start | bytes 368648 | tf_op jit(solution)/shard_map/ppermute | solution.py:25
  44.9 8.3 %collective-permute-start.7 = (bf16[960,128]{1,0:T(8,128)(2,1)S(1)}, bf16[960,128]{1,0:T(8,128)(2,1)S(1)}, u32[]{:S(2)}, u32[]{:S(2)}) collective-permute-start(bf16[960,128]{1,0:T(8,128)(2,1)S(1)} %get-tuple-element.46.mixed), channel_id=1, source_target_pairs={{0,16},{4,20},{8,24},{12,28},{16,0},{20,4},{24,8},{28,12},{1,17},{... | collective-permute-start | bytes 737288 | tf_op jit(solution)/shard_map/ppermute | solution.py:25
  49.3 13.9 %collective-permute-start.14 = (bf16[960,128]{1,0:T(8,128)(2,1)S(1)}, bf16[960,128]{1,0:T(8,128)(2,1)S(1)}, u32[]{:S(2)}, u32[]{:S(2)}) collective-permute-start(bf16[960,128]{1,0:T(8,128)(2,1)S(1)} %get-tuple-element.62.mixed), channel_id=1, source_target_pairs={{0,16},{4,20},{8,24},{12,28},{16,0},{20,4},{24,8},{28,12},{1,17},{... | collective-permute-start | bytes 737288 | tf_op jit(solution)/shard_map/ppermute | solution.py:25
  53.9 14.3 %collective-permute-start.8 = (bf16[256,128]{1,0:T(8,128)(2,1)S(1)}, bf16[256,128]{1,0:T(8,128)(2,1)S(1)}, u32[]{:S(2)}, u32[]{:S(2)}) collective-permute-start(bf16[256,128]{1,0:T(8,128)(2,1)S(1)} %get-tuple-element.48), channel_id=1, source_target_pairs={{0,3},{1,0},{2,1},{3,2},{4,7},{5,4},{6,5},{7,6},{8,11},{9,8},{10,9... | collective-permute-start | bytes 196616 | tf_op jit(solution)/shard_map/ppermute | solution.py:25
  60.5 7.8 %collective-permute-start.9 = (bf16[256,128]{1,0:T(8,128)(2,1)S(1)}, bf16[256,128]{1,0:T(8,128)(2,1)S(1)}, u32[]{:S(2)}, u32[]{:S(2)}) collective-permute-start(bf16[256,128]{1,0:T(8,128)(2,1)S(1)} %get-tuple-element.49), channel_id=1, source_target_pairs={{0,2},{1,3},{2,0},{3,1},{4,6},{5,7},{6,4},{7,5},{8,10},{9,11},{10,... | collective-permute-start | bytes 196616 | tf_op jit(solution)/shard_map/ppermute | solution.py:25
  60.5 7.8 %collective-permute-start.10 = (bf16[256,128]{1,0:T(8,128)(2,1)S(1)}, bf16[256,128]{1,0:T(8,128)(2,1)S(1)}, u32[]{:S(2)}, u32[]{:S(2)}) collective-permute-start(bf16[256,128]{1,0:T(8,128)(2,1)S(1)} %get-tuple-element.50), channel_id=1, source_target_pairs={{0,1},{1,2},{2,3},{3,0},{4,5},{5,6},{6,7},{7,4},{8,9},{9,10},{10,1... | collective-permute-start | bytes 196616 | tf_op jit(solution)/shard_map/ppermute | solution.py:25
  61.1 7.2 %copy-start = (bf16[1,10,40,1280]{3,2,1,0:T(8,128)(2,1)S(1)}, bf16[1,10,40,1280]{3,2,1,0:T(8,128)(2,1)}, u32[]{:S(2)}) copy-start(bf16[1,10,40,1280]{3,2,1,0:T(8,128)(2,1)} %param.5) | copy-start | bytes 3072004
  61.1 7.2 %copy-start.1 = (bf16[640,1280]{1,0:T(8,128)(2,1)S(1)}, bf16[640,1280]{1,0:T(8,128)(2,1)}, u32[]{:S(2)}) copy-start(bf16[640,1280]{1,0:T(8,128)(2,1)} %weight.5) | copy-start | bytes 4915204
  63.9 5.3 %collective-permute-start.15 = (bf16[256,128]{1,0:T(8,128)(2,1)S(1)}, bf16[256,128]{1,0:T(8,128)(2,1)S(1)}, u32[]{:S(2)}, u32[]{:S(2)}) collective-permute-start(bf16[256,128]{1,0:T(8,128)(2,1)S(1)} %get-tuple-element.64), channel_id=1, source_target_pairs={{0,3},{1,0},{2,1},{3,2},{4,7},{5,4},{6,5},{7,6},{8,11},{9,8},{10,9... | collective-permute-start | bytes 196616 | tf_op jit(solution)/shard_map/ppermute | solution.py:25
  67.1 5.2 %collective-permute-start.16 = (bf16[256,128]{1,0:T(8,128)(2,1)S(1)}, bf16[256,128]{1,0:T(8,128)(2,1)S(1)}, u32[]{:S(2)}, u32[]{:S(2)}) collective-permute-start(bf16[256,128]{1,0:T(8,128)(2,1)S(1)} %get-tuple-element.65), channel_id=1, source_target_pairs={{0,2},{1,3},{2,0},{3,1},{4,6},{5,7},{6,4},{7,5},{8,10},{9,11},{10,... | collective-permute-start | bytes 196616 | tf_op jit(solution)/shard_map/ppermute | solution.py:25
  68.3 6.1 %collective-permute-start.17 = (bf16[256,128]{1,0:T(8,128)(2,1)S(1)}, bf16[256,128]{1,0:T(8,128)(2,1)S(1)}, u32[]{:S(2)}, u32[]{:S(2)}) collective-permute-start(bf16[256,128]{1,0:T(8,128)(2,1)S(1)} %get-tuple-element.66), channel_id=1, source_target_pairs={{0,1},{1,2},{2,3},{3,0},{4,5},{5,6},{6,7},{7,4},{8,9},{9,10},{10,1... | collective-permute-start | bytes 196616 | tf_op jit(solution)/shard_map/ppermute | solution.py:25

commit v7 on v3

v7 whole, which is shorter than its diff:
```python
import functools

import jax
import jax.numpy as jnp
from jax import lax
from jax.experimental import pallas as pl
from jax.experimental.pallas import tpu as pltpu
from jax.sharding import PartitionSpec as P

HEADS = 8
HD = 80
LAT_WINDOWS = 4
LANES = 128
SUBLANES = 8
MIB = 1024 * 1024


def round_up(value, unit):
    return -(-value // unit) * unit


def shifted(block, axis, distance):
    count = lax.axis_size(axis)
    return lax.ppermute(block, axis, [(i, (i + distance) % count) for i in range(count)])


def after(blocks, arrived):
    return [
        block if other is None else lax.optimization_barrier((block, other))[0]
        for block, other in zip(blocks, arrived)
    ]


def column_offset(lon_shift):
    return lon_shift[lax.rem(lax.axis_index("win"), LAT_WINDOWS)]


def project(tokens, gain, weight, copy, slots, outs):
    groups = slots.shape[0]
    local = HEADS // groups
    count, features = tokens.shape
    span = slots.shape[2] // local
    factor = lax.rsqrt(jnp.mean(tokens * tokens, axis=-1, keepdims=True) + 1e-06)
    normed = (tokens * factor * gain[...].reshape(1, features)).astype(jnp.bfloat16)
    copy.wait()
    qkv = jnp.dot(normed, weight[...], preferred_element_type=jnp.float32).astype(jnp.bfloat16)
    tail = jnp.ones((count, span - 3 * HD), jnp.bfloat16)
    place = lax.axis_index("tok")
    for group in range(groups):
        slot = lax.rem(group - place + groups, groups)
        columns = []
        for head in range(group * local, (group + 1) * local):
            columns += [
                qkv[:, (kind * HEADS + head) * HD : (kind * HEADS + head + 1) * HD]
                for kind in range(3)
            ] + [tail]
        slots[slot] = jnp.concatenate(columns, axis=1)
    for index, out in enumerate(outs):
        first = index // groups * out.shape[1]
        out[...] = slots[index % groups, :, first : first + out.shape[1]]


def kept_kernel(split, field, gain, weight, *refs):
    *outs, slots, held_weight, sems, held_field, held_gain = refs
    copy = pltpu.make_async_copy(weight, held_weight, sems.at[0])
    first = pltpu.make_async_copy(field, held_field, sems.at[1])
    second = pltpu.make_async_copy(gain, held_gain, sems.at[2])
    first.start()
    second.start()
    copy.start()
    first.wait()
    second.wait()
    rows, columns, features = field.shape
    tokens = held_field[...].astype(jnp.float32)[:, split:]
    tokens = tokens.reshape(rows * (columns - split), features)
    project(tokens, held_gain, held_weight, copy, slots, outs)


def mixed_kernel(split, field, gain, weight, lon_shift, eastern, *refs):
    *outs, slots, held_weight, sems = refs
    copy = pltpu.make_async_copy(weight, held_weight, sems.at[0])
    copy.start()
    rows, _, features = field.shape
    own = field[...].astype(jnp.float32)[:, :split]
    column = lax.broadcasted_iota(jnp.int32, own.shape, 1)
    tokens = jnp.where(column < column_offset(lon_shift), eastern[...].astype(jnp.float32), own)
    project(tokens.reshape(rows * split, features), gain, held_weight, copy, slots, outs)


def gather(head, kept, mixed, held, keys):
    span = held.shape[1]
    start = 0
    for block in kept:
        held[start : start + block.shape[0]] = block[:, head * span : (head + 1) * span]
        start += block.shape[0]
    for block in mixed:
        held[start : start + block.shape[0]] = block[...]
        start += block.shape[0]
    keys[...] = held[...].T


def attend(held, keys, attended, scores, weights):
    span = held.shape[1]
    factor = HD ** (-0.5) * 1.4426950408889634
    step = scores[0].shape[0]
    chunk = 16
    steps = held.shape[0] // step

    def score(index, out):
        first = index * step
        queries = pltpu.roll(held[first : first + step].astype(jnp.float32), HD, axis=1)
        lane = lax.broadcasted_iota(jnp.int32, queries.shape, 1)
        queries = jnp.where((lane >= HD) & (lane < 2 * HD), queries, 0.0).astype(jnp.bfloat16)
        out[...] = jnp.dot(queries, keys[...], preferred_element_type=jnp.float32)

    score(0, scores[0])
    for index in range(steps):
        if index + 1 < steps:
            score(index + 1, scores[(index + 1) % 2])
        now, out = scores[index % 2], weights[index % 2]
        for first in range(0, step, chunk):
            part = now[first : first + chunk]
            top = jnp.max(part, axis=-1, keepdims=True)
            out[first : first + chunk] = jnp.exp2((part - top) * factor).astype(jnp.bfloat16)
        mixed_values = jnp.dot(out[...], held[...], preferred_element_type=jnp.float32)
        scaled = mixed_values / mixed_values[:, 3 * HD : 3 * HD + 1]
        values = pltpu.roll(scaled, span - 2 * HD, axis=1)[:, :LANES]
        attended[index * step : (index + 1) * step] = values


def packed_rows(count):
    part = round_up(-(-count * (HD - LANES // 2) // LANES), SUBLANES)
    return count // 2 + part, part


def pack(rows):
    count = rows.shape[0]
    half = LANES // 2
    rest = HD - half
    part = packed_rows(count)[1]
    lane = lax.broadcasted_iota(jnp.int32, (count // 2, LANES), 1)
    main = jnp.where(lane < half, rows[: count // 2], pltpu.roll(rows[count // 2 :], half, axis=1))
    lane = lax.broadcasted_iota(jnp.int32, (part, LANES), 1)
    rests = jnp.zeros((part, LANES), jnp.float32)
    for index in range(-(-count // part)):
        piece = rows[index * part : (index + 1) * part]
        if piece.shape[0] < part:
            empty = jnp.zeros((part - piece.shape[0], LANES), jnp.float32)
            piece = jnp.concatenate([piece, empty], axis=0)
        turn = (index * rest + half) % LANES
        piece = pltpu.roll(piece, turn, axis=1) if turn else piece
        rests = jnp.where(lane // rest == index, piece, rests)
    return jnp.concatenate([main, rests], axis=0)


def unpack(block, count):
    half = LANES // 2
    rest = HD - half
    part = packed_rows(count)[1]
    main, rests = block[: count // 2], block[count // 2 : count // 2 + part]
    main = jnp.concatenate([main, pltpu.roll(main, half, axis=1)], axis=0)
    pieces = []
    for index in range(-(-count // part)):
        turn = (half - index * rest) % LANES
        piece = pltpu.roll(rests, turn, axis=1) if turn else rests
        pieces.append(piece[: min(part, count - index * part)])
    lane = lax.broadcasted_iota(jnp.int32, main.shape, 1)
    return jnp.where(lane < half, main, jnp.concatenate(pieces, axis=0))


def packed_tokens(count):
    half = LANES // 2
    total, part = packed_rows(count)
    row = lax.broadcasted_iota(jnp.int32, (total, LANES), 0)
    lane = lax.broadcasted_iota(jnp.int32, (total, LANES), 1)
    main = row + jnp.where(lane < half, 0, count // 2)
    rests = row - count // 2 + lane // (HD - half) * part
    return jnp.where(row < count // 2, main, rests)


def attention_kernel(head, groups, *refs):
    kept, mixed = refs[:groups], refs[groups : 2 * groups]
    outs, (held, keys, attended, *rest) = refs[2 * groups : -7], refs[-7:]
    gather(head, kept, mixed, held, keys)
    attend(held, keys, attended, rest[:2], rest[2:])
    kept_count, mixed_count = kept[0].shape[0], mixed[0].shape[0]
    for group in range(groups):
        first = groups * kept_count + group * mixed_count
        left = pack(attended[first : first + mixed_count])
        right = pack(attended[group * kept_count : (group + 1) * kept_count])
        outs[group][...] = jnp.concatenate([left, right], axis=0).astype(jnp.bfloat16)
        if len(outs) > groups:
            outs[groups + group][...] = left.astype(jnp.bfloat16)


def mixed_rows_kernel(*refs):
    *blocks, out = refs
    rows = out.shape[0] // len(blocks)
    pieces = [block[...].astype(jnp.float32)[:rows] for block in blocks]
    out[...] = jnp.concatenate(pieces, axis=0).astype(jnp.bfloat16)


def projected_rows(split, lon_shift, shape, blocks, western, weight):
    rows, columns, _ = shape
    kept_count, mixed_count = rows * (columns - split), rows * split
    total = packed_rows(mixed_count)[0]
    taken = lax.rem(packed_tokens(mixed_count), split) < column_offset(lon_shift)
    attended = []
    for block, west in zip(blocks, western):
        block = block[...].astype(jnp.float32)
        left = unpack(jnp.where(taken, west, block[:total]), mixed_count)
        right = unpack(block[total:], kept_count)
        attended.append(jnp.concatenate([right, left], axis=0))
    attended = jnp.concatenate(attended, axis=1).astype(jnp.bfloat16)
    projected = jnp.dot(attended, weight[...], preferred_element_type=jnp.float32)
    return by_column(projected, rows, columns, split)


def by_column(projected, rows, columns, split):
    kept_count = rows * (columns - split)
    right = projected[:kept_count].reshape(rows, columns - split, -1)
    left = projected[kept_count:].reshape(rows, split, -1)
    return jnp.concatenate([left, right], axis=1)


def first_output_kernel(split, groups, lon_shift, field, weight, *refs):
    *blocks, western, out, second, first = refs
    features = field.shape[2]
    for slot in range(groups):
        group = lax.rem(lax.axis_index("tok") + slot, groups)
        for head, ordered in enumerate((first, second)):
            at = pl.multiple_of((group * HEADS // groups + head) * HD, 16)
            ordered[slot * LANES : slot * LANES + HD] = weight[pl.ds(at, HD)]
            ordered[slot * LANES + HD : (slot + 1) * LANES] = jnp.zeros(
                (LANES - HD, features), jnp.bfloat16
            )
    west = western[...].astype(jnp.float32)
    total = west.shape[0] // groups
    west = [west[slot * total : (slot + 1) * total] for slot in range(groups)]
    projected = projected_rows(split, lon_shift, field.shape, blocks, west, first)
    out[...] = field[...].astype(jnp.float32) + projected


def second_output_kernel(split, groups, lon_shift, partial, weight, *refs):
    *blocks, out = refs
    west = [block[...].astype(jnp.float32) for block in blocks[groups:]]
    projected = projected_rows(split, lon_shift, partial.shape, blocks[:groups], west, weight)
    out[...] = (partial[...] + projected).astype(jnp.bfloat16)


def whole(count):
    return [pl.BlockSpec(memory_space=pltpu.VMEM)] * count


def shards(field_tokens, lon_shift, norm_gain, qkv_weight, out_weight):
    _, rows, columns, features = field_tokens.shape
    groups = lax.axis_size("tok")
    local = HEADS // groups
    width = local * HD
    span = round_up(3 * HD + 1, LANES)
    split = round_up(columns // 2, SUBLANES)
    field = field_tokens[0]
    smem = pl.BlockSpec(memory_space=pltpu.SMEM)
    kept_count, mixed_count = rows * (columns - split), rows * split

    def limit(size):
        return pltpu.CompilerParams(vmem_limit_bytes=size * MIB)

    def projection(kernel, count, parts, specs, held, params, *operands):
        block = jax.ShapeDtypeStruct((count, local * span // parts), jnp.bfloat16)
        return pl.pallas_call(
            functools.partial(kernel, split),
            out_shape=[block] * (parts * groups),
            in_specs=specs,
            out_specs=whole(parts * groups),
            scratch_shapes=[
                pltpu.VMEM((groups, count, local * span), jnp.bfloat16),
                *held,
            ],
            compiler_params=params,
            cost_estimate=pl.CostEstimate(
                flops=2 * count * features * 3 * HEADS * HD,
                bytes_accessed=2 * features * (3 * HEADS * HD + 2 * count),
                transcendentals=0,
            ),
        )(*operands)

    def spread(blocks, sign):
        return [blocks[0]] + [
            shifted(blocks[distance], "tok", sign * distance) for distance in range(1, groups)
        ]

    eastern = shifted(field[:, :split], "win", -LAT_WINDOWS)
    hbm = pl.BlockSpec(memory_space=pltpu.HBM)
    operands = (field, norm_gain, qkv_weight)
    held = [
        pltpu.VMEM(qkv_weight.shape, qkv_weight.dtype),
        pltpu.SemaphoreType.DMA((3,)),
        pltpu.VMEM(field.shape, field.dtype),
        pltpu.VMEM(norm_gain.shape, norm_gain.dtype),
    ]
    kept = spread(projection(kept_kernel, kept_count, 1, [hbm] * 3, held, limit(60), *operands), 1)
    specs = [*whole(2), hbm, smem, *whole(1)]
    operands += (lon_shift, eastern)
    mixed = projection(mixed_kernel, mixed_count, local, specs, held[:2], limit(52), *operands)
    ahead = [None] * (groups - 1)
    first_mixed = spread(after(mixed[:groups], [*ahead, kept[1]]), 1)

    second_mixed = spread(after(mixed[groups:], [None, *kept[2:], first_mixed[1]]), 1)

    total = groups * rows * columns
    step = total // 5
    mixed_packed = packed_rows(mixed_count)[0]
    all_packed = mixed_packed + packed_rows(kept_count)[0]

    def block(count):
        return jax.ShapeDtypeStruct((count, LANES), jnp.bfloat16)

    def attention(head, out_shape, blocks):
        return pl.pallas_call(
            functools.partial(attention_kernel, head, groups),
            out_shape=out_shape,
            in_specs=whole(len(blocks)),
            out_specs=whole(len(out_shape)),
            scratch_shapes=[
                pltpu.VMEM((total, span), jnp.bfloat16),
                pltpu.VMEM((span, total), jnp.bfloat16),
                pltpu.VMEM((total, LANES), jnp.float32),
                pltpu.VMEM((step, total), jnp.float32),
                pltpu.VMEM((step, total), jnp.float32),
                pltpu.VMEM((step, total), jnp.bfloat16),
                pltpu.VMEM((step, total), jnp.bfloat16),
            ],
            compiler_params=limit(32),
            cost_estimate=pl.CostEstimate(
                flops=4 * total * total * span,
                bytes_accessed=2 * total * (span + LANES),
                transcendentals=total * total,
            ),
        )(*blocks)

    first = attention(0, [block(all_packed)] * groups, [*kept, *first_mixed])
    first = spread(first, -1)
    second = attention(
        1,
        [block(all_packed)] * groups + [block(mixed_packed)] * groups,
        [*kept, *second_mixed],
    )
    windows = lax.axis_size("win")
    western = []
    for distance in range(groups):
        route = [
            (
                win * groups + tok,
                (win + LAT_WINDOWS) % windows * groups + (tok - distance) % groups,
            )
            for win in range(windows)
            for tok in range(groups)
        ]
        western.append(lax.ppermute(second[groups + distance], ("win", "tok"), route))
    returned = [lax.optimization_barrier((block, second[0]))[0] for block in first]
    second = spread(after(second[:groups], [None, *first[1:]]), -1)
    first_western = pl.pallas_call(
        mixed_rows_kernel,
        out_shape=block(groups * mixed_packed),
        in_specs=whole(groups),
        out_specs=pl.BlockSpec(memory_space=pltpu.VMEM),
        compiler_params=limit(16),
        cost_estimate=pl.CostEstimate(
            flops=0, bytes_accessed=4 * groups * all_packed * LANES, transcendentals=0
        ),
    )(*returned)
    first_western = shifted(first_western, "win", LAT_WINDOWS)

    cost = pl.CostEstimate(
        flops=2 * rows * columns * groups * LANES * features,
        bytes_accessed=features * (HEADS * HD + 6 * rows * columns),
        transcendentals=0,
    )
    ordered = (groups * LANES, features)
    partial, weight = pl.pallas_call(
        functools.partial(first_output_kernel, split, groups),
        out_shape=[
            jax.ShapeDtypeStruct(field.shape, jnp.float32),
            jax.ShapeDtypeStruct(ordered, jnp.bfloat16),
        ],
        in_specs=[smem] + whole(3 + groups),
        out_specs=whole(2),
        scratch_shapes=[pltpu.VMEM(ordered, jnp.bfloat16)],
        compiler_params=limit(24),
        cost_estimate=cost,
    )(lon_shift, field, out_weight, *first, first_western)
    result = pl.pallas_call(
        functools.partial(second_output_kernel, split, groups),
        out_shape=jax.ShapeDtypeStruct(field.shape, jnp.bfloat16),
        in_specs=[smem] + whole(2 + 2 * groups),
        out_specs=pl.BlockSpec(memory_space=pltpu.VMEM),
        compiler_params=limit(24),
        cost_estimate=cost,
    )(lon_shift, partial, weight, *second, *western)
    return result[None]


def solution(mesh):
    placed = (P("win", "tok", None, None), P(), P(), P(), P())
    return jax.shard_map(
        shards, mesh=mesh, in_specs=placed, out_specs=P("win", "tok", None, None), check_vma=False
    )
```

time: 73.6 us -> 77.4 us (1.052)
  waiting for transfers between devices: 9.24 us -> 14.2 us
  local copies, waits for them, and re-layouts: 4.61 us -> 1.14 us
  starting transfers between devices: 37.4 us -> 39.5 us
    ppermute x0 -> x4, starting transfers between devices: none -> 6.24 us  [shards(): lax.ppermute(second[groups + distance], ('win', 'tok'), route)]
    ppermute x18 -> x17, starting transfers between devices: 37.4 us -> 33.2 us  [shifted(): lax.ppermute(block, axis, [(i, (i + distance) % count) for i in range(cou...]
    ppermute x0 -> x4, waiting for transfers between devices: none -> 3.86 us  [shards(): lax.ppermute(second[groups + distance], ('win', 'tok'), route)]
    unnamed x12 -> x10, local copies, waits for them, and re-layouts: 3.5 us -> 0.03 us
    pallas_call x2, Pallas kernels: 8.16 us -> 10.1 us  [projection(): pl.pallas_call(functools.partial(kernel, split), out_shape=[block] * (par...]
    ppermute x18 -> x17, waiting for transfers between devices: 9.24 us -> 10.3 us  [shifted(): lax.ppermute(block, axis, [(i, (i + distance) % count) for i in range(cou...]
    pallas_call x3 -> x2, Pallas kernels: 3.31 us -> 2.32 us  [the longest x1 2.29 us: shards(): pl.pallas_call(functools.partial(second_output_kernel, split, groups), ou...]
    pallas_call x1, Pallas kernels: 2.16 us -> 1.38 us  [shards(): pl.pallas_call(functools.partial(first_output_kernel, split, groups), out...]
  transfers between devices with their start and end apart: 18 -> 21, of which waited for: 6 -> 7; matrix products, arithmetic and copies ran while one was open for 0% -> 0% of each run, Pallas kernels for 28% -> 26%
where the time goes in v7:
time: 77.4 us; the launch traced here: 77.2 us
  starting transfers between devices  39.5 us (51%)
  Pallas kernels  22.3 us (29%)
  waiting for transfers between devices  14.2 us (18%)
  local copies, waits for them, and re-layouts  1.14 us (1%)
    ppermute x17, starting transfers between devices, shifted(): lax.ppermute(block, axis, [(i, (i + distance) % count) for i in range(cou...  33.2 us
    ppermute x17, waiting for transfers between devices, shifted(): lax.ppermute(block, axis, [(i, (i + distance) % count) for i in range(cou...  10.3 us
    pallas_call x2, Pallas kernels, projection(): pl.pallas_call(functools.partial(kernel, split), out_shape=[block] * (par...  10.1 us
    pallas_call x2, Pallas kernels, attention(): pl.pallas_call(functools.partial(attention_kernel, head, groups), out_sha...  8.48 us
    ppermute x4, starting transfers between devices, shards(): lax.ppermute(second[groups + distance], ('win', 'tok'), route)  6.24 us
    ppermute x4, waiting for transfers between devices, shards(): lax.ppermute(second[groups + distance], ('win', 'tok'), route)  3.86 us
    pallas_call x1, Pallas kernels, shards(): pl.pallas_call(functools.partial(second_output_kernel, split, groups), ou...  2.29 us
  transfers between devices with their start and end apart: 21, of which 7 were waited for; matrix products, arithmetic and copies ran while one was open for 0% of the time, Pallas kernels for 26%

profile of v7, /device:TPU:0, one launch (start us, length us, event | category | flops | bytes accessed | tf_op | source)
XLA Modules:
  0.0 77.2 jit_solution(16067278237004485407)
XLA Ops:
  0.0 1.1 %slice.4 = bf16[10,24,1280]{2,1,0:T(8,128)(2,1)S(1)} slice(bf16[10,40,1280]{2,1,0:T(8,128)(2,1)} %bitcast.2), slice={[0:10], [0:24], [0:1280]} | slice | bytes 1228800 | tf_op jit(solution)/shard_map/slice | solution.py:293
  1.1 0.0 copy-start.2
  1.1 0.0 copy-start.3
  1.1 3.0 %collective-permute-start.3 = (bf16[10,24,1280]{2,1,0:T(8,128)(2,1)S(1)}, bf16[10,24,1280]{2,1,0:T(8,128)(2,1)S(1)}, u32[]{:S(2)}, u32[]{:S(2)}) collective-permute-start(bf16[10,24,1280]{2,1,0:T(8,128)(2,1)S(1)} %slice.4), channel_id=1, source_target_pairs={{0,16},{4,20},{8,24},{12,28},{16,0},{20,4},{24,8},{28,12},{1,17},{... | collective-permute-start | bytes 1843208 | tf_op jit(solution)/shard_map/ppermute | solution.py:24
  4.2 4.8 %shard_map.55 = (bf16[160,512]{1,0:T(8,128)(2,1)}, bf16[160,512]{1,0:T(8,128)(2,1)}, bf16[160,512]{1,0:T(8,128)(2,1)}, bf16[160,512]{1,0:T(8,128)(2,1)}) custom-call(bf16[10,40,1280]{2,1,0:T(8,128)(2,1)} %bitcast.3, f32[1280]{0:T(1024)} %gain.3, bf16[1280,1920]{1,0:T(8,128)(2,1)} %weight.4), custom_call_target="tpu_custom_call" | custom-call | flops 786432000 | bytes 5734400 | tf_op jit(solution)/shard_map/pallas_call | solution.py:271
  9.0 1.6 %collective-permute-start = (bf16[160,512]{1,0:T(8,128)(2,1)}, bf16[160,512]{1,0:T(8,128)(2,1)S(1)}, u32[]{:S(2)}, u32[]{:S(2)}) collective-permute-start(bf16[160,512]{1,0:T(8,128)(2,1)} %get-tuple-element.43), channel_id=1, source_target_pairs={{0,1},{1,2},{2,3},{3,0},{4,5},{5,6},{6,7},{7,4},{8,9},{9,10},{10,1... | collective-permute-start | bytes 491528 | tf_op jit(solution)/shard_map/ppermute | solution.py:24
  10.6 2.6 %collective-permute-start.1 = (bf16[160,512]{1,0:T(8,128)(2,1)}, bf16[160,512]{1,0:T(8,128)(2,1)S(1)}, u32[]{:S(2)}, u32[]{:S(2)}) collective-permute-start(bf16[160,512]{1,0:T(8,128)(2,1)} %get-tuple-element.44), channel_id=1, source_target_pairs={{0,2},{1,3},{2,0},{3,1},{4,6},{5,7},{6,4},{7,5},{8,10},{9,11},{10,... | collective-permute-start | bytes 491528 | tf_op jit(solution)/shard_map/ppermute | solution.py:24
  13.2 0.0 copy-start.4
  13.2 1.3 %collective-permute-start.2 = (bf16[160,512]{1,0:T(8,128)(2,1)}, bf16[160,512]{1,0:T(8,128)(2,1)S(1)}, u32[]{:S(2)}, u32[]{:S(2)}) collective-permute-start(bf16[160,512]{1,0:T(8,128)(2,1)} %get-tuple-element.45), channel_id=1, source_target_pairs={{0,3},{1,0},{2,1},{3,2},{4,7},{5,4},{6,5},{7,6},{8,11},{9,8},{10,9... | collective-permute-start | bytes 491528 | tf_op jit(solution)/shard_map/ppermute | solution.py:24
  14.5 3.5 %collective-permute-done.3.eastern = bf16[10,24,1280]{2,1,0:T(8,128)(2,1)S(1)} collective-permute-done((bf16[10,24,1280]{2,1,0:T(8,128)(2,1)S(1)}, bf16[10,24,1280]{2,1,0:T(8,128)(2,1)S(1)}, u32[]{:S(2)}, u32[]{:S(2)}) %collective-permute-start.3) | collective-permute-done | bytes 614432 | tf_op jit(solution)/shard_map/ppermute | solution.py:24
  18.0 0.0 copy-done.2
  18.0 0.0 copy-done.3
  18.0 5.3 %shard_map.56 = (bf16[240,256]{1,0:T(8,128)(2,1)S(1)}, bf16[240,256]{1,0:T(8,128)(2,1)S(1)}, bf16[240,256]{1,0:T(8,128)(2,1)S(1)}, bf16[240,256]{1,0:T(8,128)(2,...) custom-call(bf16[10,40,1280]{2,1,0:T(8,128)(2,1)} %bitcast.4, ...), custom_call_target="tpu_custom_call" | custom-call | flops 1179648000 | bytes 6144000 | tf_op jit(solution)/shard_map/pallas_call | solution.py:271
  23.4 1.9 %collective-permute-start.4 = (bf16[240,256]{1,0:T(8,128)(2,1)S(1)}, bf16[240,256]{1,0:T(8,128)(2,1)S(1)}, u32[]{:S(2)}, u32[]{:S(2)}) collective-permute-start(bf16[240,256]{1,0:T(8,128)(2,1)S(1)} %get-tuple-element.47), channel_id=1, source_target_pairs={{0,1},{1,2},{2,3},{3,0},{4,5},{5,6},{6,7},{7,4},{8,9},{9,10},{10,1... | collective-permute-start | bytes 368648 | tf_op jit(solution)/shard_map/ppermute | solution.py:24
  25.2 2.6 %collective-permute-start.5 = (bf16[240,256]{1,0:T(8,128)(2,1)S(1)}, bf16[240,256]{1,0:T(8,128)(2,1)S(1)}, u32[]{:S(2)}, u32[]{:S(2)}) collective-permute-start(bf16[240,256]{1,0:T(8,128)(2,1)S(1)} %get-tuple-element.48), channel_id=1, source_target_pairs={{0,2},{1,3},{2,0},{3,1},{4,6},{5,7},{6,4},{7,5},{8,10},{9,11},{10,... | collective-permute-start | bytes 368648 | tf_op jit(solution)/shard_map/ppermute | solution.py:24
  27.8 0.0 collective-permute-done.refs_1_
  27.8 1.3 %collective-permute-start.6 = (bf16[240,256]{1,0:T(8,128)(2,1)S(1)}, bf16[240,256]{1,0:T(8,128)(2,1)S(1)}, u32[]{:S(2)}, u32[]{:S(2)}) collective-permute-start(bf16[240,256]{1,0:T(8,128)(2,1)S(1)} %get-tuple-element.50), channel_id=1, source_target_pairs={{0,3},{1,0},{2,1},{3,2},{4,7},{5,4},{6,5},{7,6},{8,11},{9,8},{10,9... | collective-permute-start | bytes 368648 | tf_op jit(solution)/shard_map/ppermute | solution.py:24
  29.2 0.0 collective-permute-done.1.refs_2_
  29.2 0.7 collective-permute-start.10
  29.9 0.0 collective-permute-done.2.refs_3_
  29.9 0.3 collective-permute-start.11
  30.2 1.4 %collective-permute-done.4.refs_5_ = bf16[240,256]{1,0:T(8,128)(2,1)S(1)} collective-permute-done((bf16[240,256]{1,0:T(8,128)(2,1)S(1)}, bf16[240,256]{1,0:T(8,128)(2,1)S(1)}, u32[]{:S(2)}, u32[]{:S(2)}) %collective-permute-start.4) | collective-permute-done | bytes 122912 | tf_op jit(solution)/shard_map/ppermute | solution.py:24
  31.6 3.3 %collective-permute-start.12 = (bf16[240,256]{1,0:T(8,128)(2,1)S(1)}, bf16[240,256]{1,0:T(8,128)(2,1)S(1)}, u32[]{:S(2)}, u32[]{:S(2)}) collective-permute-start(bf16[240,256]{1,0:T(8,128)(2,1)S(1)} %get-tuple-element.61), channel_id=1, source_target_pairs={{0,3},{1,0},{2,1},{3,2},{4,7},{5,4},{6,5},{7,6},{8,11},{9,8},{10,9... | collective-permute-start | bytes 368648 | tf_op jit(solution)/shard_map/ppermute | solution.py:24
  34.8 4.1 %collective-permute-done.5.refs_6_ = bf16[240,256]{1,0:T(8,128)(2,1)S(1)} collective-permute-done((bf16[240,256]{1,0:T(8,128)(2,1)S(1)}, bf16[240,256]{1,0:T(8,128)(2,1)S(1)}, u32[]{:S(2)}, u32[]{:S(2)}) %collective-permute-start.5) | collective-permute-done | bytes 122912 | tf_op jit(solution)/shard_map/ppermute | solution.py:24
  38.9 0.2 collective-permute-done.6.refs_7_
  39.1 0.0 copy-done.4
  39.1 4.2 %shard_map.57 = (bf16[256,128]{1,0:T(8,128)(2,1)S(1)}, bf16[256,128]{1,0:T(8,128)(2,1)S(1)}, bf16[256,128]{1,0:T(8,128)(2,1)S(1)}, bf16[256,128]{1,0:T(8,128)(2,1)S(1)}) custom-call(bf16[160,512]{1,0:T(8,128)(2,1)S(1)} %copy-done.4, bf16[160,512]{1,0:T(8,128)(2,1)S(1)} %collective-permute-done.refs_1_, bf16[160,512]{1,0:T(8,128)(2,1)S(1)} %collective-permute-done.1.refs_2_, ...), custom_call_target="tpu_custom_call" | custom-call | flops 2621440000 | bytes 1228800 | tf_op jit(solution)/shard_map/pallas_call | solution.py:320
  43.3 7.5 %collective-permute-start.7 = (bf16[256,128]{1,0:T(8,128)(2,1)S(1)}, bf16[256,128]{1,0:T(8,128)(2,1)S(1)}, u32[]{:S(2)}, u32[]{:S(2)}) collective-permute-start(bf16[256,128]{1,0:T(8,128)(2,1)S(1)} %get-tuple-element.52), channel_id=1, source_target_pairs={{0,3},{1,0},{2,1},{3,2},{4,7},{5,4},{6,5},{7,6},{8,11},{9,8},{10,9... | collective-permute-start | bytes 196616 | tf_op jit(solution)/shard_map/ppermute | solution.py:24
  50.9 0.0 collective-permute-start.8
  50.9 0.0 collective-permute-done.10.refs_5_
  50.9 0.6 collective-permute-start.9
  51.5 0.0 collective-permute-done.11.refs_6_
  51.5 0.0 collective-permute-done.12.refs_7_
  51.5 0.0 copy-start
  51.5 0.0 copy-start.1
  51.6 4.2 %shard_map.58 = (bf16[256,128]{1,0:T(8,128)(2,1)S(1)}, bf16[256,128]{1,0:T(8,128)(2,1)S(1)}, bf16[256,128]{1,0:T(8,128)(2,1)S(1)}, bf16[256,128]{1,0:T(8,128)(2,...) custom-call(bf16[160,512]{1,0:T(8,128)(2,1)S(1)} %copy-done.4, ...), custom_call_target="tpu_custom_call" | custom-call | flops 2621440000 | bytes 1228800 | tf_op jit(solution)/shard_map/pallas_call | solution.py:320
  55.8 1.2 %collective-permute-done.9.refs_3_ = bf16[256,128]{1,0:T(8,128)(2,1)S(1)} collective-permute-done((bf16[256,128]{1,0:T(8,128)(2,1)S(1)}, bf16[256,128]{1,0:T(8,128)(2,1)S(1)}, u32[]{:S(2)}, u32[]{:S(2)}) %collective-permute-start.9) | collective-permute-done | bytes 65568 | tf_op jit(solution)/shard_map/ppermute | solution.py:24
  57.0 0.0 collective-permute-done.8.refs_2_
  57.0 0.0 collective-permute-done.7.refs_1_
  57.0 2.3 %collective-permute-start.13 = (bf16[608,128]{1,0:T(8,128)(2,1)S(1)}, bf16[608,128]{1,0:T(8,128)(2,1)S(1)}, u32[]{:S(2)}, u32[]{:S(2)}) collective-permute-start(bf16[608,128]{1,0:T(8,128)(2,1)S(1)} %shard_map.59), channel_id=1, source_target_pairs={{0,16},{4,20},{8,24},{12,28},{16,0},{20,4},{24,8},{28,12},{1,17},{... | collective-permute-start | bytes 466952 | tf_op jit(solution)/shard_map/ppermute | solution.py:24
  59.3 0.1 collective-permute-start.17
  59.4 3.4 %collective-permute-start.18 = (bf16[152,128]{1,0:T(8,128)(2,1)S(1)}, bf16[152,128]{1,0:T(8,128)(2,1)S(1)}, u32[]{:S(2)}, u32[]{:S(2)}) collective-permute-start(bf16[152,128]{1,0:T(8,128)(2,1)S(1)} %get-tuple-element.76), channel_id=1, source_target_pairs={{0,19},{1,16},{2,17},{3,18},{4,23},{5,20},{6,21},{7,22},{8,27},{9,... | collective-permute-start | bytes 116744 | tf_op jit(solution)/shard_map/ppermute | solution.py:360
  62.8 0.0 collective-permute-start.16
  62.8 1.1 %collective-permute-start.15 = (bf16[256,128]{1,0:T(8,128)(2,1)S(1)}, bf16[256,128]{1,0:T(8,128)(2,1)S(1)}, u32[]{:S(2)}, u32[]{:S(2)}) collective-permute-start(bf16[256,128]{1,0:T(8,128)(2,1)S(1)} %get-tuple-element.72), channel_id=1, source_target_pairs={{0,2},{1,3},{2,0},{3,1},{4,6},{5,7},{6,4},{7,5},{8,10},{9,11},{10,... | collective-permute-start | bytes 196616 | tf_op jit(solution)/shard_map/ppermute | solution.py:24
  63.9 0.0 collective-permute-done.17.refs_4_
  64.0 2.9 %collective-permute-start.14 = (bf16[256,128]{1,0:T(8,128)(2,1)S(1)}, bf16[256,128]{1,0:T(8,128)(2,1)S(1)}, u32[]{:S(2)}, u32[]{:S(2)}) collective-permute-start(bf16[256,128]{1,0:T(8,128)(2,1)S(1)} %get-tuple-element.70), channel_id=1, source_target_pairs={{0,3},{1,0},{2,1},{3,2},{4,7},{5,4},{6,5},{7,6},{8,11},{9,8},{10,9... | collective-permute-start | bytes 196616 | tf_op jit(solution)/shard_map/ppermute | solution.py:24
  66.9 0.0 collective-permute-done.18.refs_5_
  66.9 1.3 %collective-permute-start.19 = (bf16[152,128]{1,0:T(8,128)(2,1)S(1)}, bf16[152,128]{1,0:T(8,128)(2,1)S(1)}, u32[]{:S(2)}, u32[]{:S(2)}) collective-permute-start(bf16[152,128]{1,0:T(8,128)(2,1)S(1)} %get-tuple-element.77), channel_id=1, source_target_pairs={{0,18},{1,19},{2,16},{3,17},{4,22},{5,23},{6,20},{7,21},{8,26},{9,... | collective-permute-start | bytes 116744 | tf_op jit(solution)/shard_map/ppermute | solution.py:360
  68.2 0.0 collective-permute-done.13.refs_4_
  68.2 1.4 %collective-permute-start.20 = (bf16[152,128]{1,0:T(8,128)(2,1)S(1)}, bf16[152,128]{1,0:T(8,128)(2,1)S(1)}, u32[]{:S(2)}, u32[]{:S(2)}) collective-permute-start(bf16[152,128]{1,0:T(8,128)(2,1)S(1)} %get-tuple-element.78), channel_id=1, source_target_pairs={{0,17},{1,18},{2,19},{3,16},{4,21},{5,22},{6,23},{7,20},{8,25},{9,... | collective-permute-start | bytes 116744 | tf_op jit(solution)/shard_map/ppermute | solution.py:360
  69.6 0.0 copy-done
  69.6 0.0 copy-done.1
  69.6 1.4 %shard_map.60 = (f32[10,40,1280]{2,1,0:T(8,128)S(1)}, bf16[512,1280]{1,0:T(8,128)(2,1)S(1)}) custom-call(s32[4]{0:T(128)S(1)} %copy-done.3, bf16[10,40,1280]{2,1,0:T(8,128)(2,1)S(1)} %bitcast.5, bf16[640,1280]{1,0:T(8,128)(2,1)S(1)} %copy-done.1, bf16[256,128]{1,0:T(8,128)(2,1)S(1)} %get-tuple-element.63.refs_0_, ...), custom_call_target="tpu_custom_call" | custom-call | flops 524288000 | bytes 3891200 | tf_op jit(solution)/shard_map/pallas_call | solution.py:381
  71.0 1.9 %collective-permute-done.19.refs_6_ = bf16[152,128]{1,0:T(8,128)(2,1)S(1)} collective-permute-done((bf16[152,128]{1,0:T(8,128)(2,1)S(1)}, bf16[152,128]{1,0:T(8,128)(2,1)S(1)}, u32[]{:S(2)}, u32[]{:S(2)}) %collective-permute-start.19) | collective-permute-done | bytes 38944 | tf_op jit(solution)/shard_map/ppermute | solution.py:360
  72.9 2.0 %collective-permute-done.20.refs_7_ = bf16[152,128]{1,0:T(8,128)(2,1)S(1)} collective-permute-done((bf16[152,128]{1,0:T(8,128)(2,1)S(1)}, bf16[152,128]{1,0:T(8,128)(2,1)S(1)}, u32[]{:S(2)}, u32[]{:S(2)}) %collective-permute-start.20) | collective-permute-done | bytes 38944 | tf_op jit(solution)/shard_map/ppermute | solution.py:360
  74.9 0.0 collective-permute-done.16.refs_3_
  74.9 0.0 collective-permute-done.15.refs_2_
  74.9 0.0 collective-permute-done.14.refs_1_
  74.9 2.3 %shard_map.61 = bf16[10,40,1280]{2,1,0:T(8,128)(2,1)} custom-call(s32[4]{0:T(128)S(1)} %copy-done.3, f32[10,40,1280]{2,1,0:T(8,128)S(1)} %get-tuple-element.67.partial, bf16[512,1280]{1,0:T(8,128)(2,1)S(1)} %get-tuple-element.68.weight, bf16[256,128]{1,0:T(8,128)(2,1)S(1)} %get-tuple-element.62.refs_0_, ...), custom_call_target="tpu_custom_call" | custom-call | flops 524288000 | bytes 3891200 | tf_op jit(solution)/shard_map/pallas_call | solution.py:393
  (1 shorter events, 0.0 us)
Async XLA Ops:
  1.1 16.9 %copy-start.2 = (f32[1280]{0:T(1024)S(1)}, f32[1280]{0:T(1024)}, u32[]{:S(2)}) copy-start(f32[1280]{0:T(1024)} %gain.3) | copy-start | bytes 15364
  1.1 16.9 %copy-start.3 = (s32[4]{0:T(128)S(1)}, s32[4]{0:T(128)}, u32[]{:S(2)}) copy-start(s32[4]{0:T(128)} %lon_shift.5) | copy-start | bytes 52
  1.1 16.9 %collective-permute-start.3 = (bf16[10,24,1280]{2,1,0:T(8,128)(2,1)S(1)}, bf16[10,24,1280]{2,1,0:T(8,128)(2,1)S(1)}, u32[]{:S(2)}, u32[]{:S(2)}) collective-permute-start(bf16[10,24,1280]{2,1,0:T(8,128)(2,1)S(1)} %slice.4), channel_id=1, source_target_pairs={{0,16},{4,20},{8,24},{12,28},{16,0},{20,4},{24,8},{28,12},{1,17},{... | collective-permute-start | bytes 1843208 | tf_op jit(solution)/shard_map/ppermute | solution.py:24
  9.0 18.9 %collective-permute-start = (bf16[160,512]{1,0:T(8,128)(2,1)}, bf16[160,512]{1,0:T(8,128)(2,1)S(1)}, u32[]{:S(2)}, u32[]{:S(2)}) collective-permute-start(bf16[160,512]{1,0:T(8,128)(2,1)} %get-tuple-element.43), channel_id=1, source_target_pairs={{0,1},{1,2},{2,3},{3,0},{4,5},{5,6},{6,7},{7,4},{8,9},{9,10},{10,1... | collective-permute-start | bytes 491528 | tf_op jit(solution)/shard_map/ppermute | solution.py:24
  10.6 18.6 %collective-permute-start.1 = (bf16[160,512]{1,0:T(8,128)(2,1)}, bf16[160,512]{1,0:T(8,128)(2,1)S(1)}, u32[]{:S(2)}, u32[]{:S(2)}) collective-permute-start(bf16[160,512]{1,0:T(8,128)(2,1)} %get-tuple-element.44), channel_id=1, source_target_pairs={{0,2},{1,3},{2,0},{3,1},{4,6},{5,7},{6,4},{7,5},{8,10},{9,11},{10,... | collective-permute-start | bytes 491528 | tf_op jit(solution)/shard_map/ppermute | solution.py:24
  13.2 25.9 %copy-start.4 = (bf16[160,512]{1,0:T(8,128)(2,1)S(1)}, bf16[160,512]{1,0:T(8,128)(2,1)}, u32[]{:S(2)}) copy-start(bf16[160,512]{1,0:T(8,128)(2,1)} %get-tuple-element.42.refs_0_) | copy-start | bytes 491524
  13.2 16.7 %collective-permute-start.2 = (bf16[160,512]{1,0:T(8,128)(2,1)}, bf16[160,512]{1,0:T(8,128)(2,1)S(1)}, u32[]{:S(2)}, u32[]{:S(2)}) collective-permute-start(bf16[160,512]{1,0:T(8,128)(2,1)} %get-tuple-element.45), channel_id=1, source_target_pairs={{0,3},{1,0},{2,1},{3,2},{4,7},{5,4},{6,5},{7,6},{8,11},{9,8},{10,9... | collective-permute-start | bytes 491528 | tf_op jit(solution)/shard_map/ppermute | solution.py:24
  23.4 8.2 %collective-permute-start.4 = (bf16[240,256]{1,0:T(8,128)(2,1)S(1)}, bf16[240,256]{1,0:T(8,128)(2,1)S(1)}, u32[]{:S(2)}, u32[]{:S(2)}) collective-permute-start(bf16[240,256]{1,0:T(8,128)(2,1)S(1)} %get-tuple-element.47), channel_id=1, source_target_pairs={{0,1},{1,2},{2,3},{3,0},{4,5},{5,6},{6,7},{7,4},{8,9},{9,10},{10,1... | collective-permute-start | bytes 368648 | tf_op jit(solution)/shard_map/ppermute | solution.py:24
  25.2 13.7 %collective-permute-start.5 = (bf16[240,256]{1,0:T(8,128)(2,1)S(1)}, bf16[240,256]{1,0:T(8,128)(2,1)S(1)}, u32[]{:S(2)}, u32[]{:S(2)}) collective-permute-start(bf16[240,256]{1,0:T(8,128)(2,1)S(1)} %get-tuple-element.48), channel_id=1, source_target_pairs={{0,2},{1,3},{2,0},{3,1},{4,6},{5,7},{6,4},{7,5},{8,10},{9,11},{10,... | collective-permute-start | bytes 368648 | tf_op jit(solution)/shard_map/ppermute | solution.py:24
  27.8 11.3 %collective-permute-start.6 = (bf16[240,256]{1,0:T(8,128)(2,1)S(1)}, bf16[240,256]{1,0:T(8,128)(2,1)S(1)}, u32[]{:S(2)}, u32[]{:S(2)}) collective-permute-start(bf16[240,256]{1,0:T(8,128)(2,1)S(1)} %get-tuple-element.50), channel_id=1, source_target_pairs={{0,3},{1,0},{2,1},{3,2},{4,7},{5,4},{6,5},{7,6},{8,11},{9,8},{10,9... | collective-permute-start | bytes 368648 | tf_op jit(solution)/shard_map/ppermute | solution.py:24
  29.2 21.7 %collective-permute-start.10 = (bf16[240,256]{1,0:T(8,128)(2,1)S(1)}, bf16[240,256]{1,0:T(8,128)(2,1)S(1)}, u32[]{:S(2)}, u32[]{:S(2)}) collective-permute-start(bf16[240,256]{1,0:T(8,128)(2,1)S(1)} %get-tuple-element.57), channel_id=1, source_target_pairs={{0,1},{1,2},{2,3},{3,0},{4,5},{5,6},{6,7},{7,4},{8,9},{9,10},{10,1... | collective-permute-start | bytes 368648 | tf_op jit(solution)/shard_map/ppermute | solution.py:24
  29.9 21.7 %collective-permute-start.11 = (bf16[240,256]{1,0:T(8,128)(2,1)S(1)}, bf16[240,256]{1,0:T(8,128)(2,1)S(1)}, u32[]{:S(2)}, u32[]{:S(2)}) collective-permute-start(bf16[240,256]{1,0:T(8,128)(2,1)S(1)} %get-tuple-element.59), channel_id=1, source_target_pairs={{0,2},{1,3},{2,0},{3,1},{4,6},{5,7},{6,4},{7,5},{8,10},{9,11},{10,... | collective-permute-start | bytes 368648 | tf_op jit(solution)/shard_map/ppermute | solution.py:24
  31.6 20.0 %collective-permute-start.12 = (bf16[240,256]{1,0:T(8,128)(2,1)S(1)}, bf16[240,256]{1,0:T(8,128)(2,1)S(1)}, u32[]{:S(2)}, u32[]{:S(2)}) collective-permute-start(bf16[240,256]{1,0:T(8,128)(2,1)S(1)} %get-tuple-element.61), channel_id=1, source_target_pairs={{0,3},{1,0},{2,1},{3,2},{4,7},{5,4},{6,5},{7,6},{8,11},{9,8},{10,9... | collective-permute-start | bytes 368648 | tf_op jit(solution)/shard_map/ppermute | solution.py:24
  43.3 13.6 %collective-permute-start.7 = (bf16[256,128]{1,0:T(8,128)(2,1)S(1)}, bf16[256,128]{1,0:T(8,128)(2,1)S(1)}, u32[]{:S(2)}, u32[]{:S(2)}) collective-permute-start(bf16[256,128]{1,0:T(8,128)(2,1)S(1)} %get-tuple-element.52), channel_id=1, source_target_pairs={{0,3},{1,0},{2,1},{3,2},{4,7},{5,4},{6,5},{7,6},{8,11},{9,8},{10,9... | collective-permute-start | bytes 196616 | tf_op jit(solution)/shard_map/ppermute | solution.py:24
  50.9 6.1 %collective-permute-start.8 = (bf16[256,128]{1,0:T(8,128)(2,1)S(1)}, bf16[256,128]{1,0:T(8,128)(2,1)S(1)}, u32[]{:S(2)}, u32[]{:S(2)}) collective-permute-start(bf16[256,128]{1,0:T(8,128)(2,1)S(1)} %get-tuple-element.53), channel_id=1, source_target_pairs={{0,2},{1,3},{2,0},{3,1},{4,6},{5,7},{6,4},{7,5},{8,10},{9,11},{10,... | collective-permute-start | bytes 196616 | tf_op jit(solution)/shard_map/ppermute | solution.py:24
  50.9 6.1 %collective-permute-start.9 = (bf16[256,128]{1,0:T(8,128)(2,1)S(1)}, bf16[256,128]{1,0:T(8,128)(2,1)S(1)}, u32[]{:S(2)}, u32[]{:S(2)}) collective-permute-start(bf16[256,128]{1,0:T(8,128)(2,1)S(1)} %get-tuple-element.54), channel_id=1, source_target_pairs={{0,1},{1,2},{2,3},{3,0},{4,5},{5,6},{6,7},{7,4},{8,9},{9,10},{10,1... | collective-permute-start | bytes 196616 | tf_op jit(solution)/shard_map/ppermute | solution.py:24
  51.5 18.1 %copy-start = (bf16[1,10,40,1280]{3,2,1,0:T(8,128)(2,1)S(1)}, bf16[1,10,40,1280]{3,2,1,0:T(8,128)(2,1)}, u32[]{:S(2)}) copy-start(bf16[1,10,40,1280]{3,2,1,0:T(8,128)(2,1)} %param.5) | copy-start | bytes 3072004
  51.5 18.1 %copy-start.1 = (bf16[640,1280]{1,0:T(8,128)(2,1)S(1)}, bf16[640,1280]{1,0:T(8,128)(2,1)}, u32[]{:S(2)}) copy-start(bf16[640,1280]{1,0:T(8,128)(2,1)} %weight.5) | copy-start | bytes 4915204
  57.0 11.2 %collective-permute-start.13 = (bf16[608,128]{1,0:T(8,128)(2,1)S(1)}, bf16[608,128]{1,0:T(8,128)(2,1)S(1)}, u32[]{:S(2)}, u32[]{:S(2)}) collective-permute-start(bf16[608,128]{1,0:T(8,128)(2,1)S(1)} %shard_map.59), channel_id=1, source_target_pairs={{0,16},{4,20},{8,24},{12,28},{16,0},{20,4},{24,8},{28,12},{1,17},{... | collective-permute-start | bytes 466952 | tf_op jit(solution)/shard_map/ppermute | solution.py:24
  59.3 4.6 %collective-permute-start.17 = (bf16[152,128]{1,0:T(8,128)(2,1)S(1)}, bf16[152,128]{1,0:T(8,128)(2,1)S(1)}, u32[]{:S(2)}, u32[]{:S(2)}) collective-permute-start(bf16[152,128]{1,0:T(8,128)(2,1)S(1)} %get-tuple-element.75), channel_id=1, source_target_pairs={{0,16},{1,17},{2,18},{3,19},{4,20},{5,21},{6,22},{7,23},{8,24},{9,... | collective-permute-start | bytes 116744 | tf_op jit(solution)/shard_map/ppermute | solution.py:360
  59.4 7.5 %collective-permute-start.18 = (bf16[152,128]{1,0:T(8,128)(2,1)S(1)}, bf16[152,128]{1,0:T(8,128)(2,1)S(1)}, u32[]{:S(2)}, u32[]{:S(2)}) collective-permute-start(bf16[152,128]{1,0:T(8,128)(2,1)S(1)} %get-tuple-element.76), channel_id=1, source_target_pairs={{0,19},{1,16},{2,17},{3,18},{4,23},{5,20},{6,21},{7,22},{8,27},{9,... | collective-permute-start | bytes 116744 | tf_op jit(solution)/shard_map/ppermute | solution.py:360
  62.8 12.1 %collective-permute-start.16 = (bf16[256,128]{1,0:T(8,128)(2,1)S(1)}, bf16[256,128]{1,0:T(8,128)(2,1)S(1)}, u32[]{:S(2)}, u32[]{:S(2)}) collective-permute-start(bf16[256,128]{1,0:T(8,128)(2,1)S(1)} %get-tuple-element.74), channel_id=1, source_target_pairs={{0,1},{1,2},{2,3},{3,0},{4,5},{5,6},{6,7},{7,4},{8,9},{9,10},{10,1... | collective-permute-start | bytes 196616 | tf_op jit(solution)/shard_map/ppermute | solution.py:24
  62.8 12.1 %collective-permute-start.15 = (bf16[256,128]{1,0:T(8,128)(2,1)S(1)}, bf16[256,128]{1,0:T(8,128)(2,1)S(1)}, u32[]{:S(2)}, u32[]{:S(2)}) collective-permute-start(bf16[256,128]{1,0:T(8,128)(2,1)S(1)} %get-tuple-element.72), channel_id=1, source_target_pairs={{0,2},{1,3},{2,0},{3,1},{4,6},{5,7},{6,4},{7,5},{8,10},{9,11},{10,... | collective-permute-start | bytes 196616 | tf_op jit(solution)/shard_map/ppermute | solution.py:24
  64.0 10.9 %collective-permute-start.14 = (bf16[256,128]{1,0:T(8,128)(2,1)S(1)}, bf16[256,128]{1,0:T(8,128)(2,1)S(1)}, u32[]{:S(2)}, u32[]{:S(2)}) collective-permute-start(bf16[256,128]{1,0:T(8,128)(2,1)S(1)} %get-tuple-element.70), channel_id=1, source_target_pairs={{0,3},{1,0},{2,1},{3,2},{4,7},{5,4},{6,5},{7,6},{8,11},{9,8},{10,9... | collective-permute-start | bytes 196616 | tf_op jit(solution)/shard_map/ppermute | solution.py:24
  66.9 6.0 %collective-permute-start.19 = (bf16[152,128]{1,0:T(8,128)(2,1)S(1)}, bf16[152,128]{1,0:T(8,128)(2,1)S(1)}, u32[]{:S(2)}, u32[]{:S(2)}) collective-permute-start(bf16[152,128]{1,0:T(8,128)(2,1)S(1)} %get-tuple-element.77), channel_id=1, source_target_pairs={{0,18},{1,19},{2,16},{3,17},{4,22},{5,23},{6,20},{7,21},{8,26},{9,... | collective-permute-start | bytes 116744 | tf_op jit(solution)/shard_map/ppermute | solution.py:360
  68.2 6.7 %collective-permute-start.20 = (bf16[152,128]{1,0:T(8,128)(2,1)S(1)}, bf16[152,128]{1,0:T(8,128)(2,1)S(1)}, u32[]{:S(2)}, u32[]{:S(2)}) collective-permute-start(bf16[152,128]{1,0:T(8,128)(2,1)S(1)} %get-tuple-element.78), channel_id=1, source_target_pairs={{0,17},{1,18},{2,19},{3,16},{4,21},{5,22},{6,23},{7,20},{8,25},{9,... | collective-permute-start | bytes 116744 | tf_op jit(solution)/shard_map/ppermute | solution.py:360

commit v8 on v7

--- a/solution.py
+++ b/solution.py
@@ -42,7 +42,8 @@
     span = slots.shape[2] // local
     factor = lax.rsqrt(jnp.mean(tokens * tokens, axis=-1, keepdims=True) + 1e-06)
     normed = (tokens * factor * gain[...].reshape(1, features)).astype(jnp.bfloat16)
-    copy.wait()
+    if copy is not None:
+        copy.wait()
     qkv = jnp.dot(normed, weight[...], preferred_element_type=jnp.float32).astype(jnp.bfloat16)
     tail = jnp.ones((count, span - 3 * HD), jnp.bfloat16)
     place = lax.axis_index("tok")
@@ -52,7 +53,7 @@
         for head in range(group * local, (group + 1) * local):
             columns += [
                 qkv[:, (kind * HEADS + head) * HD : (kind * HEADS + head + 1) * HD]
-                for kind in range(3)
+                for kind in (1, 0, 2)
             ] + [tail]
         slots[slot] = jnp.concatenate(columns, axis=1)
     for index, out in enumerate(outs):
@@ -77,14 +78,12 @@
 
 
 def mixed_kernel(split, field, gain, weight, lon_shift, eastern, *refs):
-    *outs, slots, held_weight, sems = refs
-    copy = pltpu.make_async_copy(weight, held_weight, sems.at[0])
-    copy.start()
+    *outs, slots = refs
     rows, _, features = field.shape
     own = field[...].astype(jnp.float32)[:, :split]
     column = lax.broadcasted_iota(jnp.int32, own.shape, 1)
     tokens = jnp.where(column < column_offset(lon_shift), eastern[...].astype(jnp.float32), own)
-    project(tokens.reshape(rows * split, features), gain, held_weight, copy, slots, outs)
+    project(tokens.reshape(rows * split, features), gain, weight, None, slots, outs)
 
 
 def gather(head, kept, mixed, held, keys):
@@ -96,7 +95,7 @@
     for block in mixed:
         held[start : start + block.shape[0]] = block[...]
         start += block.shape[0]
-    keys[...] = held[...].T
+    keys[...] = held[:, :LANES].T
 
 
 def attend(held, keys, attended, scores, weights):
@@ -108,9 +107,10 @@
 
     def score(index, out):
         first = index * step
-        queries = pltpu.roll(held[first : first + step].astype(jnp.float32), HD, axis=1)
+        queries = pltpu.roll(held[first : first + step].astype(jnp.float32), span - HD, axis=1)
+        queries = queries[:, :LANES]
         lane = lax.broadcasted_iota(jnp.int32, queries.shape, 1)
-        queries = jnp.where((lane >= HD) & (lane < 2 * HD), queries, 0.0).astype(jnp.bfloat16)
+        queries = jnp.where(lane < HD, queries, 0.0).astype(jnp.bfloat16)
         out[...] = jnp.dot(queries, keys[...], preferred_element_type=jnp.float32)
 
     score(0, scores[0])
@@ -122,10 +122,10 @@
             part = now[first : first + chunk]
             top = jnp.max(part, axis=-1, keepdims=True)
             out[first : first + chunk] = jnp.exp2((part - top) * factor).astype(jnp.bfloat16)
-        mixed_values = jnp.dot(out[...], held[...], preferred_element_type=jnp.float32)
-        scaled = mixed_values / mixed_values[:, 3 * HD : 3 * HD + 1]
-        values = pltpu.roll(scaled, span - 2 * HD, axis=1)[:, :LANES]
-        attended[index * step : (index + 1) * step] = values
+        values = jnp.dot(out[...], held[:, span - LANES :], preferred_element_type=jnp.float32)
+        first = 2 * HD - (span - LANES)
+        values = values / values[:, first + HD : first + HD + 1]
+        attended[index * step : (index + 1) * step] = pltpu.roll(values, LANES - first, axis=1)
 
 
 def packed_rows(count):
@@ -180,36 +180,39 @@
 
 def attention_kernel(head, groups, *refs):
     kept, mixed = refs[:groups], refs[groups : 2 * groups]
-    outs, (held, keys, attended, *rest) = refs[2 * groups : -7], refs[-7:]
+    kept_out, mixed_out, held, keys, attended, *rest = refs[2 * groups :]
     gather(head, kept, mixed, held, keys)
     attend(held, keys, attended, rest[:2], rest[2:])
-    kept_count, mixed_count = kept[0].shape[0], mixed[0].shape[0]
-    for group in range(groups):
-        first = groups * kept_count + group * mixed_count
-        left = pack(attended[first : first + mixed_count])
-        right = pack(attended[group * kept_count : (group + 1) * kept_count])
-        outs[group][...] = jnp.concatenate([left, right], axis=0).astype(jnp.bfloat16)
-        if len(outs) > groups:
-            outs[groups + group][...] = left.astype(jnp.bfloat16)
-
-
-def mixed_rows_kernel(*refs):
-    *blocks, out = refs
-    rows = out.shape[0] // len(blocks)
-    pieces = [block[...].astype(jnp.float32)[:rows] for block in blocks]
-    out[...] = jnp.concatenate(pieces, axis=0).astype(jnp.bfloat16)
-
-
-def projected_rows(split, lon_shift, shape, blocks, western, weight):
+    start = 0
+    for blocks, out in ((kept, kept_out), (mixed, mixed_out)):
+        packed = []
+        for block in blocks:
+            packed.append(pack(attended[start : start + block.shape[0]]))
+            start += block.shape[0]
+        out[...] = jnp.concatenate(packed, axis=0).astype(jnp.bfloat16)
+
+
+def select_kernel(split, count, lon_shift, kept, mixed, western, *outs):
+    taken = lax.rem(packed_tokens(count), split) < column_offset(lon_shift)
+    own, west = mixed[...].astype(jnp.float32), western[...].astype(jnp.float32)
+    rest = kept[...].astype(jnp.float32)
+    left, right = own.shape[0] // len(outs), rest.shape[0] // len(outs)
+    for group, out in enumerate(outs):
+        rows = slice(group * left, (group + 1) * left)
+        chosen = jnp.where(taken, west[rows], own[rows])
+        out[...] = jnp.concatenate(
+            [chosen, rest[group * right : (group + 1) * right]], axis=0
+        ).astype(jnp.bfloat16)
+
+
+def projected_rows(split, shape, blocks, weight):
     rows, columns, _ = shape
     kept_count, mixed_count = rows * (columns - split), rows * split
     total = packed_rows(mixed_count)[0]
-    taken = lax.rem(packed_tokens(mixed_count), split) < column_offset(lon_shift)
     attended = []
-    for block, west in zip(blocks, western):
+    for block in blocks:
         block = block[...].astype(jnp.float32)
-        left = unpack(jnp.where(taken, west, block[:total]), mixed_count)
-        right = unpack(block[total:], kept_count)
+        left, right = unpack(block[:total], mixed_count), unpack(block[total:], kept_count)
         attended.append(jnp.concatenate([right, left], axis=0))
     attended = jnp.concatenate(attended, axis=1).astype(jnp.bfloat16)
     projected = jnp.dot(attended, weight[...], preferred_element_type=jnp.float32)
@@ -223,8 +226,8 @@
     return jnp.concatenate([left, right], axis=1)
 
 
-def first_output_kernel(split, groups, lon_shift, field, weight, *refs):
-    *blocks, western, out, second, first = refs
+def first_output_kernel(split, groups, field, weight, *refs):
+    *blocks, out, second, first = refs
     features = field.shape[2]
     for slot in range(groups):
         group = lax.rem(lax.axis_index("tok") + slot, groups)
@@ -234,17 +237,13 @@
             ordered[slot * LANES + HD : (slot + 1) * LANES] = jnp.zeros(
                 (LANES - HD, features), jnp.bfloat16
             )
-    west = western[...].astype(jnp.float32)
-    total = west.shape[0] // groups
-    west = [west[slot * total : (slot + 1) * total] for slot in range(groups)]
-    projected = projected_rows(split, lon_shift, field.shape, blocks, west, first)
+    projected = projected_rows(split, field.shape, blocks, first)
     out[...] = field[...].astype(jnp.float32) + projected
 
 
-def second_output_kernel(split, groups, lon_shift, partial, weight, *refs):
+def second_output_kernel(split, partial, weight, *refs):
     *blocks, out = refs
-    west = [block[...].astype(jnp.float32) for block in blocks[groups:]]
-    projected = projected_rows(split, lon_shift, partial.shape, blocks[:groups], west, weight)
+    projected = projected_rows(split, partial.shape, blocks, weight)
     out[...] = (partial[...] + projected).astype(jnp.bfloat16)
 
 
@@ -286,9 +285,10 @@
         )(*operands)
 
     def spread(blocks, sign):
-        return [blocks[0]] + [
-            shifted(blocks[distance], "tok", sign * distance) for distance in range(1, groups)
-        ]
+        arrived = list(blocks)
+        for distance in sorted(range(1, groups), key=lambda step: step * (step - groups)):
+            arrived[distance] = shifted(blocks[distance], "tok", sign * distance)
+        return arrived
 
     eastern = shifted(field[:, :split], "win", -LAT_WINDOWS)
     hbm = pl.BlockSpec(memory_space=pltpu.HBM)
@@ -300,31 +300,28 @@
         pltpu.VMEM(norm_gain.shape, norm_gain.dtype),
     ]
     kept = spread(projection(kept_kernel, kept_count, 1, [hbm] * 3, held, limit(60), *operands), 1)
-    specs = [*whole(2), hbm, smem, *whole(1)]
+    specs = [*whole(3), smem, *whole(1)]
     operands += (lon_shift, eastern)
-    mixed = projection(mixed_kernel, mixed_count, local, specs, held[:2], limit(52), *operands)
-    ahead = [None] * (groups - 1)
-    first_mixed = spread(after(mixed[:groups], [*ahead, kept[1]]), 1)
-
-    second_mixed = spread(after(mixed[groups:], [None, *kept[2:], first_mixed[1]]), 1)
+    mixed = projection(mixed_kernel, mixed_count, local, specs, [], limit(48), *operands)
+    first_mixed = spread(after(mixed[:groups], [None, *kept[1:]]), 1)
+    second_mixed = spread(after(mixed[groups:], [None, *first_mixed[1:]]), 1)
 
     total = groups * rows * columns
     step = total // 5
-    mixed_packed = packed_rows(mixed_count)[0]
-    all_packed = mixed_packed + packed_rows(kept_count)[0]
+    mixed_packed, kept_packed = packed_rows(mixed_count)[0], packed_rows(kept_count)[0]
 
     def block(count):
         return jax.ShapeDtypeStruct((count, LANES), jnp.bfloat16)
 
-    def attention(head, out_shape, blocks):
+    def attention(head, *blocks):
         return pl.pallas_call(
             functools.partial(attention_kernel, head, groups),
-            out_shape=out_shape,
+            out_shape=[block(groups * kept_packed), block(groups * mixed_packed)],
             in_specs=whole(len(blocks)),
-            out_specs=whole(len(out_shape)),
+            out_specs=whole(2),
             scratch_shapes=[
                 pltpu.VMEM((total, span), jnp.bfloat16),
-                pltpu.VMEM((span, total), jnp.bfloat16),
+                pltpu.VMEM((LANES, total), jnp.bfloat16),
                 pltpu.VMEM((total, LANES), jnp.float32),
                 pltpu.VMEM((step, total), jnp.float32),
                 pltpu.VMEM((step, total), jnp.float32),
@@ -339,38 +336,22 @@
             ),
         )(*blocks)
 
-    first = attention(0, [block(all_packed)] * groups, [*kept, *first_mixed])
-    first = spread(first, -1)
-    second = attention(
-        1,
-        [block(all_packed)] * groups + [block(mixed_packed)] * groups,
-        [*kept, *second_mixed],
-    )
-    windows = lax.axis_size("win")
-    western = []
-    for distance in range(groups):
-        route = [
-            (
-                win * groups + tok,
-                (win + LAT_WINDOWS) % windows * groups + (tok - distance) % groups,
-            )
-            for win in range(windows)
-            for tok in range(groups)
-        ]
-        western.append(lax.ppermute(second[groups + distance], ("win", "tok"), route))
-    returned = [lax.optimization_barrier((block, second[0]))[0] for block in first]
-    second = spread(after(second[:groups], [None, *first[1:]]), -1)
-    first_western = pl.pallas_call(
-        mixed_rows_kernel,
-        out_shape=block(groups * mixed_packed),
-        in_specs=whole(groups),
-        out_specs=pl.BlockSpec(memory_space=pltpu.VMEM),
-        compiler_params=limit(16),
-        cost_estimate=pl.CostEstimate(
-            flops=0, bytes_accessed=4 * groups * all_packed * LANES, transcendentals=0
-        ),
-    )(*returned)
-    first_western = shifted(first_western, "win", LAT_WINDOWS)
+    def back(kept_values, mixed_values):
+        western = shifted(mixed_values, "win", LAT_WINDOWS)
+        selected = pl.pallas_call(
+            functools.partial(select_kernel, split, mixed_count),
+            out_shape=[block(mixed_packed + kept_packed)] * groups,
+            in_specs=[smem] + whole(3),
+            out_specs=whole(groups),
+            compiler_params=limit(16),
+            cost_estimate=pl.CostEstimate(
+                flops=total * LANES * 20, bytes_accessed=8 * total * LANES, transcendentals=0
+            ),
+        )(lon_shift, kept_values, mixed_values, western)
+        return spread(selected, -1)
+
+    first = back(*attention(0, *kept, *first_mixed))
+    second = back(*attention(1, *kept, *second_mixed))
 
     cost = pl.CostEstimate(
         flops=2 * rows * columns * groups * LANES * features,
@@ -384,20 +365,20 @@
             jax.ShapeDtypeStruct(field.shape, jnp.float32),
             jax.ShapeDtypeStruct(ordered, jnp.bfloat16),
         ],
-        in_specs=[smem] + whole(3 + groups),
+        in_specs=whole(2 + groups),
         out_specs=whole(2),
         scratch_shapes=[pltpu.VMEM(ordered, jnp.bfloat16)],
         compiler_params=limit(24),
         cost_estimate=cost,
-    )(lon_shift, field, out_weight, *first, first_western)
+    )(field, out_weight, *first)
     result = pl.pallas_call(
-        functools.partial(second_output_kernel, split, groups),
+        functools.partial(second_output_kernel, split),
         out_shape=jax.ShapeDtypeStruct(field.shape, jnp.bfloat16),
-        in_specs=[smem] + whole(2 + 2 * groups),
+        in_specs=whole(2 + groups),
         out_specs=pl.BlockSpec(memory_space=pltpu.VMEM),
         compiler_params=limit(24),
         cost_estimate=cost,
-    )(lon_shift, partial, weight, *second, *western)
+    )(partial, weight, *second)
     return result[None]
 
 

time: 77.4 us -> 69.6 us (0.90)
  starting transfers between devices: 39.5 us -> 31.6 us
  waiting for transfers between devices: 14.2 us -> 15.7 us
  Pallas kernels: 22.3 us -> 20.9 us
    ppermute x4 -> x0, starting transfers between devices: 6.24 us -> none  [shards(): lax.ppermute(second[groups + distance], ('win', 'tok'), route)]
    ppermute x17 -> x18, waiting for transfers between devices: 10.3 us -> 15.7 us  [shifted(): lax.ppermute(block, axis, [(i, (i + distance) % count) for i in range(cou...]
    ppermute x4 -> x0, waiting for transfers between devices: 3.86 us -> none  [shards(): lax.ppermute(second[groups + distance], ('win', 'tok'), route)]
    ppermute x17 -> x18, starting transfers between devices: 33.2 us -> 31.6 us  [shifted(): lax.ppermute(block, axis, [(i, (i + distance) % count) for i in range(cou...]
    pallas_call x2, Pallas kernels: 10.1 us -> 9.09 us  [projection(): pl.pallas_call(functools.partial(kernel, split), out_shape=[block] * (par...]
    pallas_call x2 -> x3, Pallas kernels: 2.32 us -> 2.97 us  [the longest x1 1.75 us: shards(): pl.pallas_call(functools.partial(second_output_kernel, split), out_shape=...]
  transfers between devices with their start and end apart: 21 -> 18, of which waited for: 7 -> 9; matrix products, arithmetic and copies ran while one was open for 0% -> 0% of each run, Pallas kernels for 26% -> 28%
where the time goes in v8:
time: 69.6 us; the launch traced here: 69.4 us
  starting transfers between devices  31.6 us (45%)
  Pallas kernels  20.9 us (30%)
  waiting for transfers between devices  15.7 us (23%)
  local copies, waits for them, and re-layouts  1.14 us (2%)
    ppermute x18, starting transfers between devices, shifted(): lax.ppermute(block, axis, [(i, (i + distance) % count) for i in range(cou...  31.6 us
    ppermute x18, waiting for transfers between devices, shifted(): lax.ppermute(block, axis, [(i, (i + distance) % count) for i in range(cou...  15.7 us
    pallas_call x2, Pallas kernels, projection(): pl.pallas_call(functools.partial(kernel, split), out_shape=[block] * (par...  9.09 us
    pallas_call x2, Pallas kernels, attention(): pl.pallas_call(functools.partial(attention_kernel, head, groups), out_sha...  8.01 us
    pallas_call x1, Pallas kernels, shards(): pl.pallas_call(functools.partial(second_output_kernel, split), out_shape=...  1.75 us
  transfers between devices with their start and end apart: 18, of which 9 were waited for; matrix products, arithmetic and copies ran while one was open for 0% of the time, Pallas kernels for 28%

profile of v8, /device:TPU:0, one launch (start us, length us, event | category | flops | bytes accessed | tf_op | source)
XLA Modules:
  0.0 69.4 jit_solution(2673178200730955819)
XLA Ops:
  0.0 1.1 %slice.4 = bf16[10,24,1280]{2,1,0:T(8,128)(2,1)S(1)} slice(bf16[10,40,1280]{2,1,0:T(8,128)(2,1)} %bitcast.2), slice={[0:10], [0:24], [0:1280]} | slice | bytes 1228800 | tf_op jit(solution)/shard_map/slice | solution.py:293
  1.1 0.0 copy-start
  1.1 0.0 copy-start.2
  1.1 0.0 copy-start.3
  1.2 3.0 %collective-permute-start.3 = (bf16[10,24,1280]{2,1,0:T(8,128)(2,1)S(1)}, bf16[10,24,1280]{2,1,0:T(8,128)(2,1)S(1)}, u32[]{:S(2)}, u32[]{:S(2)}) collective-permute-start(bf16[10,24,1280]{2,1,0:T(8,128)(2,1)S(1)} %slice.4), channel_id=1, source_target_pairs={{0,16},{4,20},{8,24},{12,28},{16,0},{20,4},{24,8},{28,12},{1,17},{... | collective-permute-start | bytes 1843208 | tf_op jit(solution)/shard_map/ppermute | solution.py:24
  4.2 4.8 %shard_map.55 = (bf16[160,512]{1,0:T(8,128)(2,1)}, bf16[160,512]{1,0:T(8,128)(2,1)}, bf16[160,512]{1,0:T(8,128)(2,1)}, bf16[160,512]{1,0:T(8,128)(2,1)}) custom-call(bf16[10,40,1280]{2,1,0:T(8,128)(2,1)} %bitcast.3, f32[1280]{0:T(1024)} %gain.3, bf16[1280,1920]{1,0:T(8,128)(2,1)} %weight.4), custom_call_target="tpu_custom_call" | custom-call | flops 786432000 | bytes 5734400 | tf_op jit(solution)/shard_map/pallas_call | solution.py:270
  9.0 1.6 %collective-permute-start = (bf16[160,512]{1,0:T(8,128)(2,1)}, bf16[160,512]{1,0:T(8,128)(2,1)S(1)}, u32[]{:S(2)}, u32[]{:S(2)}) collective-permute-start(bf16[160,512]{1,0:T(8,128)(2,1)} %get-tuple-element.38), channel_id=1, source_target_pairs={{0,1},{1,2},{2,3},{3,0},{4,5},{5,6},{6,7},{7,4},{8,9},{9,10},{10,1... | collective-permute-start | bytes 491528 | tf_op jit(solution)/shard_map/ppermute | solution.py:24
  10.6 2.6 %collective-permute-start.1 = (bf16[160,512]{1,0:T(8,128)(2,1)}, bf16[160,512]{1,0:T(8,128)(2,1)S(1)}, u32[]{:S(2)}, u32[]{:S(2)}) collective-permute-start(bf16[160,512]{1,0:T(8,128)(2,1)} %get-tuple-element.39), channel_id=1, source_target_pairs={{0,2},{1,3},{2,0},{3,1},{4,6},{5,7},{6,4},{7,5},{8,10},{9,11},{10,... | collective-permute-start | bytes 491528 | tf_op jit(solution)/shard_map/ppermute | solution.py:24
  13.2 0.0 copy-start.4
  13.2 1.3 %collective-permute-start.2 = (bf16[160,512]{1,0:T(8,128)(2,1)}, bf16[160,512]{1,0:T(8,128)(2,1)S(1)}, u32[]{:S(2)}, u32[]{:S(2)}) collective-permute-start(bf16[160,512]{1,0:T(8,128)(2,1)} %get-tuple-element.40), channel_id=1, source_target_pairs={{0,3},{1,0},{2,1},{3,2},{4,7},{5,4},{6,5},{7,6},{8,11},{9,8},{10,9... | collective-permute-start | bytes 491528 | tf_op jit(solution)/shard_map/ppermute | solution.py:24
  14.6 3.5 %collective-permute-done.3.eastern = bf16[10,24,1280]{2,1,0:T(8,128)(2,1)S(1)} collective-permute-done((bf16[10,24,1280]{2,1,0:T(8,128)(2,1)S(1)}, bf16[10,24,1280]{2,1,0:T(8,128)(2,1)S(1)}, u32[]{:S(2)}, u32[]{:S(2)}) %collective-permute-start.3) | collective-permute-done | bytes 614432 | tf_op jit(solution)/shard_map/ppermute | solution.py:24
  18.0 0.0 copy-done
  18.0 0.0 copy-done.2
  18.0 0.0 copy-done.3
  18.1 4.3 %shard_map.56 = (bf16[240,256]{1,0:T(8,128)(2,1)S(1)}, bf16[240,256]{1,0:T(8,128)(2,1)S(1)}, bf16[240,256]{1,0:T(8,128)(2,1)S(1)}, bf16[240,256]{1,0:T(8,128)(2,...) custom-call(bf16[10,40,1280]{2,1,0:T(8,128)(2,1)S(1)} %bitcast.4, ...), custom_call_target="tpu_custom_call" | custom-call | flops 1179648000 | bytes 6144000 | tf_op jit(solution)/shard_map/pallas_call | solution.py:270
  22.4 0.0 collective-permute-done.refs_1_
  22.4 1.9 %collective-permute-start.4 = (bf16[240,256]{1,0:T(8,128)(2,1)S(1)}, bf16[240,256]{1,0:T(8,128)(2,1)S(1)}, u32[]{:S(2)}, u32[]{:S(2)}) collective-permute-start(bf16[240,256]{1,0:T(8,128)(2,1)S(1)} %get-tuple-element.43), channel_id=1, source_target_pairs={{0,1},{1,2},{2,3},{3,0},{4,5},{5,6},{6,7},{7,4},{8,9},{9,10},{10,1... | collective-permute-start | bytes 368648 | tf_op jit(solution)/shard_map/ppermute | solution.py:24
  24.2 0.0 collective-permute-done.1.refs_2_
  24.2 2.6 %collective-permute-start.5 = (bf16[240,256]{1,0:T(8,128)(2,1)S(1)}, bf16[240,256]{1,0:T(8,128)(2,1)S(1)}, u32[]{:S(2)}, u32[]{:S(2)}) collective-permute-start(bf16[240,256]{1,0:T(8,128)(2,1)S(1)} %get-tuple-element.45), channel_id=1, source_target_pairs={{0,2},{1,3},{2,0},{3,1},{4,6},{5,7},{6,4},{7,5},{8,10},{9,11},{10,... | collective-permute-start | bytes 368648 | tf_op jit(solution)/shard_map/ppermute | solution.py:24
  26.8 0.0 collective-permute-done.2.refs_3_
  26.8 3.4 %collective-permute-start.6 = (bf16[240,256]{1,0:T(8,128)(2,1)S(1)}, bf16[240,256]{1,0:T(8,128)(2,1)S(1)}, u32[]{:S(2)}, u32[]{:S(2)}) collective-permute-start(bf16[240,256]{1,0:T(8,128)(2,1)S(1)} %get-tuple-element.47), channel_id=1, source_target_pairs={{0,3},{1,0},{2,1},{3,2},{4,7},{5,4},{6,5},{7,6},{8,11},{9,8},{10,9... | collective-permute-start | bytes 368648 | tf_op jit(solution)/shard_map/ppermute | solution.py:24
  30.2 0.0 collective-permute-done.4.refs_5_
  30.2 4.7 %collective-permute-start.11 = (bf16[240,256]{1,0:T(8,128)(2,1)S(1)}, bf16[240,256]{1,0:T(8,128)(2,1)S(1)}, u32[]{:S(2)}, u32[]{:S(2)}) collective-permute-start(bf16[240,256]{1,0:T(8,128)(2,1)S(1)} %get-tuple-element.58), channel_id=1, source_target_pairs={{0,1},{1,2},{2,3},{3,0},{4,5},{5,6},{6,7},{7,4},{8,9},{9,10},{10,1... | collective-permute-start | bytes 368648 | tf_op jit(solution)/shard_map/ppermute | solution.py:24
  34.9 1.0 %collective-permute-done.5.refs_6_ = bf16[240,256]{1,0:T(8,128)(2,1)S(1)} collective-permute-done((bf16[240,256]{1,0:T(8,128)(2,1)S(1)}, bf16[240,256]{1,0:T(8,128)(2,1)S(1)}, u32[]{:S(2)}, u32[]{:S(2)}) %collective-permute-start.5) | collective-permute-done | bytes 122912 | tf_op jit(solution)/shard_map/ppermute | solution.py:24
  35.9 1.1 %collective-permute-start.12 = (bf16[240,256]{1,0:T(8,128)(2,1)S(1)}, bf16[240,256]{1,0:T(8,128)(2,1)S(1)}, u32[]{:S(2)}, u32[]{:S(2)}) collective-permute-start(bf16[240,256]{1,0:T(8,128)(2,1)S(1)} %get-tuple-element.60), channel_id=1, source_target_pairs={{0,2},{1,3},{2,0},{3,1},{4,6},{5,7},{6,4},{7,5},{8,10},{9,11},{10,... | collective-permute-start | bytes 368648 | tf_op jit(solution)/shard_map/ppermute | solution.py:24
  37.0 3.0 %collective-permute-done.6.refs_7_ = bf16[240,256]{1,0:T(8,128)(2,1)S(1)} collective-permute-done((bf16[240,256]{1,0:T(8,128)(2,1)S(1)}, bf16[240,256]{1,0:T(8,128)(2,1)S(1)}, u32[]{:S(2)}, u32[]{:S(2)}) %collective-permute-start.6) | collective-permute-done | bytes 122912 | tf_op jit(solution)/shard_map/ppermute | solution.py:24
  40.0 0.8 %collective-permute-start.13 = (bf16[240,256]{1,0:T(8,128)(2,1)S(1)}, bf16[240,256]{1,0:T(8,128)(2,1)S(1)}, u32[]{:S(2)}, u32[]{:S(2)}) collective-permute-start(bf16[240,256]{1,0:T(8,128)(2,1)S(1)} %get-tuple-element.62), channel_id=1, source_target_pairs={{0,3},{1,0},{2,1},{3,2},{4,7},{5,4},{6,5},{7,6},{8,11},{9,8},{10,9... | collective-permute-start | bytes 368648 | tf_op jit(solution)/shard_map/ppermute | solution.py:24
  40.8 0.0 copy-done.4
  40.8 4.0 %shard_map.57 = (bf16[416,128]{1,0:T(8,128)(2,1)S(1)}, bf16[608,128]{1,0:T(8,128)(2,1)S(1)}) custom-call(bf16[160,512]{1,0:T(8,128)(2,1)S(1)} %copy-done.4, bf16[160,512]{1,0:T(8,128)(2,1)S(1)} %collective-permute-done.refs_1_, bf16[160,512]{1,0:T(8,128)(2,1)S(1)} %collective-permute-done.1.refs_2_, bf16[160,512]{1,0:T(8,128)(2,1)S(1)} %collective-permute-done.2.refs_3_, ...), custom_call_target="tpu_custom_call" | custom-call | flops 2621440000 | bytes 1228800 | tf_op jit(solution)/shard_map/pallas_call | solution.py:317
  44.8 0.8 %collective-permute-start.7 = (bf16[608,128]{1,0:T(8,128)(2,1)S(1)}, bf16[608,128]{1,0:T(8,128)(2,1)S(1)}, u32[]{:S(2)}, u32[]{:S(2)}) collective-permute-start(bf16[608,128]{1,0:T(8,128)(2,1)S(1)} %get-tuple-element.49.mixed), channel_id=1, source_target_pairs={{0,16},{4,20},{8,24},{12,28},{16,0},{20,4},{24,8},{28,12},{1,17},{... | collective-permute-start | bytes 466952 | tf_op jit(solution)/shard_map/ppermute | solution.py:24
  45.6 0.0 collective-permute-done.11.refs_5_
  45.6 0.3 collective-permute-done.12.refs_6_
  45.9 2.0 %collective-permute-done.13.refs_7_ = bf16[240,256]{1,0:T(8,128)(2,1)S(1)} collective-permute-done((bf16[240,256]{1,0:T(8,128)(2,1)S(1)}, bf16[240,256]{1,0:T(8,128)(2,1)S(1)}, u32[]{:S(2)}, u32[]{:S(2)}) %collective-permute-start.13) | collective-permute-done | bytes 122912 | tf_op jit(solution)/shard_map/ppermute | solution.py:24
  47.9 0.0 copy-start.1
  47.9 4.0 %shard_map.60 = (bf16[416,128]{1,0:T(8,128)(2,1)S(1)}, bf16[608,128]{1,0:T(8,128)(2,1)S(1)}) custom-call(bf16[160,512]{1,0:T(8,128)(2,1)S(1)} %copy-done.4, bf16[160,512]{1,0:T(8,128)(2,1)S(1)} %collective-permute-done.refs_1_, bf16[160,512]{1,0:T(8,128)(2,1)S(1)} %collective-permute-done.1.refs_2_, bf16[160,512]{1,0:T(8,128)(2,1)S(1)} %collective-permute-done.2.refs_3_, ...), custom_call_target="tpu_custom_call" | custom-call | flops 2621440000 | bytes 1228800 | tf_op jit(solution)/shard_map/pallas_call | solution.py:317
  51.9 0.4 collective-permute-start.14
  52.3 0.0 collective-permute-done.7.western
  52.3 0.6 shard_map.58
  52.9 3.0 %collective-permute-start.8 = (bf16[256,128]{1,0:T(8,128)(2,1)S(1)}, bf16[256,128]{1,0:T(8,128)(2,1)S(1)}, u32[]{:S(2)}, u32[]{:S(2)}) collective-permute-start(bf16[256,128]{1,0:T(8,128)(2,1)S(1)} %get-tuple-element.51), channel_id=1, source_target_pairs={{0,3},{1,0},{2,1},{3,2},{4,7},{5,4},{6,5},{7,6},{8,11},{9,8},{10,9... | collective-permute-start | bytes 196616 | tf_op jit(solution)/shard_map/ppermute | solution.py:24
  55.9 0.0 collective-permute-start.9
  55.9 0.9 %collective-permute-start.10 = (bf16[256,128]{1,0:T(8,128)(2,1)S(1)}, bf16[256,128]{1,0:T(8,128)(2,1)S(1)}, u32[]{:S(2)}, u32[]{:S(2)}) collective-permute-start(bf16[256,128]{1,0:T(8,128)(2,1)S(1)} %get-tuple-element.53), channel_id=1, source_target_pairs={{0,1},{1,2},{2,3},{3,0},{4,5},{5,6},{6,7},{7,4},{8,9},{9,10},{10,1... | collective-permute-start | bytes 196616 | tf_op jit(solution)/shard_map/ppermute | solution.py:24
  56.9 0.7 collective-permute-done.14.western
  57.5 0.6 shard_map.61
  58.1 2.3 %collective-permute-start.15 = (bf16[256,128]{1,0:T(8,128)(2,1)S(1)}, bf16[256,128]{1,0:T(8,128)(2,1)S(1)}, u32[]{:S(2)}, u32[]{:S(2)}) collective-permute-start(bf16[256,128]{1,0:T(8,128)(2,1)S(1)} %get-tuple-element.66), channel_id=1, source_target_pairs={{0,3},{1,0},{2,1},{3,2},{4,7},{5,4},{6,5},{7,6},{8,11},{9,8},{10,9... | collective-permute-start | bytes 196616 | tf_op jit(solution)/shard_map/ppermute | solution.py:24
  60.4 1.1 %collective-permute-start.16 = (bf16[256,128]{1,0:T(8,128)(2,1)S(1)}, bf16[256,128]{1,0:T(8,128)(2,1)S(1)}, u32[]{:S(2)}, u32[]{:S(2)}) collective-permute-start(bf16[256,128]{1,0:T(8,128)(2,1)S(1)} %get-tuple-element.67), channel_id=1, source_target_pairs={{0,2},{1,3},{2,0},{3,1},{4,6},{5,7},{6,4},{7,5},{8,10},{9,11},{10,... | collective-permute-start | bytes 196616 | tf_op jit(solution)/shard_map/ppermute | solution.py:24
  61.6 0.0 collective-permute-done.8.refs_1_
  61.6 0.0 collective-permute-start.17
  61.6 1.5 %collective-permute-done.9.refs_2_ = bf16[256,128]{1,0:T(8,128)(2,1)S(1)} collective-permute-done((bf16[256,128]{1,0:T(8,128)(2,1)S(1)}, bf16[256,128]{1,0:T(8,128)(2,1)S(1)}, u32[]{:S(2)}, u32[]{:S(2)}) %collective-permute-start.9) | collective-permute-done | bytes 65568 | tf_op jit(solution)/shard_map/ppermute | solution.py:24
  63.1 0.0 collective-permute-done.10.refs_3_
  63.1 0.0 copy-done.1
  63.1 0.8 %shard_map.59 = (f32[10,40,1280]{2,1,0:T(8,128)S(1)}, bf16[512,1280]{1,0:T(8,128)(2,1)S(1)}) custom-call(bf16[10,40,1280]{2,1,0:T(8,128)(2,1)S(1)} %bitcast.5, bf16[640,1280]{1,0:T(8,128)(2,1)S(1)} %copy-done.1, bf16[256,128]{1,0:T(8,128)(2,1)S(1)} %get-tuple-element.50.refs_0_, bf16[256,128]{1,0:T(8,128)(2,1)S(1)} %collective-permute-done.8.refs_1_, ...), custom_call_target="tpu_custom_call" | custom-call | flops 524288000 | bytes 3891200 | tf_op jit(solution)/shard_map/pallas_call | solution.py:362
  63.9 0.0 collective-permute-done.15.refs_1_
  63.9 3.0 %collective-permute-done.16.refs_2_ = bf16[256,128]{1,0:T(8,128)(2,1)S(1)} collective-permute-done((bf16[256,128]{1,0:T(8,128)(2,1)S(1)}, bf16[256,128]{1,0:T(8,128)(2,1)S(1)}, u32[]{:S(2)}, u32[]{:S(2)}) %collective-permute-start.16) | collective-permute-done | bytes 65568 | tf_op jit(solution)/shard_map/ppermute | solution.py:24
  67.0 0.7 collective-permute-done.17.refs_3_
  67.6 1.8 %shard_map.62 = bf16[10,40,1280]{2,1,0:T(8,128)(2,1)} custom-call(f32[10,40,1280]{2,1,0:T(8,128)S(1)} %get-tuple-element.54.partial, bf16[512,1280]{1,0:T(8,128)(2,1)S(1)} %get-tuple-element.55.weight, bf16[256,128]{1,0:T(8,128)(2,1)S(1)} %get-tuple-element.65.refs_0_, bf16[256,128]{1,0:T(8,128)(2,1)S(1)} %collective-permute-done.15.refs_1_, ...), custom_call_target="tpu_custom_call" | custom-call | flops 524288000 | bytes 3891200 | tf_op jit(solution)/shard_map/pallas_call | solution.py:374
Async XLA Ops:
  1.1 16.9 %copy-start = (bf16[1,10,40,1280]{3,2,1,0:T(8,128)(2,1)S(1)}, bf16[1,10,40,1280]{3,2,1,0:T(8,128)(2,1)}, u32[]{:S(2)}) copy-start(bf16[1,10,40,1280]{3,2,1,0:T(8,128)(2,1)} %param.5) | copy-start | bytes 3072004
  1.1 16.9 %copy-start.2 = (f32[1280]{0:T(1024)S(1)}, f32[1280]{0:T(1024)}, u32[]{:S(2)}) copy-start(f32[1280]{0:T(1024)} %gain.3) | copy-start | bytes 15364
  1.1 16.9 %copy-start.3 = (s32[4]{0:T(128)S(1)}, s32[4]{0:T(128)}, u32[]{:S(2)}) copy-start(s32[4]{0:T(128)} %lon_shift.5) | copy-start | bytes 52
  1.2 16.9 %collective-permute-start.3 = (bf16[10,24,1280]{2,1,0:T(8,128)(2,1)S(1)}, bf16[10,24,1280]{2,1,0:T(8,128)(2,1)S(1)}, u32[]{:S(2)}, u32[]{:S(2)}) collective-permute-start(bf16[10,24,1280]{2,1,0:T(8,128)(2,1)S(1)} %slice.4), channel_id=1, source_target_pairs={{0,16},{4,20},{8,24},{12,28},{16,0},{20,4},{24,8},{28,12},{1,17},{... | collective-permute-start | bytes 1843208 | tf_op jit(solution)/shard_map/ppermute | solution.py:24
  9.0 13.4 %collective-permute-start = (bf16[160,512]{1,0:T(8,128)(2,1)}, bf16[160,512]{1,0:T(8,128)(2,1)S(1)}, u32[]{:S(2)}, u32[]{:S(2)}) collective-permute-start(bf16[160,512]{1,0:T(8,128)(2,1)} %get-tuple-element.38), channel_id=1, source_target_pairs={{0,1},{1,2},{2,3},{3,0},{4,5},{5,6},{6,7},{7,4},{8,9},{9,10},{10,1... | collective-permute-start | bytes 491528 | tf_op jit(solution)/shard_map/ppermute | solution.py:24
  10.6 13.6 %collective-permute-start.1 = (bf16[160,512]{1,0:T(8,128)(2,1)}, bf16[160,512]{1,0:T(8,128)(2,1)S(1)}, u32[]{:S(2)}, u32[]{:S(2)}) collective-permute-start(bf16[160,512]{1,0:T(8,128)(2,1)} %get-tuple-element.39), channel_id=1, source_target_pairs={{0,2},{1,3},{2,0},{3,1},{4,6},{5,7},{6,4},{7,5},{8,10},{9,11},{10,... | collective-permute-start | bytes 491528 | tf_op jit(solution)/shard_map/ppermute | solution.py:24
  13.2 27.6 %copy-start.4 = (bf16[160,512]{1,0:T(8,128)(2,1)S(1)}, bf16[160,512]{1,0:T(8,128)(2,1)}, u32[]{:S(2)}) copy-start(bf16[160,512]{1,0:T(8,128)(2,1)} %get-tuple-element.37.refs_0_) | copy-start | bytes 491524
  13.2 13.6 %collective-permute-start.2 = (bf16[160,512]{1,0:T(8,128)(2,1)}, bf16[160,512]{1,0:T(8,128)(2,1)S(1)}, u32[]{:S(2)}, u32[]{:S(2)}) collective-permute-start(bf16[160,512]{1,0:T(8,128)(2,1)} %get-tuple-element.40), channel_id=1, source_target_pairs={{0,3},{1,0},{2,1},{3,2},{4,7},{5,4},{6,5},{7,6},{8,11},{9,8},{10,9... | collective-permute-start | bytes 491528 | tf_op jit(solution)/shard_map/ppermute | solution.py:24
  22.4 7.8 %collective-permute-start.4 = (bf16[240,256]{1,0:T(8,128)(2,1)S(1)}, bf16[240,256]{1,0:T(8,128)(2,1)S(1)}, u32[]{:S(2)}, u32[]{:S(2)}) collective-permute-start(bf16[240,256]{1,0:T(8,128)(2,1)S(1)} %get-tuple-element.43), channel_id=1, source_target_pairs={{0,1},{1,2},{2,3},{3,0},{4,5},{5,6},{6,7},{7,4},{8,9},{9,10},{10,1... | collective-permute-start | bytes 368648 | tf_op jit(solution)/shard_map/ppermute | solution.py:24
  24.2 11.6 %collective-permute-start.5 = (bf16[240,256]{1,0:T(8,128)(2,1)S(1)}, bf16[240,256]{1,0:T(8,128)(2,1)S(1)}, u32[]{:S(2)}, u32[]{:S(2)}) collective-permute-start(bf16[240,256]{1,0:T(8,128)(2,1)S(1)} %get-tuple-element.45), channel_id=1, source_target_pairs={{0,2},{1,3},{2,0},{3,1},{4,6},{5,7},{6,4},{7,5},{8,10},{9,11},{10,... | collective-permute-start | bytes 368648 | tf_op jit(solution)/shard_map/ppermute | solution.py:24
  26.8 13.1 %collective-permute-start.6 = (bf16[240,256]{1,0:T(8,128)(2,1)S(1)}, bf16[240,256]{1,0:T(8,128)(2,1)S(1)}, u32[]{:S(2)}, u32[]{:S(2)}) collective-permute-start(bf16[240,256]{1,0:T(8,128)(2,1)S(1)} %get-tuple-element.47), channel_id=1, source_target_pairs={{0,3},{1,0},{2,1},{3,2},{4,7},{5,4},{6,5},{7,6},{8,11},{9,8},{10,9... | collective-permute-start | bytes 368648 | tf_op jit(solution)/shard_map/ppermute | solution.py:24
  30.2 15.4 %collective-permute-start.11 = (bf16[240,256]{1,0:T(8,128)(2,1)S(1)}, bf16[240,256]{1,0:T(8,128)(2,1)S(1)}, u32[]{:S(2)}, u32[]{:S(2)}) collective-permute-start(bf16[240,256]{1,0:T(8,128)(2,1)S(1)} %get-tuple-element.58), channel_id=1, source_target_pairs={{0,1},{1,2},{2,3},{3,0},{4,5},{5,6},{6,7},{7,4},{8,9},{9,10},{10,1... | collective-permute-start | bytes 368648 | tf_op jit(solution)/shard_map/ppermute | solution.py:24
  35.9 10.1 %collective-permute-start.12 = (bf16[240,256]{1,0:T(8,128)(2,1)S(1)}, bf16[240,256]{1,0:T(8,128)(2,1)S(1)}, u32[]{:S(2)}, u32[]{:S(2)}) collective-permute-start(bf16[240,256]{1,0:T(8,128)(2,1)S(1)} %get-tuple-element.60), channel_id=1, source_target_pairs={{0,2},{1,3},{2,0},{3,1},{4,6},{5,7},{6,4},{7,5},{8,10},{9,11},{10,... | collective-permute-start | bytes 368648 | tf_op jit(solution)/shard_map/ppermute | solution.py:24
  40.0 7.9 %collective-permute-start.13 = (bf16[240,256]{1,0:T(8,128)(2,1)S(1)}, bf16[240,256]{1,0:T(8,128)(2,1)S(1)}, u32[]{:S(2)}, u32[]{:S(2)}) collective-permute-start(bf16[240,256]{1,0:T(8,128)(2,1)S(1)} %get-tuple-element.62), channel_id=1, source_target_pairs={{0,3},{1,0},{2,1},{3,2},{4,7},{5,4},{6,5},{7,6},{8,11},{9,8},{10,9... | collective-permute-start | bytes 368648 | tf_op jit(solution)/shard_map/ppermute | solution.py:24
  44.8 7.5 %collective-permute-start.7 = (bf16[608,128]{1,0:T(8,128)(2,1)S(1)}, bf16[608,128]{1,0:T(8,128)(2,1)S(1)}, u32[]{:S(2)}, u32[]{:S(2)}) collective-permute-start(bf16[608,128]{1,0:T(8,128)(2,1)S(1)} %get-tuple-element.49.mixed), channel_id=1, source_target_pairs={{0,16},{4,20},{8,24},{12,28},{16,0},{20,4},{24,8},{28,12},{1,17},{... | collective-permute-start | bytes 466952 | tf_op jit(solution)/shard_map/ppermute | solution.py:24
  47.9 15.2 %copy-start.1 = (bf16[640,1280]{1,0:T(8,128)(2,1)S(1)}, bf16[640,1280]{1,0:T(8,128)(2,1)}, u32[]{:S(2)}) copy-start(bf16[640,1280]{1,0:T(8,128)(2,1)} %weight.5) | copy-start | bytes 4915204
  51.9 5.6 %collective-permute-start.14 = (bf16[608,128]{1,0:T(8,128)(2,1)S(1)}, bf16[608,128]{1,0:T(8,128)(2,1)S(1)}, u32[]{:S(2)}, u32[]{:S(2)}) collective-permute-start(bf16[608,128]{1,0:T(8,128)(2,1)S(1)} %get-tuple-element.64.mixed), channel_id=1, source_target_pairs={{0,16},{4,20},{8,24},{12,28},{16,0},{20,4},{24,8},{28,12},{1,17},{... | collective-permute-start | bytes 466952 | tf_op jit(solution)/shard_map/ppermute | solution.py:24
  52.9 8.6 %collective-permute-start.8 = (bf16[256,128]{1,0:T(8,128)(2,1)S(1)}, bf16[256,128]{1,0:T(8,128)(2,1)S(1)}, u32[]{:S(2)}, u32[]{:S(2)}) collective-permute-start(bf16[256,128]{1,0:T(8,128)(2,1)S(1)} %get-tuple-element.51), channel_id=1, source_target_pairs={{0,3},{1,0},{2,1},{3,2},{4,7},{5,4},{6,5},{7,6},{8,11},{9,8},{10,9... | collective-permute-start | bytes 196616 | tf_op jit(solution)/shard_map/ppermute | solution.py:24
  55.9 7.1 %collective-permute-start.9 = (bf16[256,128]{1,0:T(8,128)(2,1)S(1)}, bf16[256,128]{1,0:T(8,128)(2,1)S(1)}, u32[]{:S(2)}, u32[]{:S(2)}) collective-permute-start(bf16[256,128]{1,0:T(8,128)(2,1)S(1)} %get-tuple-element.52), channel_id=1, source_target_pairs={{0,2},{1,3},{2,0},{3,1},{4,6},{5,7},{6,4},{7,5},{8,10},{9,11},{10,... | collective-permute-start | bytes 196616 | tf_op jit(solution)/shard_map/ppermute | solution.py:24
  55.9 7.1 %collective-permute-start.10 = (bf16[256,128]{1,0:T(8,128)(2,1)S(1)}, bf16[256,128]{1,0:T(8,128)(2,1)S(1)}, u32[]{:S(2)}, u32[]{:S(2)}) collective-permute-start(bf16[256,128]{1,0:T(8,128)(2,1)S(1)} %get-tuple-element.53), channel_id=1, source_target_pairs={{0,1},{1,2},{2,3},{3,0},{4,5},{5,6},{6,7},{7,4},{8,9},{9,10},{10,1... | collective-permute-start | bytes 196616 | tf_op jit(solution)/shard_map/ppermute | solution.py:24
  58.1 5.8 %collective-permute-start.15 = (bf16[256,128]{1,0:T(8,128)(2,1)S(1)}, bf16[256,128]{1,0:T(8,128)(2,1)S(1)}, u32[]{:S(2)}, u32[]{:S(2)}) collective-permute-start(bf16[256,128]{1,0:T(8,128)(2,1)S(1)} %get-tuple-element.66), channel_id=1, source_target_pairs={{0,3},{1,0},{2,1},{3,2},{4,7},{5,4},{6,5},{7,6},{8,11},{9,8},{10,9... | collective-permute-start | bytes 196616 | tf_op jit(solution)/shard_map/ppermute | solution.py:24
  60.4 6.5 %collective-permute-start.16 = (bf16[256,128]{1,0:T(8,128)(2,1)S(1)}, bf16[256,128]{1,0:T(8,128)(2,1)S(1)}, u32[]{:S(2)}, u32[]{:S(2)}) collective-permute-start(bf16[256,128]{1,0:T(8,128)(2,1)S(1)} %get-tuple-element.67), channel_id=1, source_target_pairs={{0,2},{1,3},{2,0},{3,1},{4,6},{5,7},{6,4},{7,5},{8,10},{9,11},{10,... | collective-permute-start | bytes 196616 | tf_op jit(solution)/shard_map/ppermute | solution.py:24
  61.6 6.1 %collective-permute-start.17 = (bf16[256,128]{1,0:T(8,128)(2,1)S(1)}, bf16[256,128]{1,0:T(8,128)(2,1)S(1)}, u32[]{:S(2)}, u32[]{:S(2)}) collective-permute-start(bf16[256,128]{1,0:T(8,128)(2,1)S(1)} %get-tuple-element.68), channel_id=1, source_target_pairs={{0,1},{1,2},{2,3},{3,0},{4,5},{5,6},{6,7},{7,4},{8,9},{9,10},{10,1... | collective-permute-start | bytes 196616 | tf_op jit(solution)/shard_map/ppermute | solution.py:24

commit v9 on v8

--- a/solution.py
+++ b/solution.py
@@ -24,6 +24,10 @@
     return lax.ppermute(block, axis, [(i, (i + distance) % count) for i in range(count)])
 
 
+def travel_order(groups):
+    return sorted(range(groups), key=lambda distance: (distance > 0, distance * (distance - groups)))
+
+
 def after(blocks, arrived):
     return [
         block if other is None else lax.optimization_barrier((block, other))[0]
@@ -35,16 +39,21 @@
     return lon_shift[lax.rem(lax.axis_index("win"), LAT_WINDOWS)]
 
 
-def project(tokens, gain, weight, copy, slots, outs):
+def project(tokens, gain, weight, copies, slots, outs):
     groups = slots.shape[0]
     local = HEADS // groups
     count, features = tokens.shape
     span = slots.shape[2] // local
     factor = lax.rsqrt(jnp.mean(tokens * tokens, axis=-1, keepdims=True) + 1e-06)
     normed = (tokens * factor * gain[...].reshape(1, features)).astype(jnp.bfloat16)
-    if copy is not None:
-        copy.wait()
-    qkv = jnp.dot(normed, weight[...], preferred_element_type=jnp.float32).astype(jnp.bfloat16)
+    qkv = None
+    for copy, first, size in copies:
+        if copy is not None:
+            copy.wait()
+        inner = slice(first, first + size)
+        share = jnp.dot(normed[:, inner], weight[inner], preferred_element_type=jnp.float32)
+        qkv = share if qkv is None else qkv + share
+    qkv = qkv.astype(jnp.bfloat16)
     tail = jnp.ones((count, span - 3 * HD), jnp.bfloat16)
     place = lax.axis_index("tok")
     for group in range(groups):
@@ -58,23 +67,30 @@
         slots[slot] = jnp.concatenate(columns, axis=1)
     for index, out in enumerate(outs):
         first = index // groups * out.shape[1]
-        out[...] = slots[index % groups, :, first : first + out.shape[1]]
+        slot = travel_order(groups)[index % groups]
+        out[...] = slots[slot, :, first : first + out.shape[1]]
 
 
 def kept_kernel(split, field, gain, weight, *refs):
     *outs, slots, held_weight, sems, held_field, held_gain = refs
-    copy = pltpu.make_async_copy(weight, held_weight, sems.at[0])
-    first = pltpu.make_async_copy(field, held_field, sems.at[1])
-    second = pltpu.make_async_copy(gain, held_gain, sems.at[2])
+    half = weight.shape[0] // (2 * LANES) // 2 * 2 * LANES
+    copies = []
+    for start, size in ((0, half), (half, weight.shape[0] - half)):
+        inner = pl.ds(start, size)
+        copy = pltpu.make_async_copy(weight.at[inner], held_weight.at[inner], sems.at[len(copies)])
+        copies.append((copy, start, size))
+    first = pltpu.make_async_copy(field, held_field, sems.at[2])
+    second = pltpu.make_async_copy(gain, held_gain, sems.at[3])
     first.start()
     second.start()
-    copy.start()
+    for copy, _, _ in copies:
+        copy.start()
     first.wait()
     second.wait()
     rows, columns, features = field.shape
     tokens = held_field[...].astype(jnp.float32)[:, split:]
     tokens = tokens.reshape(rows * (columns - split), features)
-    project(tokens, held_gain, held_weight, copy, slots, outs)
+    project(tokens, held_gain, held_weight, copies, slots, outs)
 
 
 def mixed_kernel(split, field, gain, weight, lon_shift, eastern, *refs):
@@ -83,7 +99,8 @@
     own = field[...].astype(jnp.float32)[:, :split]
     column = lax.broadcasted_iota(jnp.int32, own.shape, 1)
     tokens = jnp.where(column < column_offset(lon_shift), eastern[...].astype(jnp.float32), own)
-    project(tokens.reshape(rows * split, features), gain, weight, None, slots, outs)
+    copies = [(None, 0, features)]
+    project(tokens.reshape(rows * split, features), gain, weight, copies, slots, outs)
 
 
 def gather(head, kept, mixed, held, keys):
@@ -229,8 +246,8 @@
 def first_output_kernel(split, groups, field, weight, *refs):
     *blocks, out, second, first = refs
     features = field.shape[2]
-    for slot in range(groups):
-        group = lax.rem(lax.axis_index("tok") + slot, groups)
+    for slot, distance in enumerate(travel_order(groups)):
+        group = lax.rem(lax.axis_index("tok") + distance, groups)
         for head, ordered in enumerate((first, second)):
             at = pl.multiple_of((group * HEADS // groups + head) * HD, 16)
             ordered[slot * LANES : slot * LANES + HD] = weight[pl.ds(at, HD)]
@@ -285,17 +302,17 @@
         )(*operands)
 
     def spread(blocks, sign):
-        arrived = list(blocks)
-        for distance in sorted(range(1, groups), key=lambda step: step * (step - groups)):
-            arrived[distance] = shifted(blocks[distance], "tok", sign * distance)
-        return arrived
+        return [blocks[0]] + [
+            shifted(block, "tok", sign * distance)
+            for block, distance in zip(blocks[1:], travel_order(groups)[1:])
+        ]
 
     eastern = shifted(field[:, :split], "win", -LAT_WINDOWS)
     hbm = pl.BlockSpec(memory_space=pltpu.HBM)
     operands = (field, norm_gain, qkv_weight)
     held = [
         pltpu.VMEM(qkv_weight.shape, qkv_weight.dtype),
-        pltpu.SemaphoreType.DMA((3,)),
+        pltpu.SemaphoreType.DMA((4,)),
         pltpu.VMEM(field.shape, field.dtype),
         pltpu.VMEM(norm_gain.shape, norm_gain.dtype),
     ]

time: 69.6 us -> 69.9 us (level)
  waiting for transfers between devices: 15.7 us -> 16.5 us
    ppermute x18, waiting for transfers between devices: 15.7 us -> 16.5 us  [shifted(): lax.ppermute(block, axis, [(i, (i + distance) % count) for i in range(cou...]
  transfers between devices with their start and end apart: 18 -> 18, of which waited for: 9 -> 8; matrix products, arithmetic and copies ran while one was open for 0% -> 0% of each run, Pallas kernels for 28% -> 28%
where the time goes in v9:
time: 69.9 us; the launch traced here: 69.7 us
  starting transfers between devices  31.1 us (44%)
  Pallas kernels  20.9 us (30%)
  waiting for transfers between devices  16.5 us (24%)
  local copies, waits for them, and re-layouts  1.14 us (2%)
    ppermute x18, starting transfers between devices, shifted(): lax.ppermute(block, axis, [(i, (i + distance) % count) for i in range(cou...  31.1 us
    ppermute x18, waiting for transfers between devices, shifted(): lax.ppermute(block, axis, [(i, (i + distance) % count) for i in range(cou...  16.5 us
    pallas_call x2, Pallas kernels, projection(): pl.pallas_call(functools.partial(kernel, split), out_shape=[block] * (par...  9.14 us
    pallas_call x2, Pallas kernels, attention(): pl.pallas_call(functools.partial(attention_kernel, head, groups), out_sha...  8.01 us
    pallas_call x1, Pallas kernels, shards(): pl.pallas_call(functools.partial(second_output_kernel, split), out_shape=...  1.75 us
  transfers between devices with their start and end apart: 18, of which 8 were waited for; matrix products, arithmetic and copies ran while one was open for 0% of the time, Pallas kernels for 28%

profile of v9, /device:TPU:0, one launch (start us, length us, event | category | flops | bytes accessed | tf_op | source)
XLA Modules:
  0.0 69.7 jit_solution(5043509204447557077)
XLA Ops:
  0.0 1.1 %slice.4 = bf16[10,24,1280]{2,1,0:T(8,128)(2,1)S(1)} slice(bf16[10,40,1280]{2,1,0:T(8,128)(2,1)} %bitcast.2), slice={[0:10], [0:24], [0:1280]} | slice | bytes 1228800 | tf_op jit(solution)/shard_map/slice | solution.py:310
  1.1 0.0 copy-start
  1.1 0.0 copy-start.2
  1.1 0.0 copy-start.3
  1.2 3.0 %collective-permute-start.3 = (bf16[10,24,1280]{2,1,0:T(8,128)(2,1)S(1)}, bf16[10,24,1280]{2,1,0:T(8,128)(2,1)S(1)}, u32[]{:S(2)}, u32[]{:S(2)}) collective-permute-start(bf16[10,24,1280]{2,1,0:T(8,128)(2,1)S(1)} %slice.4), channel_id=1, source_target_pairs={{0,16},{4,20},{8,24},{12,28},{16,0},{20,4},{24,8},{28,12},{1,17},{... | collective-permute-start | bytes 1843208 | tf_op jit(solution)/shard_map/ppermute | solution.py:24
  4.2 4.8 %shard_map.55 = (bf16[160,512]{1,0:T(8,128)(2,1)}, bf16[160,512]{1,0:T(8,128)(2,1)}, bf16[160,512]{1,0:T(8,128)(2,1)}, bf16[160,512]{1,0:T(8,128)(2,1)}) custom-call(bf16[10,40,1280]{2,1,0:T(8,128)(2,1)} %bitcast.3, f32[1280]{0:T(1024)} %gain.3, bf16[1280,1920]{1,0:T(8,128)(2,1)} %weight.4), custom_call_target="tpu_custom_call" | custom-call | flops 786432000 | bytes 5734400 | tf_op jit(solution)/shard_map/pallas_call | solution.py:287
  9.0 2.7 %collective-permute-start = (bf16[160,512]{1,0:T(8,128)(2,1)}, bf16[160,512]{1,0:T(8,128)(2,1)S(1)}, u32[]{:S(2)}, u32[]{:S(2)}) collective-permute-start(bf16[160,512]{1,0:T(8,128)(2,1)} %get-tuple-element.38), channel_id=1, source_target_pairs={{0,2},{1,3},{2,0},{3,1},{4,6},{5,7},{6,4},{7,5},{8,10},{9,11},{10,... | collective-permute-start | bytes 491528 | tf_op jit(solution)/shard_map/ppermute | solution.py:24
  11.7 1.6 %collective-permute-start.1 = (bf16[160,512]{1,0:T(8,128)(2,1)}, bf16[160,512]{1,0:T(8,128)(2,1)S(1)}, u32[]{:S(2)}, u32[]{:S(2)}) collective-permute-start(bf16[160,512]{1,0:T(8,128)(2,1)} %get-tuple-element.39), channel_id=1, source_target_pairs={{0,1},{1,2},{2,3},{3,0},{4,5},{5,6},{6,7},{7,4},{8,9},{9,10},{10,1... | collective-permute-start | bytes 491528 | tf_op jit(solution)/shard_map/ppermute | solution.py:24
  13.3 0.0 copy-start.4
  13.3 2.2 %collective-permute-start.2 = (bf16[160,512]{1,0:T(8,128)(2,1)}, bf16[160,512]{1,0:T(8,128)(2,1)S(1)}, u32[]{:S(2)}, u32[]{:S(2)}) collective-permute-start(bf16[160,512]{1,0:T(8,128)(2,1)} %get-tuple-element.40), channel_id=1, source_target_pairs={{0,3},{1,0},{2,1},{3,2},{4,7},{5,4},{6,5},{7,6},{8,11},{9,8},{10,9... | collective-permute-start | bytes 491528 | tf_op jit(solution)/shard_map/ppermute | solution.py:24
  15.5 2.5 %collective-permute-done.3.eastern = bf16[10,24,1280]{2,1,0:T(8,128)(2,1)S(1)} collective-permute-done((bf16[10,24,1280]{2,1,0:T(8,128)(2,1)S(1)}, bf16[10,24,1280]{2,1,0:T(8,128)(2,1)S(1)}, u32[]{:S(2)}, u32[]{:S(2)}) %collective-permute-start.3) | collective-permute-done | bytes 614432 | tf_op jit(solution)/shard_map/ppermute | solution.py:24
  18.0 0.0 copy-done
  18.0 0.0 copy-done.2
  18.0 0.0 copy-done.3
  18.1 4.3 %shard_map.56 = (bf16[240,256]{1,0:T(8,128)(2,1)S(1)}, bf16[240,256]{1,0:T(8,128)(2,1)S(1)}, bf16[240,256]{1,0:T(8,128)(2,1)S(1)}, bf16[240,256]{1,0:T(8,128)(2,...) custom-call(bf16[10,40,1280]{2,1,0:T(8,128)(2,1)S(1)} %bitcast.4, ...), custom_call_target="tpu_custom_call" | custom-call | flops 1179648000 | bytes 6144000 | tf_op jit(solution)/shard_map/pallas_call | solution.py:287
  22.4 1.7 %collective-permute-done.refs_1_ = bf16[160,512]{1,0:T(8,128)(2,1)S(1)} collective-permute-done((bf16[160,512]{1,0:T(8,128)(2,1)}, bf16[160,512]{1,0:T(8,128)(2,1)S(1)}, u32[]{:S(2)}, u32[]{:S(2)}) %collective-permute-start) | collective-permute-done | bytes 163872 | tf_op jit(solution)/shard_map/ppermute | solution.py:24
  24.1 1.2 %collective-permute-start.4 = (bf16[240,256]{1,0:T(8,128)(2,1)S(1)}, bf16[240,256]{1,0:T(8,128)(2,1)S(1)}, u32[]{:S(2)}, u32[]{:S(2)}) collective-permute-start(bf16[240,256]{1,0:T(8,128)(2,1)S(1)} %get-tuple-element.43), channel_id=1, source_target_pairs={{0,2},{1,3},{2,0},{3,1},{4,6},{5,7},{6,4},{7,5},{8,10},{9,11},{10,... | collective-permute-start | bytes 368648 | tf_op jit(solution)/shard_map/ppermute | solution.py:24
  25.3 0.0 collective-permute-done.1.refs_2_
  25.3 4.6 %collective-permute-start.5 = (bf16[240,256]{1,0:T(8,128)(2,1)S(1)}, bf16[240,256]{1,0:T(8,128)(2,1)S(1)}, u32[]{:S(2)}, u32[]{:S(2)}) collective-permute-start(bf16[240,256]{1,0:T(8,128)(2,1)S(1)} %get-tuple-element.45), channel_id=1, source_target_pairs={{0,1},{1,2},{2,3},{3,0},{4,5},{5,6},{6,7},{7,4},{8,9},{9,10},{10,1... | collective-permute-start | bytes 368648 | tf_op jit(solution)/shard_map/ppermute | solution.py:24
  29.8 0.0 collective-permute-done.2.refs_3_
  29.8 0.0 collective-permute-start.6
  29.8 4.7 %collective-permute-done.4.refs_5_ = bf16[240,256]{1,0:T(8,128)(2,1)S(1)} collective-permute-done((bf16[240,256]{1,0:T(8,128)(2,1)S(1)}, bf16[240,256]{1,0:T(8,128)(2,1)S(1)}, u32[]{:S(2)}, u32[]{:S(2)}) %collective-permute-start.4) | collective-permute-done | bytes 122912 | tf_op jit(solution)/shard_map/ppermute | solution.py:24
  34.6 0.2 collective-permute-start.11
  34.8 0.0 collective-permute-done.5.refs_6_
  34.8 6.0 %collective-permute-start.12 = (bf16[240,256]{1,0:T(8,128)(2,1)S(1)}, bf16[240,256]{1,0:T(8,128)(2,1)S(1)}, u32[]{:S(2)}, u32[]{:S(2)}) collective-permute-start(bf16[240,256]{1,0:T(8,128)(2,1)S(1)} %get-tuple-element.60), channel_id=1, source_target_pairs={{0,1},{1,2},{2,3},{3,0},{4,5},{5,6},{6,7},{7,4},{8,9},{9,10},{10,1... | collective-permute-start | bytes 368648 | tf_op jit(solution)/shard_map/ppermute | solution.py:24
  40.8 0.0 collective-permute-done.6.refs_7_
  40.8 0.0 collective-permute-start.13
  40.8 0.0 copy-done.4
  40.8 4.0 %shard_map.57 = (bf16[416,128]{1,0:T(8,128)(2,1)S(1)}, bf16[608,128]{1,0:T(8,128)(2,1)S(1)}) custom-call(bf16[160,512]{1,0:T(8,128)(2,1)S(1)} %copy-done.4, bf16[160,512]{1,0:T(8,128)(2,1)S(1)} %collective-permute-done.refs_1_, bf16[160,512]{1,0:T(8,128)(2,1)S(1)} %collective-permute-done.1.refs_2_, bf16[160,512]{1,0:T(8,128)(2,1)S(1)} %collective-permute-done.2.refs_3_, ...), custom_call_target="tpu_custom_call" | custom-call | flops 2621440000 | bytes 1228800 | tf_op jit(solution)/shard_map/pallas_call | solution.py:334
  44.8 0.6 collective-permute-start.7
  45.4 1.1 %collective-permute-done.11.refs_5_ = bf16[240,256]{1,0:T(8,128)(2,1)S(1)} collective-permute-done((bf16[240,256]{1,0:T(8,128)(2,1)S(1)}, bf16[240,256]{1,0:T(8,128)(2,1)S(1)}, u32[]{:S(2)}, u32[]{:S(2)}) %collective-permute-start.11) | collective-permute-done | bytes 122912 | tf_op jit(solution)/shard_map/ppermute | solution.py:24
  46.5 0.0 collective-permute-done.12.refs_6_
  46.5 1.5 %collective-permute-done.13.refs_7_ = bf16[240,256]{1,0:T(8,128)(2,1)S(1)} collective-permute-done((bf16[240,256]{1,0:T(8,128)(2,1)S(1)}, bf16[240,256]{1,0:T(8,128)(2,1)S(1)}, u32[]{:S(2)}, u32[]{:S(2)}) %collective-permute-start.13) | collective-permute-done | bytes 122912 | tf_op jit(solution)/shard_map/ppermute | solution.py:24
  48.0 0.0 copy-start.1
  48.0 4.0 %shard_map.60 = (bf16[416,128]{1,0:T(8,128)(2,1)S(1)}, bf16[608,128]{1,0:T(8,128)(2,1)S(1)}) custom-call(bf16[160,512]{1,0:T(8,128)(2,1)S(1)} %copy-done.4, bf16[160,512]{1,0:T(8,128)(2,1)S(1)} %collective-permute-done.refs_1_, bf16[160,512]{1,0:T(8,128)(2,1)S(1)} %collective-permute-done.1.refs_2_, bf16[160,512]{1,0:T(8,128)(2,1)S(1)} %collective-permute-done.2.refs_3_, ...), custom_call_target="tpu_custom_call" | custom-call | flops 2621440000 | bytes 1228800 | tf_op jit(solution)/shard_map/pallas_call | solution.py:334
  52.0 0.1 collective-permute-start.14
  52.1 0.0 collective-permute-done.7.western
  52.1 0.6 shard_map.58
  52.7 3.4 %collective-permute-start.8 = (bf16[256,128]{1,0:T(8,128)(2,1)S(1)}, bf16[256,128]{1,0:T(8,128)(2,1)S(1)}, u32[]{:S(2)}, u32[]{:S(2)}) collective-permute-start(bf16[256,128]{1,0:T(8,128)(2,1)S(1)} %get-tuple-element.51), channel_id=1, source_target_pairs={{0,2},{1,3},{2,0},{3,1},{4,6},{5,7},{6,4},{7,5},{8,10},{9,11},{10,... | collective-permute-start | bytes 196616 | tf_op jit(solution)/shard_map/ppermute | solution.py:24
  56.1 0.9 %collective-permute-start.9 = (bf16[256,128]{1,0:T(8,128)(2,1)S(1)}, bf16[256,128]{1,0:T(8,128)(2,1)S(1)}, u32[]{:S(2)}, u32[]{:S(2)}) collective-permute-start(bf16[256,128]{1,0:T(8,128)(2,1)S(1)} %get-tuple-element.52), channel_id=1, source_target_pairs={{0,3},{1,0},{2,1},{3,2},{4,7},{5,4},{6,5},{7,6},{8,11},{9,8},{10,9... | collective-permute-start | bytes 196616 | tf_op jit(solution)/shard_map/ppermute | solution.py:24
  57.0 1.1 %collective-permute-start.10 = (bf16[256,128]{1,0:T(8,128)(2,1)S(1)}, bf16[256,128]{1,0:T(8,128)(2,1)S(1)}, u32[]{:S(2)}, u32[]{:S(2)}) collective-permute-start(bf16[256,128]{1,0:T(8,128)(2,1)S(1)} %get-tuple-element.53), channel_id=1, source_target_pairs={{0,1},{1,2},{2,3},{3,0},{4,5},{5,6},{6,7},{7,4},{8,9},{9,10},{10,1... | collective-permute-start | bytes 196616 | tf_op jit(solution)/shard_map/ppermute | solution.py:24
  58.1 0.0 collective-permute-done.14.western
  58.1 0.6 shard_map.61
  58.8 1.4 %collective-permute-start.15 = (bf16[256,128]{1,0:T(8,128)(2,1)S(1)}, bf16[256,128]{1,0:T(8,128)(2,1)S(1)}, u32[]{:S(2)}, u32[]{:S(2)}) collective-permute-start(bf16[256,128]{1,0:T(8,128)(2,1)S(1)} %get-tuple-element.66), channel_id=1, source_target_pairs={{0,2},{1,3},{2,0},{3,1},{4,6},{5,7},{6,4},{7,5},{8,10},{9,11},{10,... | collective-permute-start | bytes 196616 | tf_op jit(solution)/shard_map/ppermute | solution.py:24
  60.2 1.7 %collective-permute-start.16 = (bf16[256,128]{1,0:T(8,128)(2,1)S(1)}, bf16[256,128]{1,0:T(8,128)(2,1)S(1)}, u32[]{:S(2)}, u32[]{:S(2)}) collective-permute-start(bf16[256,128]{1,0:T(8,128)(2,1)S(1)} %get-tuple-element.67), channel_id=1, source_target_pairs={{0,3},{1,0},{2,1},{3,2},{4,7},{5,4},{6,5},{7,6},{8,11},{9,8},{10,9... | collective-permute-start | bytes 196616 | tf_op jit(solution)/shard_map/ppermute | solution.py:24
  61.9 0.0 collective-permute-done.8.refs_1_
  61.9 0.3 collective-permute-start.17
  62.2 0.0 collective-permute-done.9.refs_2_
  62.2 1.2 %collective-permute-done.10.refs_3_ = bf16[256,128]{1,0:T(8,128)(2,1)S(1)} collective-permute-done((bf16[256,128]{1,0:T(8,128)(2,1)S(1)}, bf16[256,128]{1,0:T(8,128)(2,1)S(1)}, u32[]{:S(2)}, u32[]{:S(2)}) %collective-permute-start.10) | collective-permute-done | bytes 65568 | tf_op jit(solution)/shard_map/ppermute | solution.py:24
  63.4 0.0 copy-done.1
  63.4 0.8 %shard_map.59 = (f32[10,40,1280]{2,1,0:T(8,128)S(1)}, bf16[512,1280]{1,0:T(8,128)(2,1)S(1)}) custom-call(bf16[10,40,1280]{2,1,0:T(8,128)(2,1)S(1)} %bitcast.5, bf16[640,1280]{1,0:T(8,128)(2,1)S(1)} %copy-done.1, bf16[256,128]{1,0:T(8,128)(2,1)S(1)} %get-tuple-element.50.refs_0_, bf16[256,128]{1,0:T(8,128)(2,1)S(1)} %collective-permute-done.8.refs_1_, ...), custom_call_target="tpu_custom_call" | custom-call | flops 524288000 | bytes 3891200 | tf_op jit(solution)/shard_map/pallas_call | solution.py:379
  64.2 1.9 %collective-permute-done.15.refs_1_ = bf16[256,128]{1,0:T(8,128)(2,1)S(1)} collective-permute-done((bf16[256,128]{1,0:T(8,128)(2,1)S(1)}, bf16[256,128]{1,0:T(8,128)(2,1)S(1)}, u32[]{:S(2)}, u32[]{:S(2)}) %collective-permute-start.15) | collective-permute-done | bytes 65568 | tf_op jit(solution)/shard_map/ppermute | solution.py:24
  66.1 0.0 collective-permute-done.16.refs_2_
  66.1 1.8 %collective-permute-done.17.refs_3_ = bf16[256,128]{1,0:T(8,128)(2,1)S(1)} collective-permute-done((bf16[256,128]{1,0:T(8,128)(2,1)S(1)}, bf16[256,128]{1,0:T(8,128)(2,1)S(1)}, u32[]{:S(2)}, u32[]{:S(2)}) %collective-permute-start.17) | collective-permute-done | bytes 65568 | tf_op jit(solution)/shard_map/ppermute | solution.py:24
  67.9 1.8 %shard_map.62 = bf16[10,40,1280]{2,1,0:T(8,128)(2,1)} custom-call(f32[10,40,1280]{2,1,0:T(8,128)S(1)} %get-tuple-element.54.partial, bf16[512,1280]{1,0:T(8,128)(2,1)S(1)} %get-tuple-element.55.weight, bf16[256,128]{1,0:T(8,128)(2,1)S(1)} %get-tuple-element.65.refs_0_, bf16[256,128]{1,0:T(8,128)(2,1)S(1)} %collective-permute-done.15.refs_1_, ...), custom_call_target="tpu_custom_call" | custom-call | flops 524288000 | bytes 3891200 | tf_op jit(solution)/shard_map/pallas_call | solution.py:391
Async XLA Ops:
  1.1 16.9 %copy-start = (bf16[1,10,40,1280]{3,2,1,0:T(8,128)(2,1)S(1)}, bf16[1,10,40,1280]{3,2,1,0:T(8,128)(2,1)}, u32[]{:S(2)}) copy-start(bf16[1,10,40,1280]{3,2,1,0:T(8,128)(2,1)} %param.5) | copy-start | bytes 3072004
  1.1 16.9 %copy-start.2 = (f32[1280]{0:T(1024)S(1)}, f32[1280]{0:T(1024)}, u32[]{:S(2)}) copy-start(f32[1280]{0:T(1024)} %gain.3) | copy-start | bytes 15364
  1.1 16.9 %copy-start.3 = (s32[4]{0:T(128)S(1)}, s32[4]{0:T(128)}, u32[]{:S(2)}) copy-start(s32[4]{0:T(128)} %lon_shift.5) | copy-start | bytes 52
  1.2 16.9 %collective-permute-start.3 = (bf16[10,24,1280]{2,1,0:T(8,128)(2,1)S(1)}, bf16[10,24,1280]{2,1,0:T(8,128)(2,1)S(1)}, u32[]{:S(2)}, u32[]{:S(2)}) collective-permute-start(bf16[10,24,1280]{2,1,0:T(8,128)(2,1)S(1)} %slice.4), channel_id=1, source_target_pairs={{0,16},{4,20},{8,24},{12,28},{16,0},{20,4},{24,8},{28,12},{1,17},{... | collective-permute-start | bytes 1843208 | tf_op jit(solution)/shard_map/ppermute | solution.py:24
  9.0 15.0 %collective-permute-start = (bf16[160,512]{1,0:T(8,128)(2,1)}, bf16[160,512]{1,0:T(8,128)(2,1)S(1)}, u32[]{:S(2)}, u32[]{:S(2)}) collective-permute-start(bf16[160,512]{1,0:T(8,128)(2,1)} %get-tuple-element.38), channel_id=1, source_target_pairs={{0,2},{1,3},{2,0},{3,1},{4,6},{5,7},{6,4},{7,5},{8,10},{9,11},{10,... | collective-permute-start | bytes 491528 | tf_op jit(solution)/shard_map/ppermute | solution.py:24
  11.7 13.6 %collective-permute-start.1 = (bf16[160,512]{1,0:T(8,128)(2,1)}, bf16[160,512]{1,0:T(8,128)(2,1)S(1)}, u32[]{:S(2)}, u32[]{:S(2)}) collective-permute-start(bf16[160,512]{1,0:T(8,128)(2,1)} %get-tuple-element.39), channel_id=1, source_target_pairs={{0,1},{1,2},{2,3},{3,0},{4,5},{5,6},{6,7},{7,4},{8,9},{9,10},{10,1... | collective-permute-start | bytes 491528 | tf_op jit(solution)/shard_map/ppermute | solution.py:24
  13.3 27.6 %copy-start.4 = (bf16[160,512]{1,0:T(8,128)(2,1)S(1)}, bf16[160,512]{1,0:T(8,128)(2,1)}, u32[]{:S(2)}) copy-start(bf16[160,512]{1,0:T(8,128)(2,1)} %get-tuple-element.37.refs_0_) | copy-start | bytes 491524
  13.3 16.6 %collective-permute-start.2 = (bf16[160,512]{1,0:T(8,128)(2,1)}, bf16[160,512]{1,0:T(8,128)(2,1)S(1)}, u32[]{:S(2)}, u32[]{:S(2)}) collective-permute-start(bf16[160,512]{1,0:T(8,128)(2,1)} %get-tuple-element.40), channel_id=1, source_target_pairs={{0,3},{1,0},{2,1},{3,2},{4,7},{5,4},{6,5},{7,6},{8,11},{9,8},{10,9... | collective-permute-start | bytes 491528 | tf_op jit(solution)/shard_map/ppermute | solution.py:24
  24.1 10.5 %collective-permute-start.4 = (bf16[240,256]{1,0:T(8,128)(2,1)S(1)}, bf16[240,256]{1,0:T(8,128)(2,1)S(1)}, u32[]{:S(2)}, u32[]{:S(2)}) collective-permute-start(bf16[240,256]{1,0:T(8,128)(2,1)S(1)} %get-tuple-element.43), channel_id=1, source_target_pairs={{0,2},{1,3},{2,0},{3,1},{4,6},{5,7},{6,4},{7,5},{8,10},{9,11},{10,... | collective-permute-start | bytes 368648 | tf_op jit(solution)/shard_map/ppermute | solution.py:24
  25.3 9.5 %collective-permute-start.5 = (bf16[240,256]{1,0:T(8,128)(2,1)S(1)}, bf16[240,256]{1,0:T(8,128)(2,1)S(1)}, u32[]{:S(2)}, u32[]{:S(2)}) collective-permute-start(bf16[240,256]{1,0:T(8,128)(2,1)S(1)} %get-tuple-element.45), channel_id=1, source_target_pairs={{0,1},{1,2},{2,3},{3,0},{4,5},{5,6},{6,7},{7,4},{8,9},{9,10},{10,1... | collective-permute-start | bytes 368648 | tf_op jit(solution)/shard_map/ppermute | solution.py:24
  29.8 11.0 %collective-permute-start.6 = (bf16[240,256]{1,0:T(8,128)(2,1)S(1)}, bf16[240,256]{1,0:T(8,128)(2,1)S(1)}, u32[]{:S(2)}, u32[]{:S(2)}) collective-permute-start(bf16[240,256]{1,0:T(8,128)(2,1)S(1)} %get-tuple-element.47), channel_id=1, source_target_pairs={{0,3},{1,0},{2,1},{3,2},{4,7},{5,4},{6,5},{7,6},{8,11},{9,8},{10,9... | collective-permute-start | bytes 368648 | tf_op jit(solution)/shard_map/ppermute | solution.py:24
  34.6 11.9 %collective-permute-start.11 = (bf16[240,256]{1,0:T(8,128)(2,1)S(1)}, bf16[240,256]{1,0:T(8,128)(2,1)S(1)}, u32[]{:S(2)}, u32[]{:S(2)}) collective-permute-start(bf16[240,256]{1,0:T(8,128)(2,1)S(1)} %get-tuple-element.58), channel_id=1, source_target_pairs={{0,2},{1,3},{2,0},{3,1},{4,6},{5,7},{6,4},{7,5},{8,10},{9,11},{10,... | collective-permute-start | bytes 368648 | tf_op jit(solution)/shard_map/ppermute | solution.py:24
  34.8 11.7 %collective-permute-start.12 = (bf16[240,256]{1,0:T(8,128)(2,1)S(1)}, bf16[240,256]{1,0:T(8,128)(2,1)S(1)}, u32[]{:S(2)}, u32[]{:S(2)}) collective-permute-start(bf16[240,256]{1,0:T(8,128)(2,1)S(1)} %get-tuple-element.60), channel_id=1, source_target_pairs={{0,1},{1,2},{2,3},{3,0},{4,5},{5,6},{6,7},{7,4},{8,9},{9,10},{10,1... | collective-permute-start | bytes 368648 | tf_op jit(solution)/shard_map/ppermute | solution.py:24
  40.8 7.2 %collective-permute-start.13 = (bf16[240,256]{1,0:T(8,128)(2,1)S(1)}, bf16[240,256]{1,0:T(8,128)(2,1)S(1)}, u32[]{:S(2)}, u32[]{:S(2)}) collective-permute-start(bf16[240,256]{1,0:T(8,128)(2,1)S(1)} %get-tuple-element.62), channel_id=1, source_target_pairs={{0,3},{1,0},{2,1},{3,2},{4,7},{5,4},{6,5},{7,6},{8,11},{9,8},{10,9... | collective-permute-start | bytes 368648 | tf_op jit(solution)/shard_map/ppermute | solution.py:24
  44.8 7.3 %collective-permute-start.7 = (bf16[608,128]{1,0:T(8,128)(2,1)S(1)}, bf16[608,128]{1,0:T(8,128)(2,1)S(1)}, u32[]{:S(2)}, u32[]{:S(2)}) collective-permute-start(bf16[608,128]{1,0:T(8,128)(2,1)S(1)} %get-tuple-element.49.mixed), channel_id=1, source_target_pairs={{0,16},{4,20},{8,24},{12,28},{16,0},{20,4},{24,8},{28,12},{1,17},{... | collective-permute-start | bytes 466952 | tf_op jit(solution)/shard_map/ppermute | solution.py:24
  48.0 15.4 %copy-start.1 = (bf16[640,1280]{1,0:T(8,128)(2,1)S(1)}, bf16[640,1280]{1,0:T(8,128)(2,1)}, u32[]{:S(2)}) copy-start(bf16[640,1280]{1,0:T(8,128)(2,1)} %weight.5) | copy-start | bytes 4915204
  52.0 6.1 %collective-permute-start.14 = (bf16[608,128]{1,0:T(8,128)(2,1)S(1)}, bf16[608,128]{1,0:T(8,128)(2,1)S(1)}, u32[]{:S(2)}, u32[]{:S(2)}) collective-permute-start(bf16[608,128]{1,0:T(8,128)(2,1)S(1)} %get-tuple-element.64.mixed), channel_id=1, source_target_pairs={{0,16},{4,20},{8,24},{12,28},{16,0},{20,4},{24,8},{28,12},{1,17},{... | collective-permute-start | bytes 466952 | tf_op jit(solution)/shard_map/ppermute | solution.py:24
  52.7 9.1 %collective-permute-start.8 = (bf16[256,128]{1,0:T(8,128)(2,1)S(1)}, bf16[256,128]{1,0:T(8,128)(2,1)S(1)}, u32[]{:S(2)}, u32[]{:S(2)}) collective-permute-start(bf16[256,128]{1,0:T(8,128)(2,1)S(1)} %get-tuple-element.51), channel_id=1, source_target_pairs={{0,2},{1,3},{2,0},{3,1},{4,6},{5,7},{6,4},{7,5},{8,10},{9,11},{10,... | collective-permute-start | bytes 196616 | tf_op jit(solution)/shard_map/ppermute | solution.py:24
  56.1 6.1 %collective-permute-start.9 = (bf16[256,128]{1,0:T(8,128)(2,1)S(1)}, bf16[256,128]{1,0:T(8,128)(2,1)S(1)}, u32[]{:S(2)}, u32[]{:S(2)}) collective-permute-start(bf16[256,128]{1,0:T(8,128)(2,1)S(1)} %get-tuple-element.52), channel_id=1, source_target_pairs={{0,3},{1,0},{2,1},{3,2},{4,7},{5,4},{6,5},{7,6},{8,11},{9,8},{10,9... | collective-permute-start | bytes 196616 | tf_op jit(solution)/shard_map/ppermute | solution.py:24
  57.0 6.4 %collective-permute-start.10 = (bf16[256,128]{1,0:T(8,128)(2,1)S(1)}, bf16[256,128]{1,0:T(8,128)(2,1)S(1)}, u32[]{:S(2)}, u32[]{:S(2)}) collective-permute-start(bf16[256,128]{1,0:T(8,128)(2,1)S(1)} %get-tuple-element.53), channel_id=1, source_target_pairs={{0,1},{1,2},{2,3},{3,0},{4,5},{5,6},{6,7},{7,4},{8,9},{9,10},{10,1... | collective-permute-start | bytes 196616 | tf_op jit(solution)/shard_map/ppermute | solution.py:24
  58.8 7.4 %collective-permute-start.15 = (bf16[256,128]{1,0:T(8,128)(2,1)S(1)}, bf16[256,128]{1,0:T(8,128)(2,1)S(1)}, u32[]{:S(2)}, u32[]{:S(2)}) collective-permute-start(bf16[256,128]{1,0:T(8,128)(2,1)S(1)} %get-tuple-element.66), channel_id=1, source_target_pairs={{0,2},{1,3},{2,0},{3,1},{4,6},{5,7},{6,4},{7,5},{8,10},{9,11},{10,... | collective-permute-start | bytes 196616 | tf_op jit(solution)/shard_map/ppermute | solution.py:24
  60.2 5.9 %collective-permute-start.16 = (bf16[256,128]{1,0:T(8,128)(2,1)S(1)}, bf16[256,128]{1,0:T(8,128)(2,1)S(1)}, u32[]{:S(2)}, u32[]{:S(2)}) collective-permute-start(bf16[256,128]{1,0:T(8,128)(2,1)S(1)} %get-tuple-element.67), channel_id=1, source_target_pairs={{0,3},{1,0},{2,1},{3,2},{4,7},{5,4},{6,5},{7,6},{8,11},{9,8},{10,9... | collective-permute-start | bytes 196616 | tf_op jit(solution)/shard_map/ppermute | solution.py:24
  61.9 6.1 %collective-permute-start.17 = (bf16[256,128]{1,0:T(8,128)(2,1)S(1)}, bf16[256,128]{1,0:T(8,128)(2,1)S(1)}, u32[]{:S(2)}, u32[]{:S(2)}) collective-permute-start(bf16[256,128]{1,0:T(8,128)(2,1)S(1)} %get-tuple-element.68), channel_id=1, source_target_pairs={{0,1},{1,2},{2,3},{3,0},{4,5},{5,6},{6,7},{7,4},{8,9},{9,10},{10,1... | collective-permute-start | bytes 196616 | tf_op jit(solution)/shard_map/ppermute | solution.py:24

commit v10 on v8

--- a/solution.py
+++ b/solution.py
@@ -192,38 +192,26 @@
         out[...] = jnp.concatenate(packed, axis=0).astype(jnp.bfloat16)
 
 
-def select_kernel(split, count, lon_shift, kept, mixed, western, *outs):
+def select_kernel(split, count, groups, lon_shift, mixed, western, *refs):
+    kept, outs = refs[:-groups], refs[-groups:]
     taken = lax.rem(packed_tokens(count), split) < column_offset(lon_shift)
     own, west = mixed[...].astype(jnp.float32), western[...].astype(jnp.float32)
-    rest = kept[...].astype(jnp.float32)
-    left, right = own.shape[0] // len(outs), rest.shape[0] // len(outs)
+    rests = [rest[...].astype(jnp.float32) for rest in kept]
+    size = own.shape[0] // groups
     for group, out in enumerate(outs):
-        rows = slice(group * left, (group + 1) * left)
-        chosen = jnp.where(taken, west[rows], own[rows])
-        out[...] = jnp.concatenate(
-            [chosen, rest[group * right : (group + 1) * right]], axis=0
-        ).astype(jnp.bfloat16)
-
-
-def projected_rows(split, shape, blocks, weight):
-    rows, columns, _ = shape
-    kept_count, mixed_count = rows * (columns - split), rows * split
-    total = packed_rows(mixed_count)[0]
-    attended = []
-    for block in blocks:
-        block = block[...].astype(jnp.float32)
-        left, right = unpack(block[:total], mixed_count), unpack(block[total:], kept_count)
-        attended.append(jnp.concatenate([right, left], axis=0))
-    attended = jnp.concatenate(attended, axis=1).astype(jnp.bfloat16)
-    projected = jnp.dot(attended, weight[...], preferred_element_type=jnp.float32)
-    return by_column(projected, rows, columns, split)
-
-
-def by_column(projected, rows, columns, split):
-    kept_count = rows * (columns - split)
-    right = projected[:kept_count].reshape(rows, columns - split, -1)
-    left = projected[kept_count:].reshape(rows, split, -1)
-    return jnp.concatenate([left, right], axis=1)
+        rows = slice(group * size, (group + 1) * size)
+        pieces = [jnp.where(taken, west[rows], own[rows])]
+        for rest in rests:
+            part = rest.shape[0] // groups
+            pieces.append(rest[group * part : (group + 1) * part])
+        out[...] = jnp.concatenate(pieces, axis=0).astype(jnp.bfloat16)
+
+
+def projected(blocks, first, count, weight, shape):
+    total = packed_rows(count)[0]
+    columns = [unpack(block[first : first + total], count) for block in blocks]
+    attended = jnp.concatenate(columns, axis=1).astype(jnp.bfloat16)
+    return jnp.dot(attended, weight[...], preferred_element_type=jnp.float32).reshape(shape)
 
 
 def first_output_kernel(split, groups, field, weight, *refs):
@@ -237,14 +225,29 @@
             ordered[slot * LANES + HD : (slot + 1) * LANES] = jnp.zeros(
                 (LANES - HD, features), jnp.bfloat16
             )
-    projected = projected_rows(split, field.shape, blocks, first)
-    out[...] = field[...].astype(jnp.float32) + projected
+    rows, columns, _ = field.shape
+    kept_count, mixed_count = rows * (columns - split), rows * split
+    blocks = [block[...].astype(jnp.float32) for block in blocks]
+    tokens = field[...].astype(jnp.float32)
+    at = packed_rows(mixed_count)[0]
+    shape = (rows, split, features)
+    left = tokens[:, :split] + projected(blocks, 0, mixed_count, first, shape)
+    shape = (rows, columns - split, features)
+    right = tokens[:, split:] + projected(blocks, at, kept_count, first, shape)
+    at += packed_rows(kept_count)[0]
+    right += projected(blocks, at, kept_count, second, shape)
+    out[...] = jnp.concatenate([left, right], axis=1)
 
 
 def second_output_kernel(split, partial, weight, *refs):
     *blocks, out = refs
-    projected = projected_rows(split, partial.shape, blocks, weight)
-    out[...] = (partial[...] + projected).astype(jnp.bfloat16)
+    rows, _, features = partial.shape
+    blocks = [block[...].astype(jnp.float32) for block in blocks]
+    tokens = partial[...]
+    left = projected(blocks, 0, rows * split, weight, (rows, split, features))
+    out[...] = jnp.concatenate(
+        [tokens[:, :split] + left, tokens[:, split:]], axis=1
+    ).astype(jnp.bfloat16)
 
 
 def whole(count):
@@ -336,22 +339,24 @@
             ),
         )(*blocks)
 
-    def back(kept_values, mixed_values):
+    def back(mixed_values, *kept_values):
         western = shifted(mixed_values, "win", LAT_WINDOWS)
         selected = pl.pallas_call(
-            functools.partial(select_kernel, split, mixed_count),
-            out_shape=[block(mixed_packed + kept_packed)] * groups,
-            in_specs=[smem] + whole(3),
+            functools.partial(select_kernel, split, mixed_count, groups),
+            out_shape=[block(mixed_packed + len(kept_values) * kept_packed)] * groups,
+            in_specs=[smem] + whole(2 + len(kept_values)),
             out_specs=whole(groups),
             compiler_params=limit(16),
             cost_estimate=pl.CostEstimate(
                 flops=total * LANES * 20, bytes_accessed=8 * total * LANES, transcendentals=0
             ),
-        )(lon_shift, kept_values, mixed_values, western)
+        )(lon_shift, mixed_values, western, *kept_values)
         return spread(selected, -1)
 
-    first = back(*attention(0, *kept, *first_mixed))
-    second = back(*attention(1, *kept, *second_mixed))
+    first_kept_values, first_mixed_values = attention(0, *kept, *first_mixed)
+    second_kept_values, second_mixed_values = attention(1, *kept, *second_mixed)
+    first = back(first_mixed_values, first_kept_values, second_kept_values)
+    second = back(second_mixed_values)
 
     cost = pl.CostEstimate(
         flops=2 * rows * columns * groups * LANES * features,

time: 69.6 us -> 69.1 us (level)
  waiting for transfers between devices: 15.7 us -> 12.8 us
  starting transfers between devices: 31.6 us -> 34 us
    ppermute x18, waiting for transfers between devices: 15.7 us -> 12.8 us  [shifted(): lax.ppermute(block, axis, [(i, (i + distance) % count) for i in range(cou...]
    ppermute x18, starting transfers between devices: 31.6 us -> 34 us  [shifted(): lax.ppermute(block, axis, [(i, (i + distance) % count) for i in range(cou...]
  transfers between devices with their start and end apart: 18 -> 18, of which waited for: 9 -> 8; matrix products, arithmetic and copies ran while one was open for 0% -> 0% of each run, Pallas kernels for 28% -> 28%
where the time goes in v10:
time: 69.1 us; the launch traced here: 68.9 us
  starting transfers between devices  34 us (49%)
  Pallas kernels  20.9 us (30%)
  waiting for transfers between devices  12.8 us (19%)
  local copies, waits for them, and re-layouts  1.14 us (2%)
    ppermute x18, starting transfers between devices, shifted(): lax.ppermute(block, axis, [(i, (i + distance) % count) for i in range(cou...  34 us
    ppermute x18, waiting for transfers between devices, shifted(): lax.ppermute(block, axis, [(i, (i + distance) % count) for i in range(cou...  12.8 us
    pallas_call x2, Pallas kernels, projection(): pl.pallas_call(functools.partial(kernel, split), out_shape=[block] * (par...  9.09 us
    pallas_call x2, Pallas kernels, attention(): pl.pallas_call(functools.partial(attention_kernel, head, groups), out_sha...  8.01 us
    pallas_call x1, Pallas kernels, shards(): pl.pallas_call(functools.partial(second_output_kernel, split), out_shape=...  1.52 us
  transfers between devices with their start and end apart: 18, of which 8 were waited for; matrix products, arithmetic and copies ran while one was open for 0% of the time, Pallas kernels for 28%

profile of v10, /device:TPU:0, one launch (start us, length us, event | category | flops | bytes accessed | tf_op | source)
XLA Modules:
  0.0 68.9 jit_solution(8113689801043677411)
XLA Ops:
  0.0 1.1 %slice.4 = bf16[10,24,1280]{2,1,0:T(8,128)(2,1)S(1)} slice(bf16[10,40,1280]{2,1,0:T(8,128)(2,1)} %bitcast.2), slice={[0:10], [0:24], [0:1280]} | slice | bytes 1228800 | tf_op jit(solution)/shard_map/slice | solution.py:296
  1.1 0.0 copy-start
  1.1 0.0 copy-start.2
  1.1 0.0 copy-start.3
  1.2 3.0 %collective-permute-start.3 = (bf16[10,24,1280]{2,1,0:T(8,128)(2,1)S(1)}, bf16[10,24,1280]{2,1,0:T(8,128)(2,1)S(1)}, u32[]{:S(2)}, u32[]{:S(2)}) collective-permute-start(bf16[10,24,1280]{2,1,0:T(8,128)(2,1)S(1)} %slice.4), channel_id=1, source_target_pairs={{0,16},{4,20},{8,24},{12,28},{16,0},{20,4},{24,8},{28,12},{1,17},{... | collective-permute-start | bytes 1843208 | tf_op jit(solution)/shard_map/ppermute | solution.py:24
  4.2 4.8 %shard_map.55 = (bf16[160,512]{1,0:T(8,128)(2,1)}, bf16[160,512]{1,0:T(8,128)(2,1)}, bf16[160,512]{1,0:T(8,128)(2,1)}, bf16[160,512]{1,0:T(8,128)(2,1)}) custom-call(bf16[10,40,1280]{2,1,0:T(8,128)(2,1)} %bitcast.3, f32[1280]{0:T(1024)} %gain.3, bf16[1280,1920]{1,0:T(8,128)(2,1)} %weight.4), custom_call_target="tpu_custom_call" | custom-call | flops 786432000 | bytes 5734400 | tf_op jit(solution)/shard_map/pallas_call | solution.py:273
  9.0 1.6 %collective-permute-start = (bf16[160,512]{1,0:T(8,128)(2,1)}, bf16[160,512]{1,0:T(8,128)(2,1)S(1)}, u32[]{:S(2)}, u32[]{:S(2)}) collective-permute-start(bf16[160,512]{1,0:T(8,128)(2,1)} %get-tuple-element.38), channel_id=1, source_target_pairs={{0,1},{1,2},{2,3},{3,0},{4,5},{5,6},{6,7},{7,4},{8,9},{9,10},{10,1... | collective-permute-start | bytes 491528 | tf_op jit(solution)/shard_map/ppermute | solution.py:24
  10.6 2.6 %collective-permute-start.1 = (bf16[160,512]{1,0:T(8,128)(2,1)}, bf16[160,512]{1,0:T(8,128)(2,1)S(1)}, u32[]{:S(2)}, u32[]{:S(2)}) collective-permute-start(bf16[160,512]{1,0:T(8,128)(2,1)} %get-tuple-element.39), channel_id=1, source_target_pairs={{0,2},{1,3},{2,0},{3,1},{4,6},{5,7},{6,4},{7,5},{8,10},{9,11},{10,... | collective-permute-start | bytes 491528 | tf_op jit(solution)/shard_map/ppermute | solution.py:24
  13.2 0.0 copy-start.4
  13.2 1.3 %collective-permute-start.2 = (bf16[160,512]{1,0:T(8,128)(2,1)}, bf16[160,512]{1,0:T(8,128)(2,1)S(1)}, u32[]{:S(2)}, u32[]{:S(2)}) collective-permute-start(bf16[160,512]{1,0:T(8,128)(2,1)} %get-tuple-element.40), channel_id=1, source_target_pairs={{0,3},{1,0},{2,1},{3,2},{4,7},{5,4},{6,5},{7,6},{8,11},{9,8},{10,9... | collective-permute-start | bytes 491528 | tf_op jit(solution)/shard_map/ppermute | solution.py:24
  14.6 3.5 %collective-permute-done.3.eastern = bf16[10,24,1280]{2,1,0:T(8,128)(2,1)S(1)} collective-permute-done((bf16[10,24,1280]{2,1,0:T(8,128)(2,1)S(1)}, bf16[10,24,1280]{2,1,0:T(8,128)(2,1)S(1)}, u32[]{:S(2)}, u32[]{:S(2)}) %collective-permute-start.3) | collective-permute-done | bytes 614432 | tf_op jit(solution)/shard_map/ppermute | solution.py:24
  18.0 0.0 copy-done
  18.0 0.0 copy-done.2
  18.0 0.0 copy-done.3
  18.1 4.3 %shard_map.56 = (bf16[240,256]{1,0:T(8,128)(2,1)S(1)}, bf16[240,256]{1,0:T(8,128)(2,1)S(1)}, bf16[240,256]{1,0:T(8,128)(2,1)S(1)}, bf16[240,256]{1,0:T(8,128)(2,...) custom-call(bf16[10,40,1280]{2,1,0:T(8,128)(2,1)S(1)} %bitcast.4, ...), custom_call_target="tpu_custom_call" | custom-call | flops 1179648000 | bytes 6144000 | tf_op jit(solution)/shard_map/pallas_call | solution.py:273
  22.4 0.0 collective-permute-done.refs_1_
  22.4 1.9 %collective-permute-start.4 = (bf16[240,256]{1,0:T(8,128)(2,1)S(1)}, bf16[240,256]{1,0:T(8,128)(2,1)S(1)}, u32[]{:S(2)}, u32[]{:S(2)}) collective-permute-start(bf16[240,256]{1,0:T(8,128)(2,1)S(1)} %get-tuple-element.43), channel_id=1, source_target_pairs={{0,1},{1,2},{2,3},{3,0},{4,5},{5,6},{6,7},{7,4},{8,9},{9,10},{10,1... | collective-permute-start | bytes 368648 | tf_op jit(solution)/shard_map/ppermute | solution.py:24
  24.2 0.0 collective-permute-done.1.refs_2_
  24.2 2.6 %collective-permute-start.5 = (bf16[240,256]{1,0:T(8,128)(2,1)S(1)}, bf16[240,256]{1,0:T(8,128)(2,1)S(1)}, u32[]{:S(2)}, u32[]{:S(2)}) collective-permute-start(bf16[240,256]{1,0:T(8,128)(2,1)S(1)} %get-tuple-element.45), channel_id=1, source_target_pairs={{0,2},{1,3},{2,0},{3,1},{4,6},{5,7},{6,4},{7,5},{8,10},{9,11},{10,... | collective-permute-start | bytes 368648 | tf_op jit(solution)/shard_map/ppermute | solution.py:24
  26.8 0.0 collective-permute-done.2.refs_3_
  26.8 3.4 %collective-permute-start.6 = (bf16[240,256]{1,0:T(8,128)(2,1)S(1)}, bf16[240,256]{1,0:T(8,128)(2,1)S(1)}, u32[]{:S(2)}, u32[]{:S(2)}) collective-permute-start(bf16[240,256]{1,0:T(8,128)(2,1)S(1)} %get-tuple-element.47), channel_id=1, source_target_pairs={{0,3},{1,0},{2,1},{3,2},{4,7},{5,4},{6,5},{7,6},{8,11},{9,8},{10,9... | collective-permute-start | bytes 368648 | tf_op jit(solution)/shard_map/ppermute | solution.py:24
  30.2 0.0 collective-permute-done.4.refs_5_
  30.2 4.7 %collective-permute-start.8 = (bf16[240,256]{1,0:T(8,128)(2,1)S(1)}, bf16[240,256]{1,0:T(8,128)(2,1)S(1)}, u32[]{:S(2)}, u32[]{:S(2)}) collective-permute-start(bf16[240,256]{1,0:T(8,128)(2,1)S(1)} %get-tuple-element.52), channel_id=1, source_target_pairs={{0,1},{1,2},{2,3},{3,0},{4,5},{5,6},{6,7},{7,4},{8,9},{9,10},{10,1... | collective-permute-start | bytes 368648 | tf_op jit(solution)/shard_map/ppermute | solution.py:24
  34.9 1.0 %collective-permute-done.5.refs_6_ = bf16[240,256]{1,0:T(8,128)(2,1)S(1)} collective-permute-done((bf16[240,256]{1,0:T(8,128)(2,1)S(1)}, bf16[240,256]{1,0:T(8,128)(2,1)S(1)}, u32[]{:S(2)}, u32[]{:S(2)}) %collective-permute-start.5) | collective-permute-done | bytes 122912 | tf_op jit(solution)/shard_map/ppermute | solution.py:24
  35.9 1.1 %collective-permute-start.9 = (bf16[240,256]{1,0:T(8,128)(2,1)S(1)}, bf16[240,256]{1,0:T(8,128)(2,1)S(1)}, u32[]{:S(2)}, u32[]{:S(2)}) collective-permute-start(bf16[240,256]{1,0:T(8,128)(2,1)S(1)} %get-tuple-element.54), channel_id=1, source_target_pairs={{0,2},{1,3},{2,0},{3,1},{4,6},{5,7},{6,4},{7,5},{8,10},{9,11},{10,... | collective-permute-start | bytes 368648 | tf_op jit(solution)/shard_map/ppermute | solution.py:24
  37.0 3.0 %collective-permute-done.6.refs_7_ = bf16[240,256]{1,0:T(8,128)(2,1)S(1)} collective-permute-done((bf16[240,256]{1,0:T(8,128)(2,1)S(1)}, bf16[240,256]{1,0:T(8,128)(2,1)S(1)}, u32[]{:S(2)}, u32[]{:S(2)}) %collective-permute-start.6) | collective-permute-done | bytes 122912 | tf_op jit(solution)/shard_map/ppermute | solution.py:24
  40.0 0.8 %collective-permute-start.10 = (bf16[240,256]{1,0:T(8,128)(2,1)S(1)}, bf16[240,256]{1,0:T(8,128)(2,1)S(1)}, u32[]{:S(2)}, u32[]{:S(2)}) collective-permute-start(bf16[240,256]{1,0:T(8,128)(2,1)S(1)} %get-tuple-element.56), channel_id=1, source_target_pairs={{0,3},{1,0},{2,1},{3,2},{4,7},{5,4},{6,5},{7,6},{8,11},{9,8},{10,9... | collective-permute-start | bytes 368648 | tf_op jit(solution)/shard_map/ppermute | solution.py:24
  40.8 0.0 copy-done.4
  40.8 4.0 %shard_map.57 = (bf16[416,128]{1,0:T(8,128)(2,1)S(1)}, bf16[608,128]{1,0:T(8,128)(2,1)S(1)}) custom-call(bf16[160,512]{1,0:T(8,128)(2,1)S(1)} %copy-done.4, bf16[160,512]{1,0:T(8,128)(2,1)S(1)} %collective-permute-done.refs_1_, bf16[160,512]{1,0:T(8,128)(2,1)S(1)} %collective-permute-done.1.refs_2_, bf16[160,512]{1,0:T(8,128)(2,1)S(1)} %collective-permute-done.2.refs_3_, ...), custom_call_target="tpu_custom_call" | custom-call | flops 2621440000 | bytes 1228800 | tf_op jit(solution)/shard_map/pallas_call | solution.py:320
  44.8 0.8 %collective-permute-start.7 = (bf16[608,128]{1,0:T(8,128)(2,1)S(1)}, bf16[608,128]{1,0:T(8,128)(2,1)S(1)}, u32[]{:S(2)}, u32[]{:S(2)}) collective-permute-start(bf16[608,128]{1,0:T(8,128)(2,1)S(1)} %get-tuple-element.48.mixed), channel_id=1, source_target_pairs={{0,16},{4,20},{8,24},{12,28},{16,0},{20,4},{24,8},{28,12},{1,17},{... | collective-permute-start | bytes 466952 | tf_op jit(solution)/shard_map/ppermute | solution.py:24
  45.6 0.0 collective-permute-done.8.refs_5_
  45.6 0.3 collective-permute-done.9.refs_6_
  45.9 2.0 %collective-permute-done.10.refs_7_ = bf16[240,256]{1,0:T(8,128)(2,1)S(1)} collective-permute-done((bf16[240,256]{1,0:T(8,128)(2,1)S(1)}, bf16[240,256]{1,0:T(8,128)(2,1)S(1)}, u32[]{:S(2)}, u32[]{:S(2)}) %collective-permute-start.10) | collective-permute-done | bytes 122912 | tf_op jit(solution)/shard_map/ppermute | solution.py:24
  47.9 0.0 copy-start.1
  47.9 4.0 %shard_map.58 = (bf16[416,128]{1,0:T(8,128)(2,1)S(1)}, bf16[608,128]{1,0:T(8,128)(2,1)S(1)}) custom-call(bf16[160,512]{1,0:T(8,128)(2,1)S(1)} %copy-done.4, bf16[160,512]{1,0:T(8,128)(2,1)S(1)} %collective-permute-done.refs_1_, bf16[160,512]{1,0:T(8,128)(2,1)S(1)} %collective-permute-done.1.refs_2_, bf16[160,512]{1,0:T(8,128)(2,1)S(1)} %collective-permute-done.2.refs_3_, ...), custom_call_target="tpu_custom_call" | custom-call | flops 2621440000 | bytes 1228800 | tf_op jit(solution)/shard_map/pallas_call | solution.py:320
  51.9 0.4 collective-permute-start.14
  52.3 0.0 collective-permute-done.7.western
  52.3 0.6 shard_map.59
  52.9 3.0 %collective-permute-start.11 = (bf16[360,128]{1,0:T(8,128)(2,1)S(1)}, bf16[360,128]{1,0:T(8,128)(2,1)S(1)}, u32[]{:S(2)}, u32[]{:S(2)}) collective-permute-start(bf16[360,128]{1,0:T(8,128)(2,1)S(1)} %get-tuple-element.59), channel_id=1, source_target_pairs={{0,3},{1,0},{2,1},{3,2},{4,7},{5,4},{6,5},{7,6},{8,11},{9,8},{10,9... | collective-permute-start | bytes 276488 | tf_op jit(solution)/shard_map/ppermute | solution.py:24
  55.9 0.0 collective-permute-start.12
  55.9 0.9 %collective-permute-start.13 = (bf16[360,128]{1,0:T(8,128)(2,1)S(1)}, bf16[360,128]{1,0:T(8,128)(2,1)S(1)}, u32[]{:S(2)}, u32[]{:S(2)}) collective-permute-start(bf16[360,128]{1,0:T(8,128)(2,1)S(1)} %get-tuple-element.61), channel_id=1, source_target_pairs={{0,1},{1,2},{2,3},{3,0},{4,5},{5,6},{6,7},{7,4},{8,9},{9,10},{10,1... | collective-permute-start | bytes 276488 | tf_op jit(solution)/shard_map/ppermute | solution.py:24
  56.9 0.7 collective-permute-done.14.western
  57.5 0.6 shard_map.61
  58.1 2.3 %collective-permute-start.15 = (bf16[152,128]{1,0:T(8,128)(2,1)S(1)}, bf16[152,128]{1,0:T(8,128)(2,1)S(1)}, u32[]{:S(2)}, u32[]{:S(2)}) collective-permute-start(bf16[152,128]{1,0:T(8,128)(2,1)S(1)} %get-tuple-element.66), channel_id=1, source_target_pairs={{0,3},{1,0},{2,1},{3,2},{4,7},{5,4},{6,5},{7,6},{8,11},{9,8},{10,9... | collective-permute-start | bytes 116744 | tf_op jit(solution)/shard_map/ppermute | solution.py:24
  60.4 1.1 %collective-permute-start.16 = (bf16[152,128]{1,0:T(8,128)(2,1)S(1)}, bf16[152,128]{1,0:T(8,128)(2,1)S(1)}, u32[]{:S(2)}, u32[]{:S(2)}) collective-permute-start(bf16[152,128]{1,0:T(8,128)(2,1)S(1)} %get-tuple-element.67), channel_id=1, source_target_pairs={{0,2},{1,3},{2,0},{3,1},{4,6},{5,7},{6,4},{7,5},{8,10},{9,11},{10,... | collective-permute-start | bytes 116744 | tf_op jit(solution)/shard_map/ppermute | solution.py:24
  61.6 0.0 collective-permute-done.11.refs_1_
  61.6 2.4 %collective-permute-start.17 = (bf16[152,128]{1,0:T(8,128)(2,1)S(1)}, bf16[152,128]{1,0:T(8,128)(2,1)S(1)}, u32[]{:S(2)}, u32[]{:S(2)}) collective-permute-start(bf16[152,128]{1,0:T(8,128)(2,1)S(1)} %get-tuple-element.68), channel_id=1, source_target_pairs={{0,1},{1,2},{2,3},{3,0},{4,5},{5,6},{6,7},{7,4},{8,9},{9,10},{10,1... | collective-permute-start | bytes 116744 | tf_op jit(solution)/shard_map/ppermute | solution.py:24
  64.0 2.1 %collective-permute-done.12.refs_2_ = bf16[360,128]{1,0:T(8,128)(2,1)S(1)} collective-permute-done((bf16[360,128]{1,0:T(8,128)(2,1)S(1)}, bf16[360,128]{1,0:T(8,128)(2,1)S(1)}, u32[]{:S(2)}, u32[]{:S(2)}) %collective-permute-start.12) | collective-permute-done | bytes 92192 | tf_op jit(solution)/shard_map/ppermute | solution.py:24
  66.1 0.0 collective-permute-done.13.refs_3_
  66.1 0.0 copy-done.1
  66.1 1.0 %shard_map.60 = (f32[10,40,1280]{2,1,0:T(8,128)S(1)}, bf16[512,1280]{1,0:T(8,128)(2,1)S(1)}) custom-call(bf16[10,40,1280]{2,1,0:T(8,128)(2,1)S(1)} %bitcast.5, bf16[640,1280]{1,0:T(8,128)(2,1)S(1)} %copy-done.1, bf16[360,128]{1,0:T(8,128)(2,1)S(1)} %get-tuple-element.58.refs_0_, bf16[360,128]{1,0:T(8,128)(2,1)S(1)} %collective-permute-done.11.refs_1_, ...), custom_call_target="tpu_custom_call" | custom-call | flops 524288000 | bytes 3891200 | tf_op jit(solution)/shard_map/pallas_call | solution.py:367
  67.2 0.0 collective-permute-done.15.refs_1_
  67.2 0.0 collective-permute-done.16.refs_2_
  67.2 0.2 collective-permute-done.17.refs_3_
  67.4 1.5 %shard_map.62 = bf16[10,40,1280]{2,1,0:T(8,128)(2,1)} custom-call(f32[10,40,1280]{2,1,0:T(8,128)S(1)} %get-tuple-element.62.partial, bf16[512,1280]{1,0:T(8,128)(2,1)S(1)} %get-tuple-element.63.weight, bf16[152,128]{1,0:T(8,128)(2,1)S(1)} %get-tuple-element.65.refs_0_, bf16[152,128]{1,0:T(8,128)(2,1)S(1)} %collective-permute-done.15.refs_1_, ...), custom_call_target="tpu_custom_call" | custom-call | flops 524288000 | bytes 3891200 | tf_op jit(solution)/shard_map/pallas_call | solution.py:379
Async XLA Ops:
  1.1 16.9 %copy-start = (bf16[1,10,40,1280]{3,2,1,0:T(8,128)(2,1)S(1)}, bf16[1,10,40,1280]{3,2,1,0:T(8,128)(2,1)}, u32[]{:S(2)}) copy-start(bf16[1,10,40,1280]{3,2,1,0:T(8,128)(2,1)} %param.5) | copy-start | bytes 3072004
  1.1 16.9 %copy-start.2 = (f32[1280]{0:T(1024)S(1)}, f32[1280]{0:T(1024)}, u32[]{:S(2)}) copy-start(f32[1280]{0:T(1024)} %gain.3) | copy-start | bytes 15364
  1.1 16.9 %copy-start.3 = (s32[4]{0:T(128)S(1)}, s32[4]{0:T(128)}, u32[]{:S(2)}) copy-start(s32[4]{0:T(128)} %lon_shift.5) | copy-start | bytes 52
  1.2 16.9 %collective-permute-start.3 = (bf16[10,24,1280]{2,1,0:T(8,128)(2,1)S(1)}, bf16[10,24,1280]{2,1,0:T(8,128)(2,1)S(1)}, u32[]{:S(2)}, u32[]{:S(2)}) collective-permute-start(bf16[10,24,1280]{2,1,0:T(8,128)(2,1)S(1)} %slice.4), channel_id=1, source_target_pairs={{0,16},{4,20},{8,24},{12,28},{16,0},{20,4},{24,8},{28,12},{1,17},{... | collective-permute-start | bytes 1843208 | tf_op jit(solution)/shard_map/ppermute | solution.py:24
  9.0 13.4 %collective-permute-start = (bf16[160,512]{1,0:T(8,128)(2,1)}, bf16[160,512]{1,0:T(8,128)(2,1)S(1)}, u32[]{:S(2)}, u32[]{:S(2)}) collective-permute-start(bf16[160,512]{1,0:T(8,128)(2,1)} %get-tuple-element.38), channel_id=1, source_target_pairs={{0,1},{1,2},{2,3},{3,0},{4,5},{5,6},{6,7},{7,4},{8,9},{9,10},{10,1... | collective-permute-start | bytes 491528 | tf_op jit(solution)/shard_map/ppermute | solution.py:24
  10.6 13.6 %collective-permute-start.1 = (bf16[160,512]{1,0:T(8,128)(2,1)}, bf16[160,512]{1,0:T(8,128)(2,1)S(1)}, u32[]{:S(2)}, u32[]{:S(2)}) collective-permute-start(bf16[160,512]{1,0:T(8,128)(2,1)} %get-tuple-element.39), channel_id=1, source_target_pairs={{0,2},{1,3},{2,0},{3,1},{4,6},{5,7},{6,4},{7,5},{8,10},{9,11},{10,... | collective-permute-start | bytes 491528 | tf_op jit(solution)/shard_map/ppermute | solution.py:24
  13.2 27.6 %copy-start.4 = (bf16[160,512]{1,0:T(8,128)(2,1)S(1)}, bf16[160,512]{1,0:T(8,128)(2,1)}, u32[]{:S(2)}) copy-start(bf16[160,512]{1,0:T(8,128)(2,1)} %get-tuple-element.37.refs_0_) | copy-start | bytes 491524
  13.2 13.6 %collective-permute-start.2 = (bf16[160,512]{1,0:T(8,128)(2,1)}, bf16[160,512]{1,0:T(8,128)(2,1)S(1)}, u32[]{:S(2)}, u32[]{:S(2)}) collective-permute-start(bf16[160,512]{1,0:T(8,128)(2,1)} %get-tuple-element.40), channel_id=1, source_target_pairs={{0,3},{1,0},{2,1},{3,2},{4,7},{5,4},{6,5},{7,6},{8,11},{9,8},{10,9... | collective-permute-start | bytes 491528 | tf_op jit(solution)/shard_map/ppermute | solution.py:24
  22.4 7.8 %collective-permute-start.4 = (bf16[240,256]{1,0:T(8,128)(2,1)S(1)}, bf16[240,256]{1,0:T(8,128)(2,1)S(1)}, u32[]{:S(2)}, u32[]{:S(2)}) collective-permute-start(bf16[240,256]{1,0:T(8,128)(2,1)S(1)} %get-tuple-element.43), channel_id=1, source_target_pairs={{0,1},{1,2},{2,3},{3,0},{4,5},{5,6},{6,7},{7,4},{8,9},{9,10},{10,1... | collective-permute-start | bytes 368648 | tf_op jit(solution)/shard_map/ppermute | solution.py:24
  24.2 11.6 %collective-permute-start.5 = (bf16[240,256]{1,0:T(8,128)(2,1)S(1)}, bf16[240,256]{1,0:T(8,128)(2,1)S(1)}, u32[]{:S(2)}, u32[]{:S(2)}) collective-permute-start(bf16[240,256]{1,0:T(8,128)(2,1)S(1)} %get-tuple-element.45), channel_id=1, source_target_pairs={{0,2},{1,3},{2,0},{3,1},{4,6},{5,7},{6,4},{7,5},{8,10},{9,11},{10,... | collective-permute-start | bytes 368648 | tf_op jit(solution)/shard_map/ppermute | solution.py:24
  26.8 13.1 %collective-permute-start.6 = (bf16[240,256]{1,0:T(8,128)(2,1)S(1)}, bf16[240,256]{1,0:T(8,128)(2,1)S(1)}, u32[]{:S(2)}, u32[]{:S(2)}) collective-permute-start(bf16[240,256]{1,0:T(8,128)(2,1)S(1)} %get-tuple-element.47), channel_id=1, source_target_pairs={{0,3},{1,0},{2,1},{3,2},{4,7},{5,4},{6,5},{7,6},{8,11},{9,8},{10,9... | collective-permute-start | bytes 368648 | tf_op jit(solution)/shard_map/ppermute | solution.py:24
  30.2 15.4 %collective-permute-start.8 = (bf16[240,256]{1,0:T(8,128)(2,1)S(1)}, bf16[240,256]{1,0:T(8,128)(2,1)S(1)}, u32[]{:S(2)}, u32[]{:S(2)}) collective-permute-start(bf16[240,256]{1,0:T(8,128)(2,1)S(1)} %get-tuple-element.52), channel_id=1, source_target_pairs={{0,1},{1,2},{2,3},{3,0},{4,5},{5,6},{6,7},{7,4},{8,9},{9,10},{10,1... | collective-permute-start | bytes 368648 | tf_op jit(solution)/shard_map/ppermute | solution.py:24
  35.9 10.1 %collective-permute-start.9 = (bf16[240,256]{1,0:T(8,128)(2,1)S(1)}, bf16[240,256]{1,0:T(8,128)(2,1)S(1)}, u32[]{:S(2)}, u32[]{:S(2)}) collective-permute-start(bf16[240,256]{1,0:T(8,128)(2,1)S(1)} %get-tuple-element.54), channel_id=1, source_target_pairs={{0,2},{1,3},{2,0},{3,1},{4,6},{5,7},{6,4},{7,5},{8,10},{9,11},{10,... | collective-permute-start | bytes 368648 | tf_op jit(solution)/shard_map/ppermute | solution.py:24
  40.0 7.9 %collective-permute-start.10 = (bf16[240,256]{1,0:T(8,128)(2,1)S(1)}, bf16[240,256]{1,0:T(8,128)(2,1)S(1)}, u32[]{:S(2)}, u32[]{:S(2)}) collective-permute-start(bf16[240,256]{1,0:T(8,128)(2,1)S(1)} %get-tuple-element.56), channel_id=1, source_target_pairs={{0,3},{1,0},{2,1},{3,2},{4,7},{5,4},{6,5},{7,6},{8,11},{9,8},{10,9... | collective-permute-start | bytes 368648 | tf_op jit(solution)/shard_map/ppermute | solution.py:24
  44.8 7.5 %collective-permute-start.7 = (bf16[608,128]{1,0:T(8,128)(2,1)S(1)}, bf16[608,128]{1,0:T(8,128)(2,1)S(1)}, u32[]{:S(2)}, u32[]{:S(2)}) collective-permute-start(bf16[608,128]{1,0:T(8,128)(2,1)S(1)} %get-tuple-element.48.mixed), channel_id=1, source_target_pairs={{0,16},{4,20},{8,24},{12,28},{16,0},{20,4},{24,8},{28,12},{1,17},{... | collective-permute-start | bytes 466952 | tf_op jit(solution)/shard_map/ppermute | solution.py:24
  47.9 18.2 %copy-start.1 = (bf16[640,1280]{1,0:T(8,128)(2,1)S(1)}, bf16[640,1280]{1,0:T(8,128)(2,1)}, u32[]{:S(2)}) copy-start(bf16[640,1280]{1,0:T(8,128)(2,1)} %weight.5) | copy-start | bytes 4915204
  51.9 5.6 %collective-permute-start.14 = (bf16[608,128]{1,0:T(8,128)(2,1)S(1)}, bf16[608,128]{1,0:T(8,128)(2,1)S(1)}, u32[]{:S(2)}, u32[]{:S(2)}) collective-permute-start(bf16[608,128]{1,0:T(8,128)(2,1)S(1)} %get-tuple-element.64.mixed), channel_id=1, source_target_pairs={{0,16},{4,20},{8,24},{12,28},{16,0},{20,4},{24,8},{28,12},{1,17},{... | collective-permute-start | bytes 466952 | tf_op jit(solution)/shard_map/ppermute | solution.py:24
  52.9 8.6 %collective-permute-start.11 = (bf16[360,128]{1,0:T(8,128)(2,1)S(1)}, bf16[360,128]{1,0:T(8,128)(2,1)S(1)}, u32[]{:S(2)}, u32[]{:S(2)}) collective-permute-start(bf16[360,128]{1,0:T(8,128)(2,1)S(1)} %get-tuple-element.59), channel_id=1, source_target_pairs={{0,3},{1,0},{2,1},{3,2},{4,7},{5,4},{6,5},{7,6},{8,11},{9,8},{10,9... | collective-permute-start | bytes 276488 | tf_op jit(solution)/shard_map/ppermute | solution.py:24
  55.9 10.2 %collective-permute-start.12 = (bf16[360,128]{1,0:T(8,128)(2,1)S(1)}, bf16[360,128]{1,0:T(8,128)(2,1)S(1)}, u32[]{:S(2)}, u32[]{:S(2)}) collective-permute-start(bf16[360,128]{1,0:T(8,128)(2,1)S(1)} %get-tuple-element.60), channel_id=1, source_target_pairs={{0,2},{1,3},{2,0},{3,1},{4,6},{5,7},{6,4},{7,5},{8,10},{9,11},{10,... | collective-permute-start | bytes 276488 | tf_op jit(solution)/shard_map/ppermute | solution.py:24
  55.9 10.2 %collective-permute-start.13 = (bf16[360,128]{1,0:T(8,128)(2,1)S(1)}, bf16[360,128]{1,0:T(8,128)(2,1)S(1)}, u32[]{:S(2)}, u32[]{:S(2)}) collective-permute-start(bf16[360,128]{1,0:T(8,128)(2,1)S(1)} %get-tuple-element.61), channel_id=1, source_target_pairs={{0,1},{1,2},{2,3},{3,0},{4,5},{5,6},{6,7},{7,4},{8,9},{9,10},{10,1... | collective-permute-start | bytes 276488 | tf_op jit(solution)/shard_map/ppermute | solution.py:24
  58.1 9.0 %collective-permute-start.15 = (bf16[152,128]{1,0:T(8,128)(2,1)S(1)}, bf16[152,128]{1,0:T(8,128)(2,1)S(1)}, u32[]{:S(2)}, u32[]{:S(2)}) collective-permute-start(bf16[152,128]{1,0:T(8,128)(2,1)S(1)} %get-tuple-element.66), channel_id=1, source_target_pairs={{0,3},{1,0},{2,1},{3,2},{4,7},{5,4},{6,5},{7,6},{8,11},{9,8},{10,9... | collective-permute-start | bytes 116744 | tf_op jit(solution)/shard_map/ppermute | solution.py:24
  60.4 6.7 %collective-permute-start.16 = (bf16[152,128]{1,0:T(8,128)(2,1)S(1)}, bf16[152,128]{1,0:T(8,128)(2,1)S(1)}, u32[]{:S(2)}, u32[]{:S(2)}) collective-permute-start(bf16[152,128]{1,0:T(8,128)(2,1)S(1)} %get-tuple-element.67), channel_id=1, source_target_pairs={{0,2},{1,3},{2,0},{3,1},{4,6},{5,7},{6,4},{7,5},{8,10},{9,11},{10,... | collective-permute-start | bytes 116744 | tf_op jit(solution)/shard_map/ppermute | solution.py:24
  61.6 5.8 %collective-permute-start.17 = (bf16[152,128]{1,0:T(8,128)(2,1)S(1)}, bf16[152,128]{1,0:T(8,128)(2,1)S(1)}, u32[]{:S(2)}, u32[]{:S(2)}) collective-permute-start(bf16[152,128]{1,0:T(8,128)(2,1)S(1)} %get-tuple-element.68), channel_id=1, source_target_pairs={{0,1},{1,2},{2,3},{3,0},{4,5},{5,6},{6,7},{7,4},{8,9},{9,10},{10,1... | collective-permute-start | bytes 116744 | tf_op jit(solution)/shard_map/ppermute | solution.py:24

commit v11 on v10

--- a/solution.py
+++ b/solution.py
@@ -13,6 +13,7 @@
 LANES = 128
 SUBLANES = 8
 MIB = 1024 * 1024
+CHUNKS = 5
 
 
 def round_up(value, unit):
@@ -35,16 +36,22 @@
     return lon_shift[lax.rem(lax.axis_index("win"), LAT_WINDOWS)]
 
 
-def project(tokens, gain, weight, copy, slots, outs):
+def project(tokens, gain, weight, copies, slots):
     groups = slots.shape[0]
     local = HEADS // groups
     count, features = tokens.shape
     span = slots.shape[2] // local
     factor = lax.rsqrt(jnp.mean(tokens * tokens, axis=-1, keepdims=True) + 1e-06)
     normed = (tokens * factor * gain[...].reshape(1, features)).astype(jnp.bfloat16)
-    if copy is not None:
-        copy.wait()
-    qkv = jnp.dot(normed, weight[...], preferred_element_type=jnp.float32).astype(jnp.bfloat16)
+    chunk = features // len(copies)
+    qkv = None
+    for index, copy in enumerate(copies):
+        if copy is not None:
+            copy.wait()
+        inner = slice(index * chunk, (index + 1) * chunk)
+        share = jnp.dot(normed[:, inner], weight[inner], preferred_element_type=jnp.float32)
+        qkv = share if qkv is None else qkv + share
+    qkv = qkv.astype(jnp.bfloat16)
     tail = jnp.ones((count, span - 3 * HD), jnp.bfloat16)
     place = lax.axis_index("tok")
     for group in range(groups):
@@ -56,25 +63,35 @@
                 for kind in (1, 0, 2)
             ] + [tail]
         slots[slot] = jnp.concatenate(columns, axis=1)
-    for index, out in enumerate(outs):
-        first = index // groups * out.shape[1]
-        out[...] = slots[index % groups, :, first : first + out.shape[1]]
 
 
 def kept_kernel(split, field, gain, weight, *refs):
     *outs, slots, held_weight, sems, held_field, held_gain = refs
-    copy = pltpu.make_async_copy(weight, held_weight, sems.at[0])
-    first = pltpu.make_async_copy(field, held_field, sems.at[1])
-    second = pltpu.make_async_copy(gain, held_gain, sems.at[2])
-    first.start()
-    second.start()
-    copy.start()
+    first = pltpu.make_async_copy(field, held_field, sems.at[CHUNKS])
+    second = pltpu.make_async_copy(gain, held_gain, sems.at[CHUNKS + 1])
+    chunk = weight.shape[0] // CHUNKS
+    copies = []
+    for index in range(CHUNKS):
+        inner = pl.ds(index * chunk, chunk)
+        copies.append(
+            pltpu.make_async_copy(weight.at[inner], held_weight.at[inner], sems.at[index])
+        )
+    for copy in (first, second, *copies):
+        copy.start()
     first.wait()
     second.wait()
     rows, columns, features = field.shape
     tokens = held_field[...].astype(jnp.float32)[:, split:]
     tokens = tokens.reshape(rows * (columns - split), features)
-    project(tokens, held_gain, held_weight, copy, slots, outs)
+    project(tokens, held_gain, held_weight, copies, slots)
+    copies = [
+        pltpu.make_async_copy(slots.at[index], out, sems.at[index])
+        for index, out in enumerate(outs)
+    ]
+    for copy in copies:
+        copy.start()
+    for copy in copies:
+        copy.wait()
 
 
 def mixed_kernel(split, field, gain, weight, lon_shift, eastern, *refs):
@@ -83,7 +100,11 @@
     own = field[...].astype(jnp.float32)[:, :split]
     column = lax.broadcasted_iota(jnp.int32, own.shape, 1)
     tokens = jnp.where(column < column_offset(lon_shift), eastern[...].astype(jnp.float32), own)
-    project(tokens.reshape(rows * split, features), gain, weight, None, slots, outs)
+    project(tokens.reshape(rows * split, features), gain, weight, [None], slots)
+    groups = slots.shape[0]
+    for index, out in enumerate(outs):
+        first = index // groups * out.shape[1]
+        out[...] = slots[index % groups, :, first : first + out.shape[1]]
 
 
 def gather(head, kept, mixed, held, keys):
@@ -110,7 +131,7 @@
         queries = pltpu.roll(held[first : first + step].astype(jnp.float32), span - HD, axis=1)
         queries = queries[:, :LANES]
         lane = lax.broadcasted_iota(jnp.int32, queries.shape, 1)
-        queries = jnp.where(lane < HD, queries, 0.0).astype(jnp.bfloat16)
+        queries = jnp.where(lane < HD, queries * factor, 0.0).astype(jnp.bfloat16)
         out[...] = jnp.dot(queries, keys[...], preferred_element_type=jnp.float32)
 
     score(0, scores[0])
@@ -121,7 +142,7 @@
         for first in range(0, step, chunk):
             part = now[first : first + chunk]
             top = jnp.max(part, axis=-1, keepdims=True)
-            out[first : first + chunk] = jnp.exp2((part - top) * factor).astype(jnp.bfloat16)
+            out[first : first + chunk] = jnp.exp2(part - top).astype(jnp.bfloat16)
         values = jnp.dot(out[...], held[:, span - LANES :], preferred_element_type=jnp.float32)
         first = 2 * HD - (span - LANES)
         values = values / values[:, first + HD : first + HD + 1]
@@ -268,13 +289,13 @@
     def limit(size):
         return pltpu.CompilerParams(vmem_limit_bytes=size * MIB)
 
-    def projection(kernel, count, parts, specs, held, params, *operands):
+    def projection(kernel, count, parts, specs, out_specs, held, params, *operands):
         block = jax.ShapeDtypeStruct((count, local * span // parts), jnp.bfloat16)
         return pl.pallas_call(
             functools.partial(kernel, split),
             out_shape=[block] * (parts * groups),
             in_specs=specs,
-            out_specs=whole(parts * groups),
+            out_specs=out_specs,
             scratch_shapes=[
                 pltpu.VMEM((groups, count, local * span), jnp.bfloat16),
                 *held,
@@ -298,14 +319,19 @@
     operands = (field, norm_gain, qkv_weight)
     held = [
         pltpu.VMEM(qkv_weight.shape, qkv_weight.dtype),
-        pltpu.SemaphoreType.DMA((3,)),
+        pltpu.SemaphoreType.DMA((CHUNKS + 2,)),
         pltpu.VMEM(field.shape, field.dtype),
         pltpu.VMEM(norm_gain.shape, norm_gain.dtype),
     ]
-    kept = spread(projection(kept_kernel, kept_count, 1, [hbm] * 3, held, limit(60), *operands), 1)
+    kept = projection(
+        kept_kernel, kept_count, 1, [hbm] * 3, [hbm] * groups, held, limit(60), *operands
+    )
+    kept = spread(kept, 1)
     specs = [*whole(3), smem, *whole(1)]
     operands += (lon_shift, eastern)
-    mixed = projection(mixed_kernel, mixed_count, local, specs, [], limit(48), *operands)
+    mixed = projection(
+        mixed_kernel, mixed_count, local, specs, whole(local * groups), [], limit(48), *operands
+    )
     first_mixed = spread(after(mixed[:groups], [None, *kept[1:]]), 1)
     second_mixed = spread(after(mixed[groups:], [None, *first_mixed[1:]]), 1)
 

time: 69.1 us -> 69.1 us (level)
  waiting for transfers between devices: 12.8 us -> 14.5 us
  starting transfers between devices: 34 us -> 32.6 us
    ppermute x18, waiting for transfers between devices: 12.8 us -> 14.5 us  [shifted(): lax.ppermute(block, axis, [(i, (i + distance) % count) for i in range(cou...]
    ppermute x18, starting transfers between devices: 34 us -> 32.6 us  [shifted(): lax.ppermute(block, axis, [(i, (i + distance) % count) for i in range(cou...]
where the time goes in v11:
time: 69.1 us; the launch traced here: 68.9 us
  starting transfers between devices  32.6 us (47%)
  Pallas kernels  20.5 us (30%)
  waiting for transfers between devices  14.5 us (21%)
  local copies, waits for them, and re-layouts  1.14 us (2%)
    ppermute x18, starting transfers between devices, shifted(): lax.ppermute(block, axis, [(i, (i + distance) % count) for i in range(cou...  32.6 us
    ppermute x18, waiting for transfers between devices, shifted(): lax.ppermute(block, axis, [(i, (i + distance) % count) for i in range(cou...  14.5 us
    pallas_call x2, Pallas kernels, projection(): pl.pallas_call(functools.partial(kernel, split), out_shape=[block] * (par...  8.77 us
    pallas_call x2, Pallas kernels, attention(): pl.pallas_call(functools.partial(attention_kernel, head, groups), out_sha...  7.99 us
    pallas_call x1, Pallas kernels, shards(): pl.pallas_call(functools.partial(second_output_kernel, split), out_shape=...  1.52 us
  transfers between devices with their start and end apart: 18, of which 8 were waited for; matrix products, arithmetic and copies ran while one was open for 0% of the time, Pallas kernels for 28%

profile of v11, /device:TPU:0, one launch (start us, length us, event | category | flops | bytes accessed | tf_op | source)
XLA Modules:
  0.0 68.9 jit_solution(3057024450718389813)
XLA Ops:
  0.0 1.1 %slice.4 = bf16[10,24,1280]{2,1,0:T(8,128)(2,1)S(1)} slice(bf16[10,40,1280]{2,1,0:T(8,128)(2,1)} %bitcast.2), slice={[0:10], [0:24], [0:1280]} | slice | bytes 1228800 | tf_op jit(solution)/shard_map/slice | solution.py:317
  1.1 0.0 copy-start
  1.1 0.0 copy-start.2
  1.1 0.0 copy-start.3
  1.2 3.0 %collective-permute-start.3 = (bf16[10,24,1280]{2,1,0:T(8,128)(2,1)S(1)}, bf16[10,24,1280]{2,1,0:T(8,128)(2,1)S(1)}, u32[]{:S(2)}, u32[]{:S(2)}) collective-permute-start(bf16[10,24,1280]{2,1,0:T(8,128)(2,1)S(1)} %slice.4), channel_id=1, source_target_pairs={{0,16},{4,20},{8,24},{12,28},{16,0},{20,4},{24,8},{28,12},{1,17},{... | collective-permute-start | bytes 1843208 | tf_op jit(solution)/shard_map/ppermute | solution.py:25
  4.2 4.5 %shard_map.55 = (bf16[160,512]{1,0:T(8,128)(2,1)}, bf16[160,512]{1,0:T(8,128)(2,1)}, bf16[160,512]{1,0:T(8,128)(2,1)}, bf16[160,512]{1,0:T(8,128)(2,1)}) custom-call(bf16[10,40,1280]{2,1,0:T(8,128)(2,1)} %bitcast.3, f32[1280]{0:T(1024)} %gain.3, bf16[1280,1920]{1,0:T(8,128)(2,1)} %weight.4), custom_call_target="tpu_custom_call" | custom-call | flops 786432000 | bytes 5734400 | tf_op jit(solution)/shard_map/pallas_call | solution.py:294
  8.7 1.6 %collective-permute-start = (bf16[160,512]{1,0:T(8,128)(2,1)}, bf16[160,512]{1,0:T(8,128)(2,1)S(1)}, u32[]{:S(2)}, u32[]{:S(2)}) collective-permute-start(bf16[160,512]{1,0:T(8,128)(2,1)} %get-tuple-element.38), channel_id=1, source_target_pairs={{0,1},{1,2},{2,3},{3,0},{4,5},{5,6},{6,7},{7,4},{8,9},{9,10},{10,1... | collective-permute-start | bytes 491528 | tf_op jit(solution)/shard_map/ppermute | solution.py:25
  10.3 2.6 %collective-permute-start.1 = (bf16[160,512]{1,0:T(8,128)(2,1)}, bf16[160,512]{1,0:T(8,128)(2,1)S(1)}, u32[]{:S(2)}, u32[]{:S(2)}) collective-permute-start(bf16[160,512]{1,0:T(8,128)(2,1)} %get-tuple-element.39), channel_id=1, source_target_pairs={{0,2},{1,3},{2,0},{3,1},{4,6},{5,7},{6,4},{7,5},{8,10},{9,11},{10,... | collective-permute-start | bytes 491528 | tf_op jit(solution)/shard_map/ppermute | solution.py:25
  12.9 0.0 copy-start.4
  12.9 1.3 %collective-permute-start.2 = (bf16[160,512]{1,0:T(8,128)(2,1)}, bf16[160,512]{1,0:T(8,128)(2,1)S(1)}, u32[]{:S(2)}, u32[]{:S(2)}) collective-permute-start(bf16[160,512]{1,0:T(8,128)(2,1)} %get-tuple-element.40), channel_id=1, source_target_pairs={{0,3},{1,0},{2,1},{3,2},{4,7},{5,4},{6,5},{7,6},{8,11},{9,8},{10,9... | collective-permute-start | bytes 491528 | tf_op jit(solution)/shard_map/ppermute | solution.py:25
  14.2 3.8 %collective-permute-done.3.eastern = bf16[10,24,1280]{2,1,0:T(8,128)(2,1)S(1)} collective-permute-done((bf16[10,24,1280]{2,1,0:T(8,128)(2,1)S(1)}, bf16[10,24,1280]{2,1,0:T(8,128)(2,1)S(1)}, u32[]{:S(2)}, u32[]{:S(2)}) %collective-permute-start.3) | collective-permute-done | bytes 614432 | tf_op jit(solution)/shard_map/ppermute | solution.py:25
  18.0 0.0 copy-done
  18.0 0.0 copy-done.2
  18.0 0.0 copy-done.3
  18.1 4.3 %shard_map.56 = (bf16[240,256]{1,0:T(8,128)(2,1)S(1)}, bf16[240,256]{1,0:T(8,128)(2,1)S(1)}, bf16[240,256]{1,0:T(8,128)(2,1)S(1)}, bf16[240,256]{1,0:T(8,128)(2,...) custom-call(bf16[10,40,1280]{2,1,0:T(8,128)(2,1)S(1)} %bitcast.4, ...), custom_call_target="tpu_custom_call" | custom-call | flops 1179648000 | bytes 6144000 | tf_op jit(solution)/shard_map/pallas_call | solution.py:294
  22.4 0.0 collective-permute-done.refs_1_
  22.4 1.9 %collective-permute-start.4 = (bf16[240,256]{1,0:T(8,128)(2,1)S(1)}, bf16[240,256]{1,0:T(8,128)(2,1)S(1)}, u32[]{:S(2)}, u32[]{:S(2)}) collective-permute-start(bf16[240,256]{1,0:T(8,128)(2,1)S(1)} %get-tuple-element.43), channel_id=1, source_target_pairs={{0,1},{1,2},{2,3},{3,0},{4,5},{5,6},{6,7},{7,4},{8,9},{9,10},{10,1... | collective-permute-start | bytes 368648 | tf_op jit(solution)/shard_map/ppermute | solution.py:25
  24.2 0.0 collective-permute-done.1.refs_2_
  24.2 2.6 %collective-permute-start.5 = (bf16[240,256]{1,0:T(8,128)(2,1)S(1)}, bf16[240,256]{1,0:T(8,128)(2,1)S(1)}, u32[]{:S(2)}, u32[]{:S(2)}) collective-permute-start(bf16[240,256]{1,0:T(8,128)(2,1)S(1)} %get-tuple-element.45), channel_id=1, source_target_pairs={{0,2},{1,3},{2,0},{3,1},{4,6},{5,7},{6,4},{7,5},{8,10},{9,11},{10,... | collective-permute-start | bytes 368648 | tf_op jit(solution)/shard_map/ppermute | solution.py:25
  26.8 0.0 collective-permute-done.2.refs_3_
  26.8 2.6 %collective-permute-start.6 = (bf16[240,256]{1,0:T(8,128)(2,1)S(1)}, bf16[240,256]{1,0:T(8,128)(2,1)S(1)}, u32[]{:S(2)}, u32[]{:S(2)}) collective-permute-start(bf16[240,256]{1,0:T(8,128)(2,1)S(1)} %get-tuple-element.47), channel_id=1, source_target_pairs={{0,3},{1,0},{2,1},{3,2},{4,7},{5,4},{6,5},{7,6},{8,11},{9,8},{10,9... | collective-permute-start | bytes 368648 | tf_op jit(solution)/shard_map/ppermute | solution.py:25
  29.4 0.8 %collective-permute-done.4.refs_5_ = bf16[240,256]{1,0:T(8,128)(2,1)S(1)} collective-permute-done((bf16[240,256]{1,0:T(8,128)(2,1)S(1)}, bf16[240,256]{1,0:T(8,128)(2,1)S(1)}, u32[]{:S(2)}, u32[]{:S(2)}) %collective-permute-start.4) | collective-permute-done | bytes 122912 | tf_op jit(solution)/shard_map/ppermute | solution.py:25
  30.2 4.6 %collective-permute-start.8 = (bf16[240,256]{1,0:T(8,128)(2,1)S(1)}, bf16[240,256]{1,0:T(8,128)(2,1)S(1)}, u32[]{:S(2)}, u32[]{:S(2)}) collective-permute-start(bf16[240,256]{1,0:T(8,128)(2,1)S(1)} %get-tuple-element.52), channel_id=1, source_target_pairs={{0,1},{1,2},{2,3},{3,0},{4,5},{5,6},{6,7},{7,4},{8,9},{9,10},{10,1... | collective-permute-start | bytes 368648 | tf_op jit(solution)/shard_map/ppermute | solution.py:25
  34.8 2.8 %collective-permute-done.5.refs_6_ = bf16[240,256]{1,0:T(8,128)(2,1)S(1)} collective-permute-done((bf16[240,256]{1,0:T(8,128)(2,1)S(1)}, bf16[240,256]{1,0:T(8,128)(2,1)S(1)}, u32[]{:S(2)}, u32[]{:S(2)}) %collective-permute-start.5) | collective-permute-done | bytes 122912 | tf_op jit(solution)/shard_map/ppermute | solution.py:25
  37.6 0.0 collective-permute-start.9
  37.6 1.9 %collective-permute-done.6.refs_7_ = bf16[240,256]{1,0:T(8,128)(2,1)S(1)} collective-permute-done((bf16[240,256]{1,0:T(8,128)(2,1)S(1)}, bf16[240,256]{1,0:T(8,128)(2,1)S(1)}, u32[]{:S(2)}, u32[]{:S(2)}) %collective-permute-start.6) | collective-permute-done | bytes 122912 | tf_op jit(solution)/shard_map/ppermute | solution.py:25
  39.5 0.8 %collective-permute-start.10 = (bf16[240,256]{1,0:T(8,128)(2,1)S(1)}, bf16[240,256]{1,0:T(8,128)(2,1)S(1)}, u32[]{:S(2)}, u32[]{:S(2)}) collective-permute-start(bf16[240,256]{1,0:T(8,128)(2,1)S(1)} %get-tuple-element.56), channel_id=1, source_target_pairs={{0,3},{1,0},{2,1},{3,2},{4,7},{5,4},{6,5},{7,6},{8,11},{9,8},{10,9... | collective-permute-start | bytes 368648 | tf_op jit(solution)/shard_map/ppermute | solution.py:25
  40.2 0.0 copy-done.4
  40.2 4.0 %shard_map.57 = (bf16[416,128]{1,0:T(8,128)(2,1)S(1)}, bf16[608,128]{1,0:T(8,128)(2,1)S(1)}) custom-call(bf16[160,512]{1,0:T(8,128)(2,1)S(1)} %copy-done.4, bf16[160,512]{1,0:T(8,128)(2,1)S(1)} %collective-permute-done.refs_1_, bf16[160,512]{1,0:T(8,128)(2,1)S(1)} %collective-permute-done.1.refs_2_, bf16[160,512]{1,0:T(8,128)(2,1)S(1)} %collective-permute-done.2.refs_3_, ...), custom_call_target="tpu_custom_call" | custom-call | flops 2621440000 | bytes 1228800 | tf_op jit(solution)/shard_map/pallas_call | solution.py:346
  44.2 1.8 %collective-permute-start.7 = (bf16[608,128]{1,0:T(8,128)(2,1)S(1)}, bf16[608,128]{1,0:T(8,128)(2,1)S(1)}, u32[]{:S(2)}, u32[]{:S(2)}) collective-permute-start(bf16[608,128]{1,0:T(8,128)(2,1)S(1)} %get-tuple-element.48.mixed), channel_id=1, source_target_pairs={{0,16},{4,20},{8,24},{12,28},{16,0},{20,4},{24,8},{28,12},{1,17},{... | collective-permute-start | bytes 466952 | tf_op jit(solution)/shard_map/ppermute | solution.py:25
  46.1 0.0 collective-permute-done.8.refs_5_
  46.1 0.0 collective-permute-done.9.refs_6_
  46.1 1.6 %collective-permute-done.10.refs_7_ = bf16[240,256]{1,0:T(8,128)(2,1)S(1)} collective-permute-done((bf16[240,256]{1,0:T(8,128)(2,1)S(1)}, bf16[240,256]{1,0:T(8,128)(2,1)S(1)}, u32[]{:S(2)}, u32[]{:S(2)}) %collective-permute-start.10) | collective-permute-done | bytes 122912 | tf_op jit(solution)/shard_map/ppermute | solution.py:25
  47.7 0.0 copy-start.1
  47.7 4.0 %shard_map.58 = (bf16[416,128]{1,0:T(8,128)(2,1)S(1)}, bf16[608,128]{1,0:T(8,128)(2,1)S(1)}) custom-call(bf16[160,512]{1,0:T(8,128)(2,1)S(1)} %copy-done.4, bf16[160,512]{1,0:T(8,128)(2,1)S(1)} %collective-permute-done.refs_1_, bf16[160,512]{1,0:T(8,128)(2,1)S(1)} %collective-permute-done.1.refs_2_, bf16[160,512]{1,0:T(8,128)(2,1)S(1)} %collective-permute-done.2.refs_3_, ...), custom_call_target="tpu_custom_call" | custom-call | flops 2621440000 | bytes 1228800 | tf_op jit(solution)/shard_map/pallas_call | solution.py:346
  51.7 0.1 collective-permute-start.14
  51.8 0.0 collective-permute-done.7.western
  51.8 0.6 shard_map.59
  52.4 3.6 %collective-permute-start.11 = (bf16[360,128]{1,0:T(8,128)(2,1)S(1)}, bf16[360,128]{1,0:T(8,128)(2,1)S(1)}, u32[]{:S(2)}, u32[]{:S(2)}) collective-permute-start(bf16[360,128]{1,0:T(8,128)(2,1)S(1)} %get-tuple-element.59), channel_id=1, source_target_pairs={{0,3},{1,0},{2,1},{3,2},{4,7},{5,4},{6,5},{7,6},{8,11},{9,8},{10,9... | collective-permute-start | bytes 276488 | tf_op jit(solution)/shard_map/ppermute | solution.py:25
  56.0 0.0 collective-permute-start.12
  56.0 0.6 collective-permute-start.13
  56.6 0.8 %collective-permute-done.14.western = bf16[608,128]{1,0:T(8,128)(2,1)S(1)} collective-permute-done((bf16[608,128]{1,0:T(8,128)(2,1)S(1)}, bf16[608,128]{1,0:T(8,128)(2,1)S(1)}, u32[]{:S(2)}, u32[]{:S(2)}) %collective-permute-start.14) | collective-permute-done | bytes 155680 | tf_op jit(solution)/shard_map/ppermute | solution.py:25
  57.5 0.6 shard_map.61
  58.1 2.4 %collective-permute-start.15 = (bf16[152,128]{1,0:T(8,128)(2,1)S(1)}, bf16[152,128]{1,0:T(8,128)(2,1)S(1)}, u32[]{:S(2)}, u32[]{:S(2)}) collective-permute-start(bf16[152,128]{1,0:T(8,128)(2,1)S(1)} %get-tuple-element.66), channel_id=1, source_target_pairs={{0,3},{1,0},{2,1},{3,2},{4,7},{5,4},{6,5},{7,6},{8,11},{9,8},{10,9... | collective-permute-start | bytes 116744 | tf_op jit(solution)/shard_map/ppermute | solution.py:25
  60.5 1.1 %collective-permute-start.16 = (bf16[152,128]{1,0:T(8,128)(2,1)S(1)}, bf16[152,128]{1,0:T(8,128)(2,1)S(1)}, u32[]{:S(2)}, u32[]{:S(2)}) collective-permute-start(bf16[152,128]{1,0:T(8,128)(2,1)S(1)} %get-tuple-element.67), channel_id=1, source_target_pairs={{0,2},{1,3},{2,0},{3,1},{4,6},{5,7},{6,4},{7,5},{8,10},{9,11},{10,... | collective-permute-start | bytes 116744 | tf_op jit(solution)/shard_map/ppermute | solution.py:25
  61.6 0.0 collective-permute-done.11.refs_1_
  61.6 2.0 %collective-permute-start.17 = (bf16[152,128]{1,0:T(8,128)(2,1)S(1)}, bf16[152,128]{1,0:T(8,128)(2,1)S(1)}, u32[]{:S(2)}, u32[]{:S(2)}) collective-permute-start(bf16[152,128]{1,0:T(8,128)(2,1)S(1)} %get-tuple-element.68), channel_id=1, source_target_pairs={{0,1},{1,2},{2,3},{3,0},{4,5},{5,6},{6,7},{7,4},{8,9},{9,10},{10,1... | collective-permute-start | bytes 116744 | tf_op jit(solution)/shard_map/ppermute | solution.py:25
  63.7 2.2 %collective-permute-done.12.refs_2_ = bf16[360,128]{1,0:T(8,128)(2,1)S(1)} collective-permute-done((bf16[360,128]{1,0:T(8,128)(2,1)S(1)}, bf16[360,128]{1,0:T(8,128)(2,1)S(1)}, u32[]{:S(2)}, u32[]{:S(2)}) %collective-permute-start.12) | collective-permute-done | bytes 92192 | tf_op jit(solution)/shard_map/ppermute | solution.py:25
  65.9 0.0 collective-permute-done.13.refs_3_
  65.9 0.0 copy-done.1
  65.9 1.0 %shard_map.60 = (f32[10,40,1280]{2,1,0:T(8,128)S(1)}, bf16[512,1280]{1,0:T(8,128)(2,1)S(1)}) custom-call(bf16[10,40,1280]{2,1,0:T(8,128)(2,1)S(1)} %bitcast.5, bf16[640,1280]{1,0:T(8,128)(2,1)S(1)} %copy-done.1, bf16[360,128]{1,0:T(8,128)(2,1)S(1)} %get-tuple-element.58.refs_0_, bf16[360,128]{1,0:T(8,128)(2,1)S(1)} %collective-permute-done.11.refs_1_, ...), custom_call_target="tpu_custom_call" | custom-call | flops 524288000 | bytes 3891200 | tf_op jit(solution)/shard_map/pallas_call | solution.py:393
  67.0 0.0 collective-permute-done.15.refs_1_
  67.0 0.0 collective-permute-done.16.refs_2_
  67.0 0.4 collective-permute-done.17.refs_3_
  67.4 1.5 %shard_map.62 = bf16[10,40,1280]{2,1,0:T(8,128)(2,1)} custom-call(f32[10,40,1280]{2,1,0:T(8,128)S(1)} %get-tuple-element.62.partial, bf16[512,1280]{1,0:T(8,128)(2,1)S(1)} %get-tuple-element.63.weight, bf16[152,128]{1,0:T(8,128)(2,1)S(1)} %get-tuple-element.65.refs_0_, bf16[152,128]{1,0:T(8,128)(2,1)S(1)} %collective-permute-done.15.refs_1_, ...), custom_call_target="tpu_custom_call" | custom-call | flops 524288000 | bytes 3891200 | tf_op jit(solution)/shard_map/pallas_call | solution.py:405
Async XLA Ops:
  1.1 16.9 %copy-start = (bf16[1,10,40,1280]{3,2,1,0:T(8,128)(2,1)S(1)}, bf16[1,10,40,1280]{3,2,1,0:T(8,128)(2,1)}, u32[]{:S(2)}) copy-start(bf16[1,10,40,1280]{3,2,1,0:T(8,128)(2,1)} %param.5) | copy-start | bytes 3072004
  1.1 16.9 %copy-start.2 = (f32[1280]{0:T(1024)S(1)}, f32[1280]{0:T(1024)}, u32[]{:S(2)}) copy-start(f32[1280]{0:T(1024)} %gain.3) | copy-start | bytes 15364
  1.1 16.9 %copy-start.3 = (s32[4]{0:T(128)S(1)}, s32[4]{0:T(128)}, u32[]{:S(2)}) copy-start(s32[4]{0:T(128)} %lon_shift.5) | copy-start | bytes 52
  1.2 16.9 %collective-permute-start.3 = (bf16[10,24,1280]{2,1,0:T(8,128)(2,1)S(1)}, bf16[10,24,1280]{2,1,0:T(8,128)(2,1)S(1)}, u32[]{:S(2)}, u32[]{:S(2)}) collective-permute-start(bf16[10,24,1280]{2,1,0:T(8,128)(2,1)S(1)} %slice.4), channel_id=1, source_target_pairs={{0,16},{4,20},{8,24},{12,28},{16,0},{20,4},{24,8},{28,12},{1,17},{... | collective-permute-start | bytes 1843208 | tf_op jit(solution)/shard_map/ppermute | solution.py:25
  8.7 13.7 %collective-permute-start = (bf16[160,512]{1,0:T(8,128)(2,1)}, bf16[160,512]{1,0:T(8,128)(2,1)S(1)}, u32[]{:S(2)}, u32[]{:S(2)}) collective-permute-start(bf16[160,512]{1,0:T(8,128)(2,1)} %get-tuple-element.38), channel_id=1, source_target_pairs={{0,1},{1,2},{2,3},{3,0},{4,5},{5,6},{6,7},{7,4},{8,9},{9,10},{10,1... | collective-permute-start | bytes 491528 | tf_op jit(solution)/shard_map/ppermute | solution.py:25
  10.3 14.0 %collective-permute-start.1 = (bf16[160,512]{1,0:T(8,128)(2,1)}, bf16[160,512]{1,0:T(8,128)(2,1)S(1)}, u32[]{:S(2)}, u32[]{:S(2)}) collective-permute-start(bf16[160,512]{1,0:T(8,128)(2,1)} %get-tuple-element.39), channel_id=1, source_target_pairs={{0,2},{1,3},{2,0},{3,1},{4,6},{5,7},{6,4},{7,5},{8,10},{9,11},{10,... | collective-permute-start | bytes 491528 | tf_op jit(solution)/shard_map/ppermute | solution.py:25
  12.9 27.4 %copy-start.4 = (bf16[160,512]{1,0:T(8,128)(2,1)S(1)}, bf16[160,512]{1,0:T(8,128)(2,1)}, u32[]{:S(2)}) copy-start(bf16[160,512]{1,0:T(8,128)(2,1)} %get-tuple-element.37.refs_0_) | copy-start | bytes 491524
  12.9 14.0 %collective-permute-start.2 = (bf16[160,512]{1,0:T(8,128)(2,1)}, bf16[160,512]{1,0:T(8,128)(2,1)S(1)}, u32[]{:S(2)}, u32[]{:S(2)}) collective-permute-start(bf16[160,512]{1,0:T(8,128)(2,1)} %get-tuple-element.40), channel_id=1, source_target_pairs={{0,3},{1,0},{2,1},{3,2},{4,7},{5,4},{6,5},{7,6},{8,11},{9,8},{10,9... | collective-permute-start | bytes 491528 | tf_op jit(solution)/shard_map/ppermute | solution.py:25
  22.4 7.8 %collective-permute-start.4 = (bf16[240,256]{1,0:T(8,128)(2,1)S(1)}, bf16[240,256]{1,0:T(8,128)(2,1)S(1)}, u32[]{:S(2)}, u32[]{:S(2)}) collective-permute-start(bf16[240,256]{1,0:T(8,128)(2,1)S(1)} %get-tuple-element.43), channel_id=1, source_target_pairs={{0,1},{1,2},{2,3},{3,0},{4,5},{5,6},{6,7},{7,4},{8,9},{9,10},{10,1... | collective-permute-start | bytes 368648 | tf_op jit(solution)/shard_map/ppermute | solution.py:25
  24.2 13.4 %collective-permute-start.5 = (bf16[240,256]{1,0:T(8,128)(2,1)S(1)}, bf16[240,256]{1,0:T(8,128)(2,1)S(1)}, u32[]{:S(2)}, u32[]{:S(2)}) collective-permute-start(bf16[240,256]{1,0:T(8,128)(2,1)S(1)} %get-tuple-element.45), channel_id=1, source_target_pairs={{0,2},{1,3},{2,0},{3,1},{4,6},{5,7},{6,4},{7,5},{8,10},{9,11},{10,... | collective-permute-start | bytes 368648 | tf_op jit(solution)/shard_map/ppermute | solution.py:25
  26.8 12.6 %collective-permute-start.6 = (bf16[240,256]{1,0:T(8,128)(2,1)S(1)}, bf16[240,256]{1,0:T(8,128)(2,1)S(1)}, u32[]{:S(2)}, u32[]{:S(2)}) collective-permute-start(bf16[240,256]{1,0:T(8,128)(2,1)S(1)} %get-tuple-element.47), channel_id=1, source_target_pairs={{0,3},{1,0},{2,1},{3,2},{4,7},{5,4},{6,5},{7,6},{8,11},{9,8},{10,9... | collective-permute-start | bytes 368648 | tf_op jit(solution)/shard_map/ppermute | solution.py:25
  30.2 15.9 %collective-permute-start.8 = (bf16[240,256]{1,0:T(8,128)(2,1)S(1)}, bf16[240,256]{1,0:T(8,128)(2,1)S(1)}, u32[]{:S(2)}, u32[]{:S(2)}) collective-permute-start(bf16[240,256]{1,0:T(8,128)(2,1)S(1)} %get-tuple-element.52), channel_id=1, source_target_pairs={{0,1},{1,2},{2,3},{3,0},{4,5},{5,6},{6,7},{7,4},{8,9},{9,10},{10,1... | collective-permute-start | bytes 368648 | tf_op jit(solution)/shard_map/ppermute | solution.py:25
  37.6 8.5 %collective-permute-start.9 = (bf16[240,256]{1,0:T(8,128)(2,1)S(1)}, bf16[240,256]{1,0:T(8,128)(2,1)S(1)}, u32[]{:S(2)}, u32[]{:S(2)}) collective-permute-start(bf16[240,256]{1,0:T(8,128)(2,1)S(1)} %get-tuple-element.54), channel_id=1, source_target_pairs={{0,2},{1,3},{2,0},{3,1},{4,6},{5,7},{6,4},{7,5},{8,10},{9,11},{10,... | collective-permute-start | bytes 368648 | tf_op jit(solution)/shard_map/ppermute | solution.py:25
  39.5 8.2 %collective-permute-start.10 = (bf16[240,256]{1,0:T(8,128)(2,1)S(1)}, bf16[240,256]{1,0:T(8,128)(2,1)S(1)}, u32[]{:S(2)}, u32[]{:S(2)}) collective-permute-start(bf16[240,256]{1,0:T(8,128)(2,1)S(1)} %get-tuple-element.56), channel_id=1, source_target_pairs={{0,3},{1,0},{2,1},{3,2},{4,7},{5,4},{6,5},{7,6},{8,11},{9,8},{10,9... | collective-permute-start | bytes 368648 | tf_op jit(solution)/shard_map/ppermute | solution.py:25
  44.2 7.6 %collective-permute-start.7 = (bf16[608,128]{1,0:T(8,128)(2,1)S(1)}, bf16[608,128]{1,0:T(8,128)(2,1)S(1)}, u32[]{:S(2)}, u32[]{:S(2)}) collective-permute-start(bf16[608,128]{1,0:T(8,128)(2,1)S(1)} %get-tuple-element.48.mixed), channel_id=1, source_target_pairs={{0,16},{4,20},{8,24},{12,28},{16,0},{20,4},{24,8},{28,12},{1,17},{... | collective-permute-start | bytes 466952 | tf_op jit(solution)/shard_map/ppermute | solution.py:25
  47.7 18.2 %copy-start.1 = (bf16[640,1280]{1,0:T(8,128)(2,1)S(1)}, bf16[640,1280]{1,0:T(8,128)(2,1)}, u32[]{:S(2)}) copy-start(bf16[640,1280]{1,0:T(8,128)(2,1)} %weight.5) | copy-start | bytes 4915204
  51.7 5.7 %collective-permute-start.14 = (bf16[608,128]{1,0:T(8,128)(2,1)S(1)}, bf16[608,128]{1,0:T(8,128)(2,1)S(1)}, u32[]{:S(2)}, u32[]{:S(2)}) collective-permute-start(bf16[608,128]{1,0:T(8,128)(2,1)S(1)} %get-tuple-element.64.mixed), channel_id=1, source_target_pairs={{0,16},{4,20},{8,24},{12,28},{16,0},{20,4},{24,8},{28,12},{1,17},{... | collective-permute-start | bytes 466952 | tf_op jit(solution)/shard_map/ppermute | solution.py:25
  52.4 9.2 %collective-permute-start.11 = (bf16[360,128]{1,0:T(8,128)(2,1)S(1)}, bf16[360,128]{1,0:T(8,128)(2,1)S(1)}, u32[]{:S(2)}, u32[]{:S(2)}) collective-permute-start(bf16[360,128]{1,0:T(8,128)(2,1)S(1)} %get-tuple-element.59), channel_id=1, source_target_pairs={{0,3},{1,0},{2,1},{3,2},{4,7},{5,4},{6,5},{7,6},{8,11},{9,8},{10,9... | collective-permute-start | bytes 276488 | tf_op jit(solution)/shard_map/ppermute | solution.py:25
  56.0 9.9 %collective-permute-start.12 = (bf16[360,128]{1,0:T(8,128)(2,1)S(1)}, bf16[360,128]{1,0:T(8,128)(2,1)S(1)}, u32[]{:S(2)}, u32[]{:S(2)}) collective-permute-start(bf16[360,128]{1,0:T(8,128)(2,1)S(1)} %get-tuple-element.60), channel_id=1, source_target_pairs={{0,2},{1,3},{2,0},{3,1},{4,6},{5,7},{6,4},{7,5},{8,10},{9,11},{10,... | collective-permute-start | bytes 276488 | tf_op jit(solution)/shard_map/ppermute | solution.py:25
  56.0 9.9 %collective-permute-start.13 = (bf16[360,128]{1,0:T(8,128)(2,1)S(1)}, bf16[360,128]{1,0:T(8,128)(2,1)S(1)}, u32[]{:S(2)}, u32[]{:S(2)}) collective-permute-start(bf16[360,128]{1,0:T(8,128)(2,1)S(1)} %get-tuple-element.61), channel_id=1, source_target_pairs={{0,1},{1,2},{2,3},{3,0},{4,5},{5,6},{6,7},{7,4},{8,9},{9,10},{10,1... | collective-permute-start | bytes 276488 | tf_op jit(solution)/shard_map/ppermute | solution.py:25
  58.1 8.9 %collective-permute-start.15 = (bf16[152,128]{1,0:T(8,128)(2,1)S(1)}, bf16[152,128]{1,0:T(8,128)(2,1)S(1)}, u32[]{:S(2)}, u32[]{:S(2)}) collective-permute-start(bf16[152,128]{1,0:T(8,128)(2,1)S(1)} %get-tuple-element.66), channel_id=1, source_target_pairs={{0,3},{1,0},{2,1},{3,2},{4,7},{5,4},{6,5},{7,6},{8,11},{9,8},{10,9... | collective-permute-start | bytes 116744 | tf_op jit(solution)/shard_map/ppermute | solution.py:25
  60.5 6.5 %collective-permute-start.16 = (bf16[152,128]{1,0:T(8,128)(2,1)S(1)}, bf16[152,128]{1,0:T(8,128)(2,1)S(1)}, u32[]{:S(2)}, u32[]{:S(2)}) collective-permute-start(bf16[152,128]{1,0:T(8,128)(2,1)S(1)} %get-tuple-element.67), channel_id=1, source_target_pairs={{0,2},{1,3},{2,0},{3,1},{4,6},{5,7},{6,4},{7,5},{8,10},{9,11},{10,... | collective-permute-start | bytes 116744 | tf_op jit(solution)/shard_map/ppermute | solution.py:25
  61.6 5.8 %collective-permute-start.17 = (bf16[152,128]{1,0:T(8,128)(2,1)S(1)}, bf16[152,128]{1,0:T(8,128)(2,1)S(1)}, u32[]{:S(2)}, u32[]{:S(2)}) collective-permute-start(bf16[152,128]{1,0:T(8,128)(2,1)S(1)} %get-tuple-element.68), channel_id=1, source_target_pairs={{0,1},{1,2},{2,3},{3,0},{4,5},{5,6},{6,7},{7,4},{8,9},{9,10},{10,1... | collective-permute-start | bytes 116744 | tf_op jit(solution)/shard_map/ppermute | solution.py:25

commit v12 on v11

--- a/solution.py
+++ b/solution.py
@@ -14,6 +14,7 @@
 SUBLANES = 8
 MIB = 1024 * 1024
 CHUNKS = 5
+MAX_STEP = 320
 
 
 def round_up(value, unit):
@@ -107,6 +108,14 @@
         out[...] = slots[index % groups, :, first : first + out.shape[1]]
 
 
+FACTOR = HD ** (-0.5) * 1.4426950408889634
+CHUNK = 16
+
+
+def step_of(count):
+    return max(step for step in range(CHUNK, MAX_STEP + 1, CHUNK) if count % step == 0)
+
+
 def gather(head, kept, mixed, held, keys):
     span = held.shape[1]
     start = 0
@@ -119,34 +128,105 @@
     keys[...] = held[:, :LANES].T
 
 
-def attend(held, keys, attended, scores, weights):
-    span = held.shape[1]
-    factor = HD ** (-0.5) * 1.4426950408889634
-    step = scores[0].shape[0]
-    chunk = 16
-    steps = held.shape[0] // step
-
-    def score(index, out):
-        first = index * step
-        queries = pltpu.roll(held[first : first + step].astype(jnp.float32), span - HD, axis=1)
-        queries = queries[:, :LANES]
-        lane = lax.broadcasted_iota(jnp.int32, queries.shape, 1)
-        queries = jnp.where(lane < HD, queries * factor, 0.0).astype(jnp.bfloat16)
-        out[...] = jnp.dot(queries, keys[...], preferred_element_type=jnp.float32)
-
-    score(0, scores[0])
-    for index in range(steps):
-        if index + 1 < steps:
-            score(index + 1, scores[(index + 1) % 2])
+def queries_of(held, first, count):
+    queries = pltpu.roll(held[first : first + count].astype(jnp.float32), held.shape[1] - HD, axis=1)
+    queries = queries[:, :LANES]
+    lane = lax.broadcasted_iota(jnp.int32, queries.shape, 1)
+    return jnp.where(lane < HD, queries, 0.0).astype(jnp.bfloat16)
+
+
+def scaled(values, span):
+    first = 2 * HD - (span - LANES)
+    values = values / values[:, first + HD : first + HD + 1]
+    return pltpu.roll(values, LANES - first, axis=1)
+
+
+def attend(queries, sources, scores, weights, finish):
+    count = queries.shape[0]
+    step = step_of(count)
+    span = queries.shape[1]
+
+    def score(index):
+        block = queries_of(queries, index * step, step)
+        start = 0
+        for _, keys in sources:
+            columns = slice(start, start + keys.shape[1])
+            scores[index % 2][:step, columns] = jnp.dot(
+                block, keys[...], preferred_element_type=jnp.float32
+            )
+            start += round_up(keys.shape[1], LANES)
+
+    score(0)
+    for index in range(count // step):
+        if (index + 1) * step < count:
+            score(index + 1)
         now, out = scores[index % 2], weights[index % 2]
-        for first in range(0, step, chunk):
-            part = now[first : first + chunk]
-            top = jnp.max(part, axis=-1, keepdims=True)
-            out[first : first + chunk] = jnp.exp2(part - top).astype(jnp.bfloat16)
-        values = jnp.dot(out[...], held[:, span - LANES :], preferred_element_type=jnp.float32)
-        first = 2 * HD - (span - LANES)
-        values = values / values[:, first + HD : first + HD + 1]
-        attended[index * step : (index + 1) * step] = pltpu.roll(values, LANES - first, axis=1)
+        spots, start = [], 0
+        for held, keys in sources:
+            spots.append((held, slice(start, start + keys.shape[1])))
+            start += round_up(keys.shape[1], LANES)
+        finish(index * step, step, now, out, spots)
+
+
+def top_of(now, rows, spots):
+    tops = [jnp.max(now[rows, columns], axis=-1, keepdims=True) for _, columns in spots]
+    return functools.reduce(jnp.maximum, tops)
+
+
+def weigh(now, out, rows, spots, top):
+    for _, columns in spots:
+        out[rows, columns] = jnp.exp2((now[rows, columns] - top) * FACTOR).astype(jnp.bfloat16)
+
+
+def summed(out, step, spots):
+    shares = [
+        jnp.dot(
+            out[:step, columns],
+            held[:, held.shape[1] - LANES :],
+            preferred_element_type=jnp.float32,
+        )
+        for held, columns in spots
+    ]
+    return functools.reduce(jnp.add, shares)
+
+
+def chunks(step):
+    return [slice(first, first + CHUNK) for first in range(0, step, CHUNK)]
+
+
+def finish_whole(attended, base, span):
+    def finish(first, step, now, out, spots):
+        for rows in chunks(step):
+            weigh(now, out, rows, spots, top_of(now, rows, spots))
+        attended[base + first : base + first + step] = scaled(summed(out, step, spots), span)
+
+    return finish
+
+
+def finish_early(sums, tops):
+    def finish(first, step, now, out, spots):
+        for rows in chunks(step):
+            top = top_of(now, rows, spots)
+            weigh(now, out, rows, spots, top)
+            tops[first + rows.start : first + rows.stop] = jnp.broadcast_to(top, (CHUNK, LANES))
+        sums[first : first + step] = summed(out, step, spots)
+
+    return finish
+
+
+def finish_late(attended, sums, tops, span):
+    def finish(first, step, now, out, spots):
+        shrinks = []
+        for rows in chunks(step):
+            before = tops[first + rows.start : first + rows.stop]
+            top = jnp.maximum(top_of(now, rows, spots), before[:, :1])
+            weigh(now, out, rows, spots, top)
+            shrinks.append(jnp.exp2((before - top) * FACTOR))
+        shrink = jnp.concatenate(shrinks, axis=0)
+        values = summed(out, step, spots) + sums[first : first + step] * shrink
+        attended[first : first + step] = scaled(values, span)
+
+    return finish
 
 
 def packed_rows(count):
@@ -199,18 +279,44 @@
     return jnp.where(row < count // 2, main, rests)
 
 
-def attention_kernel(head, groups, *refs):
+def pack_all(attended, kept_count, mixed_count, kept_out, mixed_out):
+    start = 0
+    for count, out in ((kept_count, kept_out), (mixed_count, mixed_out)):
+        size = packed_rows(count)[0]
+        packed = []
+        for _ in range(out.shape[0] // size):
+            packed.append(pack(attended[start : start + count]))
+            start += count
+        out[...] = jnp.concatenate(packed, axis=0).astype(jnp.bfloat16)
+
+
+def first_head_kernel(groups, *refs):
     kept, mixed = refs[:groups], refs[groups : 2 * groups]
     kept_out, mixed_out, held, keys, attended, *rest = refs[2 * groups :]
-    gather(head, kept, mixed, held, keys)
-    attend(held, keys, attended, rest[:2], rest[2:])
-    start = 0
-    for blocks, out in ((kept, kept_out), (mixed, mixed_out)):
-        packed = []
-        for block in blocks:
-            packed.append(pack(attended[start : start + block.shape[0]]))
-            start += block.shape[0]
-        out[...] = jnp.concatenate(packed, axis=0).astype(jnp.bfloat16)
+    gather(0, kept, mixed, held, keys)
+    finish = finish_whole(attended, 0, held.shape[1])
+    attend(held, [(held, keys)], rest[:2], rest[2:], finish)
+    pack_all(attended, kept[0].shape[0], mixed[0].shape[0], kept_out, mixed_out)
+
+
+def early_kernel(groups, early, *refs):
+    kept, mixed = refs[:groups], refs[groups : groups + early]
+    sums, tops, held, keys, *rest = refs[groups + early :]
+    gather(1, kept, mixed, held, keys)
+    attend(held, [(held, keys)], rest[:2], rest[2:], finish_early(sums, tops))
+
+
+def late_kernel(kept_count, sums, tops, early_held, early_keys, *refs):
+    *mixed, kept_out, mixed_out, held, keys, attended, s0, s1, w0, w1 = refs
+    gather(1, [], mixed, held, keys)
+    span = held.shape[1]
+    early = early_held.shape[0]
+    attend(
+        early_held, [(held, keys)], (s0, s1), (w0, w1), finish_late(attended, sums, tops, span)
+    )
+    both = [(early_held, early_keys), (held, keys)]
+    attend(held, both, (s0, s1), (w0, w1), finish_whole(attended, early, span))
+    pack_all(attended, kept_count, mixed[0].shape[0], kept_out, mixed_out)
 
 
 def select_kernel(split, count, groups, lon_shift, mixed, western, *refs):
@@ -336,35 +442,66 @@
     second_mixed = spread(after(mixed[groups:], [None, *first_mixed[1:]]), 1)
 
     total = groups * rows * columns
-    step = total // 5
+    ahead = max(groups // 2, 1)
+    early = groups * kept_count + ahead * mixed_count
     mixed_packed, kept_packed = packed_rows(mixed_count)[0], packed_rows(kept_count)[0]
 
     def block(count):
         return jax.ShapeDtypeStruct((count, LANES), jnp.bfloat16)
 
-    def attention(head, *blocks):
+    def rows_of(count, lanes, dtype):
+        return jax.ShapeDtypeStruct((count, lanes), dtype)
+
+    def gathered(count):
+        return [rows_of(count, span, jnp.bfloat16), rows_of(LANES, count, jnp.bfloat16)]
+
+    def attention(kernel, out_shape, held, scores, pairs, *blocks):
+        scratch = [pltpu.VMEM(leaf.shape, leaf.dtype) for leaf in held]
+        scratch += [pltpu.VMEM(scores, jnp.float32)] * 2 + [pltpu.VMEM(scores, jnp.bfloat16)] * 2
         return pl.pallas_call(
-            functools.partial(attention_kernel, head, groups),
-            out_shape=[block(groups * kept_packed), block(groups * mixed_packed)],
+            kernel,
+            out_shape=out_shape,
             in_specs=whole(len(blocks)),
-            out_specs=whole(2),
-            scratch_shapes=[
-                pltpu.VMEM((total, span), jnp.bfloat16),
-                pltpu.VMEM((LANES, total), jnp.bfloat16),
-                pltpu.VMEM((total, LANES), jnp.float32),
-                pltpu.VMEM((step, total), jnp.float32),
-                pltpu.VMEM((step, total), jnp.float32),
-                pltpu.VMEM((step, total), jnp.bfloat16),
-                pltpu.VMEM((step, total), jnp.bfloat16),
-            ],
+            out_specs=whole(len(out_shape)),
+            scratch_shapes=scratch,
             compiler_params=limit(32),
             cost_estimate=pl.CostEstimate(
-                flops=4 * total * total * span,
+                flops=4 * pairs * span,
                 bytes_accessed=2 * total * (span + LANES),
-                transcendentals=total * total,
+                transcendentals=pairs,
             ),
         )(*blocks)
 
+    values = [block(groups * kept_packed), block(groups * mixed_packed)]
+    attended = rows_of(total, LANES, jnp.float32)
+    wide = round_up(early, LANES) + round_up(total - early, LANES)
+    first_kept_values, first_mixed_values = attention(
+        functools.partial(first_head_kernel, groups),
+        values,
+        [*gathered(total), attended],
+        (MAX_STEP, total),
+        total * total,
+        *kept,
+        *first_mixed,
+    )
+    partial = attention(
+        functools.partial(early_kernel, groups, ahead),
+        [rows_of(early, LANES, jnp.float32)] * 2 + gathered(early),
+        [],
+        (MAX_STEP, early),
+        early * early,
+        *kept,
+        *second_mixed[:ahead],
+    )
+    second_kept_values, second_mixed_values = attention(
+        functools.partial(late_kernel, kept_count),
+        values,
+        [*gathered(total - early), attended],
+        (MAX_STEP, wide),
+        total * total - early * early,
+        *partial,
+        *second_mixed[ahead:],
+    )
     def back(mixed_values, *kept_values):
         western = shifted(mixed_values, "win", LAT_WINDOWS)
         selected = pl.pallas_call(
@@ -379,8 +516,6 @@
         )(lon_shift, mixed_values, western, *kept_values)
         return spread(selected, -1)
 
-    first_kept_values, first_mixed_values = attention(0, *kept, *first_mixed)
-    second_kept_values, second_mixed_values = attention(1, *kept, *second_mixed)
     first = back(first_mixed_values, first_kept_values, second_kept_values)
     second = back(second_mixed_values)
 

time: 69.1 us -> 70.1 us (1.014)
  Pallas kernels: 20.5 us -> 23 us
  waiting for transfers between devices: 14.5 us -> 13.3 us
    pallas_call x2 -> x3, Pallas kernels: 7.99 us -> 10.5 us  [attention(): pl.pallas_call(kernel, out_shape=out_shape, in_specs=whole(len(blocks)),...]
    ppermute x18, waiting for transfers between devices: 14.5 us -> 13.3 us  [shifted(): lax.ppermute(block, axis, [(i, (i + distance) % count) for i in range(cou...]
  transfers between devices with their start and end apart: 18 -> 18, of which waited for: 8 -> 6; matrix products, arithmetic and copies ran while one was open for 0% -> 0% of each run, Pallas kernels for 28% -> 31%
where the time goes in v12:
time: 70.1 us; the launch traced here: 69.9 us
  starting transfers between devices  32.3 us (46%)
  Pallas kernels  23 us (33%)
  waiting for transfers between devices  13.3 us (19%)
  local copies, waits for them, and re-layouts  1.14 us (2%)
    ppermute x18, starting transfers between devices, shifted(): lax.ppermute(block, axis, [(i, (i + distance) % count) for i in range(cou...  32.3 us
    ppermute x18, waiting for transfers between devices, shifted(): lax.ppermute(block, axis, [(i, (i + distance) % count) for i in range(cou...  13.3 us
    pallas_call x3, Pallas kernels, attention(): pl.pallas_call(kernel, out_shape=out_shape, in_specs=whole(len(blocks)),...  10.5 us
    pallas_call x2, Pallas kernels, projection(): pl.pallas_call(functools.partial(kernel, split), out_shape=[block] * (par...  8.77 us
    pallas_call x1, Pallas kernels, shards(): pl.pallas_call(functools.partial(second_output_kernel, split), out_shape=...  1.52 us
  transfers between devices with their start and end apart: 18, of which 6 were waited for; matrix products, arithmetic and copies ran while one was open for 0% of the time, Pallas kernels for 31%

profile of v12, /device:TPU:0, one launch (start us, length us, event | category | flops | bytes accessed | tf_op | source)
XLA Modules:
  0.0 69.9 jit_solution(16540731022636640494)
XLA Ops:
  0.0 1.1 %slice.4 = bf16[10,24,1280]{2,1,0:T(8,128)(2,1)S(1)} slice(bf16[10,40,1280]{2,1,0:T(8,128)(2,1)} %bitcast.2), slice={[0:10], [0:24], [0:1280]} | slice | bytes 1228800 | tf_op jit(solution)/shard_map/slice | solution.py:423
  1.1 0.0 copy-start
  1.1 0.0 copy-start.2
  1.1 0.0 copy-start.3
  1.2 3.0 %collective-permute-start.3 = (bf16[10,24,1280]{2,1,0:T(8,128)(2,1)S(1)}, bf16[10,24,1280]{2,1,0:T(8,128)(2,1)S(1)}, u32[]{:S(2)}, u32[]{:S(2)}) collective-permute-start(bf16[10,24,1280]{2,1,0:T(8,128)(2,1)S(1)} %slice.4), channel_id=1, source_target_pairs={{0,16},{4,20},{8,24},{12,28},{16,0},{20,4},{24,8},{28,12},{1,17},{... | collective-permute-start | bytes 1843208 | tf_op jit(solution)/shard_map/ppermute | solution.py:26
  4.2 4.5 %shard_map.55 = (bf16[160,512]{1,0:T(8,128)(2,1)}, bf16[160,512]{1,0:T(8,128)(2,1)}, bf16[160,512]{1,0:T(8,128)(2,1)}, bf16[160,512]{1,0:T(8,128)(2,1)}) custom-call(bf16[10,40,1280]{2,1,0:T(8,128)(2,1)} %bitcast.3, f32[1280]{0:T(1024)} %gain.3, bf16[1280,1920]{1,0:T(8,128)(2,1)} %weight.4), custom_call_target="tpu_custom_call" | custom-call | flops 786432000 | bytes 5734400 | tf_op jit(solution)/shard_map/pallas_call | solution.py:400
  8.7 1.6 %collective-permute-start = (bf16[160,512]{1,0:T(8,128)(2,1)}, bf16[160,512]{1,0:T(8,128)(2,1)S(1)}, u32[]{:S(2)}, u32[]{:S(2)}) collective-permute-start(bf16[160,512]{1,0:T(8,128)(2,1)} %get-tuple-element.42), channel_id=1, source_target_pairs={{0,1},{1,2},{2,3},{3,0},{4,5},{5,6},{6,7},{7,4},{8,9},{9,10},{10,1... | collective-permute-start | bytes 491528 | tf_op jit(solution)/shard_map/ppermute | solution.py:26
  10.3 2.6 %collective-permute-start.1 = (bf16[160,512]{1,0:T(8,128)(2,1)}, bf16[160,512]{1,0:T(8,128)(2,1)S(1)}, u32[]{:S(2)}, u32[]{:S(2)}) collective-permute-start(bf16[160,512]{1,0:T(8,128)(2,1)} %get-tuple-element.43), channel_id=1, source_target_pairs={{0,2},{1,3},{2,0},{3,1},{4,6},{5,7},{6,4},{7,5},{8,10},{9,11},{10,... | collective-permute-start | bytes 491528 | tf_op jit(solution)/shard_map/ppermute | solution.py:26
  12.9 0.0 copy-start.4
  12.9 1.3 %collective-permute-start.2 = (bf16[160,512]{1,0:T(8,128)(2,1)}, bf16[160,512]{1,0:T(8,128)(2,1)S(1)}, u32[]{:S(2)}, u32[]{:S(2)}) collective-permute-start(bf16[160,512]{1,0:T(8,128)(2,1)} %get-tuple-element.44), channel_id=1, source_target_pairs={{0,3},{1,0},{2,1},{3,2},{4,7},{5,4},{6,5},{7,6},{8,11},{9,8},{10,9... | collective-permute-start | bytes 491528 | tf_op jit(solution)/shard_map/ppermute | solution.py:26
  14.2 3.8 %collective-permute-done.3.eastern = bf16[10,24,1280]{2,1,0:T(8,128)(2,1)S(1)} collective-permute-done((bf16[10,24,1280]{2,1,0:T(8,128)(2,1)S(1)}, bf16[10,24,1280]{2,1,0:T(8,128)(2,1)S(1)}, u32[]{:S(2)}, u32[]{:S(2)}) %collective-permute-start.3) | collective-permute-done | bytes 614432 | tf_op jit(solution)/shard_map/ppermute | solution.py:26
  18.0 0.0 copy-done
  18.0 0.0 copy-done.2
  18.0 0.0 copy-done.3
  18.1 4.3 %shard_map.56 = (bf16[240,256]{1,0:T(8,128)(2,1)S(1)}, bf16[240,256]{1,0:T(8,128)(2,1)S(1)}, bf16[240,256]{1,0:T(8,128)(2,1)S(1)}, bf16[240,256]{1,0:T(8,128)(2,...) custom-call(bf16[10,40,1280]{2,1,0:T(8,128)(2,1)S(1)} %bitcast.4, ...), custom_call_target="tpu_custom_call" | custom-call | flops 1179648000 | bytes 6144000 | tf_op jit(solution)/shard_map/pallas_call | solution.py:400
  22.4 0.0 collective-permute-done.refs_1_
  22.4 1.9 %collective-permute-start.4 = (bf16[240,256]{1,0:T(8,128)(2,1)S(1)}, bf16[240,256]{1,0:T(8,128)(2,1)S(1)}, u32[]{:S(2)}, u32[]{:S(2)}) collective-permute-start(bf16[240,256]{1,0:T(8,128)(2,1)S(1)} %get-tuple-element.47), channel_id=1, source_target_pairs={{0,1},{1,2},{2,3},{3,0},{4,5},{5,6},{6,7},{7,4},{8,9},{9,10},{10,1... | collective-permute-start | bytes 368648 | tf_op jit(solution)/shard_map/ppermute | solution.py:26
  24.2 0.0 collective-permute-done.1.refs_2_
  24.2 2.6 %collective-permute-start.5 = (bf16[240,256]{1,0:T(8,128)(2,1)S(1)}, bf16[240,256]{1,0:T(8,128)(2,1)S(1)}, u32[]{:S(2)}, u32[]{:S(2)}) collective-permute-start(bf16[240,256]{1,0:T(8,128)(2,1)S(1)} %get-tuple-element.49), channel_id=1, source_target_pairs={{0,2},{1,3},{2,0},{3,1},{4,6},{5,7},{6,4},{7,5},{8,10},{9,11},{10,... | collective-permute-start | bytes 368648 | tf_op jit(solution)/shard_map/ppermute | solution.py:26
  26.8 0.0 collective-permute-done.2.refs_3_
  26.8 2.6 %collective-permute-start.6 = (bf16[240,256]{1,0:T(8,128)(2,1)S(1)}, bf16[240,256]{1,0:T(8,128)(2,1)S(1)}, u32[]{:S(2)}, u32[]{:S(2)}) collective-permute-start(bf16[240,256]{1,0:T(8,128)(2,1)S(1)} %get-tuple-element.51), channel_id=1, source_target_pairs={{0,3},{1,0},{2,1},{3,2},{4,7},{5,4},{6,5},{7,6},{8,11},{9,8},{10,9... | collective-permute-start | bytes 368648 | tf_op jit(solution)/shard_map/ppermute | solution.py:26
  29.4 0.8 %collective-permute-done.4.refs_5_ = bf16[240,256]{1,0:T(8,128)(2,1)S(1)} collective-permute-done((bf16[240,256]{1,0:T(8,128)(2,1)S(1)}, bf16[240,256]{1,0:T(8,128)(2,1)S(1)}, u32[]{:S(2)}, u32[]{:S(2)}) %collective-permute-start.4) | collective-permute-done | bytes 122912 | tf_op jit(solution)/shard_map/ppermute | solution.py:26
  30.2 4.6 %collective-permute-start.8 = (bf16[240,256]{1,0:T(8,128)(2,1)S(1)}, bf16[240,256]{1,0:T(8,128)(2,1)S(1)}, u32[]{:S(2)}, u32[]{:S(2)}) collective-permute-start(bf16[240,256]{1,0:T(8,128)(2,1)S(1)} %get-tuple-element.56), channel_id=1, source_target_pairs={{0,1},{1,2},{2,3},{3,0},{4,5},{5,6},{6,7},{7,4},{8,9},{9,10},{10,1... | collective-permute-start | bytes 368648 | tf_op jit(solution)/shard_map/ppermute | solution.py:26
  34.8 2.8 %collective-permute-done.5.refs_6_ = bf16[240,256]{1,0:T(8,128)(2,1)S(1)} collective-permute-done((bf16[240,256]{1,0:T(8,128)(2,1)S(1)}, bf16[240,256]{1,0:T(8,128)(2,1)S(1)}, u32[]{:S(2)}, u32[]{:S(2)}) %collective-permute-start.5) | collective-permute-done | bytes 122912 | tf_op jit(solution)/shard_map/ppermute | solution.py:26
  37.6 0.0 collective-permute-start.9
  37.6 1.9 %collective-permute-done.6.refs_7_ = bf16[240,256]{1,0:T(8,128)(2,1)S(1)} collective-permute-done((bf16[240,256]{1,0:T(8,128)(2,1)S(1)}, bf16[240,256]{1,0:T(8,128)(2,1)S(1)}, u32[]{:S(2)}, u32[]{:S(2)}) %collective-permute-start.6) | collective-permute-done | bytes 122912 | tf_op jit(solution)/shard_map/ppermute | solution.py:26
  39.5 0.8 %collective-permute-start.10 = (bf16[240,256]{1,0:T(8,128)(2,1)S(1)}, bf16[240,256]{1,0:T(8,128)(2,1)S(1)}, u32[]{:S(2)}, u32[]{:S(2)}) collective-permute-start(bf16[240,256]{1,0:T(8,128)(2,1)S(1)} %get-tuple-element.64), channel_id=1, source_target_pairs={{0,3},{1,0},{2,1},{3,2},{4,7},{5,4},{6,5},{7,6},{8,11},{9,8},{10,9... | collective-permute-start | bytes 368648 | tf_op jit(solution)/shard_map/ppermute | solution.py:26
  40.2 0.0 copy-done.4
  40.2 4.0 %shard_map.57 = (bf16[416,128]{1,0:T(8,128)(2,1)S(1)}, bf16[608,128]{1,0:T(8,128)(2,1)S(1)}) custom-call(bf16[160,512]{1,0:T(8,128)(2,1)S(1)} %copy-done.4, bf16[160,512]{1,0:T(8,128)(2,1)S(1)} %collective-permute-done.refs_1_, bf16[160,512]{1,0:T(8,128)(2,1)S(1)} %collective-permute-done.1.refs_2_, bf16[160,512]{1,0:T(8,128)(2,1)S(1)} %collective-permute-done.2.refs_3_, ...), custom_call_target="tpu_custom_call" | custom-call | flops 2621440000 | bytes 1228800 | tf_op jit(solution)/shard_map/pallas_call | solution.py:461
  44.3 1.8 %collective-permute-start.7 = (bf16[608,128]{1,0:T(8,128)(2,1)S(1)}, bf16[608,128]{1,0:T(8,128)(2,1)S(1)}, u32[]{:S(2)}, u32[]{:S(2)}) collective-permute-start(bf16[608,128]{1,0:T(8,128)(2,1)S(1)} %get-tuple-element.52.mixed), channel_id=1, source_target_pairs={{0,16},{4,20},{8,24},{12,28},{16,0},{20,4},{24,8},{28,12},{1,17},{... | collective-permute-start | bytes 466952 | tf_op jit(solution)/shard_map/ppermute | solution.py:26
  46.1 0.0 collective-permute-done.8.refs_5_
  46.1 2.3 %shard_map.58 = (f32[1120,128]{1,0:T(8,128)S(1)}, f32[1120,128]{1,0:T(8,128)S(1)}, bf16[1120,256]{1,0:T(8,128)(2,1)S(1)}, bf16[128,1120]{1,0:T(8,128)(2,1)S(1)}) custom-call(bf16[160,512]{1,0:T(8,128)(2,1)S(1)} %copy-done.4, bf16[160,512]{1,0:T(8,128)(2,1)S(1)} %collective-permute-done.refs_1_, bf16[160,512]{1,0:T(8,128)(2,1)S(1)} %collective-permute-done.1.refs_2_, ...), custom_call_target="tpu_custom_call" | custom-call | flops 1284505600 | bytes 1228800 | tf_op jit(solution)/shard_map/pallas_call | solution.py:461
  48.3 0.0 collective-permute-done.9.refs_0_
  48.4 0.0 collective-permute-done.10.refs_1_
  48.4 0.0 copy-start.1
  48.4 4.2 %shard_map.59 = (bf16[416,128]{1,0:T(8,128)(2,1)S(1)}, bf16[608,128]{1,0:T(8,128)(2,1)S(1)}) custom-call(f32[1120,128]{1,0:T(8,128)S(1)} %get-tuple-element.57.sums, f32[1120,128]{1,0:T(8,128)S(1)} %get-tuple-element.58.tops, bf16[1120,256]{1,0:T(8,128)(2,1)S(1)} %get-tuple-element.59.early_held, bf16[128,1120]{1,0:T(8,128)(2,1)S(1)} %get-tuple-element.60.early_keys, ...), custom_call_target="tpu_custom_call" | custom-call | flops 1336934400 | bytes 1228800 | tf_op jit(solution)/shard_map/pallas_call | solution.py:461
  52.6 0.3 collective-permute-start.14
  52.9 0.0 collective-permute-done.7.western
  53.0 0.6 shard_map.60
  53.6 2.7 %collective-permute-start.11 = (bf16[360,128]{1,0:T(8,128)(2,1)S(1)}, bf16[360,128]{1,0:T(8,128)(2,1)S(1)}, u32[]{:S(2)}, u32[]{:S(2)}) collective-permute-start(bf16[360,128]{1,0:T(8,128)(2,1)S(1)} %get-tuple-element.67), channel_id=1, source_target_pairs={{0,3},{1,0},{2,1},{3,2},{4,7},{5,4},{6,5},{7,6},{8,11},{9,8},{10,9... | collective-permute-start | bytes 276488 | tf_op jit(solution)/shard_map/ppermute | solution.py:26
  56.3 0.8 %collective-permute-start.12 = (bf16[360,128]{1,0:T(8,128)(2,1)S(1)}, bf16[360,128]{1,0:T(8,128)(2,1)S(1)}, u32[]{:S(2)}, u32[]{:S(2)}) collective-permute-start(bf16[360,128]{1,0:T(8,128)(2,1)S(1)} %get-tuple-element.68), channel_id=1, source_target_pairs={{0,2},{1,3},{2,0},{3,1},{4,6},{5,7},{6,4},{7,5},{8,10},{9,11},{10,... | collective-permute-start | bytes 276488 | tf_op jit(solution)/shard_map/ppermute | solution.py:26
  57.0 1.9 %collective-permute-start.13 = (bf16[360,128]{1,0:T(8,128)(2,1)S(1)}, bf16[360,128]{1,0:T(8,128)(2,1)S(1)}, u32[]{:S(2)}, u32[]{:S(2)}) collective-permute-start(bf16[360,128]{1,0:T(8,128)(2,1)S(1)} %get-tuple-element.69), channel_id=1, source_target_pairs={{0,1},{1,2},{2,3},{3,0},{4,5},{5,6},{6,7},{7,4},{8,9},{9,10},{10,1... | collective-permute-start | bytes 276488 | tf_op jit(solution)/shard_map/ppermute | solution.py:26
  59.0 0.0 collective-permute-done.14.western
  59.0 0.6 shard_map.62
  59.6 1.9 %collective-permute-start.15 = (bf16[152,128]{1,0:T(8,128)(2,1)S(1)}, bf16[152,128]{1,0:T(8,128)(2,1)S(1)}, u32[]{:S(2)}, u32[]{:S(2)}) collective-permute-start(bf16[152,128]{1,0:T(8,128)(2,1)S(1)} %get-tuple-element.74), channel_id=1, source_target_pairs={{0,3},{1,0},{2,1},{3,2},{4,7},{5,4},{6,5},{7,6},{8,11},{9,8},{10,9... | collective-permute-start | bytes 116744 | tf_op jit(solution)/shard_map/ppermute | solution.py:26
  61.5 0.4 collective-permute-start.16
  61.9 0.0 collective-permute-done.11.refs_1_
  61.9 1.5 %collective-permute-start.17 = (bf16[152,128]{1,0:T(8,128)(2,1)S(1)}, bf16[152,128]{1,0:T(8,128)(2,1)S(1)}, u32[]{:S(2)}, u32[]{:S(2)}) collective-permute-start(bf16[152,128]{1,0:T(8,128)(2,1)S(1)} %get-tuple-element.76), channel_id=1, source_target_pairs={{0,1},{1,2},{2,3},{3,0},{4,5},{5,6},{6,7},{7,4},{8,9},{9,10},{10,1... | collective-permute-start | bytes 116744 | tf_op jit(solution)/shard_map/ppermute | solution.py:26
  63.4 3.7 %collective-permute-done.12.refs_2_ = bf16[360,128]{1,0:T(8,128)(2,1)S(1)} collective-permute-done((bf16[360,128]{1,0:T(8,128)(2,1)S(1)}, bf16[360,128]{1,0:T(8,128)(2,1)S(1)}, u32[]{:S(2)}, u32[]{:S(2)}) %collective-permute-start.12) | collective-permute-done | bytes 92192 | tf_op jit(solution)/shard_map/ppermute | solution.py:26
  67.1 0.0 collective-permute-done.13.refs_3_
  67.1 0.0 copy-done.1
  67.1 1.0 %shard_map.61 = (f32[10,40,1280]{2,1,0:T(8,128)S(1)}, bf16[512,1280]{1,0:T(8,128)(2,1)S(1)}) custom-call(bf16[10,40,1280]{2,1,0:T(8,128)(2,1)S(1)} %bitcast.5, bf16[640,1280]{1,0:T(8,128)(2,1)S(1)} %copy-done.1, bf16[360,128]{1,0:T(8,128)(2,1)S(1)} %get-tuple-element.66.refs_0_, bf16[360,128]{1,0:T(8,128)(2,1)S(1)} %collective-permute-done.11.refs_1_, ...), custom_call_target="tpu_custom_call" | custom-call | flops 524288000 | bytes 3891200 | tf_op jit(solution)/shard_map/pallas_call | solution.py:528
  68.1 0.0 collective-permute-done.15.refs_1_
  68.1 0.2 collective-permute-done.16.refs_2_
  68.3 0.0 collective-permute-done.17.refs_3_
  68.3 1.5 %shard_map.63 = bf16[10,40,1280]{2,1,0:T(8,128)(2,1)} custom-call(f32[10,40,1280]{2,1,0:T(8,128)S(1)} %get-tuple-element.70.partial, bf16[512,1280]{1,0:T(8,128)(2,1)S(1)} %get-tuple-element.71.weight, bf16[152,128]{1,0:T(8,128)(2,1)S(1)} %get-tuple-element.73.refs_0_, bf16[152,128]{1,0:T(8,128)(2,1)S(1)} %collective-permute-done.15.refs_1_, ...), custom_call_target="tpu_custom_call" | custom-call | flops 524288000 | bytes 3891200 | tf_op jit(solution)/shard_map/pallas_call | solution.py:540
Async XLA Ops:
  1.1 16.9 %copy-start = (bf16[1,10,40,1280]{3,2,1,0:T(8,128)(2,1)S(1)}, bf16[1,10,40,1280]{3,2,1,0:T(8,128)(2,1)}, u32[]{:S(2)}) copy-start(bf16[1,10,40,1280]{3,2,1,0:T(8,128)(2,1)} %param.5) | copy-start | bytes 3072004
  1.1 16.9 %copy-start.2 = (f32[1280]{0:T(1024)S(1)}, f32[1280]{0:T(1024)}, u32[]{:S(2)}) copy-start(f32[1280]{0:T(1024)} %gain.3) | copy-start | bytes 15364
  1.1 16.9 %copy-start.3 = (s32[4]{0:T(128)S(1)}, s32[4]{0:T(128)}, u32[]{:S(2)}) copy-start(s32[4]{0:T(128)} %lon_shift.5) | copy-start | bytes 52
  1.2 16.9 %collective-permute-start.3 = (bf16[10,24,1280]{2,1,0:T(8,128)(2,1)S(1)}, bf16[10,24,1280]{2,1,0:T(8,128)(2,1)S(1)}, u32[]{:S(2)}, u32[]{:S(2)}) collective-permute-start(bf16[10,24,1280]{2,1,0:T(8,128)(2,1)S(1)} %slice.4), channel_id=1, source_target_pairs={{0,16},{4,20},{8,24},{12,28},{16,0},{20,4},{24,8},{28,12},{1,17},{... | collective-permute-start | bytes 1843208 | tf_op jit(solution)/shard_map/ppermute | solution.py:26
  8.7 13.7 %collective-permute-start = (bf16[160,512]{1,0:T(8,128)(2,1)}, bf16[160,512]{1,0:T(8,128)(2,1)S(1)}, u32[]{:S(2)}, u32[]{:S(2)}) collective-permute-start(bf16[160,512]{1,0:T(8,128)(2,1)} %get-tuple-element.42), channel_id=1, source_target_pairs={{0,1},{1,2},{2,3},{3,0},{4,5},{5,6},{6,7},{7,4},{8,9},{9,10},{10,1... | collective-permute-start | bytes 491528 | tf_op jit(solution)/shard_map/ppermute | solution.py:26
  10.3 14.0 %collective-permute-start.1 = (bf16[160,512]{1,0:T(8,128)(2,1)}, bf16[160,512]{1,0:T(8,128)(2,1)S(1)}, u32[]{:S(2)}, u32[]{:S(2)}) collective-permute-start(bf16[160,512]{1,0:T(8,128)(2,1)} %get-tuple-element.43), channel_id=1, source_target_pairs={{0,2},{1,3},{2,0},{3,1},{4,6},{5,7},{6,4},{7,5},{8,10},{9,11},{10,... | collective-permute-start | bytes 491528 | tf_op jit(solution)/shard_map/ppermute | solution.py:26
  12.9 27.4 %copy-start.4 = (bf16[160,512]{1,0:T(8,128)(2,1)S(1)}, bf16[160,512]{1,0:T(8,128)(2,1)}, u32[]{:S(2)}) copy-start(bf16[160,512]{1,0:T(8,128)(2,1)} %get-tuple-element.41.refs_0_) | copy-start | bytes 491524
  12.9 14.0 %collective-permute-start.2 = (bf16[160,512]{1,0:T(8,128)(2,1)}, bf16[160,512]{1,0:T(8,128)(2,1)S(1)}, u32[]{:S(2)}, u32[]{:S(2)}) collective-permute-start(bf16[160,512]{1,0:T(8,128)(2,1)} %get-tuple-element.44), channel_id=1, source_target_pairs={{0,3},{1,0},{2,1},{3,2},{4,7},{5,4},{6,5},{7,6},{8,11},{9,8},{10,9... | collective-permute-start | bytes 491528 | tf_op jit(solution)/shard_map/ppermute | solution.py:26
  22.4 7.8 %collective-permute-start.4 = (bf16[240,256]{1,0:T(8,128)(2,1)S(1)}, bf16[240,256]{1,0:T(8,128)(2,1)S(1)}, u32[]{:S(2)}, u32[]{:S(2)}) collective-permute-start(bf16[240,256]{1,0:T(8,128)(2,1)S(1)} %get-tuple-element.47), channel_id=1, source_target_pairs={{0,1},{1,2},{2,3},{3,0},{4,5},{5,6},{6,7},{7,4},{8,9},{9,10},{10,1... | collective-permute-start | bytes 368648 | tf_op jit(solution)/shard_map/ppermute | solution.py:26
  24.2 13.4 %collective-permute-start.5 = (bf16[240,256]{1,0:T(8,128)(2,1)S(1)}, bf16[240,256]{1,0:T(8,128)(2,1)S(1)}, u32[]{:S(2)}, u32[]{:S(2)}) collective-permute-start(bf16[240,256]{1,0:T(8,128)(2,1)S(1)} %get-tuple-element.49), channel_id=1, source_target_pairs={{0,2},{1,3},{2,0},{3,1},{4,6},{5,7},{6,4},{7,5},{8,10},{9,11},{10,... | collective-permute-start | bytes 368648 | tf_op jit(solution)/shard_map/ppermute | solution.py:26
  26.8 12.6 %collective-permute-start.6 = (bf16[240,256]{1,0:T(8,128)(2,1)S(1)}, bf16[240,256]{1,0:T(8,128)(2,1)S(1)}, u32[]{:S(2)}, u32[]{:S(2)}) collective-permute-start(bf16[240,256]{1,0:T(8,128)(2,1)S(1)} %get-tuple-element.51), channel_id=1, source_target_pairs={{0,3},{1,0},{2,1},{3,2},{4,7},{5,4},{6,5},{7,6},{8,11},{9,8},{10,9... | collective-permute-start | bytes 368648 | tf_op jit(solution)/shard_map/ppermute | solution.py:26
  30.2 15.9 %collective-permute-start.8 = (bf16[240,256]{1,0:T(8,128)(2,1)S(1)}, bf16[240,256]{1,0:T(8,128)(2,1)S(1)}, u32[]{:S(2)}, u32[]{:S(2)}) collective-permute-start(bf16[240,256]{1,0:T(8,128)(2,1)S(1)} %get-tuple-element.56), channel_id=1, source_target_pairs={{0,1},{1,2},{2,3},{3,0},{4,5},{5,6},{6,7},{7,4},{8,9},{9,10},{10,1... | collective-permute-start | bytes 368648 | tf_op jit(solution)/shard_map/ppermute | solution.py:26
  37.6 10.7 %collective-permute-start.9 = (bf16[240,256]{1,0:T(8,128)(2,1)S(1)}, bf16[240,256]{1,0:T(8,128)(2,1)S(1)}, u32[]{:S(2)}, u32[]{:S(2)}) collective-permute-start(bf16[240,256]{1,0:T(8,128)(2,1)S(1)} %get-tuple-element.62), channel_id=1, source_target_pairs={{0,2},{1,3},{2,0},{3,1},{4,6},{5,7},{6,4},{7,5},{8,10},{9,11},{10,... | collective-permute-start | bytes 368648 | tf_op jit(solution)/shard_map/ppermute | solution.py:26
  39.5 8.9 %collective-permute-start.10 = (bf16[240,256]{1,0:T(8,128)(2,1)S(1)}, bf16[240,256]{1,0:T(8,128)(2,1)S(1)}, u32[]{:S(2)}, u32[]{:S(2)}) collective-permute-start(bf16[240,256]{1,0:T(8,128)(2,1)S(1)} %get-tuple-element.64), channel_id=1, source_target_pairs={{0,3},{1,0},{2,1},{3,2},{4,7},{5,4},{6,5},{7,6},{8,11},{9,8},{10,9... | collective-permute-start | bytes 368648 | tf_op jit(solution)/shard_map/ppermute | solution.py:26
  44.3 8.7 %collective-permute-start.7 = (bf16[608,128]{1,0:T(8,128)(2,1)S(1)}, bf16[608,128]{1,0:T(8,128)(2,1)S(1)}, u32[]{:S(2)}, u32[]{:S(2)}) collective-permute-start(bf16[608,128]{1,0:T(8,128)(2,1)S(1)} %get-tuple-element.52.mixed), channel_id=1, source_target_pairs={{0,16},{4,20},{8,24},{12,28},{16,0},{20,4},{24,8},{28,12},{1,17},{... | collective-permute-start | bytes 466952 | tf_op jit(solution)/shard_map/ppermute | solution.py:26
  48.4 18.7 %copy-start.1 = (bf16[640,1280]{1,0:T(8,128)(2,1)S(1)}, bf16[640,1280]{1,0:T(8,128)(2,1)}, u32[]{:S(2)}) copy-start(bf16[640,1280]{1,0:T(8,128)(2,1)} %weight.5) | copy-start | bytes 4915204
  52.6 6.4 %collective-permute-start.14 = (bf16[608,128]{1,0:T(8,128)(2,1)S(1)}, bf16[608,128]{1,0:T(8,128)(2,1)S(1)}, u32[]{:S(2)}, u32[]{:S(2)}) collective-permute-start(bf16[608,128]{1,0:T(8,128)(2,1)S(1)} %get-tuple-element.72.mixed), channel_id=1, source_target_pairs={{0,16},{4,20},{8,24},{12,28},{16,0},{20,4},{24,8},{28,12},{1,17},{... | collective-permute-start | bytes 466952 | tf_op jit(solution)/shard_map/ppermute | solution.py:26
  53.6 8.3 %collective-permute-start.11 = (bf16[360,128]{1,0:T(8,128)(2,1)S(1)}, bf16[360,128]{1,0:T(8,128)(2,1)S(1)}, u32[]{:S(2)}, u32[]{:S(2)}) collective-permute-start(bf16[360,128]{1,0:T(8,128)(2,1)S(1)} %get-tuple-element.67), channel_id=1, source_target_pairs={{0,3},{1,0},{2,1},{3,2},{4,7},{5,4},{6,5},{7,6},{8,11},{9,8},{10,9... | collective-permute-start | bytes 276488 | tf_op jit(solution)/shard_map/ppermute | solution.py:26
  56.3 10.8 %collective-permute-start.12 = (bf16[360,128]{1,0:T(8,128)(2,1)S(1)}, bf16[360,128]{1,0:T(8,128)(2,1)S(1)}, u32[]{:S(2)}, u32[]{:S(2)}) collective-permute-start(bf16[360,128]{1,0:T(8,128)(2,1)S(1)} %get-tuple-element.68), channel_id=1, source_target_pairs={{0,2},{1,3},{2,0},{3,1},{4,6},{5,7},{6,4},{7,5},{8,10},{9,11},{10,... | collective-permute-start | bytes 276488 | tf_op jit(solution)/shard_map/ppermute | solution.py:26
  57.0 10.1 %collective-permute-start.13 = (bf16[360,128]{1,0:T(8,128)(2,1)S(1)}, bf16[360,128]{1,0:T(8,128)(2,1)S(1)}, u32[]{:S(2)}, u32[]{:S(2)}) collective-permute-start(bf16[360,128]{1,0:T(8,128)(2,1)S(1)} %get-tuple-element.69), channel_id=1, source_target_pairs={{0,1},{1,2},{2,3},{3,0},{4,5},{5,6},{6,7},{7,4},{8,9},{9,10},{10,1... | collective-permute-start | bytes 276488 | tf_op jit(solution)/shard_map/ppermute | solution.py:26
  59.6 8.5 %collective-permute-start.15 = (bf16[152,128]{1,0:T(8,128)(2,1)S(1)}, bf16[152,128]{1,0:T(8,128)(2,1)S(1)}, u32[]{:S(2)}, u32[]{:S(2)}) collective-permute-start(bf16[152,128]{1,0:T(8,128)(2,1)S(1)} %get-tuple-element.74), channel_id=1, source_target_pairs={{0,3},{1,0},{2,1},{3,2},{4,7},{5,4},{6,5},{7,6},{8,11},{9,8},{10,9... | collective-permute-start | bytes 116744 | tf_op jit(solution)/shard_map/ppermute | solution.py:26
  61.5 6.8 %collective-permute-start.16 = (bf16[152,128]{1,0:T(8,128)(2,1)S(1)}, bf16[152,128]{1,0:T(8,128)(2,1)S(1)}, u32[]{:S(2)}, u32[]{:S(2)}) collective-permute-start(bf16[152,128]{1,0:T(8,128)(2,1)S(1)} %get-tuple-element.75), channel_id=1, source_target_pairs={{0,2},{1,3},{2,0},{3,1},{4,6},{5,7},{6,4},{7,5},{8,10},{9,11},{10,... | collective-permute-start | bytes 116744 | tf_op jit(solution)/shard_map/ppermute | solution.py:26
  61.9 6.5 %collective-permute-start.17 = (bf16[152,128]{1,0:T(8,128)(2,1)S(1)}, bf16[152,128]{1,0:T(8,128)(2,1)S(1)}, u32[]{:S(2)}, u32[]{:S(2)}) collective-permute-start(bf16[152,128]{1,0:T(8,128)(2,1)S(1)} %get-tuple-element.76), channel_id=1, source_target_pairs={{0,1},{1,2},{2,3},{3,0},{4,5},{5,6},{6,7},{7,4},{8,9},{9,10},{10,1... | collective-permute-start | bytes 116744 | tf_op jit(solution)/shard_map/ppermute | solution.py:26

commit v13 on v11

--- a/solution.py
+++ b/solution.py
@@ -14,6 +14,7 @@
 SUBLANES = 8
 MIB = 1024 * 1024
 CHUNKS = 5
+COPIES = 4
 
 
 def round_up(value, unit):
@@ -46,8 +47,8 @@
     chunk = features // len(copies)
     qkv = None
     for index, copy in enumerate(copies):
-        if copy is not None:
-            copy.wait()
+        for piece in copy:
+            piece.wait()
         inner = slice(index * chunk, (index + 1) * chunk)
         share = jnp.dot(normed[:, inner], weight[inner], preferred_element_type=jnp.float32)
         qkv = share if qkv is None else qkv + share
@@ -67,17 +68,19 @@
 
 def kept_kernel(split, field, gain, weight, *refs):
     *outs, slots, held_weight, sems, held_field, held_gain = refs
-    first = pltpu.make_async_copy(field, held_field, sems.at[CHUNKS])
-    second = pltpu.make_async_copy(gain, held_gain, sems.at[CHUNKS + 1])
-    chunk = weight.shape[0] // CHUNKS
-    copies = []
-    for index in range(CHUNKS):
+    total = CHUNKS * COPIES
+    first = pltpu.make_async_copy(field, held_field, sems.at[total])
+    second = pltpu.make_async_copy(gain, held_gain, sems.at[total + 1])
+    chunk = weight.shape[0] // total
+    pieces = []
+    for index in range(total):
         inner = pl.ds(index * chunk, chunk)
-        copies.append(
+        pieces.append(
             pltpu.make_async_copy(weight.at[inner], held_weight.at[inner], sems.at[index])
         )
-    for copy in (first, second, *copies):
+    for copy in (first, second, *pieces):
         copy.start()
+    copies = [pieces[index : index + COPIES] for index in range(0, total, COPIES)]
     first.wait()
     second.wait()
     rows, columns, features = field.shape
@@ -100,7 +103,7 @@
     own = field[...].astype(jnp.float32)[:, :split]
     column = lax.broadcasted_iota(jnp.int32, own.shape, 1)
     tokens = jnp.where(column < column_offset(lon_shift), eastern[...].astype(jnp.float32), own)
-    project(tokens.reshape(rows * split, features), gain, weight, [None], slots)
+    project(tokens.reshape(rows * split, features), gain, weight, [[]], slots)
     groups = slots.shape[0]
     for index, out in enumerate(outs):
         first = index // groups * out.shape[1]
@@ -131,7 +134,7 @@
         queries = pltpu.roll(held[first : first + step].astype(jnp.float32), span - HD, axis=1)
         queries = queries[:, :LANES]
         lane = lax.broadcasted_iota(jnp.int32, queries.shape, 1)
-        queries = jnp.where(lane < HD, queries * factor, 0.0).astype(jnp.bfloat16)
+        queries = jnp.where(lane < HD, queries, 0.0).astype(jnp.bfloat16)
         out[...] = jnp.dot(queries, keys[...], preferred_element_type=jnp.float32)
 
     score(0, scores[0])
@@ -142,7 +145,7 @@
         for first in range(0, step, chunk):
             part = now[first : first + chunk]
             top = jnp.max(part, axis=-1, keepdims=True)
-            out[first : first + chunk] = jnp.exp2(part - top).astype(jnp.bfloat16)
+            out[first : first + chunk] = jnp.exp2((part - top) * factor).astype(jnp.bfloat16)
         values = jnp.dot(out[...], held[:, span - LANES :], preferred_element_type=jnp.float32)
         first = 2 * HD - (span - LANES)
         values = values / values[:, first + HD : first + HD + 1]
@@ -319,7 +322,7 @@
     operands = (field, norm_gain, qkv_weight)
     held = [
         pltpu.VMEM(qkv_weight.shape, qkv_weight.dtype),
-        pltpu.SemaphoreType.DMA((CHUNKS + 2,)),
+        pltpu.SemaphoreType.DMA((CHUNKS * COPIES + 2,)),
         pltpu.VMEM(field.shape, field.dtype),
         pltpu.VMEM(norm_gain.shape, norm_gain.dtype),
     ]
@@ -336,13 +339,12 @@
     second_mixed = spread(after(mixed[groups:], [None, *first_mixed[1:]]), 1)
 
     total = groups * rows * columns
-    step = total // 5
     mixed_packed, kept_packed = packed_rows(mixed_count)[0], packed_rows(kept_count)[0]
 
     def block(count):
         return jax.ShapeDtypeStruct((count, LANES), jnp.bfloat16)
 
-    def attention(head, *blocks):
+    def attention(head, step, *blocks):
         return pl.pallas_call(
             functools.partial(attention_kernel, head, groups),
             out_shape=[block(groups * kept_packed), block(groups * mixed_packed)],
@@ -379,8 +381,8 @@
         )(lon_shift, mixed_values, western, *kept_values)
         return spread(selected, -1)
 
-    first_kept_values, first_mixed_values = attention(0, *kept, *first_mixed)
-    second_kept_values, second_mixed_values = attention(1, *kept, *second_mixed)
+    first_kept_values, first_mixed_values = attention(0, total // 10, *kept, *first_mixed)
+    second_kept_values, second_mixed_values = attention(1, total // 4, *kept, *second_mixed)
     first = back(first_mixed_values, first_kept_values, second_kept_values)
     second = back(second_mixed_values)
 

time: 69.1 us -> 69.1 us (level)
  no operation moved by 1% of the time
where the time goes in v13:
time: 69.1 us; the launch traced here: 68.9 us
  starting transfers between devices  32.1 us (46%)
  Pallas kernels  20.9 us (30%)
  waiting for transfers between devices  14.6 us (21%)
  local copies, waits for them, and re-layouts  1.14 us (2%)
    ppermute x18, starting transfers between devices, shifted(): lax.ppermute(block, axis, [(i, (i + distance) % count) for i in range(cou...  32.1 us
    ppermute x18, waiting for transfers between devices, shifted(): lax.ppermute(block, axis, [(i, (i + distance) % count) for i in range(cou...  14.6 us
    pallas_call x2, Pallas kernels, projection(): pl.pallas_call(functools.partial(kernel, split), out_shape=[block] * (par...  8.88 us
    pallas_call x2, Pallas kernels, attention(): pl.pallas_call(functools.partial(attention_kernel, head, groups), out_sha...  8.25 us
    pallas_call x1, Pallas kernels, shards(): pl.pallas_call(functools.partial(second_output_kernel, split), out_shape=...  1.52 us
  transfers between devices with their start and end apart: 18, of which 8 were waited for; matrix products, arithmetic and copies ran while one was open for 0% of the time, Pallas kernels for 28%

profile of v13, /device:TPU:0, one launch (start us, length us, event | category | flops | bytes accessed | tf_op | source)
XLA Modules:
  0.0 68.9 jit_solution(17821449451767355043)
XLA Ops:
  0.0 1.1 %slice.4 = bf16[10,24,1280]{2,1,0:T(8,128)(2,1)S(1)} slice(bf16[10,40,1280]{2,1,0:T(8,128)(2,1)} %bitcast.2), slice={[0:10], [0:24], [0:1280]} | slice | bytes 1228800 | tf_op jit(solution)/shard_map/slice | solution.py:320
  1.1 0.0 copy-start
  1.1 0.0 copy-start.2
  1.1 0.0 copy-start.3
  1.2 3.0 %collective-permute-start.3 = (bf16[10,24,1280]{2,1,0:T(8,128)(2,1)S(1)}, bf16[10,24,1280]{2,1,0:T(8,128)(2,1)S(1)}, u32[]{:S(2)}, u32[]{:S(2)}) collective-permute-start(bf16[10,24,1280]{2,1,0:T(8,128)(2,1)S(1)} %slice.4), channel_id=1, source_target_pairs={{0,16},{4,20},{8,24},{12,28},{16,0},{20,4},{24,8},{28,12},{1,17},{... | collective-permute-start | bytes 1843208 | tf_op jit(solution)/shard_map/ppermute | solution.py:26
  4.2 4.6 %shard_map.55 = (bf16[160,512]{1,0:T(8,128)(2,1)}, bf16[160,512]{1,0:T(8,128)(2,1)}, bf16[160,512]{1,0:T(8,128)(2,1)}, bf16[160,512]{1,0:T(8,128)(2,1)}) custom-call(bf16[10,40,1280]{2,1,0:T(8,128)(2,1)} %bitcast.3, f32[1280]{0:T(1024)} %gain.3, bf16[1280,1920]{1,0:T(8,128)(2,1)} %weight.4), custom_call_target="tpu_custom_call" | custom-call | flops 786432000 | bytes 5734400 | tf_op jit(solution)/shard_map/pallas_call | solution.py:297
  8.8 1.6 %collective-permute-start = (bf16[160,512]{1,0:T(8,128)(2,1)}, bf16[160,512]{1,0:T(8,128)(2,1)S(1)}, u32[]{:S(2)}, u32[]{:S(2)}) collective-permute-start(bf16[160,512]{1,0:T(8,128)(2,1)} %get-tuple-element.38), channel_id=1, source_target_pairs={{0,1},{1,2},{2,3},{3,0},{4,5},{5,6},{6,7},{7,4},{8,9},{9,10},{10,1... | collective-permute-start | bytes 491528 | tf_op jit(solution)/shard_map/ppermute | solution.py:26
  10.4 2.6 %collective-permute-start.1 = (bf16[160,512]{1,0:T(8,128)(2,1)}, bf16[160,512]{1,0:T(8,128)(2,1)S(1)}, u32[]{:S(2)}, u32[]{:S(2)}) collective-permute-start(bf16[160,512]{1,0:T(8,128)(2,1)} %get-tuple-element.39), channel_id=1, source_target_pairs={{0,2},{1,3},{2,0},{3,1},{4,6},{5,7},{6,4},{7,5},{8,10},{9,11},{10,... | collective-permute-start | bytes 491528 | tf_op jit(solution)/shard_map/ppermute | solution.py:26
  13.0 0.0 copy-start.4
  13.0 1.3 %collective-permute-start.2 = (bf16[160,512]{1,0:T(8,128)(2,1)}, bf16[160,512]{1,0:T(8,128)(2,1)S(1)}, u32[]{:S(2)}, u32[]{:S(2)}) collective-permute-start(bf16[160,512]{1,0:T(8,128)(2,1)} %get-tuple-element.40), channel_id=1, source_target_pairs={{0,3},{1,0},{2,1},{3,2},{4,7},{5,4},{6,5},{7,6},{8,11},{9,8},{10,9... | collective-permute-start | bytes 491528 | tf_op jit(solution)/shard_map/ppermute | solution.py:26
  14.3 3.7 %collective-permute-done.3.eastern = bf16[10,24,1280]{2,1,0:T(8,128)(2,1)S(1)} collective-permute-done((bf16[10,24,1280]{2,1,0:T(8,128)(2,1)S(1)}, bf16[10,24,1280]{2,1,0:T(8,128)(2,1)S(1)}, u32[]{:S(2)}, u32[]{:S(2)}) %collective-permute-start.3) | collective-permute-done | bytes 614432 | tf_op jit(solution)/shard_map/ppermute | solution.py:26
  18.0 0.0 copy-done
  18.0 0.0 copy-done.2
  18.0 0.0 copy-done.3
  18.1 4.3 %shard_map.56 = (bf16[240,256]{1,0:T(8,128)(2,1)S(1)}, bf16[240,256]{1,0:T(8,128)(2,1)S(1)}, bf16[240,256]{1,0:T(8,128)(2,1)S(1)}, bf16[240,256]{1,0:T(8,128)(2,...) custom-call(bf16[10,40,1280]{2,1,0:T(8,128)(2,1)S(1)} %bitcast.4, ...), custom_call_target="tpu_custom_call" | custom-call | flops 1179648000 | bytes 6144000 | tf_op jit(solution)/shard_map/pallas_call | solution.py:297
  22.4 0.0 collective-permute-done.refs_1_
  22.4 1.9 %collective-permute-start.4 = (bf16[240,256]{1,0:T(8,128)(2,1)S(1)}, bf16[240,256]{1,0:T(8,128)(2,1)S(1)}, u32[]{:S(2)}, u32[]{:S(2)}) collective-permute-start(bf16[240,256]{1,0:T(8,128)(2,1)S(1)} %get-tuple-element.43), channel_id=1, source_target_pairs={{0,1},{1,2},{2,3},{3,0},{4,5},{5,6},{6,7},{7,4},{8,9},{9,10},{10,1... | collective-permute-start | bytes 368648 | tf_op jit(solution)/shard_map/ppermute | solution.py:26
  24.2 0.0 collective-permute-done.1.refs_2_
  24.2 2.6 %collective-permute-start.5 = (bf16[240,256]{1,0:T(8,128)(2,1)S(1)}, bf16[240,256]{1,0:T(8,128)(2,1)S(1)}, u32[]{:S(2)}, u32[]{:S(2)}) collective-permute-start(bf16[240,256]{1,0:T(8,128)(2,1)S(1)} %get-tuple-element.45), channel_id=1, source_target_pairs={{0,2},{1,3},{2,0},{3,1},{4,6},{5,7},{6,4},{7,5},{8,10},{9,11},{10,... | collective-permute-start | bytes 368648 | tf_op jit(solution)/shard_map/ppermute | solution.py:26
  26.8 0.0 collective-permute-done.2.refs_3_
  26.8 2.8 %collective-permute-start.6 = (bf16[240,256]{1,0:T(8,128)(2,1)S(1)}, bf16[240,256]{1,0:T(8,128)(2,1)S(1)}, u32[]{:S(2)}, u32[]{:S(2)}) collective-permute-start(bf16[240,256]{1,0:T(8,128)(2,1)S(1)} %get-tuple-element.47), channel_id=1, source_target_pairs={{0,3},{1,0},{2,1},{3,2},{4,7},{5,4},{6,5},{7,6},{8,11},{9,8},{10,9... | collective-permute-start | bytes 368648 | tf_op jit(solution)/shard_map/ppermute | solution.py:26
  29.6 0.6 collective-permute-done.4.refs_5_
  30.2 4.6 %collective-permute-start.8 = (bf16[240,256]{1,0:T(8,128)(2,1)S(1)}, bf16[240,256]{1,0:T(8,128)(2,1)S(1)}, u32[]{:S(2)}, u32[]{:S(2)}) collective-permute-start(bf16[240,256]{1,0:T(8,128)(2,1)S(1)} %get-tuple-element.52), channel_id=1, source_target_pairs={{0,1},{1,2},{2,3},{3,0},{4,5},{5,6},{6,7},{7,4},{8,9},{9,10},{10,1... | collective-permute-start | bytes 368648 | tf_op jit(solution)/shard_map/ppermute | solution.py:26
  34.8 1.3 %collective-permute-done.5.refs_6_ = bf16[240,256]{1,0:T(8,128)(2,1)S(1)} collective-permute-done((bf16[240,256]{1,0:T(8,128)(2,1)S(1)}, bf16[240,256]{1,0:T(8,128)(2,1)S(1)}, u32[]{:S(2)}, u32[]{:S(2)}) %collective-permute-start.5) | collective-permute-done | bytes 122912 | tf_op jit(solution)/shard_map/ppermute | solution.py:26
  36.2 0.6 collective-permute-start.9
  36.8 3.3 %collective-permute-done.6.refs_7_ = bf16[240,256]{1,0:T(8,128)(2,1)S(1)} collective-permute-done((bf16[240,256]{1,0:T(8,128)(2,1)S(1)}, bf16[240,256]{1,0:T(8,128)(2,1)S(1)}, u32[]{:S(2)}, u32[]{:S(2)}) %collective-permute-start.6) | collective-permute-done | bytes 122912 | tf_op jit(solution)/shard_map/ppermute | solution.py:26
  40.1 0.2 collective-permute-start.10
  40.3 0.0 copy-done.4
  40.3 4.2 %shard_map.57 = (bf16[416,128]{1,0:T(8,128)(2,1)S(1)}, bf16[608,128]{1,0:T(8,128)(2,1)S(1)}) custom-call(bf16[160,512]{1,0:T(8,128)(2,1)S(1)} %copy-done.4, bf16[160,512]{1,0:T(8,128)(2,1)S(1)} %collective-permute-done.refs_1_, bf16[160,512]{1,0:T(8,128)(2,1)S(1)} %collective-permute-done.1.refs_2_, bf16[160,512]{1,0:T(8,128)(2,1)S(1)} %collective-permute-done.2.refs_3_, ...), custom_call_target="tpu_custom_call" | custom-call | flops 2621440000 | bytes 1228800 | tf_op jit(solution)/shard_map/pallas_call | solution.py:348
  44.5 1.4 %collective-permute-start.7 = (bf16[608,128]{1,0:T(8,128)(2,1)S(1)}, bf16[608,128]{1,0:T(8,128)(2,1)S(1)}, u32[]{:S(2)}, u32[]{:S(2)}) collective-permute-start(bf16[608,128]{1,0:T(8,128)(2,1)S(1)} %get-tuple-element.48.mixed), channel_id=1, source_target_pairs={{0,16},{4,20},{8,24},{12,28},{16,0},{20,4},{24,8},{28,12},{1,17},{... | collective-permute-start | bytes 466952 | tf_op jit(solution)/shard_map/ppermute | solution.py:26
  45.9 0.0 collective-permute-done.8.refs_5_
  45.9 0.0 collective-permute-done.9.refs_6_
  45.9 2.1 %collective-permute-done.10.refs_7_ = bf16[240,256]{1,0:T(8,128)(2,1)S(1)} collective-permute-done((bf16[240,256]{1,0:T(8,128)(2,1)S(1)}, bf16[240,256]{1,0:T(8,128)(2,1)S(1)}, u32[]{:S(2)}, u32[]{:S(2)}) %collective-permute-start.10) | collective-permute-done | bytes 122912 | tf_op jit(solution)/shard_map/ppermute | solution.py:26
  48.0 0.0 copy-start.1
  48.0 4.1 %shard_map.58 = (bf16[416,128]{1,0:T(8,128)(2,1)S(1)}, bf16[608,128]{1,0:T(8,128)(2,1)S(1)}) custom-call(bf16[160,512]{1,0:T(8,128)(2,1)S(1)} %copy-done.4, bf16[160,512]{1,0:T(8,128)(2,1)S(1)} %collective-permute-done.refs_1_, bf16[160,512]{1,0:T(8,128)(2,1)S(1)} %collective-permute-done.1.refs_2_, bf16[160,512]{1,0:T(8,128)(2,1)S(1)} %collective-permute-done.2.refs_3_, ...), custom_call_target="tpu_custom_call" | custom-call | flops 2621440000 | bytes 1228800 | tf_op jit(solution)/shard_map/pallas_call | solution.py:348
  52.1 0.1 collective-permute-start.14
  52.1 0.0 collective-permute-done.7.western
  52.2 0.6 shard_map.59
  52.8 3.2 %collective-permute-start.11 = (bf16[360,128]{1,0:T(8,128)(2,1)S(1)}, bf16[360,128]{1,0:T(8,128)(2,1)S(1)}, u32[]{:S(2)}, u32[]{:S(2)}) collective-permute-start(bf16[360,128]{1,0:T(8,128)(2,1)S(1)} %get-tuple-element.59), channel_id=1, source_target_pairs={{0,3},{1,0},{2,1},{3,2},{4,7},{5,4},{6,5},{7,6},{8,11},{9,8},{10,9... | collective-permute-start | bytes 276488 | tf_op jit(solution)/shard_map/ppermute | solution.py:26
  56.0 0.0 collective-permute-start.12
  56.0 0.9 %collective-permute-start.13 = (bf16[360,128]{1,0:T(8,128)(2,1)S(1)}, bf16[360,128]{1,0:T(8,128)(2,1)S(1)}, u32[]{:S(2)}, u32[]{:S(2)}) collective-permute-start(bf16[360,128]{1,0:T(8,128)(2,1)S(1)} %get-tuple-element.61), channel_id=1, source_target_pairs={{0,1},{1,2},{2,3},{3,0},{4,5},{5,6},{6,7},{7,4},{8,9},{9,10},{10,1... | collective-permute-start | bytes 276488 | tf_op jit(solution)/shard_map/ppermute | solution.py:26
  56.9 1.0 %collective-permute-done.14.western = bf16[608,128]{1,0:T(8,128)(2,1)S(1)} collective-permute-done((bf16[608,128]{1,0:T(8,128)(2,1)S(1)}, bf16[608,128]{1,0:T(8,128)(2,1)S(1)}, u32[]{:S(2)}, u32[]{:S(2)}) %collective-permute-start.14) | collective-permute-done | bytes 155680 | tf_op jit(solution)/shard_map/ppermute | solution.py:26
  57.9 0.6 shard_map.61
  58.5 2.0 %collective-permute-start.15 = (bf16[152,128]{1,0:T(8,128)(2,1)S(1)}, bf16[152,128]{1,0:T(8,128)(2,1)S(1)}, u32[]{:S(2)}, u32[]{:S(2)}) collective-permute-start(bf16[152,128]{1,0:T(8,128)(2,1)S(1)} %get-tuple-element.66), channel_id=1, source_target_pairs={{0,3},{1,0},{2,1},{3,2},{4,7},{5,4},{6,5},{7,6},{8,11},{9,8},{10,9... | collective-permute-start | bytes 116744 | tf_op jit(solution)/shard_map/ppermute | solution.py:26
  60.5 1.1 %collective-permute-start.16 = (bf16[152,128]{1,0:T(8,128)(2,1)S(1)}, bf16[152,128]{1,0:T(8,128)(2,1)S(1)}, u32[]{:S(2)}, u32[]{:S(2)}) collective-permute-start(bf16[152,128]{1,0:T(8,128)(2,1)S(1)} %get-tuple-element.67), channel_id=1, source_target_pairs={{0,2},{1,3},{2,0},{3,1},{4,6},{5,7},{6,4},{7,5},{8,10},{9,11},{10,... | collective-permute-start | bytes 116744 | tf_op jit(solution)/shard_map/ppermute | solution.py:26
  61.6 0.0 collective-permute-done.11.refs_1_
  61.6 2.1 %collective-permute-start.17 = (bf16[152,128]{1,0:T(8,128)(2,1)S(1)}, bf16[152,128]{1,0:T(8,128)(2,1)S(1)}, u32[]{:S(2)}, u32[]{:S(2)}) collective-permute-start(bf16[152,128]{1,0:T(8,128)(2,1)S(1)} %get-tuple-element.68), channel_id=1, source_target_pairs={{0,1},{1,2},{2,3},{3,0},{4,5},{5,6},{6,7},{7,4},{8,9},{9,10},{10,1... | collective-permute-start | bytes 116744 | tf_op jit(solution)/shard_map/ppermute | solution.py:26
  63.7 2.2 %collective-permute-done.12.refs_2_ = bf16[360,128]{1,0:T(8,128)(2,1)S(1)} collective-permute-done((bf16[360,128]{1,0:T(8,128)(2,1)S(1)}, bf16[360,128]{1,0:T(8,128)(2,1)S(1)}, u32[]{:S(2)}, u32[]{:S(2)}) %collective-permute-start.12) | collective-permute-done | bytes 92192 | tf_op jit(solution)/shard_map/ppermute | solution.py:26
  66.0 0.0 collective-permute-done.13.refs_3_
  66.0 0.0 copy-done.1
  66.0 1.0 %shard_map.60 = (f32[10,40,1280]{2,1,0:T(8,128)S(1)}, bf16[512,1280]{1,0:T(8,128)(2,1)S(1)}) custom-call(bf16[10,40,1280]{2,1,0:T(8,128)(2,1)S(1)} %bitcast.5, bf16[640,1280]{1,0:T(8,128)(2,1)S(1)} %copy-done.1, bf16[360,128]{1,0:T(8,128)(2,1)S(1)} %get-tuple-element.58.refs_0_, bf16[360,128]{1,0:T(8,128)(2,1)S(1)} %collective-permute-done.11.refs_1_, ...), custom_call_target="tpu_custom_call" | custom-call | flops 524288000 | bytes 3891200 | tf_op jit(solution)/shard_map/pallas_call | solution.py:395
  67.0 0.0 collective-permute-done.15.refs_1_
  67.0 0.0 collective-permute-done.16.refs_2_
  67.0 0.3 collective-permute-done.17.refs_3_
  67.4 1.5 %shard_map.62 = bf16[10,40,1280]{2,1,0:T(8,128)(2,1)} custom-call(f32[10,40,1280]{2,1,0:T(8,128)S(1)} %get-tuple-element.62.partial, bf16[512,1280]{1,0:T(8,128)(2,1)S(1)} %get-tuple-element.63.weight, bf16[152,128]{1,0:T(8,128)(2,1)S(1)} %get-tuple-element.65.refs_0_, bf16[152,128]{1,0:T(8,128)(2,1)S(1)} %collective-permute-done.15.refs_1_, ...), custom_call_target="tpu_custom_call" | custom-call | flops 524288000 | bytes 3891200 | tf_op jit(solution)/shard_map/pallas_call | solution.py:407
Async XLA Ops:
  1.1 16.9 %copy-start = (bf16[1,10,40,1280]{3,2,1,0:T(8,128)(2,1)S(1)}, bf16[1,10,40,1280]{3,2,1,0:T(8,128)(2,1)}, u32[]{:S(2)}) copy-start(bf16[1,10,40,1280]{3,2,1,0:T(8,128)(2,1)} %param.5) | copy-start | bytes 3072004
  1.1 16.9 %copy-start.2 = (f32[1280]{0:T(1024)S(1)}, f32[1280]{0:T(1024)}, u32[]{:S(2)}) copy-start(f32[1280]{0:T(1024)} %gain.3) | copy-start | bytes 15364
  1.1 16.9 %copy-start.3 = (s32[4]{0:T(128)S(1)}, s32[4]{0:T(128)}, u32[]{:S(2)}) copy-start(s32[4]{0:T(128)} %lon_shift.5) | copy-start | bytes 52
  1.2 16.9 %collective-permute-start.3 = (bf16[10,24,1280]{2,1,0:T(8,128)(2,1)S(1)}, bf16[10,24,1280]{2,1,0:T(8,128)(2,1)S(1)}, u32[]{:S(2)}, u32[]{:S(2)}) collective-permute-start(bf16[10,24,1280]{2,1,0:T(8,128)(2,1)S(1)} %slice.4), channel_id=1, source_target_pairs={{0,16},{4,20},{8,24},{12,28},{16,0},{20,4},{24,8},{28,12},{1,17},{... | collective-permute-start | bytes 1843208 | tf_op jit(solution)/shard_map/ppermute | solution.py:26
  8.8 13.6 %collective-permute-start = (bf16[160,512]{1,0:T(8,128)(2,1)}, bf16[160,512]{1,0:T(8,128)(2,1)S(1)}, u32[]{:S(2)}, u32[]{:S(2)}) collective-permute-start(bf16[160,512]{1,0:T(8,128)(2,1)} %get-tuple-element.38), channel_id=1, source_target_pairs={{0,1},{1,2},{2,3},{3,0},{4,5},{5,6},{6,7},{7,4},{8,9},{9,10},{10,1... | collective-permute-start | bytes 491528 | tf_op jit(solution)/shard_map/ppermute | solution.py:26
  10.4 13.8 %collective-permute-start.1 = (bf16[160,512]{1,0:T(8,128)(2,1)}, bf16[160,512]{1,0:T(8,128)(2,1)S(1)}, u32[]{:S(2)}, u32[]{:S(2)}) collective-permute-start(bf16[160,512]{1,0:T(8,128)(2,1)} %get-tuple-element.39), channel_id=1, source_target_pairs={{0,2},{1,3},{2,0},{3,1},{4,6},{5,7},{6,4},{7,5},{8,10},{9,11},{10,... | collective-permute-start | bytes 491528 | tf_op jit(solution)/shard_map/ppermute | solution.py:26
  13.0 27.3 %copy-start.4 = (bf16[160,512]{1,0:T(8,128)(2,1)S(1)}, bf16[160,512]{1,0:T(8,128)(2,1)}, u32[]{:S(2)}) copy-start(bf16[160,512]{1,0:T(8,128)(2,1)} %get-tuple-element.37.refs_0_) | copy-start | bytes 491524
  13.0 13.9 %collective-permute-start.2 = (bf16[160,512]{1,0:T(8,128)(2,1)}, bf16[160,512]{1,0:T(8,128)(2,1)S(1)}, u32[]{:S(2)}, u32[]{:S(2)}) collective-permute-start(bf16[160,512]{1,0:T(8,128)(2,1)} %get-tuple-element.40), channel_id=1, source_target_pairs={{0,3},{1,0},{2,1},{3,2},{4,7},{5,4},{6,5},{7,6},{8,11},{9,8},{10,9... | collective-permute-start | bytes 491528 | tf_op jit(solution)/shard_map/ppermute | solution.py:26
  22.4 7.8 %collective-permute-start.4 = (bf16[240,256]{1,0:T(8,128)(2,1)S(1)}, bf16[240,256]{1,0:T(8,128)(2,1)S(1)}, u32[]{:S(2)}, u32[]{:S(2)}) collective-permute-start(bf16[240,256]{1,0:T(8,128)(2,1)S(1)} %get-tuple-element.43), channel_id=1, source_target_pairs={{0,1},{1,2},{2,3},{3,0},{4,5},{5,6},{6,7},{7,4},{8,9},{9,10},{10,1... | collective-permute-start | bytes 368648 | tf_op jit(solution)/shard_map/ppermute | solution.py:26
  24.2 11.9 %collective-permute-start.5 = (bf16[240,256]{1,0:T(8,128)(2,1)S(1)}, bf16[240,256]{1,0:T(8,128)(2,1)S(1)}, u32[]{:S(2)}, u32[]{:S(2)}) collective-permute-start(bf16[240,256]{1,0:T(8,128)(2,1)S(1)} %get-tuple-element.45), channel_id=1, source_target_pairs={{0,2},{1,3},{2,0},{3,1},{4,6},{5,7},{6,4},{7,5},{8,10},{9,11},{10,... | collective-permute-start | bytes 368648 | tf_op jit(solution)/shard_map/ppermute | solution.py:26
  26.8 13.3 %collective-permute-start.6 = (bf16[240,256]{1,0:T(8,128)(2,1)S(1)}, bf16[240,256]{1,0:T(8,128)(2,1)S(1)}, u32[]{:S(2)}, u32[]{:S(2)}) collective-permute-start(bf16[240,256]{1,0:T(8,128)(2,1)S(1)} %get-tuple-element.47), channel_id=1, source_target_pairs={{0,3},{1,0},{2,1},{3,2},{4,7},{5,4},{6,5},{7,6},{8,11},{9,8},{10,9... | collective-permute-start | bytes 368648 | tf_op jit(solution)/shard_map/ppermute | solution.py:26
  30.2 15.7 %collective-permute-start.8 = (bf16[240,256]{1,0:T(8,128)(2,1)S(1)}, bf16[240,256]{1,0:T(8,128)(2,1)S(1)}, u32[]{:S(2)}, u32[]{:S(2)}) collective-permute-start(bf16[240,256]{1,0:T(8,128)(2,1)S(1)} %get-tuple-element.52), channel_id=1, source_target_pairs={{0,1},{1,2},{2,3},{3,0},{4,5},{5,6},{6,7},{7,4},{8,9},{9,10},{10,1... | collective-permute-start | bytes 368648 | tf_op jit(solution)/shard_map/ppermute | solution.py:26
  36.2 9.7 %collective-permute-start.9 = (bf16[240,256]{1,0:T(8,128)(2,1)S(1)}, bf16[240,256]{1,0:T(8,128)(2,1)S(1)}, u32[]{:S(2)}, u32[]{:S(2)}) collective-permute-start(bf16[240,256]{1,0:T(8,128)(2,1)S(1)} %get-tuple-element.54), channel_id=1, source_target_pairs={{0,2},{1,3},{2,0},{3,1},{4,6},{5,7},{6,4},{7,5},{8,10},{9,11},{10,... | collective-permute-start | bytes 368648 | tf_op jit(solution)/shard_map/ppermute | solution.py:26
  40.1 7.9 %collective-permute-start.10 = (bf16[240,256]{1,0:T(8,128)(2,1)S(1)}, bf16[240,256]{1,0:T(8,128)(2,1)S(1)}, u32[]{:S(2)}, u32[]{:S(2)}) collective-permute-start(bf16[240,256]{1,0:T(8,128)(2,1)S(1)} %get-tuple-element.56), channel_id=1, source_target_pairs={{0,3},{1,0},{2,1},{3,2},{4,7},{5,4},{6,5},{7,6},{8,11},{9,8},{10,9... | collective-permute-start | bytes 368648 | tf_op jit(solution)/shard_map/ppermute | solution.py:26
  44.5 7.6 %collective-permute-start.7 = (bf16[608,128]{1,0:T(8,128)(2,1)S(1)}, bf16[608,128]{1,0:T(8,128)(2,1)S(1)}, u32[]{:S(2)}, u32[]{:S(2)}) collective-permute-start(bf16[608,128]{1,0:T(8,128)(2,1)S(1)} %get-tuple-element.48.mixed), channel_id=1, source_target_pairs={{0,16},{4,20},{8,24},{12,28},{16,0},{20,4},{24,8},{28,12},{1,17},{... | collective-permute-start | bytes 466952 | tf_op jit(solution)/shard_map/ppermute | solution.py:26
  48.0 18.0 %copy-start.1 = (bf16[640,1280]{1,0:T(8,128)(2,1)S(1)}, bf16[640,1280]{1,0:T(8,128)(2,1)}, u32[]{:S(2)}) copy-start(bf16[640,1280]{1,0:T(8,128)(2,1)} %weight.5) | copy-start | bytes 4915204
  52.1 5.8 %collective-permute-start.14 = (bf16[608,128]{1,0:T(8,128)(2,1)S(1)}, bf16[608,128]{1,0:T(8,128)(2,1)S(1)}, u32[]{:S(2)}, u32[]{:S(2)}) collective-permute-start(bf16[608,128]{1,0:T(8,128)(2,1)S(1)} %get-tuple-element.64.mixed), channel_id=1, source_target_pairs={{0,16},{4,20},{8,24},{12,28},{16,0},{20,4},{24,8},{28,12},{1,17},{... | collective-permute-start | bytes 466952 | tf_op jit(solution)/shard_map/ppermute | solution.py:26
  52.8 8.8 %collective-permute-start.11 = (bf16[360,128]{1,0:T(8,128)(2,1)S(1)}, bf16[360,128]{1,0:T(8,128)(2,1)S(1)}, u32[]{:S(2)}, u32[]{:S(2)}) collective-permute-start(bf16[360,128]{1,0:T(8,128)(2,1)S(1)} %get-tuple-element.59), channel_id=1, source_target_pairs={{0,3},{1,0},{2,1},{3,2},{4,7},{5,4},{6,5},{7,6},{8,11},{9,8},{10,9... | collective-permute-start | bytes 276488 | tf_op jit(solution)/shard_map/ppermute | solution.py:26
  56.0 10.0 %collective-permute-start.12 = (bf16[360,128]{1,0:T(8,128)(2,1)S(1)}, bf16[360,128]{1,0:T(8,128)(2,1)S(1)}, u32[]{:S(2)}, u32[]{:S(2)}) collective-permute-start(bf16[360,128]{1,0:T(8,128)(2,1)S(1)} %get-tuple-element.60), channel_id=1, source_target_pairs={{0,2},{1,3},{2,0},{3,1},{4,6},{5,7},{6,4},{7,5},{8,10},{9,11},{10,... | collective-permute-start | bytes 276488 | tf_op jit(solution)/shard_map/ppermute | solution.py:26
  56.0 10.0 %collective-permute-start.13 = (bf16[360,128]{1,0:T(8,128)(2,1)S(1)}, bf16[360,128]{1,0:T(8,128)(2,1)S(1)}, u32[]{:S(2)}, u32[]{:S(2)}) collective-permute-start(bf16[360,128]{1,0:T(8,128)(2,1)S(1)} %get-tuple-element.61), channel_id=1, source_target_pairs={{0,1},{1,2},{2,3},{3,0},{4,5},{5,6},{6,7},{7,4},{8,9},{9,10},{10,1... | collective-permute-start | bytes 276488 | tf_op jit(solution)/shard_map/ppermute | solution.py:26
  58.5 8.6 %collective-permute-start.15 = (bf16[152,128]{1,0:T(8,128)(2,1)S(1)}, bf16[152,128]{1,0:T(8,128)(2,1)S(1)}, u32[]{:S(2)}, u32[]{:S(2)}) collective-permute-start(bf16[152,128]{1,0:T(8,128)(2,1)S(1)} %get-tuple-element.66), channel_id=1, source_target_pairs={{0,3},{1,0},{2,1},{3,2},{4,7},{5,4},{6,5},{7,6},{8,11},{9,8},{10,9... | collective-permute-start | bytes 116744 | tf_op jit(solution)/shard_map/ppermute | solution.py:26
  60.5 6.5 %collective-permute-start.16 = (bf16[152,128]{1,0:T(8,128)(2,1)S(1)}, bf16[152,128]{1,0:T(8,128)(2,1)S(1)}, u32[]{:S(2)}, u32[]{:S(2)}) collective-permute-start(bf16[152,128]{1,0:T(8,128)(2,1)S(1)} %get-tuple-element.67), channel_id=1, source_target_pairs={{0,2},{1,3},{2,0},{3,1},{4,6},{5,7},{6,4},{7,5},{8,10},{9,11},{10,... | collective-permute-start | bytes 116744 | tf_op jit(solution)/shard_map/ppermute | solution.py:26
  61.6 5.8 %collective-permute-start.17 = (bf16[152,128]{1,0:T(8,128)(2,1)S(1)}, bf16[152,128]{1,0:T(8,128)(2,1)S(1)}, u32[]{:S(2)}, u32[]{:S(2)}) collective-permute-start(bf16[152,128]{1,0:T(8,128)(2,1)S(1)} %get-tuple-element.68), channel_id=1, source_target_pairs={{0,1},{1,2},{2,3},{3,0},{4,5},{5,6},{6,7},{7,4},{8,9},{9,10},{10,1... | collective-permute-start | bytes 116744 | tf_op jit(solution)/shard_map/ppermute | solution.py:26

commit v14 on v13

--- a/solution.py
+++ b/solution.py
@@ -14,7 +14,7 @@
 SUBLANES = 8
 MIB = 1024 * 1024
 CHUNKS = 5
-COPIES = 4
+COPIES = 1
 
 
 def round_up(value, unit):
@@ -37,11 +37,29 @@
     return lon_shift[lax.rem(lax.axis_index("win"), LAT_WINDOWS)]
 
 
+SPARE = 2 * LANES - 3 * HD
+
+
+def dense_rows(count):
+    return 2 * count - SPARE
+
+
+def dense(block):
+    count, width = block.shape
+    second = block[:, LANES:]
+    last = second[count - SPARE :]
+    pieces = [last[:, at : at + SPARE] for at in range(0, width - LANES, SPARE)]
+    empty = count - SPARE - SPARE * len(pieces)
+    if empty:
+        pieces.append(jnp.zeros((empty, SPARE), block.dtype))
+    filled = jnp.concatenate([second[: count - SPARE], jnp.concatenate(pieces, axis=0)], axis=1)
+    return jnp.concatenate([block[:, :LANES], filled], axis=0)
+
+
 def project(tokens, gain, weight, copies, slots):
     groups = slots.shape[0]
     local = HEADS // groups
-    count, features = tokens.shape
-    span = slots.shape[2] // local
+    features = tokens.shape[1]
     factor = lax.rsqrt(jnp.mean(tokens * tokens, axis=-1, keepdims=True) + 1e-06)
     normed = (tokens * factor * gain[...].reshape(1, features)).astype(jnp.bfloat16)
     chunk = features // len(copies)
@@ -53,17 +71,17 @@
         share = jnp.dot(normed[:, inner], weight[inner], preferred_element_type=jnp.float32)
         qkv = share if qkv is None else qkv + share
     qkv = qkv.astype(jnp.bfloat16)
-    tail = jnp.ones((count, span - 3 * HD), jnp.bfloat16)
     place = lax.axis_index("tok")
     for group in range(groups):
         slot = lax.rem(group - place + groups, groups)
-        columns = []
+        blocks = []
         for head in range(group * local, (group + 1) * local):
-            columns += [
+            columns = [
                 qkv[:, (kind * HEADS + head) * HD : (kind * HEADS + head + 1) * HD]
                 for kind in (1, 0, 2)
-            ] + [tail]
-        slots[slot] = jnp.concatenate(columns, axis=1)
+            ]
+            blocks.append(dense(jnp.concatenate(columns, axis=1)))
+        slots[slot] = jnp.concatenate(blocks, axis=0)
 
 
 def kept_kernel(split, field, gain, weight, *refs):
@@ -106,19 +124,30 @@
     project(tokens.reshape(rows * split, features), gain, weight, [[]], slots)
     groups = slots.shape[0]
     for index, out in enumerate(outs):
-        first = index // groups * out.shape[1]
-        out[...] = slots[index % groups, :, first : first + out.shape[1]]
-
-
-def gather(head, kept, mixed, held, keys):
-    span = held.shape[1]
+        first = index // groups * out.shape[0]
+        out[...] = slots[index % groups, first : first + out.shape[0]]
+
+
+def place_rows(block, first, count, held, start):
+    held[start : start + count, :LANES] = block[first : first + count]
+    second = block[first + count : first + dense_rows(count)]
+    used = LANES - SPARE
+    lane = lax.broadcasted_iota(jnp.int32, second.shape, 1)
+    ones = jnp.ones(second.shape, second.dtype)
+    held[start : start + count - SPARE, LANES:] = jnp.where(lane < used, second, ones)
+    pieces = [second[at : at + SPARE, used:] for at in range(0, used, SPARE)]
+    pieces.append(jnp.ones((SPARE, SPARE), second.dtype))
+    held[start + count - SPARE : start + count, LANES:] = jnp.concatenate(pieces, axis=1)
+
+
+def gather(head, kept, kept_count, mixed, mixed_count, held, keys):
     start = 0
     for block in kept:
-        held[start : start + block.shape[0]] = block[:, head * span : (head + 1) * span]
-        start += block.shape[0]
+        place_rows(block, head * dense_rows(kept_count), kept_count, held, start)
+        start += kept_count
     for block in mixed:
-        held[start : start + block.shape[0]] = block[...]
-        start += block.shape[0]
+        place_rows(block, 0, mixed_count, held, start)
+        start += mixed_count
     keys[...] = held[:, :LANES].T
 
 
@@ -202,17 +231,17 @@
     return jnp.where(row < count // 2, main, rests)
 
 
-def attention_kernel(head, groups, *refs):
+def attention_kernel(head, groups, kept_count, mixed_count, *refs):
     kept, mixed = refs[:groups], refs[groups : 2 * groups]
     kept_out, mixed_out, held, keys, attended, *rest = refs[2 * groups :]
-    gather(head, kept, mixed, held, keys)
+    gather(head, kept, kept_count, mixed, mixed_count, held, keys)
     attend(held, keys, attended, rest[:2], rest[2:])
     start = 0
-    for blocks, out in ((kept, kept_out), (mixed, mixed_out)):
+    for count, out in ((kept_count, kept_out), (mixed_count, mixed_out)):
         packed = []
-        for block in blocks:
-            packed.append(pack(attended[start : start + block.shape[0]]))
-            start += block.shape[0]
+        for _ in range(groups):
+            packed.append(pack(attended[start : start + count]))
+            start += count
         out[...] = jnp.concatenate(packed, axis=0).astype(jnp.bfloat16)
 
 
@@ -293,14 +322,15 @@
         return pltpu.CompilerParams(vmem_limit_bytes=size * MIB)
 
     def projection(kernel, count, parts, specs, out_specs, held, params, *operands):
-        block = jax.ShapeDtypeStruct((count, local * span // parts), jnp.bfloat16)
+        size = local * dense_rows(count)
+        block = jax.ShapeDtypeStruct((size // parts, LANES), jnp.bfloat16)
         return pl.pallas_call(
             functools.partial(kernel, split),
             out_shape=[block] * (parts * groups),
             in_specs=specs,
             out_specs=out_specs,
             scratch_shapes=[
-                pltpu.VMEM((groups, count, local * span), jnp.bfloat16),
+                pltpu.VMEM((groups, size, LANES), jnp.bfloat16),
                 *held,
             ],
             compiler_params=params,
@@ -346,7 +376,7 @@
 
     def attention(head, step, *blocks):
         return pl.pallas_call(
-            functools.partial(attention_kernel, head, groups),
+            functools.partial(attention_kernel, head, groups, kept_count, mixed_count),
             out_shape=[block(groups * kept_packed), block(groups * mixed_packed)],
             in_specs=whole(len(blocks)),
             out_specs=whole(2),
@@ -381,8 +411,8 @@
         )(lon_shift, mixed_values, western, *kept_values)
         return spread(selected, -1)
 
-    first_kept_values, first_mixed_values = attention(0, total // 10, *kept, *first_mixed)
-    second_kept_values, second_mixed_values = attention(1, total // 4, *kept, *second_mixed)
+    first_kept_values, first_mixed_values = attention(0, total // 5, *kept, *first_mixed)
+    second_kept_values, second_mixed_values = attention(1, total // 5, *kept, *second_mixed)
     first = back(first_mixed_values, first_kept_values, second_kept_values)
     second = back(second_mixed_values)
 

time: 69.1 us -> 69.7 us (level)
  transfers between devices with their start and end apart: 18 -> 18, of which waited for: 8 -> 6; matrix products, arithmetic and copies ran while one was open for 0% -> 0% of each run, Pallas kernels for 28% -> 28%
where the time goes in v14:
time: 69.7 us; the launch traced here: 69.6 us
  starting transfers between devices  32.5 us (47%)
  Pallas kernels  20.9 us (30%)
  waiting for transfers between devices  14.9 us (21%)
  local copies, waits for them, and re-layouts  1.14 us (2%)
    ppermute x18, starting transfers between devices, shifted(): lax.ppermute(block, axis, [(i, (i + distance) % count) for i in range(cou...  32.5 us
    ppermute x18, waiting for transfers between devices, shifted(): lax.ppermute(block, axis, [(i, (i + distance) % count) for i in range(cou...  14.9 us
    pallas_call x2, Pallas kernels, projection(): pl.pallas_call(functools.partial(kernel, split), out_shape=[block] * (par...  9.08 us
    pallas_call x2, Pallas kernels, attention(): pl.pallas_call(functools.partial(attention_kernel, head, groups, kept_cou...  8.07 us
    pallas_call x1, Pallas kernels, shards(): pl.pallas_call(functools.partial(second_output_kernel, split), out_shape=...  1.52 us
  transfers between devices with their start and end apart: 18, of which 6 were waited for; matrix products, arithmetic and copies ran while one was open for 0% of the time, Pallas kernels for 28%

profile of v14, /device:TPU:0, one launch (start us, length us, event | category | flops | bytes accessed | tf_op | source)
XLA Modules:
  0.0 69.6 jit_solution(4239737581988104090)
XLA Ops:
  0.0 1.1 %slice.4 = bf16[10,24,1280]{2,1,0:T(8,128)(2,1)S(1)} slice(bf16[10,40,1280]{2,1,0:T(8,128)(2,1)} %bitcast.2), slice={[0:10], [0:24], [0:1280]} | slice | bytes 1228800 | tf_op jit(solution)/shard_map/slice | solution.py:350
  1.1 0.0 copy-start
  1.1 0.0 copy-start.2
  1.1 0.0 copy-start.3
  1.2 3.0 %collective-permute-start.3 = (bf16[10,24,1280]{2,1,0:T(8,128)(2,1)S(1)}, bf16[10,24,1280]{2,1,0:T(8,128)(2,1)S(1)}, u32[]{:S(2)}, u32[]{:S(2)}) collective-permute-start(bf16[10,24,1280]{2,1,0:T(8,128)(2,1)S(1)} %slice.4), channel_id=1, source_target_pairs={{0,16},{4,20},{8,24},{12,28},{16,0},{20,4},{24,8},{28,12},{1,17},{... | collective-permute-start | bytes 1843208 | tf_op jit(solution)/shard_map/ppermute | solution.py:26
  4.2 4.6 %shard_map.55 = (bf16[608,128]{1,0:T(8,128)(2,1)}, bf16[608,128]{1,0:T(8,128)(2,1)}, bf16[608,128]{1,0:T(8,128)(2,1)}, bf16[608,128]{1,0:T(8,128)(2,1)}) custom-call(bf16[10,40,1280]{2,1,0:T(8,128)(2,1)} %bitcast.3, f32[1280]{0:T(1024)} %gain.3, bf16[1280,1920]{1,0:T(8,128)(2,1)} %weight.4), custom_call_target="tpu_custom_call" | custom-call | flops 786432000 | bytes 5734400 | tf_op jit(solution)/shard_map/pallas_call | solution.py:327
  8.8 3.6 %collective-permute-start.2 = (bf16[608,128]{1,0:T(8,128)(2,1)}, bf16[608,128]{1,0:T(8,128)(2,1)S(1)}, u32[]{:S(2)}, u32[]{:S(2)}) collective-permute-start(bf16[608,128]{1,0:T(8,128)(2,1)} %get-tuple-element.40), channel_id=1, source_target_pairs={{0,3},{1,0},{2,1},{3,2},{4,7},{5,4},{6,5},{7,6},{8,11},{9,8},{10,9... | collective-permute-start | bytes 466952 | tf_op jit(solution)/shard_map/ppermute | solution.py:26
  12.4 0.0 collective-permute-start.1
  12.4 0.0 copy-start.4
  12.4 1.0 %collective-permute-start = (bf16[608,128]{1,0:T(8,128)(2,1)}, bf16[608,128]{1,0:T(8,128)(2,1)S(1)}, u32[]{:S(2)}, u32[]{:S(2)}) collective-permute-start(bf16[608,128]{1,0:T(8,128)(2,1)} %get-tuple-element.38), channel_id=1, source_target_pairs={{0,1},{1,2},{2,3},{3,0},{4,5},{5,6},{6,7},{7,4},{8,9},{9,10},{10,1... | collective-permute-start | bytes 466952 | tf_op jit(solution)/shard_map/ppermute | solution.py:26
  13.5 4.6 %collective-permute-done.3.eastern = bf16[10,24,1280]{2,1,0:T(8,128)(2,1)S(1)} collective-permute-done((bf16[10,24,1280]{2,1,0:T(8,128)(2,1)S(1)}, bf16[10,24,1280]{2,1,0:T(8,128)(2,1)S(1)}, u32[]{:S(2)}, u32[]{:S(2)}) %collective-permute-start.3) | collective-permute-done | bytes 614432 | tf_op jit(solution)/shard_map/ppermute | solution.py:26
  18.0 0.0 copy-done
  18.0 0.0 copy-done.2
  18.0 0.0 copy-done.3
  18.1 4.5 %shard_map.56 = (bf16[464,128]{1,0:T(8,128)(2,1)S(1)}, bf16[464,128]{1,0:T(8,128)(2,1)S(1)}, bf16[464,128]{1,0:T(8,128)(2,1)S(1)}, bf16[464,128]{1,0:T(8,128)(2,...) custom-call(bf16[10,40,1280]{2,1,0:T(8,128)(2,1)S(1)} %bitcast.4, ...), custom_call_target="tpu_custom_call" | custom-call | flops 1179648000 | bytes 6144000 | tf_op jit(solution)/shard_map/pallas_call | solution.py:327
  22.5 0.0 collective-permute-done.2.refs_3_
  22.6 3.9 %collective-permute-start.6 = (bf16[464,128]{1,0:T(8,128)(2,1)S(1)}, bf16[464,128]{1,0:T(8,128)(2,1)S(1)}, u32[]{:S(2)}, u32[]{:S(2)}) collective-permute-start(bf16[464,128]{1,0:T(8,128)(2,1)S(1)} %get-tuple-element.47), channel_id=1, source_target_pairs={{0,3},{1,0},{2,1},{3,2},{4,7},{5,4},{6,5},{7,6},{8,11},{9,8},{10,9... | collective-permute-start | bytes 356360 | tf_op jit(solution)/shard_map/ppermute | solution.py:26
  26.4 0.0 collective-permute-done.1.refs_2_
  26.4 0.0 collective-permute-start.5
  26.4 0.0 collective-permute-done.refs_1_
  26.4 1.0 %collective-permute-start.4 = (bf16[464,128]{1,0:T(8,128)(2,1)S(1)}, bf16[464,128]{1,0:T(8,128)(2,1)S(1)}, u32[]{:S(2)}, u32[]{:S(2)}) collective-permute-start(bf16[464,128]{1,0:T(8,128)(2,1)S(1)} %get-tuple-element.43), channel_id=1, source_target_pairs={{0,1},{1,2},{2,3},{3,0},{4,5},{5,6},{6,7},{7,4},{8,9},{9,10},{10,1... | collective-permute-start | bytes 356360 | tf_op jit(solution)/shard_map/ppermute | solution.py:26
  27.5 2.7 %collective-permute-done.6.refs_7_ = bf16[464,128]{1,0:T(8,128)(2,1)S(1)} collective-permute-done((bf16[464,128]{1,0:T(8,128)(2,1)S(1)}, bf16[464,128]{1,0:T(8,128)(2,1)S(1)}, u32[]{:S(2)}, u32[]{:S(2)}) %collective-permute-start.6) | collective-permute-done | bytes 118816 | tf_op jit(solution)/shard_map/ppermute | solution.py:26
  30.1 4.3 %collective-permute-start.10 = (bf16[464,128]{1,0:T(8,128)(2,1)S(1)}, bf16[464,128]{1,0:T(8,128)(2,1)S(1)}, u32[]{:S(2)}, u32[]{:S(2)}) collective-permute-start(bf16[464,128]{1,0:T(8,128)(2,1)S(1)} %get-tuple-element.56), channel_id=1, source_target_pairs={{0,3},{1,0},{2,1},{3,2},{4,7},{5,4},{6,5},{7,6},{8,11},{9,8},{10,9... | collective-permute-start | bytes 356360 | tf_op jit(solution)/shard_map/ppermute | solution.py:26
  34.5 3.5 %collective-permute-done.5.refs_6_ = bf16[464,128]{1,0:T(8,128)(2,1)S(1)} collective-permute-done((bf16[464,128]{1,0:T(8,128)(2,1)S(1)}, bf16[464,128]{1,0:T(8,128)(2,1)S(1)}, u32[]{:S(2)}, u32[]{:S(2)}) %collective-permute-start.5) | collective-permute-done | bytes 118816 | tf_op jit(solution)/shard_map/ppermute | solution.py:26
  38.0 0.0 collective-permute-start.9
  38.0 0.0 collective-permute-done.4.refs_5_
  38.0 3.2 %collective-permute-start.8 = (bf16[464,128]{1,0:T(8,128)(2,1)S(1)}, bf16[464,128]{1,0:T(8,128)(2,1)S(1)}, u32[]{:S(2)}, u32[]{:S(2)}) collective-permute-start(bf16[464,128]{1,0:T(8,128)(2,1)S(1)} %get-tuple-element.52), channel_id=1, source_target_pairs={{0,1},{1,2},{2,3},{3,0},{4,5},{5,6},{6,7},{7,4},{8,9},{9,10},{10,1... | collective-permute-start | bytes 356360 | tf_op jit(solution)/shard_map/ppermute | solution.py:26
  41.3 0.0 copy-done.4
  41.3 4.0 %shard_map.57 = (bf16[416,128]{1,0:T(8,128)(2,1)S(1)}, bf16[608,128]{1,0:T(8,128)(2,1)S(1)}) custom-call(bf16[608,128]{1,0:T(8,128)(2,1)S(1)} %copy-done.4, bf16[608,128]{1,0:T(8,128)(2,1)S(1)} %collective-permute-done.refs_1_, bf16[608,128]{1,0:T(8,128)(2,1)S(1)} %collective-permute-done.1.refs_2_, bf16[608,128]{1,0:T(8,128)(2,1)S(1)} %collective-permute-done.2.refs_3_, ...), custom_call_target="tpu_custom_call" | custom-call | flops 2621440000 | bytes 1228800 | tf_op jit(solution)/shard_map/pallas_call | solution.py:378
  45.3 1.5 %collective-permute-start.7 = (bf16[608,128]{1,0:T(8,128)(2,1)S(1)}, bf16[608,128]{1,0:T(8,128)(2,1)S(1)}, u32[]{:S(2)}, u32[]{:S(2)}) collective-permute-start(bf16[608,128]{1,0:T(8,128)(2,1)S(1)} %get-tuple-element.48.mixed), channel_id=1, source_target_pairs={{0,16},{4,20},{8,24},{12,28},{16,0},{20,4},{24,8},{28,12},{1,17},{... | collective-permute-start | bytes 466952 | tf_op jit(solution)/shard_map/ppermute | solution.py:26
  46.8 0.0 collective-permute-done.10.refs_7_
  46.8 0.0 collective-permute-done.9.refs_6_
  46.8 0.0 collective-permute-done.8.refs_5_
  46.8 0.0 copy-start.1
  46.8 4.0 %shard_map.58 = (bf16[416,128]{1,0:T(8,128)(2,1)S(1)}, bf16[608,128]{1,0:T(8,128)(2,1)S(1)}) custom-call(bf16[608,128]{1,0:T(8,128)(2,1)S(1)} %copy-done.4, bf16[608,128]{1,0:T(8,128)(2,1)S(1)} %collective-permute-done.refs_1_, bf16[608,128]{1,0:T(8,128)(2,1)S(1)} %collective-permute-done.1.refs_2_, bf16[608,128]{1,0:T(8,128)(2,1)S(1)} %collective-permute-done.2.refs_3_, ...), custom_call_target="tpu_custom_call" | custom-call | flops 2621440000 | bytes 1228800 | tf_op jit(solution)/shard_map/pallas_call | solution.py:378
  50.9 1.2 %collective-permute-start.14 = (bf16[608,128]{1,0:T(8,128)(2,1)S(1)}, bf16[608,128]{1,0:T(8,128)(2,1)S(1)}, u32[]{:S(2)}, u32[]{:S(2)}) collective-permute-start(bf16[608,128]{1,0:T(8,128)(2,1)S(1)} %get-tuple-element.64.mixed), channel_id=1, source_target_pairs={{0,16},{4,20},{8,24},{12,28},{16,0},{20,4},{24,8},{28,12},{1,17},{... | collective-permute-start | bytes 466952 | tf_op jit(solution)/shard_map/ppermute | solution.py:26
  52.1 0.0 collective-permute-done.7.western
  52.1 0.6 shard_map.59
  52.7 2.4 %collective-permute-start.11 = (bf16[360,128]{1,0:T(8,128)(2,1)S(1)}, bf16[360,128]{1,0:T(8,128)(2,1)S(1)}, u32[]{:S(2)}, u32[]{:S(2)}) collective-permute-start(bf16[360,128]{1,0:T(8,128)(2,1)S(1)} %get-tuple-element.59), channel_id=1, source_target_pairs={{0,3},{1,0},{2,1},{3,2},{4,7},{5,4},{6,5},{7,6},{8,11},{9,8},{10,9... | collective-permute-start | bytes 276488 | tf_op jit(solution)/shard_map/ppermute | solution.py:26
  55.2 2.6 %collective-permute-start.12 = (bf16[360,128]{1,0:T(8,128)(2,1)S(1)}, bf16[360,128]{1,0:T(8,128)(2,1)S(1)}, u32[]{:S(2)}, u32[]{:S(2)}) collective-permute-start(bf16[360,128]{1,0:T(8,128)(2,1)S(1)} %get-tuple-element.60), channel_id=1, source_target_pairs={{0,2},{1,3},{2,0},{3,1},{4,6},{5,7},{6,4},{7,5},{8,10},{9,11},{10,... | collective-permute-start | bytes 276488 | tf_op jit(solution)/shard_map/ppermute | solution.py:26
  57.8 0.0 collective-permute-start.13
  57.8 0.0 collective-permute-done.14.western
  57.8 0.6 shard_map.61
  58.4 3.9 %collective-permute-start.15 = (bf16[152,128]{1,0:T(8,128)(2,1)S(1)}, bf16[152,128]{1,0:T(8,128)(2,1)S(1)}, u32[]{:S(2)}, u32[]{:S(2)}) collective-permute-start(bf16[152,128]{1,0:T(8,128)(2,1)S(1)} %get-tuple-element.66), channel_id=1, source_target_pairs={{0,3},{1,0},{2,1},{3,2},{4,7},{5,4},{6,5},{7,6},{8,11},{9,8},{10,9... | collective-permute-start | bytes 116744 | tf_op jit(solution)/shard_map/ppermute | solution.py:26
  62.2 0.0 collective-permute-start.16
  62.3 0.0 collective-permute-done.11.refs_1_
  62.3 0.6 collective-permute-start.17
  62.9 1.7 %collective-permute-done.12.refs_2_ = bf16[360,128]{1,0:T(8,128)(2,1)S(1)} collective-permute-done((bf16[360,128]{1,0:T(8,128)(2,1)S(1)}, bf16[360,128]{1,0:T(8,128)(2,1)S(1)}, u32[]{:S(2)}, u32[]{:S(2)}) %collective-permute-start.12) | collective-permute-done | bytes 92192 | tf_op jit(solution)/shard_map/ppermute | solution.py:26
  64.6 0.0 collective-permute-done.13.refs_3_
  64.6 0.0 copy-done.1
  64.6 1.0 %shard_map.60 = (f32[10,40,1280]{2,1,0:T(8,128)S(1)}, bf16[512,1280]{1,0:T(8,128)(2,1)S(1)}) custom-call(bf16[10,40,1280]{2,1,0:T(8,128)(2,1)S(1)} %bitcast.5, bf16[640,1280]{1,0:T(8,128)(2,1)S(1)} %copy-done.1, bf16[360,128]{1,0:T(8,128)(2,1)S(1)} %get-tuple-element.58.refs_0_, bf16[360,128]{1,0:T(8,128)(2,1)S(1)} %collective-permute-done.11.refs_1_, ...), custom_call_target="tpu_custom_call" | custom-call | flops 524288000 | bytes 3891200 | tf_op jit(solution)/shard_map/pallas_call | solution.py:425
  65.6 0.0 collective-permute-done.15.refs_1_
  65.7 1.5 %collective-permute-done.16.refs_2_ = bf16[152,128]{1,0:T(8,128)(2,1)S(1)} collective-permute-done((bf16[152,128]{1,0:T(8,128)(2,1)S(1)}, bf16[152,128]{1,0:T(8,128)(2,1)S(1)}, u32[]{:S(2)}, u32[]{:S(2)}) %collective-permute-start.16) | collective-permute-done | bytes 38944 | tf_op jit(solution)/shard_map/ppermute | solution.py:26
  67.1 0.9 %collective-permute-done.17.refs_3_ = bf16[152,128]{1,0:T(8,128)(2,1)S(1)} collective-permute-done((bf16[152,128]{1,0:T(8,128)(2,1)S(1)}, bf16[152,128]{1,0:T(8,128)(2,1)S(1)}, u32[]{:S(2)}, u32[]{:S(2)}) %collective-permute-start.17) | collective-permute-done | bytes 38944 | tf_op jit(solution)/shard_map/ppermute | solution.py:26
  68.0 1.5 %shard_map.62 = bf16[10,40,1280]{2,1,0:T(8,128)(2,1)} custom-call(f32[10,40,1280]{2,1,0:T(8,128)S(1)} %get-tuple-element.62.partial, bf16[512,1280]{1,0:T(8,128)(2,1)S(1)} %get-tuple-element.63.weight, bf16[152,128]{1,0:T(8,128)(2,1)S(1)} %get-tuple-element.65.refs_0_, bf16[152,128]{1,0:T(8,128)(2,1)S(1)} %collective-permute-done.15.refs_1_, ...), custom_call_target="tpu_custom_call" | custom-call | flops 524288000 | bytes 3891200 | tf_op jit(solution)/shard_map/pallas_call | solution.py:437
Async XLA Ops:
  1.1 16.9 %copy-start = (bf16[1,10,40,1280]{3,2,1,0:T(8,128)(2,1)S(1)}, bf16[1,10,40,1280]{3,2,1,0:T(8,128)(2,1)}, u32[]{:S(2)}) copy-start(bf16[1,10,40,1280]{3,2,1,0:T(8,128)(2,1)} %param.5) | copy-start | bytes 3072004
  1.1 16.9 %copy-start.2 = (f32[1280]{0:T(1024)S(1)}, f32[1280]{0:T(1024)}, u32[]{:S(2)}) copy-start(f32[1280]{0:T(1024)} %gain.3) | copy-start | bytes 15364
  1.1 16.9 %copy-start.3 = (s32[4]{0:T(128)S(1)}, s32[4]{0:T(128)}, u32[]{:S(2)}) copy-start(s32[4]{0:T(128)} %lon_shift.5) | copy-start | bytes 52
  1.2 16.9 %collective-permute-start.3 = (bf16[10,24,1280]{2,1,0:T(8,128)(2,1)S(1)}, bf16[10,24,1280]{2,1,0:T(8,128)(2,1)S(1)}, u32[]{:S(2)}, u32[]{:S(2)}) collective-permute-start(bf16[10,24,1280]{2,1,0:T(8,128)(2,1)S(1)} %slice.4), channel_id=1, source_target_pairs={{0,16},{4,20},{8,24},{12,28},{16,0},{20,4},{24,8},{28,12},{1,17},{... | collective-permute-start | bytes 1843208 | tf_op jit(solution)/shard_map/ppermute | solution.py:26
  8.8 13.8 %collective-permute-start.2 = (bf16[608,128]{1,0:T(8,128)(2,1)}, bf16[608,128]{1,0:T(8,128)(2,1)S(1)}, u32[]{:S(2)}, u32[]{:S(2)}) collective-permute-start(bf16[608,128]{1,0:T(8,128)(2,1)} %get-tuple-element.40), channel_id=1, source_target_pairs={{0,3},{1,0},{2,1},{3,2},{4,7},{5,4},{6,5},{7,6},{8,11},{9,8},{10,9... | collective-permute-start | bytes 466952 | tf_op jit(solution)/shard_map/ppermute | solution.py:26
  12.4 14.0 %collective-permute-start.1 = (bf16[608,128]{1,0:T(8,128)(2,1)}, bf16[608,128]{1,0:T(8,128)(2,1)S(1)}, u32[]{:S(2)}, u32[]{:S(2)}) collective-permute-start(bf16[608,128]{1,0:T(8,128)(2,1)} %get-tuple-element.39), channel_id=1, source_target_pairs={{0,2},{1,3},{2,0},{3,1},{4,6},{5,7},{6,4},{7,5},{8,10},{9,11},{10,... | collective-permute-start | bytes 466952 | tf_op jit(solution)/shard_map/ppermute | solution.py:26
  12.4 28.8 %copy-start.4 = (bf16[608,128]{1,0:T(8,128)(2,1)S(1)}, bf16[608,128]{1,0:T(8,128)(2,1)}, u32[]{:S(2)}) copy-start(bf16[608,128]{1,0:T(8,128)(2,1)} %get-tuple-element.37.refs_0_) | copy-start | bytes 466948
  12.4 14.0 %collective-permute-start = (bf16[608,128]{1,0:T(8,128)(2,1)}, bf16[608,128]{1,0:T(8,128)(2,1)S(1)}, u32[]{:S(2)}, u32[]{:S(2)}) collective-permute-start(bf16[608,128]{1,0:T(8,128)(2,1)} %get-tuple-element.38), channel_id=1, source_target_pairs={{0,1},{1,2},{2,3},{3,0},{4,5},{5,6},{6,7},{7,4},{8,9},{9,10},{10,1... | collective-permute-start | bytes 466952 | tf_op jit(solution)/shard_map/ppermute | solution.py:26
  22.6 7.6 %collective-permute-start.6 = (bf16[464,128]{1,0:T(8,128)(2,1)S(1)}, bf16[464,128]{1,0:T(8,128)(2,1)S(1)}, u32[]{:S(2)}, u32[]{:S(2)}) collective-permute-start(bf16[464,128]{1,0:T(8,128)(2,1)S(1)} %get-tuple-element.47), channel_id=1, source_target_pairs={{0,3},{1,0},{2,1},{3,2},{4,7},{5,4},{6,5},{7,6},{8,11},{9,8},{10,9... | collective-permute-start | bytes 356360 | tf_op jit(solution)/shard_map/ppermute | solution.py:26
  26.4 11.6 %collective-permute-start.5 = (bf16[464,128]{1,0:T(8,128)(2,1)S(1)}, bf16[464,128]{1,0:T(8,128)(2,1)S(1)}, u32[]{:S(2)}, u32[]{:S(2)}) collective-permute-start(bf16[464,128]{1,0:T(8,128)(2,1)S(1)} %get-tuple-element.45), channel_id=1, source_target_pairs={{0,2},{1,3},{2,0},{3,1},{4,6},{5,7},{6,4},{7,5},{8,10},{9,11},{10,... | collective-permute-start | bytes 356360 | tf_op jit(solution)/shard_map/ppermute | solution.py:26
  26.4 11.6 %collective-permute-start.4 = (bf16[464,128]{1,0:T(8,128)(2,1)S(1)}, bf16[464,128]{1,0:T(8,128)(2,1)S(1)}, u32[]{:S(2)}, u32[]{:S(2)}) collective-permute-start(bf16[464,128]{1,0:T(8,128)(2,1)S(1)} %get-tuple-element.43), channel_id=1, source_target_pairs={{0,1},{1,2},{2,3},{3,0},{4,5},{5,6},{6,7},{7,4},{8,9},{9,10},{10,1... | collective-permute-start | bytes 356360 | tf_op jit(solution)/shard_map/ppermute | solution.py:26
  30.1 16.7 %collective-permute-start.10 = (bf16[464,128]{1,0:T(8,128)(2,1)S(1)}, bf16[464,128]{1,0:T(8,128)(2,1)S(1)}, u32[]{:S(2)}, u32[]{:S(2)}) collective-permute-start(bf16[464,128]{1,0:T(8,128)(2,1)S(1)} %get-tuple-element.56), channel_id=1, source_target_pairs={{0,3},{1,0},{2,1},{3,2},{4,7},{5,4},{6,5},{7,6},{8,11},{9,8},{10,9... | collective-permute-start | bytes 356360 | tf_op jit(solution)/shard_map/ppermute | solution.py:26
  38.0 8.8 %collective-permute-start.9 = (bf16[464,128]{1,0:T(8,128)(2,1)S(1)}, bf16[464,128]{1,0:T(8,128)(2,1)S(1)}, u32[]{:S(2)}, u32[]{:S(2)}) collective-permute-start(bf16[464,128]{1,0:T(8,128)(2,1)S(1)} %get-tuple-element.54), channel_id=1, source_target_pairs={{0,2},{1,3},{2,0},{3,1},{4,6},{5,7},{6,4},{7,5},{8,10},{9,11},{10,... | collective-permute-start | bytes 356360 | tf_op jit(solution)/shard_map/ppermute | solution.py:26
  38.0 8.8 %collective-permute-start.8 = (bf16[464,128]{1,0:T(8,128)(2,1)S(1)}, bf16[464,128]{1,0:T(8,128)(2,1)S(1)}, u32[]{:S(2)}, u32[]{:S(2)}) collective-permute-start(bf16[464,128]{1,0:T(8,128)(2,1)S(1)} %get-tuple-element.52), channel_id=1, source_target_pairs={{0,1},{1,2},{2,3},{3,0},{4,5},{5,6},{6,7},{7,4},{8,9},{9,10},{10,1... | collective-permute-start | bytes 356360 | tf_op jit(solution)/shard_map/ppermute | solution.py:26
  45.3 6.8 %collective-permute-start.7 = (bf16[608,128]{1,0:T(8,128)(2,1)S(1)}, bf16[608,128]{1,0:T(8,128)(2,1)S(1)}, u32[]{:S(2)}, u32[]{:S(2)}) collective-permute-start(bf16[608,128]{1,0:T(8,128)(2,1)S(1)} %get-tuple-element.48.mixed), channel_id=1, source_target_pairs={{0,16},{4,20},{8,24},{12,28},{16,0},{20,4},{24,8},{28,12},{1,17},{... | collective-permute-start | bytes 466952 | tf_op jit(solution)/shard_map/ppermute | solution.py:26
  46.8 17.8 %copy-start.1 = (bf16[640,1280]{1,0:T(8,128)(2,1)S(1)}, bf16[640,1280]{1,0:T(8,128)(2,1)}, u32[]{:S(2)}) copy-start(bf16[640,1280]{1,0:T(8,128)(2,1)} %weight.5) | copy-start | bytes 4915204
  50.9 6.9 %collective-permute-start.14 = (bf16[608,128]{1,0:T(8,128)(2,1)S(1)}, bf16[608,128]{1,0:T(8,128)(2,1)S(1)}, u32[]{:S(2)}, u32[]{:S(2)}) collective-permute-start(bf16[608,128]{1,0:T(8,128)(2,1)S(1)} %get-tuple-element.64.mixed), channel_id=1, source_target_pairs={{0,16},{4,20},{8,24},{12,28},{16,0},{20,4},{24,8},{28,12},{1,17},{... | collective-permute-start | bytes 466952 | tf_op jit(solution)/shard_map/ppermute | solution.py:26
  52.7 9.5 %collective-permute-start.11 = (bf16[360,128]{1,0:T(8,128)(2,1)S(1)}, bf16[360,128]{1,0:T(8,128)(2,1)S(1)}, u32[]{:S(2)}, u32[]{:S(2)}) collective-permute-start(bf16[360,128]{1,0:T(8,128)(2,1)S(1)} %get-tuple-element.59), channel_id=1, source_target_pairs={{0,3},{1,0},{2,1},{3,2},{4,7},{5,4},{6,5},{7,6},{8,11},{9,8},{10,9... | collective-permute-start | bytes 276488 | tf_op jit(solution)/shard_map/ppermute | solution.py:26
  55.2 9.4 %collective-permute-start.12 = (bf16[360,128]{1,0:T(8,128)(2,1)S(1)}, bf16[360,128]{1,0:T(8,128)(2,1)S(1)}, u32[]{:S(2)}, u32[]{:S(2)}) collective-permute-start(bf16[360,128]{1,0:T(8,128)(2,1)S(1)} %get-tuple-element.60), channel_id=1, source_target_pairs={{0,2},{1,3},{2,0},{3,1},{4,6},{5,7},{6,4},{7,5},{8,10},{9,11},{10,... | collective-permute-start | bytes 276488 | tf_op jit(solution)/shard_map/ppermute | solution.py:26
  57.8 6.8 %collective-permute-start.13 = (bf16[360,128]{1,0:T(8,128)(2,1)S(1)}, bf16[360,128]{1,0:T(8,128)(2,1)S(1)}, u32[]{:S(2)}, u32[]{:S(2)}) collective-permute-start(bf16[360,128]{1,0:T(8,128)(2,1)S(1)} %get-tuple-element.61), channel_id=1, source_target_pairs={{0,1},{1,2},{2,3},{3,0},{4,5},{5,6},{6,7},{7,4},{8,9},{9,10},{10,1... | collective-permute-start | bytes 276488 | tf_op jit(solution)/shard_map/ppermute | solution.py:26
  58.4 7.3 %collective-permute-start.15 = (bf16[152,128]{1,0:T(8,128)(2,1)S(1)}, bf16[152,128]{1,0:T(8,128)(2,1)S(1)}, u32[]{:S(2)}, u32[]{:S(2)}) collective-permute-start(bf16[152,128]{1,0:T(8,128)(2,1)S(1)} %get-tuple-element.66), channel_id=1, source_target_pairs={{0,3},{1,0},{2,1},{3,2},{4,7},{5,4},{6,5},{7,6},{8,11},{9,8},{10,9... | collective-permute-start | bytes 116744 | tf_op jit(solution)/shard_map/ppermute | solution.py:26
  62.2 4.9 %collective-permute-start.16 = (bf16[152,128]{1,0:T(8,128)(2,1)S(1)}, bf16[152,128]{1,0:T(8,128)(2,1)S(1)}, u32[]{:S(2)}, u32[]{:S(2)}) collective-permute-start(bf16[152,128]{1,0:T(8,128)(2,1)S(1)} %get-tuple-element.67), channel_id=1, source_target_pairs={{0,2},{1,3},{2,0},{3,1},{4,6},{5,7},{6,4},{7,5},{8,10},{9,11},{10,... | collective-permute-start | bytes 116744 | tf_op jit(solution)/shard_map/ppermute | solution.py:26
  62.3 5.8 %collective-permute-start.17 = (bf16[152,128]{1,0:T(8,128)(2,1)S(1)}, bf16[152,128]{1,0:T(8,128)(2,1)S(1)}, u32[]{:S(2)}, u32[]{:S(2)}) collective-permute-start(bf16[152,128]{1,0:T(8,128)(2,1)S(1)} %get-tuple-element.68), channel_id=1, source_target_pairs={{0,1},{1,2},{2,3},{3,0},{4,5},{5,6},{6,7},{7,4},{8,9},{9,10},{10,1... | collective-permute-start | bytes 116744 | tf_op jit(solution)/shard_map/ppermute | solution.py:26

commit v15 on v14

--- a/solution.py
+++ b/solution.py
@@ -24,6 +24,10 @@
 def shifted(block, axis, distance):
     count = lax.axis_size(axis)
     return lax.ppermute(block, axis, [(i, (i + distance) % count) for i in range(count)])
+
+
+def travel_order(groups):
+    return [0, *range(groups - 1, 0, -1)]
 
 
 def after(blocks, arrived):
@@ -73,7 +77,7 @@
     qkv = qkv.astype(jnp.bfloat16)
     place = lax.axis_index("tok")
     for group in range(groups):
-        slot = lax.rem(group - place + groups, groups)
+        slot = lax.rem(place - group + groups, groups)
         blocks = []
         for head in range(group * local, (group + 1) * local):
             columns = [
@@ -270,8 +274,8 @@
 def first_output_kernel(split, groups, field, weight, *refs):
     *blocks, out, second, first = refs
     features = field.shape[2]
-    for slot in range(groups):
-        group = lax.rem(lax.axis_index("tok") + slot, groups)
+    for slot, distance in enumerate(travel_order(groups)):
+        group = lax.rem(lax.axis_index("tok") + distance, groups)
         for head, ordered in enumerate((first, second)):
             at = pl.multiple_of((group * HEADS // groups + head) * HD, 16)
             ordered[slot * LANES : slot * LANES + HD] = weight[pl.ds(at, HD)]
@@ -342,10 +346,10 @@
         )(*operands)
 
     def spread(blocks, sign):
-        arrived = list(blocks)
-        for distance in sorted(range(1, groups), key=lambda step: step * (step - groups)):
-            arrived[distance] = shifted(blocks[distance], "tok", sign * distance)
-        return arrived
+        return [blocks[0]] + [
+            shifted(block, "tok", sign * distance)
+            for block, distance in zip(blocks[1:], travel_order(groups)[1:])
+        ]
 
     eastern = shifted(field[:, :split], "win", -LAT_WINDOWS)
     hbm = pl.BlockSpec(memory_space=pltpu.HBM)

time: 69.7 us -> 67.4 us (0.967)
  waiting for transfers between devices: 14.9 us -> 11.2 us
  starting transfers between devices: 32.5 us -> 33.8 us
    ppermute x18, waiting for transfers between devices: 14.9 us -> 11.2 us  [shifted(): lax.ppermute(block, axis, [(i, (i + distance) % count) for i in range(cou...]
    ppermute x18, starting transfers between devices: 32.5 us -> 33.8 us  [shifted(): lax.ppermute(block, axis, [(i, (i + distance) % count) for i in range(cou...]
  transfers between devices with their start and end apart: 18 -> 18, of which waited for: 6 -> 6; matrix products, arithmetic and copies ran while one was open for 0% -> 0% of each run, Pallas kernels for 28% -> 29%
where the time goes in v15:
time: 67.4 us; the launch traced here: 67.3 us
  starting transfers between devices  33.8 us (50%)
  Pallas kernels  20.9 us (31%)
  waiting for transfers between devices  11.2 us (17%)
  local copies, waits for them, and re-layouts  1.14 us (2%)
    ppermute x18, starting transfers between devices, shifted(): lax.ppermute(block, axis, [(i, (i + distance) % count) for i in range(cou...  33.8 us
    ppermute x18, waiting for transfers between devices, shifted(): lax.ppermute(block, axis, [(i, (i + distance) % count) for i in range(cou...  11.2 us
    pallas_call x2, Pallas kernels, projection(): pl.pallas_call(functools.partial(kernel, split), out_shape=[block] * (par...  9.09 us
    pallas_call x2, Pallas kernels, attention(): pl.pallas_call(functools.partial(attention_kernel, head, groups, kept_cou...  8.08 us
    pallas_call x1, Pallas kernels, shards(): pl.pallas_call(functools.partial(second_output_kernel, split), out_shape=...  1.52 us
  transfers between devices with their start and end apart: 18, of which 6 were waited for; matrix products, arithmetic and copies ran while one was open for 0% of the time, Pallas kernels for 29%

profile of v15, /device:TPU:0, one launch (start us, length us, event | category | flops | bytes accessed | tf_op | source)
XLA Modules:
  0.0 67.3 jit_solution(2408858229680202953)
XLA Ops:
  0.0 1.1 %slice.4 = bf16[10,24,1280]{2,1,0:T(8,128)(2,1)S(1)} slice(bf16[10,40,1280]{2,1,0:T(8,128)(2,1)} %bitcast.2), slice={[0:10], [0:24], [0:1280]} | slice | bytes 1228800 | tf_op jit(solution)/shard_map/slice | solution.py:354
  1.1 0.0 copy-start
  1.1 0.0 copy-start.2
  1.1 0.0 copy-start.3
  1.2 3.0 %collective-permute-start.3 = (bf16[10,24,1280]{2,1,0:T(8,128)(2,1)S(1)}, bf16[10,24,1280]{2,1,0:T(8,128)(2,1)S(1)}, u32[]{:S(2)}, u32[]{:S(2)}) collective-permute-start(bf16[10,24,1280]{2,1,0:T(8,128)(2,1)S(1)} %slice.4), channel_id=1, source_target_pairs={{0,16},{4,20},{8,24},{12,28},{16,0},{20,4},{24,8},{28,12},{1,17},{... | collective-permute-start | bytes 1843208 | tf_op jit(solution)/shard_map/ppermute | solution.py:26
  4.2 4.6 %shard_map.55 = (bf16[608,128]{1,0:T(8,128)(2,1)}, bf16[608,128]{1,0:T(8,128)(2,1)}, bf16[608,128]{1,0:T(8,128)(2,1)}, bf16[608,128]{1,0:T(8,128)(2,1)}) custom-call(bf16[10,40,1280]{2,1,0:T(8,128)(2,1)} %bitcast.3, f32[1280]{0:T(1024)} %gain.3, bf16[1280,1920]{1,0:T(8,128)(2,1)} %weight.4), custom_call_target="tpu_custom_call" | custom-call | flops 786432000 | bytes 5734400 | tf_op jit(solution)/shard_map/pallas_call | solution.py:331
  8.8 1.6 %collective-permute-start.2 = (bf16[608,128]{1,0:T(8,128)(2,1)}, bf16[608,128]{1,0:T(8,128)(2,1)S(1)}, u32[]{:S(2)}, u32[]{:S(2)}) collective-permute-start(bf16[608,128]{1,0:T(8,128)(2,1)} %get-tuple-element.40), channel_id=1, source_target_pairs={{0,1},{1,2},{2,3},{3,0},{4,5},{5,6},{6,7},{7,4},{8,9},{9,10},{10,1... | collective-permute-start | bytes 466952 | tf_op jit(solution)/shard_map/ppermute | solution.py:26
  10.4 2.6 %collective-permute-start.1 = (bf16[608,128]{1,0:T(8,128)(2,1)}, bf16[608,128]{1,0:T(8,128)(2,1)S(1)}, u32[]{:S(2)}, u32[]{:S(2)}) collective-permute-start(bf16[608,128]{1,0:T(8,128)(2,1)} %get-tuple-element.39), channel_id=1, source_target_pairs={{0,2},{1,3},{2,0},{3,1},{4,6},{5,7},{6,4},{7,5},{8,10},{9,11},{10,... | collective-permute-start | bytes 466952 | tf_op jit(solution)/shard_map/ppermute | solution.py:26
  13.0 0.0 copy-start.4
  13.0 1.3 %collective-permute-start = (bf16[608,128]{1,0:T(8,128)(2,1)}, bf16[608,128]{1,0:T(8,128)(2,1)S(1)}, u32[]{:S(2)}, u32[]{:S(2)}) collective-permute-start(bf16[608,128]{1,0:T(8,128)(2,1)} %get-tuple-element.38), channel_id=1, source_target_pairs={{0,3},{1,0},{2,1},{3,2},{4,7},{5,4},{6,5},{7,6},{8,11},{9,8},{10,9... | collective-permute-start | bytes 466952 | tf_op jit(solution)/shard_map/ppermute | solution.py:26
  14.4 3.7 %collective-permute-done.3.eastern = bf16[10,24,1280]{2,1,0:T(8,128)(2,1)S(1)} collective-permute-done((bf16[10,24,1280]{2,1,0:T(8,128)(2,1)S(1)}, bf16[10,24,1280]{2,1,0:T(8,128)(2,1)S(1)}, u32[]{:S(2)}, u32[]{:S(2)}) %collective-permute-start.3) | collective-permute-done | bytes 614432 | tf_op jit(solution)/shard_map/ppermute | solution.py:26
  18.0 0.0 copy-done
  18.0 0.0 copy-done.2
  18.0 0.0 copy-done.3
  18.1 4.5 %shard_map.56 = (bf16[464,128]{1,0:T(8,128)(2,1)S(1)}, bf16[464,128]{1,0:T(8,128)(2,1)S(1)}, bf16[464,128]{1,0:T(8,128)(2,1)S(1)}, bf16[464,128]{1,0:T(8,128)(2,...) custom-call(bf16[10,40,1280]{2,1,0:T(8,128)(2,1)S(1)} %bitcast.4, ...), custom_call_target="tpu_custom_call" | custom-call | flops 1179648000 | bytes 6144000 | tf_op jit(solution)/shard_map/pallas_call | solution.py:331
  22.5 0.0 collective-permute-done.2.refs_3_
  22.6 1.8 %collective-permute-start.6 = (bf16[464,128]{1,0:T(8,128)(2,1)S(1)}, bf16[464,128]{1,0:T(8,128)(2,1)S(1)}, u32[]{:S(2)}, u32[]{:S(2)}) collective-permute-start(bf16[464,128]{1,0:T(8,128)(2,1)S(1)} %get-tuple-element.47), channel_id=1, source_target_pairs={{0,1},{1,2},{2,3},{3,0},{4,5},{5,6},{6,7},{7,4},{8,9},{9,10},{10,1... | collective-permute-start | bytes 356360 | tf_op jit(solution)/shard_map/ppermute | solution.py:26
  24.4 0.0 collective-permute-done.1.refs_2_
  24.4 2.6 %collective-permute-start.5 = (bf16[464,128]{1,0:T(8,128)(2,1)S(1)}, bf16[464,128]{1,0:T(8,128)(2,1)S(1)}, u32[]{:S(2)}, u32[]{:S(2)}) collective-permute-start(bf16[464,128]{1,0:T(8,128)(2,1)S(1)} %get-tuple-element.45), channel_id=1, source_target_pairs={{0,2},{1,3},{2,0},{3,1},{4,6},{5,7},{6,4},{7,5},{8,10},{9,11},{10,... | collective-permute-start | bytes 356360 | tf_op jit(solution)/shard_map/ppermute | solution.py:26
  27.0 0.0 collective-permute-done.refs_1_
  27.0 1.3 %collective-permute-start.4 = (bf16[464,128]{1,0:T(8,128)(2,1)S(1)}, bf16[464,128]{1,0:T(8,128)(2,1)S(1)}, u32[]{:S(2)}, u32[]{:S(2)}) collective-permute-start(bf16[464,128]{1,0:T(8,128)(2,1)S(1)} %get-tuple-element.43), channel_id=1, source_target_pairs={{0,3},{1,0},{2,1},{3,2},{4,7},{5,4},{6,5},{7,6},{8,11},{9,8},{10,9... | collective-permute-start | bytes 356360 | tf_op jit(solution)/shard_map/ppermute | solution.py:26
  28.4 2.3 %collective-permute-done.6.refs_7_ = bf16[464,128]{1,0:T(8,128)(2,1)S(1)} collective-permute-done((bf16[464,128]{1,0:T(8,128)(2,1)S(1)}, bf16[464,128]{1,0:T(8,128)(2,1)S(1)}, u32[]{:S(2)}, u32[]{:S(2)}) %collective-permute-start.6) | collective-permute-done | bytes 118816 | tf_op jit(solution)/shard_map/ppermute | solution.py:26
  30.7 3.0 %collective-permute-start.10 = (bf16[464,128]{1,0:T(8,128)(2,1)S(1)}, bf16[464,128]{1,0:T(8,128)(2,1)S(1)}, u32[]{:S(2)}, u32[]{:S(2)}) collective-permute-start(bf16[464,128]{1,0:T(8,128)(2,1)S(1)} %get-tuple-element.56), channel_id=1, source_target_pairs={{0,1},{1,2},{2,3},{3,0},{4,5},{5,6},{6,7},{7,4},{8,9},{9,10},{10,1... | collective-permute-start | bytes 356360 | tf_op jit(solution)/shard_map/ppermute | solution.py:26
  33.6 1.7 %collective-permute-done.5.refs_6_ = bf16[464,128]{1,0:T(8,128)(2,1)S(1)} collective-permute-done((bf16[464,128]{1,0:T(8,128)(2,1)S(1)}, bf16[464,128]{1,0:T(8,128)(2,1)S(1)}, u32[]{:S(2)}, u32[]{:S(2)}) %collective-permute-start.5) | collective-permute-done | bytes 118816 | tf_op jit(solution)/shard_map/ppermute | solution.py:26
  35.3 0.7 %collective-permute-start.9 = (bf16[464,128]{1,0:T(8,128)(2,1)S(1)}, bf16[464,128]{1,0:T(8,128)(2,1)S(1)}, u32[]{:S(2)}, u32[]{:S(2)}) collective-permute-start(bf16[464,128]{1,0:T(8,128)(2,1)S(1)} %get-tuple-element.54), channel_id=1, source_target_pairs={{0,2},{1,3},{2,0},{3,1},{4,6},{5,7},{6,4},{7,5},{8,10},{9,11},{10,... | collective-permute-start | bytes 356360 | tf_op jit(solution)/shard_map/ppermute | solution.py:26
  36.1 0.0 collective-permute-done.4.refs_5_
  36.1 3.7 %collective-permute-start.8 = (bf16[464,128]{1,0:T(8,128)(2,1)S(1)}, bf16[464,128]{1,0:T(8,128)(2,1)S(1)}, u32[]{:S(2)}, u32[]{:S(2)}) collective-permute-start(bf16[464,128]{1,0:T(8,128)(2,1)S(1)} %get-tuple-element.52), channel_id=1, source_target_pairs={{0,3},{1,0},{2,1},{3,2},{4,7},{5,4},{6,5},{7,6},{8,11},{9,8},{10,9... | collective-permute-start | bytes 356360 | tf_op jit(solution)/shard_map/ppermute | solution.py:26
  39.8 0.0 copy-done.4
  39.8 4.0 %shard_map.57 = (bf16[416,128]{1,0:T(8,128)(2,1)S(1)}, bf16[608,128]{1,0:T(8,128)(2,1)S(1)}) custom-call(bf16[608,128]{1,0:T(8,128)(2,1)S(1)} %copy-done.4, bf16[608,128]{1,0:T(8,128)(2,1)S(1)} %collective-permute-done.refs_1_, bf16[608,128]{1,0:T(8,128)(2,1)S(1)} %collective-permute-done.1.refs_2_, bf16[608,128]{1,0:T(8,128)(2,1)S(1)} %collective-permute-done.2.refs_3_, ...), custom_call_target="tpu_custom_call" | custom-call | flops 2621440000 | bytes 1228800 | tf_op jit(solution)/shard_map/pallas_call | solution.py:382
  43.9 1.8 %collective-permute-start.7 = (bf16[608,128]{1,0:T(8,128)(2,1)S(1)}, bf16[608,128]{1,0:T(8,128)(2,1)S(1)}, u32[]{:S(2)}, u32[]{:S(2)}) collective-permute-start(bf16[608,128]{1,0:T(8,128)(2,1)S(1)} %get-tuple-element.48.mixed), channel_id=1, source_target_pairs={{0,16},{4,20},{8,24},{12,28},{16,0},{20,4},{24,8},{28,12},{1,17},{... | collective-permute-start | bytes 466952 | tf_op jit(solution)/shard_map/ppermute | solution.py:26
  45.7 0.0 collective-permute-done.10.refs_7_
  45.7 0.0 collective-permute-done.9.refs_6_
  45.7 0.1 collective-permute-done.8.refs_5_
  45.8 0.0 copy-start.1
  45.8 4.0 %shard_map.58 = (bf16[416,128]{1,0:T(8,128)(2,1)S(1)}, bf16[608,128]{1,0:T(8,128)(2,1)S(1)}) custom-call(bf16[608,128]{1,0:T(8,128)(2,1)S(1)} %copy-done.4, bf16[608,128]{1,0:T(8,128)(2,1)S(1)} %collective-permute-done.refs_1_, bf16[608,128]{1,0:T(8,128)(2,1)S(1)} %collective-permute-done.1.refs_2_, bf16[608,128]{1,0:T(8,128)(2,1)S(1)} %collective-permute-done.2.refs_3_, ...), custom_call_target="tpu_custom_call" | custom-call | flops 2621440000 | bytes 1228800 | tf_op jit(solution)/shard_map/pallas_call | solution.py:382
  49.8 1.3 %collective-permute-start.14 = (bf16[608,128]{1,0:T(8,128)(2,1)S(1)}, bf16[608,128]{1,0:T(8,128)(2,1)S(1)}, u32[]{:S(2)}, u32[]{:S(2)}) collective-permute-start(bf16[608,128]{1,0:T(8,128)(2,1)S(1)} %get-tuple-element.64.mixed), channel_id=1, source_target_pairs={{0,16},{4,20},{8,24},{12,28},{16,0},{20,4},{24,8},{28,12},{1,17},{... | collective-permute-start | bytes 466952 | tf_op jit(solution)/shard_map/ppermute | solution.py:26
  51.1 0.0 collective-permute-done.7.western
  51.1 0.6 shard_map.59
  51.7 2.0 %collective-permute-start.11 = (bf16[360,128]{1,0:T(8,128)(2,1)S(1)}, bf16[360,128]{1,0:T(8,128)(2,1)S(1)}, u32[]{:S(2)}, u32[]{:S(2)}) collective-permute-start(bf16[360,128]{1,0:T(8,128)(2,1)S(1)} %get-tuple-element.59), channel_id=1, source_target_pairs={{0,1},{1,2},{2,3},{3,0},{4,5},{5,6},{6,7},{7,4},{8,9},{9,10},{10,1... | collective-permute-start | bytes 276488 | tf_op jit(solution)/shard_map/ppermute | solution.py:26
  53.8 1.4 %collective-permute-start.12 = (bf16[360,128]{1,0:T(8,128)(2,1)S(1)}, bf16[360,128]{1,0:T(8,128)(2,1)S(1)}, u32[]{:S(2)}, u32[]{:S(2)}) collective-permute-start(bf16[360,128]{1,0:T(8,128)(2,1)S(1)} %get-tuple-element.60), channel_id=1, source_target_pairs={{0,2},{1,3},{2,0},{3,1},{4,6},{5,7},{6,4},{7,5},{8,10},{9,11},{10,... | collective-permute-start | bytes 276488 | tf_op jit(solution)/shard_map/ppermute | solution.py:26
  55.1 1.1 %collective-permute-start.13 = (bf16[360,128]{1,0:T(8,128)(2,1)S(1)}, bf16[360,128]{1,0:T(8,128)(2,1)S(1)}, u32[]{:S(2)}, u32[]{:S(2)}) collective-permute-start(bf16[360,128]{1,0:T(8,128)(2,1)S(1)} %get-tuple-element.61), channel_id=1, source_target_pairs={{0,3},{1,0},{2,1},{3,2},{4,7},{5,4},{6,5},{7,6},{8,11},{9,8},{10,9... | collective-permute-start | bytes 276488 | tf_op jit(solution)/shard_map/ppermute | solution.py:26
  56.2 0.0 collective-permute-done.14.western
  56.2 0.6 shard_map.61
  56.9 1.2 %collective-permute-start.15 = (bf16[152,128]{1,0:T(8,128)(2,1)S(1)}, bf16[152,128]{1,0:T(8,128)(2,1)S(1)}, u32[]{:S(2)}, u32[]{:S(2)}) collective-permute-start(bf16[152,128]{1,0:T(8,128)(2,1)S(1)} %get-tuple-element.66), channel_id=1, source_target_pairs={{0,1},{1,2},{2,3},{3,0},{4,5},{5,6},{6,7},{7,4},{8,9},{9,10},{10,1... | collective-permute-start | bytes 116744 | tf_op jit(solution)/shard_map/ppermute | solution.py:26
  58.1 1.7 %collective-permute-start.16 = (bf16[152,128]{1,0:T(8,128)(2,1)S(1)}, bf16[152,128]{1,0:T(8,128)(2,1)S(1)}, u32[]{:S(2)}, u32[]{:S(2)}) collective-permute-start(bf16[152,128]{1,0:T(8,128)(2,1)S(1)} %get-tuple-element.67), channel_id=1, source_target_pairs={{0,2},{1,3},{2,0},{3,1},{4,6},{5,7},{6,4},{7,5},{8,10},{9,11},{10,... | collective-permute-start | bytes 116744 | tf_op jit(solution)/shard_map/ppermute | solution.py:26
  59.8 0.0 collective-permute-done.11.refs_1_
  59.8 1.5 %collective-permute-start.17 = (bf16[152,128]{1,0:T(8,128)(2,1)S(1)}, bf16[152,128]{1,0:T(8,128)(2,1)S(1)}, u32[]{:S(2)}, u32[]{:S(2)}) collective-permute-start(bf16[152,128]{1,0:T(8,128)(2,1)S(1)} %get-tuple-element.68), channel_id=1, source_target_pairs={{0,3},{1,0},{2,1},{3,2},{4,7},{5,4},{6,5},{7,6},{8,11},{9,8},{10,9... | collective-permute-start | bytes 116744 | tf_op jit(solution)/shard_map/ppermute | solution.py:26
  61.2 2.1 %collective-permute-done.12.refs_2_ = bf16[360,128]{1,0:T(8,128)(2,1)S(1)} collective-permute-done((bf16[360,128]{1,0:T(8,128)(2,1)S(1)}, bf16[360,128]{1,0:T(8,128)(2,1)S(1)}, u32[]{:S(2)}, u32[]{:S(2)}) %collective-permute-start.12) | collective-permute-done | bytes 92192 | tf_op jit(solution)/shard_map/ppermute | solution.py:26
  63.4 0.0 collective-permute-done.13.refs_3_
  63.4 0.0 copy-done.1
  63.4 1.0 %shard_map.60 = (f32[10,40,1280]{2,1,0:T(8,128)S(1)}, bf16[512,1280]{1,0:T(8,128)(2,1)S(1)}) custom-call(bf16[10,40,1280]{2,1,0:T(8,128)(2,1)S(1)} %bitcast.5, bf16[640,1280]{1,0:T(8,128)(2,1)S(1)} %copy-done.1, bf16[360,128]{1,0:T(8,128)(2,1)S(1)} %get-tuple-element.58.refs_0_, bf16[360,128]{1,0:T(8,128)(2,1)S(1)} %collective-permute-done.11.refs_1_, ...), custom_call_target="tpu_custom_call" | custom-call | flops 524288000 | bytes 3891200 | tf_op jit(solution)/shard_map/pallas_call | solution.py:429
  64.4 0.0 collective-permute-done.15.refs_1_
  64.4 1.3 %collective-permute-done.16.refs_2_ = bf16[152,128]{1,0:T(8,128)(2,1)S(1)} collective-permute-done((bf16[152,128]{1,0:T(8,128)(2,1)S(1)}, bf16[152,128]{1,0:T(8,128)(2,1)S(1)}, u32[]{:S(2)}, u32[]{:S(2)}) %collective-permute-start.16) | collective-permute-done | bytes 38944 | tf_op jit(solution)/shard_map/ppermute | solution.py:26
  65.7 0.0 collective-permute-done.17.refs_3_
  65.7 1.5 %shard_map.62 = bf16[10,40,1280]{2,1,0:T(8,128)(2,1)} custom-call(f32[10,40,1280]{2,1,0:T(8,128)S(1)} %get-tuple-element.62.partial, bf16[512,1280]{1,0:T(8,128)(2,1)S(1)} %get-tuple-element.63.weight, bf16[152,128]{1,0:T(8,128)(2,1)S(1)} %get-tuple-element.65.refs_0_, bf16[152,128]{1,0:T(8,128)(2,1)S(1)} %collective-permute-done.15.refs_1_, ...), custom_call_target="tpu_custom_call" | custom-call | flops 524288000 | bytes 3891200 | tf_op jit(solution)/shard_map/pallas_call | solution.py:441
Async XLA Ops:
  1.1 16.9 %copy-start = (bf16[1,10,40,1280]{3,2,1,0:T(8,128)(2,1)S(1)}, bf16[1,10,40,1280]{3,2,1,0:T(8,128)(2,1)}, u32[]{:S(2)}) copy-start(bf16[1,10,40,1280]{3,2,1,0:T(8,128)(2,1)} %param.5) | copy-start | bytes 3072004
  1.1 16.9 %copy-start.2 = (f32[1280]{0:T(1024)S(1)}, f32[1280]{0:T(1024)}, u32[]{:S(2)}) copy-start(f32[1280]{0:T(1024)} %gain.3) | copy-start | bytes 15364
  1.1 16.9 %copy-start.3 = (s32[4]{0:T(128)S(1)}, s32[4]{0:T(128)}, u32[]{:S(2)}) copy-start(s32[4]{0:T(128)} %lon_shift.5) | copy-start | bytes 52
  1.2 16.9 %collective-permute-start.3 = (bf16[10,24,1280]{2,1,0:T(8,128)(2,1)S(1)}, bf16[10,24,1280]{2,1,0:T(8,128)(2,1)S(1)}, u32[]{:S(2)}, u32[]{:S(2)}) collective-permute-start(bf16[10,24,1280]{2,1,0:T(8,128)(2,1)S(1)} %slice.4), channel_id=1, source_target_pairs={{0,16},{4,20},{8,24},{12,28},{16,0},{20,4},{24,8},{28,12},{1,17},{... | collective-permute-start | bytes 1843208 | tf_op jit(solution)/shard_map/ppermute | solution.py:26
  8.8 13.8 %collective-permute-start.2 = (bf16[608,128]{1,0:T(8,128)(2,1)}, bf16[608,128]{1,0:T(8,128)(2,1)S(1)}, u32[]{:S(2)}, u32[]{:S(2)}) collective-permute-start(bf16[608,128]{1,0:T(8,128)(2,1)} %get-tuple-element.40), channel_id=1, source_target_pairs={{0,1},{1,2},{2,3},{3,0},{4,5},{5,6},{6,7},{7,4},{8,9},{9,10},{10,1... | collective-permute-start | bytes 466952 | tf_op jit(solution)/shard_map/ppermute | solution.py:26
  10.4 14.0 %collective-permute-start.1 = (bf16[608,128]{1,0:T(8,128)(2,1)}, bf16[608,128]{1,0:T(8,128)(2,1)S(1)}, u32[]{:S(2)}, u32[]{:S(2)}) collective-permute-start(bf16[608,128]{1,0:T(8,128)(2,1)} %get-tuple-element.39), channel_id=1, source_target_pairs={{0,2},{1,3},{2,0},{3,1},{4,6},{5,7},{6,4},{7,5},{8,10},{9,11},{10,... | collective-permute-start | bytes 466952 | tf_op jit(solution)/shard_map/ppermute | solution.py:26
  13.0 26.8 %copy-start.4 = (bf16[608,128]{1,0:T(8,128)(2,1)S(1)}, bf16[608,128]{1,0:T(8,128)(2,1)}, u32[]{:S(2)}) copy-start(bf16[608,128]{1,0:T(8,128)(2,1)} %get-tuple-element.37.refs_0_) | copy-start | bytes 466948
  13.0 14.0 %collective-permute-start = (bf16[608,128]{1,0:T(8,128)(2,1)}, bf16[608,128]{1,0:T(8,128)(2,1)S(1)}, u32[]{:S(2)}, u32[]{:S(2)}) collective-permute-start(bf16[608,128]{1,0:T(8,128)(2,1)} %get-tuple-element.38), channel_id=1, source_target_pairs={{0,3},{1,0},{2,1},{3,2},{4,7},{5,4},{6,5},{7,6},{8,11},{9,8},{10,9... | collective-permute-start | bytes 466952 | tf_op jit(solution)/shard_map/ppermute | solution.py:26
  22.6 8.1 %collective-permute-start.6 = (bf16[464,128]{1,0:T(8,128)(2,1)S(1)}, bf16[464,128]{1,0:T(8,128)(2,1)S(1)}, u32[]{:S(2)}, u32[]{:S(2)}) collective-permute-start(bf16[464,128]{1,0:T(8,128)(2,1)S(1)} %get-tuple-element.47), channel_id=1, source_target_pairs={{0,1},{1,2},{2,3},{3,0},{4,5},{5,6},{6,7},{7,4},{8,9},{9,10},{10,1... | collective-permute-start | bytes 356360 | tf_op jit(solution)/shard_map/ppermute | solution.py:26
  24.4 10.9 %collective-permute-start.5 = (bf16[464,128]{1,0:T(8,128)(2,1)S(1)}, bf16[464,128]{1,0:T(8,128)(2,1)S(1)}, u32[]{:S(2)}, u32[]{:S(2)}) collective-permute-start(bf16[464,128]{1,0:T(8,128)(2,1)S(1)} %get-tuple-element.45), channel_id=1, source_target_pairs={{0,2},{1,3},{2,0},{3,1},{4,6},{5,7},{6,4},{7,5},{8,10},{9,11},{10,... | collective-permute-start | bytes 356360 | tf_op jit(solution)/shard_map/ppermute | solution.py:26
  27.0 9.1 %collective-permute-start.4 = (bf16[464,128]{1,0:T(8,128)(2,1)S(1)}, bf16[464,128]{1,0:T(8,128)(2,1)S(1)}, u32[]{:S(2)}, u32[]{:S(2)}) collective-permute-start(bf16[464,128]{1,0:T(8,128)(2,1)S(1)} %get-tuple-element.43), channel_id=1, source_target_pairs={{0,3},{1,0},{2,1},{3,2},{4,7},{5,4},{6,5},{7,6},{8,11},{9,8},{10,9... | collective-permute-start | bytes 356360 | tf_op jit(solution)/shard_map/ppermute | solution.py:26
  30.7 15.0 %collective-permute-start.10 = (bf16[464,128]{1,0:T(8,128)(2,1)S(1)}, bf16[464,128]{1,0:T(8,128)(2,1)S(1)}, u32[]{:S(2)}, u32[]{:S(2)}) collective-permute-start(bf16[464,128]{1,0:T(8,128)(2,1)S(1)} %get-tuple-element.56), channel_id=1, source_target_pairs={{0,1},{1,2},{2,3},{3,0},{4,5},{5,6},{6,7},{7,4},{8,9},{9,10},{10,1... | collective-permute-start | bytes 356360 | tf_op jit(solution)/shard_map/ppermute | solution.py:26
  35.3 10.4 %collective-permute-start.9 = (bf16[464,128]{1,0:T(8,128)(2,1)S(1)}, bf16[464,128]{1,0:T(8,128)(2,1)S(1)}, u32[]{:S(2)}, u32[]{:S(2)}) collective-permute-start(bf16[464,128]{1,0:T(8,128)(2,1)S(1)} %get-tuple-element.54), channel_id=1, source_target_pairs={{0,2},{1,3},{2,0},{3,1},{4,6},{5,7},{6,4},{7,5},{8,10},{9,11},{10,... | collective-permute-start | bytes 356360 | tf_op jit(solution)/shard_map/ppermute | solution.py:26
  36.1 9.7 %collective-permute-start.8 = (bf16[464,128]{1,0:T(8,128)(2,1)S(1)}, bf16[464,128]{1,0:T(8,128)(2,1)S(1)}, u32[]{:S(2)}, u32[]{:S(2)}) collective-permute-start(bf16[464,128]{1,0:T(8,128)(2,1)S(1)} %get-tuple-element.52), channel_id=1, source_target_pairs={{0,3},{1,0},{2,1},{3,2},{4,7},{5,4},{6,5},{7,6},{8,11},{9,8},{10,9... | collective-permute-start | bytes 356360 | tf_op jit(solution)/shard_map/ppermute | solution.py:26
  43.9 7.3 %collective-permute-start.7 = (bf16[608,128]{1,0:T(8,128)(2,1)S(1)}, bf16[608,128]{1,0:T(8,128)(2,1)S(1)}, u32[]{:S(2)}, u32[]{:S(2)}) collective-permute-start(bf16[608,128]{1,0:T(8,128)(2,1)S(1)} %get-tuple-element.48.mixed), channel_id=1, source_target_pairs={{0,16},{4,20},{8,24},{12,28},{16,0},{20,4},{24,8},{28,12},{1,17},{... | collective-permute-start | bytes 466952 | tf_op jit(solution)/shard_map/ppermute | solution.py:26
  45.8 17.6 %copy-start.1 = (bf16[640,1280]{1,0:T(8,128)(2,1)S(1)}, bf16[640,1280]{1,0:T(8,128)(2,1)}, u32[]{:S(2)}) copy-start(bf16[640,1280]{1,0:T(8,128)(2,1)} %weight.5) | copy-start | bytes 4915204
  49.8 6.4 %collective-permute-start.14 = (bf16[608,128]{1,0:T(8,128)(2,1)S(1)}, bf16[608,128]{1,0:T(8,128)(2,1)S(1)}, u32[]{:S(2)}, u32[]{:S(2)}) collective-permute-start(bf16[608,128]{1,0:T(8,128)(2,1)S(1)} %get-tuple-element.64.mixed), channel_id=1, source_target_pairs={{0,16},{4,20},{8,24},{12,28},{16,0},{20,4},{24,8},{28,12},{1,17},{... | collective-permute-start | bytes 466952 | tf_op jit(solution)/shard_map/ppermute | solution.py:26
  51.7 8.0 %collective-permute-start.11 = (bf16[360,128]{1,0:T(8,128)(2,1)S(1)}, bf16[360,128]{1,0:T(8,128)(2,1)S(1)}, u32[]{:S(2)}, u32[]{:S(2)}) collective-permute-start(bf16[360,128]{1,0:T(8,128)(2,1)S(1)} %get-tuple-element.59), channel_id=1, source_target_pairs={{0,1},{1,2},{2,3},{3,0},{4,5},{5,6},{6,7},{7,4},{8,9},{9,10},{10,1... | collective-permute-start | bytes 276488 | tf_op jit(solution)/shard_map/ppermute | solution.py:26
  53.8 9.6 %collective-permute-start.12 = (bf16[360,128]{1,0:T(8,128)(2,1)S(1)}, bf16[360,128]{1,0:T(8,128)(2,1)S(1)}, u32[]{:S(2)}, u32[]{:S(2)}) collective-permute-start(bf16[360,128]{1,0:T(8,128)(2,1)S(1)} %get-tuple-element.60), channel_id=1, source_target_pairs={{0,2},{1,3},{2,0},{3,1},{4,6},{5,7},{6,4},{7,5},{8,10},{9,11},{10,... | collective-permute-start | bytes 276488 | tf_op jit(solution)/shard_map/ppermute | solution.py:26
  55.1 8.2 %collective-permute-start.13 = (bf16[360,128]{1,0:T(8,128)(2,1)S(1)}, bf16[360,128]{1,0:T(8,128)(2,1)S(1)}, u32[]{:S(2)}, u32[]{:S(2)}) collective-permute-start(bf16[360,128]{1,0:T(8,128)(2,1)S(1)} %get-tuple-element.61), channel_id=1, source_target_pairs={{0,3},{1,0},{2,1},{3,2},{4,7},{5,4},{6,5},{7,6},{8,11},{9,8},{10,9... | collective-permute-start | bytes 276488 | tf_op jit(solution)/shard_map/ppermute | solution.py:26
  56.9 7.6 %collective-permute-start.15 = (bf16[152,128]{1,0:T(8,128)(2,1)S(1)}, bf16[152,128]{1,0:T(8,128)(2,1)S(1)}, u32[]{:S(2)}, u32[]{:S(2)}) collective-permute-start(bf16[152,128]{1,0:T(8,128)(2,1)S(1)} %get-tuple-element.66), channel_id=1, source_target_pairs={{0,1},{1,2},{2,3},{3,0},{4,5},{5,6},{6,7},{7,4},{8,9},{9,10},{10,1... | collective-permute-start | bytes 116744 | tf_op jit(solution)/shard_map/ppermute | solution.py:26
  58.1 7.6 %collective-permute-start.16 = (bf16[152,128]{1,0:T(8,128)(2,1)S(1)}, bf16[152,128]{1,0:T(8,128)(2,1)S(1)}, u32[]{:S(2)}, u32[]{:S(2)}) collective-permute-start(bf16[152,128]{1,0:T(8,128)(2,1)S(1)} %get-tuple-element.67), channel_id=1, source_target_pairs={{0,2},{1,3},{2,0},{3,1},{4,6},{5,7},{6,4},{7,5},{8,10},{9,11},{10,... | collective-permute-start | bytes 116744 | tf_op jit(solution)/shard_map/ppermute | solution.py:26
  59.8 6.0 %collective-permute-start.17 = (bf16[152,128]{1,0:T(8,128)(2,1)S(1)}, bf16[152,128]{1,0:T(8,128)(2,1)S(1)}, u32[]{:S(2)}, u32[]{:S(2)}) collective-permute-start(bf16[152,128]{1,0:T(8,128)(2,1)S(1)} %get-tuple-element.68), channel_id=1, source_target_pairs={{0,3},{1,0},{2,1},{3,2},{4,7},{5,4},{6,5},{7,6},{8,11},{9,8},{10,9... | collective-permute-start | bytes 116744 | tf_op jit(solution)/shard_map/ppermute | solution.py:26

commit v16 on v15

--- a/solution.py
+++ b/solution.py
@@ -33,7 +33,7 @@
 def after(blocks, arrived):
     return [
         block if other is None else lax.optimization_barrier((block, other))[0]
-        for block, other in zip(blocks, arrived)
+        for block, other in zip(blocks, [*arrived, *[None] * len(blocks)])
     ]
 
 
@@ -401,7 +401,7 @@
             ),
         )(*blocks)
 
-    def back(mixed_values, *kept_values):
+    def back(arrived, mixed_values, *kept_values):
         western = shifted(mixed_values, "win", LAT_WINDOWS)
         selected = pl.pallas_call(
             functools.partial(select_kernel, split, mixed_count, groups),
@@ -413,12 +413,12 @@
                 flops=total * LANES * 20, bytes_accessed=8 * total * LANES, transcendentals=0
             ),
         )(lon_shift, mixed_values, western, *kept_values)
-        return spread(selected, -1)
+        return spread(after(selected, [None, *arrived]), -1)
 
     first_kept_values, first_mixed_values = attention(0, total // 5, *kept, *first_mixed)
     second_kept_values, second_mixed_values = attention(1, total // 5, *kept, *second_mixed)
-    first = back(first_mixed_values, first_kept_values, second_kept_values)
-    second = back(second_mixed_values)
+    first = back([], first_mixed_values, first_kept_values, second_kept_values)
+    second = back(first[1:], second_mixed_values)
 
     cost = pl.CostEstimate(
         flops=2 * rows * columns * groups * LANES * features,

time: 67.4 us -> 69.5 us (1.031)
  waiting for transfers between devices: 11.2 us -> 12.9 us
    ppermute x18, waiting for transfers between devices: 11.2 us -> 12.9 us  [shifted(): lax.ppermute(block, axis, [(i, (i + distance) % count) for i in range(cou...]
  transfers between devices with their start and end apart: 18 -> 18, of which waited for: 6 -> 7; matrix products, arithmetic and copies ran while one was open for 0% -> 0% of each run, Pallas kernels for 29% -> 28%
where the time goes in v16:
time: 69.5 us; the launch traced here: 69.3 us
  starting transfers between devices  34.2 us (49%)
  Pallas kernels  20.9 us (30%)
  waiting for transfers between devices  12.9 us (19%)
  local copies, waits for them, and re-layouts  1.14 us (2%)
    ppermute x18, starting transfers between devices, shifted(): lax.ppermute(block, axis, [(i, (i + distance) % count) for i in range(cou...  34.2 us
    ppermute x18, waiting for transfers between devices, shifted(): lax.ppermute(block, axis, [(i, (i + distance) % count) for i in range(cou...  12.9 us
    pallas_call x2, Pallas kernels, projection(): pl.pallas_call(functools.partial(kernel, split), out_shape=[block] * (par...  9.09 us
    pallas_call x2, Pallas kernels, attention(): pl.pallas_call(functools.partial(attention_kernel, head, groups, kept_cou...  8.08 us
    pallas_call x1, Pallas kernels, shards(): pl.pallas_call(functools.partial(second_output_kernel, split), out_shape=...  1.52 us
  transfers between devices with their start and end apart: 18, of which 7 were waited for; matrix products, arithmetic and copies ran while one was open for 0% of the time, Pallas kernels for 28%

profile of v16, /device:TPU:0, one launch (start us, length us, event | category | flops | bytes accessed | tf_op | source)
XLA Modules:
  0.0 69.3 jit_solution(12130093417403688803)
XLA Ops:
  0.0 1.1 %slice.4 = bf16[10,24,1280]{2,1,0:T(8,128)(2,1)S(1)} slice(bf16[10,40,1280]{2,1,0:T(8,128)(2,1)} %bitcast.2), slice={[0:10], [0:24], [0:1280]} | slice | bytes 1228800 | tf_op jit(solution)/shard_map/slice | solution.py:354
  1.1 0.0 copy-start
  1.1 0.0 copy-start.2
  1.1 0.0 copy-start.3
  1.2 3.0 %collective-permute-start.3 = (bf16[10,24,1280]{2,1,0:T(8,128)(2,1)S(1)}, bf16[10,24,1280]{2,1,0:T(8,128)(2,1)S(1)}, u32[]{:S(2)}, u32[]{:S(2)}) collective-permute-start(bf16[10,24,1280]{2,1,0:T(8,128)(2,1)S(1)} %slice.4), channel_id=1, source_target_pairs={{0,16},{4,20},{8,24},{12,28},{16,0},{20,4},{24,8},{28,12},{1,17},{... | collective-permute-start | bytes 1843208 | tf_op jit(solution)/shard_map/ppermute | solution.py:26
  4.2 4.6 %shard_map.55 = (bf16[608,128]{1,0:T(8,128)(2,1)}, bf16[608,128]{1,0:T(8,128)(2,1)}, bf16[608,128]{1,0:T(8,128)(2,1)}, bf16[608,128]{1,0:T(8,128)(2,1)}) custom-call(bf16[10,40,1280]{2,1,0:T(8,128)(2,1)} %bitcast.3, f32[1280]{0:T(1024)} %gain.3, bf16[1280,1920]{1,0:T(8,128)(2,1)} %weight.4), custom_call_target="tpu_custom_call" | custom-call | flops 786432000 | bytes 5734400 | tf_op jit(solution)/shard_map/pallas_call | solution.py:331
  8.8 1.6 %collective-permute-start.2 = (bf16[608,128]{1,0:T(8,128)(2,1)}, bf16[608,128]{1,0:T(8,128)(2,1)S(1)}, u32[]{:S(2)}, u32[]{:S(2)}) collective-permute-start(bf16[608,128]{1,0:T(8,128)(2,1)} %get-tuple-element.43), channel_id=1, source_target_pairs={{0,1},{1,2},{2,3},{3,0},{4,5},{5,6},{6,7},{7,4},{8,9},{9,10},{10,1... | collective-permute-start | bytes 466952 | tf_op jit(solution)/shard_map/ppermute | solution.py:26
  10.4 2.6 %collective-permute-start.1 = (bf16[608,128]{1,0:T(8,128)(2,1)}, bf16[608,128]{1,0:T(8,128)(2,1)S(1)}, u32[]{:S(2)}, u32[]{:S(2)}) collective-permute-start(bf16[608,128]{1,0:T(8,128)(2,1)} %get-tuple-element.42), channel_id=1, source_target_pairs={{0,2},{1,3},{2,0},{3,1},{4,6},{5,7},{6,4},{7,5},{8,10},{9,11},{10,... | collective-permute-start | bytes 466952 | tf_op jit(solution)/shard_map/ppermute | solution.py:26
  13.0 0.0 copy-start.4
  13.0 1.3 %collective-permute-start = (bf16[608,128]{1,0:T(8,128)(2,1)}, bf16[608,128]{1,0:T(8,128)(2,1)S(1)}, u32[]{:S(2)}, u32[]{:S(2)}) collective-permute-start(bf16[608,128]{1,0:T(8,128)(2,1)} %get-tuple-element.41), channel_id=1, source_target_pairs={{0,3},{1,0},{2,1},{3,2},{4,7},{5,4},{6,5},{7,6},{8,11},{9,8},{10,9... | collective-permute-start | bytes 466952 | tf_op jit(solution)/shard_map/ppermute | solution.py:26
  14.4 3.7 %collective-permute-done.3.eastern = bf16[10,24,1280]{2,1,0:T(8,128)(2,1)S(1)} collective-permute-done((bf16[10,24,1280]{2,1,0:T(8,128)(2,1)S(1)}, bf16[10,24,1280]{2,1,0:T(8,128)(2,1)S(1)}, u32[]{:S(2)}, u32[]{:S(2)}) %collective-permute-start.3) | collective-permute-done | bytes 614432 | tf_op jit(solution)/shard_map/ppermute | solution.py:26
  18.0 0.0 copy-done
  18.0 0.0 copy-done.2
  18.0 0.0 copy-done.3
  18.1 4.5 %shard_map.56 = (bf16[464,128]{1,0:T(8,128)(2,1)S(1)}, bf16[464,128]{1,0:T(8,128)(2,1)S(1)}, bf16[464,128]{1,0:T(8,128)(2,1)S(1)}, bf16[464,128]{1,0:T(8,128)(2,...) custom-call(bf16[10,40,1280]{2,1,0:T(8,128)(2,1)S(1)} %bitcast.4, ...), custom_call_target="tpu_custom_call" | custom-call | flops 1179648000 | bytes 6144000 | tf_op jit(solution)/shard_map/pallas_call | solution.py:331
  22.5 0.0 collective-permute-done.2.refs_3_
  22.6 1.8 %collective-permute-start.6 = (bf16[464,128]{1,0:T(8,128)(2,1)S(1)}, bf16[464,128]{1,0:T(8,128)(2,1)S(1)}, u32[]{:S(2)}, u32[]{:S(2)}) collective-permute-start(bf16[464,128]{1,0:T(8,128)(2,1)S(1)} %get-tuple-element.50), channel_id=1, source_target_pairs={{0,1},{1,2},{2,3},{3,0},{4,5},{5,6},{6,7},{7,4},{8,9},{9,10},{10,1... | collective-permute-start | bytes 356360 | tf_op jit(solution)/shard_map/ppermute | solution.py:26
  24.4 0.0 collective-permute-done.1.refs_2_
  24.4 2.6 %collective-permute-start.5 = (bf16[464,128]{1,0:T(8,128)(2,1)S(1)}, bf16[464,128]{1,0:T(8,128)(2,1)S(1)}, u32[]{:S(2)}, u32[]{:S(2)}) collective-permute-start(bf16[464,128]{1,0:T(8,128)(2,1)S(1)} %get-tuple-element.48), channel_id=1, source_target_pairs={{0,2},{1,3},{2,0},{3,1},{4,6},{5,7},{6,4},{7,5},{8,10},{9,11},{10,... | collective-permute-start | bytes 356360 | tf_op jit(solution)/shard_map/ppermute | solution.py:26
  27.0 0.0 collective-permute-done.refs_1_
  27.0 1.3 %collective-permute-start.4 = (bf16[464,128]{1,0:T(8,128)(2,1)S(1)}, bf16[464,128]{1,0:T(8,128)(2,1)S(1)}, u32[]{:S(2)}, u32[]{:S(2)}) collective-permute-start(bf16[464,128]{1,0:T(8,128)(2,1)S(1)} %get-tuple-element.46), channel_id=1, source_target_pairs={{0,3},{1,0},{2,1},{3,2},{4,7},{5,4},{6,5},{7,6},{8,11},{9,8},{10,9... | collective-permute-start | bytes 356360 | tf_op jit(solution)/shard_map/ppermute | solution.py:26
  28.4 2.3 %collective-permute-done.6.refs_7_ = bf16[464,128]{1,0:T(8,128)(2,1)S(1)} collective-permute-done((bf16[464,128]{1,0:T(8,128)(2,1)S(1)}, bf16[464,128]{1,0:T(8,128)(2,1)S(1)}, u32[]{:S(2)}, u32[]{:S(2)}) %collective-permute-start.6) | collective-permute-done | bytes 118816 | tf_op jit(solution)/shard_map/ppermute | solution.py:26
  30.7 3.0 %collective-permute-start.10 = (bf16[464,128]{1,0:T(8,128)(2,1)S(1)}, bf16[464,128]{1,0:T(8,128)(2,1)S(1)}, u32[]{:S(2)}, u32[]{:S(2)}) collective-permute-start(bf16[464,128]{1,0:T(8,128)(2,1)S(1)} %get-tuple-element.59), channel_id=1, source_target_pairs={{0,1},{1,2},{2,3},{3,0},{4,5},{5,6},{6,7},{7,4},{8,9},{9,10},{10,1... | collective-permute-start | bytes 356360 | tf_op jit(solution)/shard_map/ppermute | solution.py:26
  33.6 1.7 %collective-permute-done.5.refs_6_ = bf16[464,128]{1,0:T(8,128)(2,1)S(1)} collective-permute-done((bf16[464,128]{1,0:T(8,128)(2,1)S(1)}, bf16[464,128]{1,0:T(8,128)(2,1)S(1)}, u32[]{:S(2)}, u32[]{:S(2)}) %collective-permute-start.5) | collective-permute-done | bytes 118816 | tf_op jit(solution)/shard_map/ppermute | solution.py:26
  35.3 0.7 %collective-permute-start.9 = (bf16[464,128]{1,0:T(8,128)(2,1)S(1)}, bf16[464,128]{1,0:T(8,128)(2,1)S(1)}, u32[]{:S(2)}, u32[]{:S(2)}) collective-permute-start(bf16[464,128]{1,0:T(8,128)(2,1)S(1)} %get-tuple-element.57), channel_id=1, source_target_pairs={{0,2},{1,3},{2,0},{3,1},{4,6},{5,7},{6,4},{7,5},{8,10},{9,11},{10,... | collective-permute-start | bytes 356360 | tf_op jit(solution)/shard_map/ppermute | solution.py:26
  36.1 0.0 collective-permute-done.4.refs_5_
  36.1 3.7 %collective-permute-start.8 = (bf16[464,128]{1,0:T(8,128)(2,1)S(1)}, bf16[464,128]{1,0:T(8,128)(2,1)S(1)}, u32[]{:S(2)}, u32[]{:S(2)}) collective-permute-start(bf16[464,128]{1,0:T(8,128)(2,1)S(1)} %get-tuple-element.55), channel_id=1, source_target_pairs={{0,3},{1,0},{2,1},{3,2},{4,7},{5,4},{6,5},{7,6},{8,11},{9,8},{10,9... | collective-permute-start | bytes 356360 | tf_op jit(solution)/shard_map/ppermute | solution.py:26
  39.8 0.0 copy-done.4
  39.8 4.0 %shard_map.57 = (bf16[416,128]{1,0:T(8,128)(2,1)S(1)}, bf16[608,128]{1,0:T(8,128)(2,1)S(1)}) custom-call(bf16[608,128]{1,0:T(8,128)(2,1)S(1)} %copy-done.4, bf16[608,128]{1,0:T(8,128)(2,1)S(1)} %collective-permute-done.refs_1_, bf16[608,128]{1,0:T(8,128)(2,1)S(1)} %collective-permute-done.1.refs_2_, bf16[608,128]{1,0:T(8,128)(2,1)S(1)} %collective-permute-done.2.refs_3_, ...), custom_call_target="tpu_custom_call" | custom-call | flops 2621440000 | bytes 1228800 | tf_op jit(solution)/shard_map/pallas_call | solution.py:382
  43.9 1.8 %collective-permute-start.7 = (bf16[608,128]{1,0:T(8,128)(2,1)S(1)}, bf16[608,128]{1,0:T(8,128)(2,1)S(1)}, u32[]{:S(2)}, u32[]{:S(2)}) collective-permute-start(bf16[608,128]{1,0:T(8,128)(2,1)S(1)} %get-tuple-element.51.mixed), channel_id=1, source_target_pairs={{0,16},{4,20},{8,24},{12,28},{16,0},{20,4},{24,8},{28,12},{1,17},{... | collective-permute-start | bytes 466952 | tf_op jit(solution)/shard_map/ppermute | solution.py:26
  45.7 0.0 collective-permute-done.10.refs_7_
  45.7 0.0 collective-permute-done.9.refs_6_
  45.7 0.1 collective-permute-done.8.refs_5_
  45.8 0.0 copy-start.1
  45.8 4.0 %shard_map.58 = (bf16[416,128]{1,0:T(8,128)(2,1)S(1)}, bf16[608,128]{1,0:T(8,128)(2,1)S(1)}) custom-call(bf16[608,128]{1,0:T(8,128)(2,1)S(1)} %copy-done.4, bf16[608,128]{1,0:T(8,128)(2,1)S(1)} %collective-permute-done.refs_1_, bf16[608,128]{1,0:T(8,128)(2,1)S(1)} %collective-permute-done.1.refs_2_, bf16[608,128]{1,0:T(8,128)(2,1)S(1)} %collective-permute-done.2.refs_3_, ...), custom_call_target="tpu_custom_call" | custom-call | flops 2621440000 | bytes 1228800 | tf_op jit(solution)/shard_map/pallas_call | solution.py:382
  49.8 1.3 %collective-permute-start.14 = (bf16[608,128]{1,0:T(8,128)(2,1)S(1)}, bf16[608,128]{1,0:T(8,128)(2,1)S(1)}, u32[]{:S(2)}, u32[]{:S(2)}) collective-permute-start(bf16[608,128]{1,0:T(8,128)(2,1)S(1)} %get-tuple-element.67.mixed), channel_id=1, source_target_pairs={{0,16},{4,20},{8,24},{12,28},{16,0},{20,4},{24,8},{28,12},{1,17},{... | collective-permute-start | bytes 466952 | tf_op jit(solution)/shard_map/ppermute | solution.py:26
  51.1 0.0 collective-permute-done.7.western
  51.1 0.6 shard_map.59
  51.7 2.0 %collective-permute-start.11 = (bf16[360,128]{1,0:T(8,128)(2,1)S(1)}, bf16[360,128]{1,0:T(8,128)(2,1)S(1)}, u32[]{:S(2)}, u32[]{:S(2)}) collective-permute-start(bf16[360,128]{1,0:T(8,128)(2,1)S(1)} %get-tuple-element.62), channel_id=1, source_target_pairs={{0,1},{1,2},{2,3},{3,0},{4,5},{5,6},{6,7},{7,4},{8,9},{9,10},{10,1... | collective-permute-start | bytes 276488 | tf_op jit(solution)/shard_map/ppermute | solution.py:26
  53.8 1.4 %collective-permute-start.12 = (bf16[360,128]{1,0:T(8,128)(2,1)S(1)}, bf16[360,128]{1,0:T(8,128)(2,1)S(1)}, u32[]{:S(2)}, u32[]{:S(2)}) collective-permute-start(bf16[360,128]{1,0:T(8,128)(2,1)S(1)} %get-tuple-element.63), channel_id=1, source_target_pairs={{0,2},{1,3},{2,0},{3,1},{4,6},{5,7},{6,4},{7,5},{8,10},{9,11},{10,... | collective-permute-start | bytes 276488 | tf_op jit(solution)/shard_map/ppermute | solution.py:26
  55.1 1.1 %collective-permute-start.13 = (bf16[360,128]{1,0:T(8,128)(2,1)S(1)}, bf16[360,128]{1,0:T(8,128)(2,1)S(1)}, u32[]{:S(2)}, u32[]{:S(2)}) collective-permute-start(bf16[360,128]{1,0:T(8,128)(2,1)S(1)} %get-tuple-element.64), channel_id=1, source_target_pairs={{0,3},{1,0},{2,1},{3,2},{4,7},{5,4},{6,5},{7,6},{8,11},{9,8},{10,9... | collective-permute-start | bytes 276488 | tf_op jit(solution)/shard_map/ppermute | solution.py:26
  56.2 0.0 collective-permute-done.14.western
  56.2 0.6 shard_map.61
  56.9 2.2 %collective-permute-done.11.refs_1_ = bf16[360,128]{1,0:T(8,128)(2,1)S(1)} collective-permute-done((bf16[360,128]{1,0:T(8,128)(2,1)S(1)}, bf16[360,128]{1,0:T(8,128)(2,1)S(1)}, u32[]{:S(2)}, u32[]{:S(2)}) %collective-permute-start.11) | collective-permute-done | bytes 92192 | tf_op jit(solution)/shard_map/ppermute | solution.py:26
  59.0 0.8 %collective-permute-start.15 = (bf16[152,128]{1,0:T(8,128)(2,1)S(1)}, bf16[152,128]{1,0:T(8,128)(2,1)S(1)}, u32[]{:S(2)}, u32[]{:S(2)}) collective-permute-start(bf16[152,128]{1,0:T(8,128)(2,1)S(1)} %get-tuple-element.70), channel_id=1, source_target_pairs={{0,1},{1,2},{2,3},{3,0},{4,5},{5,6},{6,7},{7,4},{8,9},{9,10},{10,1... | collective-permute-start | bytes 116744 | tf_op jit(solution)/shard_map/ppermute | solution.py:26
  59.8 2.3 %collective-permute-done.12.refs_2_ = bf16[360,128]{1,0:T(8,128)(2,1)S(1)} collective-permute-done((bf16[360,128]{1,0:T(8,128)(2,1)S(1)}, bf16[360,128]{1,0:T(8,128)(2,1)S(1)}, u32[]{:S(2)}, u32[]{:S(2)}) %collective-permute-start.12) | collective-permute-done | bytes 92192 | tf_op jit(solution)/shard_map/ppermute | solution.py:26
  62.1 1.1 %collective-permute-start.16 = (bf16[152,128]{1,0:T(8,128)(2,1)S(1)}, bf16[152,128]{1,0:T(8,128)(2,1)S(1)}, u32[]{:S(2)}, u32[]{:S(2)}) collective-permute-start(bf16[152,128]{1,0:T(8,128)(2,1)S(1)} %get-tuple-element.72), channel_id=1, source_target_pairs={{0,2},{1,3},{2,0},{3,1},{4,6},{5,7},{6,4},{7,5},{8,10},{9,11},{10,... | collective-permute-start | bytes 116744 | tf_op jit(solution)/shard_map/ppermute | solution.py:26
  63.2 0.0 collective-permute-done.13.refs_3_
  63.2 2.9 %collective-permute-start.17 = (bf16[152,128]{1,0:T(8,128)(2,1)S(1)}, bf16[152,128]{1,0:T(8,128)(2,1)S(1)}, u32[]{:S(2)}, u32[]{:S(2)}) collective-permute-start(bf16[152,128]{1,0:T(8,128)(2,1)S(1)} %get-tuple-element.74), channel_id=1, source_target_pairs={{0,3},{1,0},{2,1},{3,2},{4,7},{5,4},{6,5},{7,6},{8,11},{9,8},{10,9... | collective-permute-start | bytes 116744 | tf_op jit(solution)/shard_map/ppermute | solution.py:26
  66.1 0.0 copy-done.1
  66.1 1.0 %shard_map.60 = (f32[10,40,1280]{2,1,0:T(8,128)S(1)}, bf16[512,1280]{1,0:T(8,128)(2,1)S(1)}) custom-call(bf16[10,40,1280]{2,1,0:T(8,128)(2,1)S(1)} %bitcast.5, bf16[640,1280]{1,0:T(8,128)(2,1)S(1)} %copy-done.1, bf16[360,128]{1,0:T(8,128)(2,1)S(1)} %get-tuple-element.61.refs_0_, bf16[360,128]{1,0:T(8,128)(2,1)S(1)} %collective-permute-done.11.refs_1_, ...), custom_call_target="tpu_custom_call" | custom-call | flops 524288000 | bytes 3891200 | tf_op jit(solution)/shard_map/pallas_call | solution.py:429
  67.2 0.0 collective-permute-done.15.refs_1_
  67.2 0.0 collective-permute-done.16.refs_2_
  67.2 0.6 collective-permute-done.17.refs_3_
  67.8 1.5 %shard_map.62 = bf16[10,40,1280]{2,1,0:T(8,128)(2,1)} custom-call(f32[10,40,1280]{2,1,0:T(8,128)S(1)} %get-tuple-element.65.partial, bf16[512,1280]{1,0:T(8,128)(2,1)S(1)} %get-tuple-element.66.weight, bf16[152,128]{1,0:T(8,128)(2,1)S(1)} %get-tuple-element.68.refs_0_, bf16[152,128]{1,0:T(8,128)(2,1)S(1)} %collective-permute-done.15.refs_1_, ...), custom_call_target="tpu_custom_call" | custom-call | flops 524288000 | bytes 3891200 | tf_op jit(solution)/shard_map/pallas_call | solution.py:441
Async XLA Ops:
  1.1 16.9 %copy-start = (bf16[1,10,40,1280]{3,2,1,0:T(8,128)(2,1)S(1)}, bf16[1,10,40,1280]{3,2,1,0:T(8,128)(2,1)}, u32[]{:S(2)}) copy-start(bf16[1,10,40,1280]{3,2,1,0:T(8,128)(2,1)} %param.5) | copy-start | bytes 3072004
  1.1 16.9 %copy-start.2 = (f32[1280]{0:T(1024)S(1)}, f32[1280]{0:T(1024)}, u32[]{:S(2)}) copy-start(f32[1280]{0:T(1024)} %gain.3) | copy-start | bytes 15364
  1.1 16.9 %copy-start.3 = (s32[4]{0:T(128)S(1)}, s32[4]{0:T(128)}, u32[]{:S(2)}) copy-start(s32[4]{0:T(128)} %lon_shift.5) | copy-start | bytes 52
  1.2 16.9 %collective-permute-start.3 = (bf16[10,24,1280]{2,1,0:T(8,128)(2,1)S(1)}, bf16[10,24,1280]{2,1,0:T(8,128)(2,1)S(1)}, u32[]{:S(2)}, u32[]{:S(2)}) collective-permute-start(bf16[10,24,1280]{2,1,0:T(8,128)(2,1)S(1)} %slice.4), channel_id=1, source_target_pairs={{0,16},{4,20},{8,24},{12,28},{16,0},{20,4},{24,8},{28,12},{1,17},{... | collective-permute-start | bytes 1843208 | tf_op jit(solution)/shard_map/ppermute | solution.py:26
  8.8 13.8 %collective-permute-start.2 = (bf16[608,128]{1,0:T(8,128)(2,1)}, bf16[608,128]{1,0:T(8,128)(2,1)S(1)}, u32[]{:S(2)}, u32[]{:S(2)}) collective-permute-start(bf16[608,128]{1,0:T(8,128)(2,1)} %get-tuple-element.43), channel_id=1, source_target_pairs={{0,1},{1,2},{2,3},{3,0},{4,5},{5,6},{6,7},{7,4},{8,9},{9,10},{10,1... | collective-permute-start | bytes 466952 | tf_op jit(solution)/shard_map/ppermute | solution.py:26
  10.4 14.0 %collective-permute-start.1 = (bf16[608,128]{1,0:T(8,128)(2,1)}, bf16[608,128]{1,0:T(8,128)(2,1)S(1)}, u32[]{:S(2)}, u32[]{:S(2)}) collective-permute-start(bf16[608,128]{1,0:T(8,128)(2,1)} %get-tuple-element.42), channel_id=1, source_target_pairs={{0,2},{1,3},{2,0},{3,1},{4,6},{5,7},{6,4},{7,5},{8,10},{9,11},{10,... | collective-permute-start | bytes 466952 | tf_op jit(solution)/shard_map/ppermute | solution.py:26
  13.0 26.8 %copy-start.4 = (bf16[608,128]{1,0:T(8,128)(2,1)S(1)}, bf16[608,128]{1,0:T(8,128)(2,1)}, u32[]{:S(2)}) copy-start(bf16[608,128]{1,0:T(8,128)(2,1)} %get-tuple-element.40.refs_0_) | copy-start | bytes 466948
  13.0 14.0 %collective-permute-start = (bf16[608,128]{1,0:T(8,128)(2,1)}, bf16[608,128]{1,0:T(8,128)(2,1)S(1)}, u32[]{:S(2)}, u32[]{:S(2)}) collective-permute-start(bf16[608,128]{1,0:T(8,128)(2,1)} %get-tuple-element.41), channel_id=1, source_target_pairs={{0,3},{1,0},{2,1},{3,2},{4,7},{5,4},{6,5},{7,6},{8,11},{9,8},{10,9... | collective-permute-start | bytes 466952 | tf_op jit(solution)/shard_map/ppermute | solution.py:26
  22.6 8.1 %collective-permute-start.6 = (bf16[464,128]{1,0:T(8,128)(2,1)S(1)}, bf16[464,128]{1,0:T(8,128)(2,1)S(1)}, u32[]{:S(2)}, u32[]{:S(2)}) collective-permute-start(bf16[464,128]{1,0:T(8,128)(2,1)S(1)} %get-tuple-element.50), channel_id=1, source_target_pairs={{0,1},{1,2},{2,3},{3,0},{4,5},{5,6},{6,7},{7,4},{8,9},{9,10},{10,1... | collective-permute-start | bytes 356360 | tf_op jit(solution)/shard_map/ppermute | solution.py:26
  24.4 10.9 %collective-permute-start.5 = (bf16[464,128]{1,0:T(8,128)(2,1)S(1)}, bf16[464,128]{1,0:T(8,128)(2,1)S(1)}, u32[]{:S(2)}, u32[]{:S(2)}) collective-permute-start(bf16[464,128]{1,0:T(8,128)(2,1)S(1)} %get-tuple-element.48), channel_id=1, source_target_pairs={{0,2},{1,3},{2,0},{3,1},{4,6},{5,7},{6,4},{7,5},{8,10},{9,11},{10,... | collective-permute-start | bytes 356360 | tf_op jit(solution)/shard_map/ppermute | solution.py:26
  27.0 9.1 %collective-permute-start.4 = (bf16[464,128]{1,0:T(8,128)(2,1)S(1)}, bf16[464,128]{1,0:T(8,128)(2,1)S(1)}, u32[]{:S(2)}, u32[]{:S(2)}) collective-permute-start(bf16[464,128]{1,0:T(8,128)(2,1)S(1)} %get-tuple-element.46), channel_id=1, source_target_pairs={{0,3},{1,0},{2,1},{3,2},{4,7},{5,4},{6,5},{7,6},{8,11},{9,8},{10,9... | collective-permute-start | bytes 356360 | tf_op jit(solution)/shard_map/ppermute | solution.py:26
  30.7 15.0 %collective-permute-start.10 = (bf16[464,128]{1,0:T(8,128)(2,1)S(1)}, bf16[464,128]{1,0:T(8,128)(2,1)S(1)}, u32[]{:S(2)}, u32[]{:S(2)}) collective-permute-start(bf16[464,128]{1,0:T(8,128)(2,1)S(1)} %get-tuple-element.59), channel_id=1, source_target_pairs={{0,1},{1,2},{2,3},{3,0},{4,5},{5,6},{6,7},{7,4},{8,9},{9,10},{10,1... | collective-permute-start | bytes 356360 | tf_op jit(solution)/shard_map/ppermute | solution.py:26
  35.3 10.4 %collective-permute-start.9 = (bf16[464,128]{1,0:T(8,128)(2,1)S(1)}, bf16[464,128]{1,0:T(8,128)(2,1)S(1)}, u32[]{:S(2)}, u32[]{:S(2)}) collective-permute-start(bf16[464,128]{1,0:T(8,128)(2,1)S(1)} %get-tuple-element.57), channel_id=1, source_target_pairs={{0,2},{1,3},{2,0},{3,1},{4,6},{5,7},{6,4},{7,5},{8,10},{9,11},{10,... | collective-permute-start | bytes 356360 | tf_op jit(solution)/shard_map/ppermute | solution.py:26
  36.1 9.7 %collective-permute-start.8 = (bf16[464,128]{1,0:T(8,128)(2,1)S(1)}, bf16[464,128]{1,0:T(8,128)(2,1)S(1)}, u32[]{:S(2)}, u32[]{:S(2)}) collective-permute-start(bf16[464,128]{1,0:T(8,128)(2,1)S(1)} %get-tuple-element.55), channel_id=1, source_target_pairs={{0,3},{1,0},{2,1},{3,2},{4,7},{5,4},{6,5},{7,6},{8,11},{9,8},{10,9... | collective-permute-start | bytes 356360 | tf_op jit(solution)/shard_map/ppermute | solution.py:26
  43.9 7.3 %collective-permute-start.7 = (bf16[608,128]{1,0:T(8,128)(2,1)S(1)}, bf16[608,128]{1,0:T(8,128)(2,1)S(1)}, u32[]{:S(2)}, u32[]{:S(2)}) collective-permute-start(bf16[608,128]{1,0:T(8,128)(2,1)S(1)} %get-tuple-element.51.mixed), channel_id=1, source_target_pairs={{0,16},{4,20},{8,24},{12,28},{16,0},{20,4},{24,8},{28,12},{1,17},{... | collective-permute-start | bytes 466952 | tf_op jit(solution)/shard_map/ppermute | solution.py:26
  45.8 20.4 %copy-start.1 = (bf16[640,1280]{1,0:T(8,128)(2,1)S(1)}, bf16[640,1280]{1,0:T(8,128)(2,1)}, u32[]{:S(2)}) copy-start(bf16[640,1280]{1,0:T(8,128)(2,1)} %weight.5) | copy-start | bytes 4915204
  49.8 6.4 %collective-permute-start.14 = (bf16[608,128]{1,0:T(8,128)(2,1)S(1)}, bf16[608,128]{1,0:T(8,128)(2,1)S(1)}, u32[]{:S(2)}, u32[]{:S(2)}) collective-permute-start(bf16[608,128]{1,0:T(8,128)(2,1)S(1)} %get-tuple-element.67.mixed), channel_id=1, source_target_pairs={{0,16},{4,20},{8,24},{12,28},{16,0},{20,4},{24,8},{28,12},{1,17},{... | collective-permute-start | bytes 466952 | tf_op jit(solution)/shard_map/ppermute | solution.py:26
  51.7 7.3 %collective-permute-start.11 = (bf16[360,128]{1,0:T(8,128)(2,1)S(1)}, bf16[360,128]{1,0:T(8,128)(2,1)S(1)}, u32[]{:S(2)}, u32[]{:S(2)}) collective-permute-start(bf16[360,128]{1,0:T(8,128)(2,1)S(1)} %get-tuple-element.62), channel_id=1, source_target_pairs={{0,1},{1,2},{2,3},{3,0},{4,5},{5,6},{6,7},{7,4},{8,9},{9,10},{10,1... | collective-permute-start | bytes 276488 | tf_op jit(solution)/shard_map/ppermute | solution.py:26
  53.8 8.4 %collective-permute-start.12 = (bf16[360,128]{1,0:T(8,128)(2,1)S(1)}, bf16[360,128]{1,0:T(8,128)(2,1)S(1)}, u32[]{:S(2)}, u32[]{:S(2)}) collective-permute-start(bf16[360,128]{1,0:T(8,128)(2,1)S(1)} %get-tuple-element.63), channel_id=1, source_target_pairs={{0,2},{1,3},{2,0},{3,1},{4,6},{5,7},{6,4},{7,5},{8,10},{9,11},{10,... | collective-permute-start | bytes 276488 | tf_op jit(solution)/shard_map/ppermute | solution.py:26
  55.1 8.1 %collective-permute-start.13 = (bf16[360,128]{1,0:T(8,128)(2,1)S(1)}, bf16[360,128]{1,0:T(8,128)(2,1)S(1)}, u32[]{:S(2)}, u32[]{:S(2)}) collective-permute-start(bf16[360,128]{1,0:T(8,128)(2,1)S(1)} %get-tuple-element.64), channel_id=1, source_target_pairs={{0,3},{1,0},{2,1},{3,2},{4,7},{5,4},{6,5},{7,6},{8,11},{9,8},{10,9... | collective-permute-start | bytes 276488 | tf_op jit(solution)/shard_map/ppermute | solution.py:26
  59.0 8.2 %collective-permute-start.15 = (bf16[152,128]{1,0:T(8,128)(2,1)S(1)}, bf16[152,128]{1,0:T(8,128)(2,1)S(1)}, u32[]{:S(2)}, u32[]{:S(2)}) collective-permute-start(bf16[152,128]{1,0:T(8,128)(2,1)S(1)} %get-tuple-element.70), channel_id=1, source_target_pairs={{0,1},{1,2},{2,3},{3,0},{4,5},{5,6},{6,7},{7,4},{8,9},{9,10},{10,1... | collective-permute-start | bytes 116744 | tf_op jit(solution)/shard_map/ppermute | solution.py:26
  62.1 5.1 %collective-permute-start.16 = (bf16[152,128]{1,0:T(8,128)(2,1)S(1)}, bf16[152,128]{1,0:T(8,128)(2,1)S(1)}, u32[]{:S(2)}, u32[]{:S(2)}) collective-permute-start(bf16[152,128]{1,0:T(8,128)(2,1)S(1)} %get-tuple-element.72), channel_id=1, source_target_pairs={{0,2},{1,3},{2,0},{3,1},{4,6},{5,7},{6,4},{7,5},{8,10},{9,11},{10,... | collective-permute-start | bytes 116744 | tf_op jit(solution)/shard_map/ppermute | solution.py:26
  63.2 4.6 %collective-permute-start.17 = (bf16[152,128]{1,0:T(8,128)(2,1)S(1)}, bf16[152,128]{1,0:T(8,128)(2,1)S(1)}, u32[]{:S(2)}, u32[]{:S(2)}) collective-permute-start(bf16[152,128]{1,0:T(8,128)(2,1)S(1)} %get-tuple-element.74), channel_id=1, source_target_pairs={{0,3},{1,0},{2,1},{3,2},{4,7},{5,4},{6,5},{7,6},{8,11},{9,8},{10,9... | collective-permute-start | bytes 116744 | tf_op jit(solution)/shard_map/ppermute | solution.py:26

commit v17 on v15

--- a/solution.py
+++ b/solution.py
@@ -237,31 +237,39 @@
 
 def attention_kernel(head, groups, kept_count, mixed_count, *refs):
     kept, mixed = refs[:groups], refs[groups : 2 * groups]
-    kept_out, mixed_out, held, keys, attended, *rest = refs[2 * groups :]
+    *others, held, keys, attended, s0, s1, w0, w1 = refs[2 * groups :]
     gather(head, kept, kept_count, mixed, mixed_count, held, keys)
-    attend(held, keys, attended, rest[:2], rest[2:])
-    start = 0
-    for count, out in ((kept_count, kept_out), (mixed_count, mixed_out)):
-        packed = []
-        for _ in range(groups):
-            packed.append(pack(attended[start : start + count]))
-            start += count
-        out[...] = jnp.concatenate(packed, axis=0).astype(jnp.bfloat16)
-
-
-def select_kernel(split, count, groups, lon_shift, mixed, western, *refs):
-    kept, outs = refs[:-groups], refs[-groups:]
+    attend(held, keys, attended, (s0, s1), (w0, w1))
+
+    def packed(start, count):
+        return [pack(attended[start + at * count : start + (at + 1) * count]) for at in range(groups)]
+
+    right, left = packed(0, kept_count), packed(groups * kept_count, mixed_count)
+    if head == 0:
+        mixed_out, kept_out = others
+        kept_out[...] = jnp.concatenate(right, axis=0).astype(jnp.bfloat16)
+    else:
+        first, mixed_out, *outs = others
+        first = first[...].astype(jnp.float32)
+        size = packed_rows(kept_count)[0]
+        for group, out in enumerate(outs):
+            both = [first[group * size : (group + 1) * size], right[group]]
+            out[...] = jnp.concatenate(both, axis=0).astype(jnp.bfloat16)
+    mixed_out[...] = jnp.concatenate(left, axis=0).astype(jnp.bfloat16)
+
+
+def select_kernel(split, count, groups, lon_shift, *refs):
+    pairs, outs = refs[:-groups], refs[-groups:]
     taken = lax.rem(packed_tokens(count), split) < column_offset(lon_shift)
-    own, west = mixed[...].astype(jnp.float32), western[...].astype(jnp.float32)
-    rests = [rest[...].astype(jnp.float32) for rest in kept]
-    size = own.shape[0] // groups
+    values = [ref[...].astype(jnp.float32) for ref in pairs]
+    size = values[0].shape[0] // groups
     for group, out in enumerate(outs):
         rows = slice(group * size, (group + 1) * size)
-        pieces = [jnp.where(taken, west[rows], own[rows])]
-        for rest in rests:
-            part = rest.shape[0] // groups
-            pieces.append(rest[group * part : (group + 1) * part])
-        out[...] = jnp.concatenate(pieces, axis=0).astype(jnp.bfloat16)
+        chosen = [
+            jnp.where(taken, west[rows], own[rows])
+            for own, west in zip(values[::2], values[1::2])
+        ]
+        out[...] = jnp.concatenate(chosen, axis=0).astype(jnp.bfloat16)
 
 
 def projected(blocks, first, count, weight, shape):
@@ -272,7 +280,7 @@
 
 
 def first_output_kernel(split, groups, field, weight, *refs):
-    *blocks, out, second, first = refs
+    *blocks, out, first, second = refs
     features = field.shape[2]
     for slot, distance in enumerate(travel_order(groups)):
         group = lax.rem(lax.axis_index("tok") + distance, groups)
@@ -283,28 +291,24 @@
                 (LANES - HD, features), jnp.bfloat16
             )
     rows, columns, _ = field.shape
-    kept_count, mixed_count = rows * (columns - split), rows * split
+    kept_count = rows * (columns - split)
     blocks = [block[...].astype(jnp.float32) for block in blocks]
     tokens = field[...].astype(jnp.float32)
-    at = packed_rows(mixed_count)[0]
-    shape = (rows, split, features)
-    left = tokens[:, :split] + projected(blocks, 0, mixed_count, first, shape)
     shape = (rows, columns - split, features)
-    right = tokens[:, split:] + projected(blocks, at, kept_count, first, shape)
-    at += packed_rows(kept_count)[0]
-    right += projected(blocks, at, kept_count, second, shape)
-    out[...] = jnp.concatenate([left, right], axis=1)
-
-
-def second_output_kernel(split, partial, weight, *refs):
+    right = tokens[:, split:] + projected(blocks, 0, kept_count, first, shape)
+    right += projected(blocks, packed_rows(kept_count)[0], kept_count, second, shape)
+    out[...] = jnp.concatenate([tokens[:, :split], right], axis=1)
+
+
+def second_output_kernel(split, partial, first, second, *refs):
     *blocks, out = refs
     rows, _, features = partial.shape
     blocks = [block[...].astype(jnp.float32) for block in blocks]
     tokens = partial[...]
-    left = projected(blocks, 0, rows * split, weight, (rows, split, features))
-    out[...] = jnp.concatenate(
-        [tokens[:, :split] + left, tokens[:, split:]], axis=1
-    ).astype(jnp.bfloat16)
+    count, shape = rows * split, (rows, split, features)
+    left = tokens[:, :split] + projected(blocks, 0, count, first, shape)
+    left += projected(blocks, packed_rows(count)[0], count, second, shape)
+    out[...] = jnp.concatenate([left, tokens[:, split:]], axis=1).astype(jnp.bfloat16)
 
 
 def whole(count):
@@ -378,12 +382,13 @@
     def block(count):
         return jax.ShapeDtypeStruct((count, LANES), jnp.bfloat16)
 
-    def attention(head, step, *blocks):
+    def attention(head, out_shape, *blocks):
+        step = total // 5
         return pl.pallas_call(
             functools.partial(attention_kernel, head, groups, kept_count, mixed_count),
-            out_shape=[block(groups * kept_packed), block(groups * mixed_packed)],
+            out_shape=out_shape,
             in_specs=whole(len(blocks)),
-            out_specs=whole(2),
+            out_specs=whole(len(out_shape)),
             scratch_shapes=[
                 pltpu.VMEM((total, span), jnp.bfloat16),
                 pltpu.VMEM((LANES, total), jnp.bfloat16),
@@ -401,24 +406,27 @@
             ),
         )(*blocks)
 
-    def back(mixed_values, *kept_values):
-        western = shifted(mixed_values, "win", LAT_WINDOWS)
-        selected = pl.pallas_call(
-            functools.partial(select_kernel, split, mixed_count, groups),
-            out_shape=[block(mixed_packed + len(kept_values) * kept_packed)] * groups,
-            in_specs=[smem] + whole(2 + len(kept_values)),
-            out_specs=whole(groups),
-            compiler_params=limit(16),
-            cost_estimate=pl.CostEstimate(
-                flops=total * LANES * 20, bytes_accessed=8 * total * LANES, transcendentals=0
-            ),
-        )(lon_shift, mixed_values, western, *kept_values)
-        return spread(selected, -1)
-
-    first_kept_values, first_mixed_values = attention(0, total // 5, *kept, *first_mixed)
-    second_kept_values, second_mixed_values = attention(1, total // 5, *kept, *second_mixed)
-    first = back(first_mixed_values, first_kept_values, second_kept_values)
-    second = back(second_mixed_values)
+    values = block(groups * mixed_packed)
+    first_values, kept_values = attention(
+        0, [values, block(groups * kept_packed)], *kept, *first_mixed
+    )
+    first_western = shifted(first_values, "win", LAT_WINDOWS)
+    second_values, *kept_values = attention(
+        1, [values] + [block(2 * kept_packed)] * groups, *kept, *second_mixed, kept_values
+    )
+    second_western = shifted(second_values, "win", LAT_WINDOWS)
+    first = spread(kept_values, -1)
+    selected = pl.pallas_call(
+        functools.partial(select_kernel, split, mixed_count, groups),
+        out_shape=[block(2 * mixed_packed)] * groups,
+        in_specs=[smem] + whole(4),
+        out_specs=whole(groups),
+        compiler_params=limit(16),
+        cost_estimate=pl.CostEstimate(
+            flops=total * LANES * 20, bytes_accessed=8 * total * LANES, transcendentals=0
+        ),
+    )(lon_shift, first_values, first_western, second_values, second_western)
+    second = spread(selected, -1)
 
     cost = pl.CostEstimate(
         flops=2 * rows * columns * groups * LANES * features,
@@ -426,26 +434,26 @@
         transcendentals=0,
     )
     ordered = (groups * LANES, features)
-    partial, weight = pl.pallas_call(
+    partial, *weights = pl.pallas_call(
         functools.partial(first_output_kernel, split, groups),
         out_shape=[
             jax.ShapeDtypeStruct(field.shape, jnp.float32),
             jax.ShapeDtypeStruct(ordered, jnp.bfloat16),
+            jax.ShapeDtypeStruct(ordered, jnp.bfloat16),
         ],
         in_specs=whole(2 + groups),
-        out_specs=whole(2),
-        scratch_shapes=[pltpu.VMEM(ordered, jnp.bfloat16)],
+        out_specs=whole(3),
         compiler_params=limit(24),
         cost_estimate=cost,
     )(field, out_weight, *first)
     result = pl.pallas_call(
         functools.partial(second_output_kernel, split),
         out_shape=jax.ShapeDtypeStruct(field.shape, jnp.bfloat16),
-        in_specs=whole(2 + groups),
+        in_specs=whole(3 + groups),
         out_specs=pl.BlockSpec(memory_space=pltpu.VMEM),
         compiler_params=limit(24),
         cost_estimate=cost,
-    )(partial, weight, *second)
+    )(partial, *weights, *second)
     return result[None]
 
 

time: 67.4 us -> 67.6 us (level)
  transfers between devices with their start and end apart: 18 -> 18, of which waited for: 6 -> 7; matrix products, arithmetic and copies ran while one was open for 0% -> 0% of each run, Pallas kernels for 29% -> 28%
where the time goes in v17:
time: 67.6 us; the launch traced here: 67.4 us
  starting transfers between devices  34.1 us (50%)
  Pallas kernels  20.5 us (30%)
  waiting for transfers between devices  11.6 us (17%)
  local copies, waits for them, and re-layouts  1.14 us (2%)
    ppermute x18, starting transfers between devices, shifted(): lax.ppermute(block, axis, [(i, (i + distance) % count) for i in range(cou...  34.1 us
    ppermute x18, waiting for transfers between devices, shifted(): lax.ppermute(block, axis, [(i, (i + distance) % count) for i in range(cou...  11.6 us
    pallas_call x2, Pallas kernels, projection(): pl.pallas_call(functools.partial(kernel, split), out_shape=[block] * (par...  9.09 us
    pallas_call x2, Pallas kernels, attention(): pl.pallas_call(functools.partial(attention_kernel, head, groups, kept_cou...  8.08 us
    pallas_call x1, Pallas kernels, shards(): pl.pallas_call(functools.partial(second_output_kernel, split), out_shape=...  1.84 us
  transfers between devices with their start and end apart: 18, of which 7 were waited for; matrix products, arithmetic and copies ran while one was open for 0% of the time, Pallas kernels for 28%

profile of v17, /device:TPU:0, one launch (start us, length us, event | category | flops | bytes accessed | tf_op | source)
XLA Modules:
  0.0 67.4 jit_solution(12178095783241480362)
XLA Ops:
  0.0 1.1 %slice.4 = bf16[10,24,1280]{2,1,0:T(8,128)(2,1)S(1)} slice(bf16[10,40,1280]{2,1,0:T(8,128)(2,1)} %bitcast.2), slice={[0:10], [0:24], [0:1280]} | slice | bytes 1228800 | tf_op jit(solution)/shard_map/slice | solution.py:358
  1.1 0.0 copy-start
  1.1 0.0 copy-start.2
  1.1 0.0 copy-start.3
  1.2 3.0 %collective-permute-start.3 = (bf16[10,24,1280]{2,1,0:T(8,128)(2,1)S(1)}, bf16[10,24,1280]{2,1,0:T(8,128)(2,1)S(1)}, u32[]{:S(2)}, u32[]{:S(2)}) collective-permute-start(bf16[10,24,1280]{2,1,0:T(8,128)(2,1)S(1)} %slice.4), channel_id=1, source_target_pairs={{0,16},{4,20},{8,24},{12,28},{16,0},{20,4},{24,8},{28,12},{1,17},{... | collective-permute-start | bytes 1843208 | tf_op jit(solution)/shard_map/ppermute | solution.py:26
  4.2 4.6 %shard_map.55 = (bf16[608,128]{1,0:T(8,128)(2,1)}, bf16[608,128]{1,0:T(8,128)(2,1)}, bf16[608,128]{1,0:T(8,128)(2,1)}, bf16[608,128]{1,0:T(8,128)(2,1)}) custom-call(bf16[10,40,1280]{2,1,0:T(8,128)(2,1)} %bitcast.3, f32[1280]{0:T(1024)} %gain.3, bf16[1280,1920]{1,0:T(8,128)(2,1)} %weight.4), custom_call_target="tpu_custom_call" | custom-call | flops 786432000 | bytes 5734400 | tf_op jit(solution)/shard_map/pallas_call | solution.py:335
  8.8 1.6 %collective-permute-start.2 = (bf16[608,128]{1,0:T(8,128)(2,1)}, bf16[608,128]{1,0:T(8,128)(2,1)S(1)}, u32[]{:S(2)}, u32[]{:S(2)}) collective-permute-start(bf16[608,128]{1,0:T(8,128)(2,1)} %get-tuple-element.40), channel_id=1, source_target_pairs={{0,1},{1,2},{2,3},{3,0},{4,5},{5,6},{6,7},{7,4},{8,9},{9,10},{10,1... | collective-permute-start | bytes 466952 | tf_op jit(solution)/shard_map/ppermute | solution.py:26
  10.4 2.6 %collective-permute-start.1 = (bf16[608,128]{1,0:T(8,128)(2,1)}, bf16[608,128]{1,0:T(8,128)(2,1)S(1)}, u32[]{:S(2)}, u32[]{:S(2)}) collective-permute-start(bf16[608,128]{1,0:T(8,128)(2,1)} %get-tuple-element.39), channel_id=1, source_target_pairs={{0,2},{1,3},{2,0},{3,1},{4,6},{5,7},{6,4},{7,5},{8,10},{9,11},{10,... | collective-permute-start | bytes 466952 | tf_op jit(solution)/shard_map/ppermute | solution.py:26
  13.0 0.0 copy-start.4
  13.0 1.3 %collective-permute-start = (bf16[608,128]{1,0:T(8,128)(2,1)}, bf16[608,128]{1,0:T(8,128)(2,1)S(1)}, u32[]{:S(2)}, u32[]{:S(2)}) collective-permute-start(bf16[608,128]{1,0:T(8,128)(2,1)} %get-tuple-element.38), channel_id=1, source_target_pairs={{0,3},{1,0},{2,1},{3,2},{4,7},{5,4},{6,5},{7,6},{8,11},{9,8},{10,9... | collective-permute-start | bytes 466952 | tf_op jit(solution)/shard_map/ppermute | solution.py:26
  14.4 3.7 %collective-permute-done.3.eastern = bf16[10,24,1280]{2,1,0:T(8,128)(2,1)S(1)} collective-permute-done((bf16[10,24,1280]{2,1,0:T(8,128)(2,1)S(1)}, bf16[10,24,1280]{2,1,0:T(8,128)(2,1)S(1)}, u32[]{:S(2)}, u32[]{:S(2)}) %collective-permute-start.3) | collective-permute-done | bytes 614432 | tf_op jit(solution)/shard_map/ppermute | solution.py:26
  18.0 0.0 copy-done
  18.0 0.0 copy-done.2
  18.0 0.0 copy-done.3
  18.1 4.5 %shard_map.56 = (bf16[464,128]{1,0:T(8,128)(2,1)S(1)}, bf16[464,128]{1,0:T(8,128)(2,1)S(1)}, bf16[464,128]{1,0:T(8,128)(2,1)S(1)}, bf16[464,128]{1,0:T(8,128)(2,...) custom-call(bf16[10,40,1280]{2,1,0:T(8,128)(2,1)S(1)} %bitcast.4, ...), custom_call_target="tpu_custom_call" | custom-call | flops 1179648000 | bytes 6144000 | tf_op jit(solution)/shard_map/pallas_call | solution.py:335
  22.5 0.0 collective-permute-done.2.refs_3_
  22.6 1.8 %collective-permute-start.8 = (bf16[464,128]{1,0:T(8,128)(2,1)S(1)}, bf16[464,128]{1,0:T(8,128)(2,1)S(1)}, u32[]{:S(2)}, u32[]{:S(2)}) collective-permute-start(bf16[464,128]{1,0:T(8,128)(2,1)S(1)} %get-tuple-element.52), channel_id=1, source_target_pairs={{0,1},{1,2},{2,3},{3,0},{4,5},{5,6},{6,7},{7,4},{8,9},{9,10},{10,1... | collective-permute-start | bytes 356360 | tf_op jit(solution)/shard_map/ppermute | solution.py:26
  24.4 0.0 collective-permute-done.1.refs_2_
  24.4 2.6 %collective-permute-start.6 = (bf16[464,128]{1,0:T(8,128)(2,1)S(1)}, bf16[464,128]{1,0:T(8,128)(2,1)S(1)}, u32[]{:S(2)}, u32[]{:S(2)}) collective-permute-start(bf16[464,128]{1,0:T(8,128)(2,1)S(1)} %get-tuple-element.48), channel_id=1, source_target_pairs={{0,2},{1,3},{2,0},{3,1},{4,6},{5,7},{6,4},{7,5},{8,10},{9,11},{10,... | collective-permute-start | bytes 356360 | tf_op jit(solution)/shard_map/ppermute | solution.py:26
  27.0 0.0 collective-permute-done.refs_1_
  27.0 1.3 %collective-permute-start.4 = (bf16[464,128]{1,0:T(8,128)(2,1)S(1)}, bf16[464,128]{1,0:T(8,128)(2,1)S(1)}, u32[]{:S(2)}, u32[]{:S(2)}) collective-permute-start(bf16[464,128]{1,0:T(8,128)(2,1)S(1)} %get-tuple-element.44), channel_id=1, source_target_pairs={{0,3},{1,0},{2,1},{3,2},{4,7},{5,4},{6,5},{7,6},{8,11},{9,8},{10,9... | collective-permute-start | bytes 356360 | tf_op jit(solution)/shard_map/ppermute | solution.py:26
  28.4 2.3 %collective-permute-done.8.refs_7_ = bf16[464,128]{1,0:T(8,128)(2,1)S(1)} collective-permute-done((bf16[464,128]{1,0:T(8,128)(2,1)S(1)}, bf16[464,128]{1,0:T(8,128)(2,1)S(1)}, u32[]{:S(2)}, u32[]{:S(2)}) %collective-permute-start.8) | collective-permute-done | bytes 118816 | tf_op jit(solution)/shard_map/ppermute | solution.py:26
  30.7 3.0 %collective-permute-start.9 = (bf16[464,128]{1,0:T(8,128)(2,1)S(1)}, bf16[464,128]{1,0:T(8,128)(2,1)S(1)}, u32[]{:S(2)}, u32[]{:S(2)}) collective-permute-start(bf16[464,128]{1,0:T(8,128)(2,1)S(1)} %get-tuple-element.53), channel_id=1, source_target_pairs={{0,1},{1,2},{2,3},{3,0},{4,5},{5,6},{6,7},{7,4},{8,9},{9,10},{10,1... | collective-permute-start | bytes 356360 | tf_op jit(solution)/shard_map/ppermute | solution.py:26
  33.6 1.7 %collective-permute-done.6.refs_6_ = bf16[464,128]{1,0:T(8,128)(2,1)S(1)} collective-permute-done((bf16[464,128]{1,0:T(8,128)(2,1)S(1)}, bf16[464,128]{1,0:T(8,128)(2,1)S(1)}, u32[]{:S(2)}, u32[]{:S(2)}) %collective-permute-start.6) | collective-permute-done | bytes 118816 | tf_op jit(solution)/shard_map/ppermute | solution.py:26
  35.3 0.7 %collective-permute-start.7 = (bf16[464,128]{1,0:T(8,128)(2,1)S(1)}, bf16[464,128]{1,0:T(8,128)(2,1)S(1)}, u32[]{:S(2)}, u32[]{:S(2)}) collective-permute-start(bf16[464,128]{1,0:T(8,128)(2,1)S(1)} %get-tuple-element.49), channel_id=1, source_target_pairs={{0,2},{1,3},{2,0},{3,1},{4,6},{5,7},{6,4},{7,5},{8,10},{9,11},{10,... | collective-permute-start | bytes 356360 | tf_op jit(solution)/shard_map/ppermute | solution.py:26
  36.1 0.0 collective-permute-done.4.refs_5_
  36.1 3.7 %collective-permute-start.5 = (bf16[464,128]{1,0:T(8,128)(2,1)S(1)}, bf16[464,128]{1,0:T(8,128)(2,1)S(1)}, u32[]{:S(2)}, u32[]{:S(2)}) collective-permute-start(bf16[464,128]{1,0:T(8,128)(2,1)S(1)} %get-tuple-element.45), channel_id=1, source_target_pairs={{0,3},{1,0},{2,1},{3,2},{4,7},{5,4},{6,5},{7,6},{8,11},{9,8},{10,9... | collective-permute-start | bytes 356360 | tf_op jit(solution)/shard_map/ppermute | solution.py:26
  39.8 0.0 copy-done.4
  39.8 4.0 %shard_map.57 = (bf16[608,128]{1,0:T(8,128)(2,1)S(1)}, bf16[416,128]{1,0:T(8,128)(2,1)S(1)}) custom-call(bf16[608,128]{1,0:T(8,128)(2,1)S(1)} %copy-done.4, bf16[608,128]{1,0:T(8,128)(2,1)S(1)} %collective-permute-done.refs_1_, bf16[608,128]{1,0:T(8,128)(2,1)S(1)} %collective-permute-done.1.refs_2_, bf16[608,128]{1,0:T(8,128)(2,1)S(1)} %collective-permute-done.2.refs_3_, ...), custom_call_target="tpu_custom_call" | custom-call | flops 2621440000 | bytes 1228800 | tf_op jit(solution)/shard_map/pallas_call | solution.py:387
  43.9 1.8 %collective-permute-start.13 = (bf16[608,128]{1,0:T(8,128)(2,1)S(1)}, bf16[608,128]{1,0:T(8,128)(2,1)S(1)}, u32[]{:S(2)}, u32[]{:S(2)}) collective-permute-start(bf16[608,128]{1,0:T(8,128)(2,1)S(1)} %get-tuple-element.63.refs_0_), channel_id=1, source_target_pairs={{0,16},{4,20},{8,24},{12,28},{16,0},{20,4},{24,8},{28,12},{1,17},{... | collective-permute-start | bytes 466952 | tf_op jit(solution)/shard_map/ppermute | solution.py:26
  45.7 0.0 collective-permute-done.9.refs_7_
  45.7 0.0 collective-permute-done.7.refs_6_
  45.7 0.1 collective-permute-done.5.refs_5_
  45.8 0.0 copy-start.1
  45.8 4.0 %shard_map.58 = (bf16[608,128]{1,0:T(8,128)(2,1)S(1)}, bf16[208,128]{1,0:T(8,128)(2,1)S(1)}, bf16[208,128]{1,0:T(8,128)(2,1)S(1)}, bf16[208,128]{1,0:T(8,128)(2,1)S(1)}, bf16[208,128]{1,0:T(8,128)(2,1)S(1)}) custom-call(bf16[608,128]{1,0:T(8,128)(2,1)S(1)} %copy-done.4, bf16[608,128]{1,0:T(8,128)(2,1)S(1)} %collective-permute-done.refs_1_, ...), custom_call_target="tpu_custom_call" | custom-call | flops 2621440000 | bytes 1228800 | tf_op jit(solution)/shard_map/pallas_call | solution.py:387
  49.8 1.3 %collective-permute-start.14 = (bf16[608,128]{1,0:T(8,128)(2,1)S(1)}, bf16[608,128]{1,0:T(8,128)(2,1)S(1)}, u32[]{:S(2)}, u32[]{:S(2)}) collective-permute-start(bf16[608,128]{1,0:T(8,128)(2,1)S(1)} %get-tuple-element.64.refs_2_), channel_id=1, source_target_pairs={{0,16},{4,20},{8,24},{12,28},{16,0},{20,4},{24,8},{28,12},{1,17},{... | collective-permute-start | bytes 466952 | tf_op jit(solution)/shard_map/ppermute | solution.py:26
  51.1 2.0 %collective-permute-start.10 = (bf16[208,128]{1,0:T(8,128)(2,1)S(1)}, bf16[208,128]{1,0:T(8,128)(2,1)S(1)}, u32[]{:S(2)}, u32[]{:S(2)}) collective-permute-start(bf16[208,128]{1,0:T(8,128)(2,1)S(1)} %get-tuple-element.57), channel_id=1, source_target_pairs={{0,1},{1,2},{2,3},{3,0},{4,5},{5,6},{6,7},{7,4},{8,9},{9,10},{10,1... | collective-permute-start | bytes 159752 | tf_op jit(solution)/shard_map/ppermute | solution.py:26
  53.1 1.4 %collective-permute-start.11 = (bf16[208,128]{1,0:T(8,128)(2,1)S(1)}, bf16[208,128]{1,0:T(8,128)(2,1)S(1)}, u32[]{:S(2)}, u32[]{:S(2)}) collective-permute-start(bf16[208,128]{1,0:T(8,128)(2,1)S(1)} %get-tuple-element.58), channel_id=1, source_target_pairs={{0,2},{1,3},{2,0},{3,1},{4,6},{5,7},{6,4},{7,5},{8,10},{9,11},{10,... | collective-permute-start | bytes 159752 | tf_op jit(solution)/shard_map/ppermute | solution.py:26
  54.5 1.1 %collective-permute-start.12 = (bf16[208,128]{1,0:T(8,128)(2,1)S(1)}, bf16[208,128]{1,0:T(8,128)(2,1)S(1)}, u32[]{:S(2)}, u32[]{:S(2)}) collective-permute-start(bf16[208,128]{1,0:T(8,128)(2,1)S(1)} %get-tuple-element.59), channel_id=1, source_target_pairs={{0,3},{1,0},{2,1},{3,2},{4,7},{5,4},{6,5},{7,6},{8,11},{9,8},{10,9... | collective-permute-start | bytes 159752 | tf_op jit(solution)/shard_map/ppermute | solution.py:26
  55.6 0.0 collective-permute-done.13.refs_1_
  55.6 0.1 collective-permute-done.14.refs_3_
  55.7 0.6 shard_map.60
  56.3 1.8 %collective-permute-start.15 = (bf16[304,128]{1,0:T(8,128)(2,1)S(1)}, bf16[304,128]{1,0:T(8,128)(2,1)S(1)}, u32[]{:S(2)}, u32[]{:S(2)}) collective-permute-start(bf16[304,128]{1,0:T(8,128)(2,1)S(1)} %get-tuple-element.66), channel_id=1, source_target_pairs={{0,1},{1,2},{2,3},{3,0},{4,5},{5,6},{6,7},{7,4},{8,9},{9,10},{10,1... | collective-permute-start | bytes 233480 | tf_op jit(solution)/shard_map/ppermute | solution.py:26
  58.1 1.7 %collective-permute-start.16 = (bf16[304,128]{1,0:T(8,128)(2,1)S(1)}, bf16[304,128]{1,0:T(8,128)(2,1)S(1)}, u32[]{:S(2)}, u32[]{:S(2)}) collective-permute-start(bf16[304,128]{1,0:T(8,128)(2,1)S(1)} %get-tuple-element.67), channel_id=1, source_target_pairs={{0,2},{1,3},{2,0},{3,1},{4,6},{5,7},{6,4},{7,5},{8,10},{9,11},{10,... | collective-permute-start | bytes 233480 | tf_op jit(solution)/shard_map/ppermute | solution.py:26
  59.8 0.0 collective-permute-done.10.refs_1_
  59.8 1.2 %collective-permute-start.17 = (bf16[304,128]{1,0:T(8,128)(2,1)S(1)}, bf16[304,128]{1,0:T(8,128)(2,1)S(1)}, u32[]{:S(2)}, u32[]{:S(2)}) collective-permute-start(bf16[304,128]{1,0:T(8,128)(2,1)S(1)} %get-tuple-element.68), channel_id=1, source_target_pairs={{0,3},{1,0},{2,1},{3,2},{4,7},{5,4},{6,5},{7,6},{8,11},{9,8},{10,9... | collective-permute-start | bytes 233480 | tf_op jit(solution)/shard_map/ppermute | solution.py:26
  61.0 0.0 collective-permute-done.11.refs_2_
  61.0 0.0 collective-permute-done.12.refs_3_
  61.1 0.0 copy-done.1
  61.1 0.8 %shard_map.59 = (f32[10,40,1280]{2,1,0:T(8,128)S(1)}, bf16[512,1280]{1,0:T(8,128)(2,1)S(1)}, bf16[512,1280]{1,0:T(8,128)(2,1)S(1)}) custom-call(bf16[10,40,1280]{2,1,0:T(8,128)(2,1)S(1)} %bitcast.5, bf16[640,1280]{1,0:T(8,128)(2,1)S(1)} %copy-done.1, bf16[208,128]{1,0:T(8,128)(2,1)S(1)} %get-tuple-element.56.refs_0_, ...), custom_call_target="tpu_custom_call" | custom-call | flops 524288000 | bytes 3891200 | tf_op jit(solution)/shard_map/pallas_call | solution.py:437
  61.9 1.4 %collective-permute-done.15.refs_1_ = bf16[304,128]{1,0:T(8,128)(2,1)S(1)} collective-permute-done((bf16[304,128]{1,0:T(8,128)(2,1)S(1)}, bf16[304,128]{1,0:T(8,128)(2,1)S(1)}, u32[]{:S(2)}, u32[]{:S(2)}) %collective-permute-start.15) | collective-permute-done | bytes 77856 | tf_op jit(solution)/shard_map/ppermute | solution.py:26
  63.3 2.2 %collective-permute-done.16.refs_2_ = bf16[304,128]{1,0:T(8,128)(2,1)S(1)} collective-permute-done((bf16[304,128]{1,0:T(8,128)(2,1)S(1)}, bf16[304,128]{1,0:T(8,128)(2,1)S(1)}, u32[]{:S(2)}, u32[]{:S(2)}) %collective-permute-start.16) | collective-permute-done | bytes 77856 | tf_op jit(solution)/shard_map/ppermute | solution.py:26
  65.5 0.0 collective-permute-done.17.refs_3_
  65.5 1.8 %shard_map.61 = bf16[10,40,1280]{2,1,0:T(8,128)(2,1)} custom-call(f32[10,40,1280]{2,1,0:T(8,128)S(1)} %get-tuple-element.60.partial, bf16[512,1280]{1,0:T(8,128)(2,1)S(1)} %get-tuple-element.61.first, bf16[512,1280]{1,0:T(8,128)(2,1)S(1)} %get-tuple-element.62.second, bf16[304,128]{1,0:T(8,128)(2,1)S(1)} %get-tuple-element.65.refs_0_, ...), custom_call_target="tpu_custom_call" | custom-call | flops 524288000 | bytes 3891200 | tf_op jit(solution)/shard_map/pallas_call | solution.py:449
Async XLA Ops:
  1.1 16.9 %copy-start = (bf16[1,10,40,1280]{3,2,1,0:T(8,128)(2,1)S(1)}, bf16[1,10,40,1280]{3,2,1,0:T(8,128)(2,1)}, u32[]{:S(2)}) copy-start(bf16[1,10,40,1280]{3,2,1,0:T(8,128)(2,1)} %param.5) | copy-start | bytes 3072004
  1.1 16.9 %copy-start.2 = (f32[1280]{0:T(1024)S(1)}, f32[1280]{0:T(1024)}, u32[]{:S(2)}) copy-start(f32[1280]{0:T(1024)} %gain.3) | copy-start | bytes 15364
  1.1 16.9 %copy-start.3 = (s32[4]{0:T(128)S(1)}, s32[4]{0:T(128)}, u32[]{:S(2)}) copy-start(s32[4]{0:T(128)} %lon_shift.3) | copy-start | bytes 52
  1.2 16.9 %collective-permute-start.3 = (bf16[10,24,1280]{2,1,0:T(8,128)(2,1)S(1)}, bf16[10,24,1280]{2,1,0:T(8,128)(2,1)S(1)}, u32[]{:S(2)}, u32[]{:S(2)}) collective-permute-start(bf16[10,24,1280]{2,1,0:T(8,128)(2,1)S(1)} %slice.4), channel_id=1, source_target_pairs={{0,16},{4,20},{8,24},{12,28},{16,0},{20,4},{24,8},{28,12},{1,17},{... | collective-permute-start | bytes 1843208 | tf_op jit(solution)/shard_map/ppermute | solution.py:26
  8.8 13.8 %collective-permute-start.2 = (bf16[608,128]{1,0:T(8,128)(2,1)}, bf16[608,128]{1,0:T(8,128)(2,1)S(1)}, u32[]{:S(2)}, u32[]{:S(2)}) collective-permute-start(bf16[608,128]{1,0:T(8,128)(2,1)} %get-tuple-element.40), channel_id=1, source_target_pairs={{0,1},{1,2},{2,3},{3,0},{4,5},{5,6},{6,7},{7,4},{8,9},{9,10},{10,1... | collective-permute-start | bytes 466952 | tf_op jit(solution)/shard_map/ppermute | solution.py:26
  10.4 14.0 %collective-permute-start.1 = (bf16[608,128]{1,0:T(8,128)(2,1)}, bf16[608,128]{1,0:T(8,128)(2,1)S(1)}, u32[]{:S(2)}, u32[]{:S(2)}) collective-permute-start(bf16[608,128]{1,0:T(8,128)(2,1)} %get-tuple-element.39), channel_id=1, source_target_pairs={{0,2},{1,3},{2,0},{3,1},{4,6},{5,7},{6,4},{7,5},{8,10},{9,11},{10,... | collective-permute-start | bytes 466952 | tf_op jit(solution)/shard_map/ppermute | solution.py:26
  13.0 26.8 %copy-start.4 = (bf16[608,128]{1,0:T(8,128)(2,1)S(1)}, bf16[608,128]{1,0:T(8,128)(2,1)}, u32[]{:S(2)}) copy-start(bf16[608,128]{1,0:T(8,128)(2,1)} %get-tuple-element.37.refs_0_) | copy-start | bytes 466948
  13.0 14.0 %collective-permute-start = (bf16[608,128]{1,0:T(8,128)(2,1)}, bf16[608,128]{1,0:T(8,128)(2,1)S(1)}, u32[]{:S(2)}, u32[]{:S(2)}) collective-permute-start(bf16[608,128]{1,0:T(8,128)(2,1)} %get-tuple-element.38), channel_id=1, source_target_pairs={{0,3},{1,0},{2,1},{3,2},{4,7},{5,4},{6,5},{7,6},{8,11},{9,8},{10,9... | collective-permute-start | bytes 466952 | tf_op jit(solution)/shard_map/ppermute | solution.py:26
  22.6 8.1 %collective-permute-start.8 = (bf16[464,128]{1,0:T(8,128)(2,1)S(1)}, bf16[464,128]{1,0:T(8,128)(2,1)S(1)}, u32[]{:S(2)}, u32[]{:S(2)}) collective-permute-start(bf16[464,128]{1,0:T(8,128)(2,1)S(1)} %get-tuple-element.52), channel_id=1, source_target_pairs={{0,1},{1,2},{2,3},{3,0},{4,5},{5,6},{6,7},{7,4},{8,9},{9,10},{10,1... | collective-permute-start | bytes 356360 | tf_op jit(solution)/shard_map/ppermute | solution.py:26
  24.4 10.9 %collective-permute-start.6 = (bf16[464,128]{1,0:T(8,128)(2,1)S(1)}, bf16[464,128]{1,0:T(8,128)(2,1)S(1)}, u32[]{:S(2)}, u32[]{:S(2)}) collective-permute-start(bf16[464,128]{1,0:T(8,128)(2,1)S(1)} %get-tuple-element.48), channel_id=1, source_target_pairs={{0,2},{1,3},{2,0},{3,1},{4,6},{5,7},{6,4},{7,5},{8,10},{9,11},{10,... | collective-permute-start | bytes 356360 | tf_op jit(solution)/shard_map/ppermute | solution.py:26
  27.0 9.1 %collective-permute-start.4 = (bf16[464,128]{1,0:T(8,128)(2,1)S(1)}, bf16[464,128]{1,0:T(8,128)(2,1)S(1)}, u32[]{:S(2)}, u32[]{:S(2)}) collective-permute-start(bf16[464,128]{1,0:T(8,128)(2,1)S(1)} %get-tuple-element.44), channel_id=1, source_target_pairs={{0,3},{1,0},{2,1},{3,2},{4,7},{5,4},{6,5},{7,6},{8,11},{9,8},{10,9... | collective-permute-start | bytes 356360 | tf_op jit(solution)/shard_map/ppermute | solution.py:26
  30.7 15.0 %collective-permute-start.9 = (bf16[464,128]{1,0:T(8,128)(2,1)S(1)}, bf16[464,128]{1,0:T(8,128)(2,1)S(1)}, u32[]{:S(2)}, u32[]{:S(2)}) collective-permute-start(bf16[464,128]{1,0:T(8,128)(2,1)S(1)} %get-tuple-element.53), channel_id=1, source_target_pairs={{0,1},{1,2},{2,3},{3,0},{4,5},{5,6},{6,7},{7,4},{8,9},{9,10},{10,1... | collective-permute-start | bytes 356360 | tf_op jit(solution)/shard_map/ppermute | solution.py:26
  35.3 10.4 %collective-permute-start.7 = (bf16[464,128]{1,0:T(8,128)(2,1)S(1)}, bf16[464,128]{1,0:T(8,128)(2,1)S(1)}, u32[]{:S(2)}, u32[]{:S(2)}) collective-permute-start(bf16[464,128]{1,0:T(8,128)(2,1)S(1)} %get-tuple-element.49), channel_id=1, source_target_pairs={{0,2},{1,3},{2,0},{3,1},{4,6},{5,7},{6,4},{7,5},{8,10},{9,11},{10,... | collective-permute-start | bytes 356360 | tf_op jit(solution)/shard_map/ppermute | solution.py:26
  36.1 9.7 %collective-permute-start.5 = (bf16[464,128]{1,0:T(8,128)(2,1)S(1)}, bf16[464,128]{1,0:T(8,128)(2,1)S(1)}, u32[]{:S(2)}, u32[]{:S(2)}) collective-permute-start(bf16[464,128]{1,0:T(8,128)(2,1)S(1)} %get-tuple-element.45), channel_id=1, source_target_pairs={{0,3},{1,0},{2,1},{3,2},{4,7},{5,4},{6,5},{7,6},{8,11},{9,8},{10,9... | collective-permute-start | bytes 356360 | tf_op jit(solution)/shard_map/ppermute | solution.py:26
  43.9 11.7 %collective-permute-start.13 = (bf16[608,128]{1,0:T(8,128)(2,1)S(1)}, bf16[608,128]{1,0:T(8,128)(2,1)S(1)}, u32[]{:S(2)}, u32[]{:S(2)}) collective-permute-start(bf16[608,128]{1,0:T(8,128)(2,1)S(1)} %get-tuple-element.63.refs_0_), channel_id=1, source_target_pairs={{0,16},{4,20},{8,24},{12,28},{16,0},{20,4},{24,8},{28,12},{1,17},{... | collective-permute-start | bytes 466952 | tf_op jit(solution)/shard_map/ppermute | solution.py:26
  45.8 15.3 %copy-start.1 = (bf16[640,1280]{1,0:T(8,128)(2,1)S(1)}, bf16[640,1280]{1,0:T(8,128)(2,1)}, u32[]{:S(2)}) copy-start(bf16[640,1280]{1,0:T(8,128)(2,1)} %weight.5) | copy-start | bytes 4915204
  49.8 5.8 %collective-permute-start.14 = (bf16[608,128]{1,0:T(8,128)(2,1)S(1)}, bf16[608,128]{1,0:T(8,128)(2,1)S(1)}, u32[]{:S(2)}, u32[]{:S(2)}) collective-permute-start(bf16[608,128]{1,0:T(8,128)(2,1)S(1)} %get-tuple-element.64.refs_2_), channel_id=1, source_target_pairs={{0,16},{4,20},{8,24},{12,28},{16,0},{20,4},{24,8},{28,12},{1,17},{... | collective-permute-start | bytes 466952 | tf_op jit(solution)/shard_map/ppermute | solution.py:26
  51.1 8.7 %collective-permute-start.10 = (bf16[208,128]{1,0:T(8,128)(2,1)S(1)}, bf16[208,128]{1,0:T(8,128)(2,1)S(1)}, u32[]{:S(2)}, u32[]{:S(2)}) collective-permute-start(bf16[208,128]{1,0:T(8,128)(2,1)S(1)} %get-tuple-element.57), channel_id=1, source_target_pairs={{0,1},{1,2},{2,3},{3,0},{4,5},{5,6},{6,7},{7,4},{8,9},{9,10},{10,1... | collective-permute-start | bytes 159752 | tf_op jit(solution)/shard_map/ppermute | solution.py:26
  53.1 8.0 %collective-permute-start.11 = (bf16[208,128]{1,0:T(8,128)(2,1)S(1)}, bf16[208,128]{1,0:T(8,128)(2,1)S(1)}, u32[]{:S(2)}, u32[]{:S(2)}) collective-permute-start(bf16[208,128]{1,0:T(8,128)(2,1)S(1)} %get-tuple-element.58), channel_id=1, source_target_pairs={{0,2},{1,3},{2,0},{3,1},{4,6},{5,7},{6,4},{7,5},{8,10},{9,11},{10,... | collective-permute-start | bytes 159752 | tf_op jit(solution)/shard_map/ppermute | solution.py:26
  54.5 6.6 %collective-permute-start.12 = (bf16[208,128]{1,0:T(8,128)(2,1)S(1)}, bf16[208,128]{1,0:T(8,128)(2,1)S(1)}, u32[]{:S(2)}, u32[]{:S(2)}) collective-permute-start(bf16[208,128]{1,0:T(8,128)(2,1)S(1)} %get-tuple-element.59), channel_id=1, source_target_pairs={{0,3},{1,0},{2,1},{3,2},{4,7},{5,4},{6,5},{7,6},{8,11},{9,8},{10,9... | collective-permute-start | bytes 159752 | tf_op jit(solution)/shard_map/ppermute | solution.py:26
  56.3 7.0 %collective-permute-start.15 = (bf16[304,128]{1,0:T(8,128)(2,1)S(1)}, bf16[304,128]{1,0:T(8,128)(2,1)S(1)}, u32[]{:S(2)}, u32[]{:S(2)}) collective-permute-start(bf16[304,128]{1,0:T(8,128)(2,1)S(1)} %get-tuple-element.66), channel_id=1, source_target_pairs={{0,1},{1,2},{2,3},{3,0},{4,5},{5,6},{6,7},{7,4},{8,9},{9,10},{10,1... | collective-permute-start | bytes 233480 | tf_op jit(solution)/shard_map/ppermute | solution.py:26
  58.1 7.4 %collective-permute-start.16 = (bf16[304,128]{1,0:T(8,128)(2,1)S(1)}, bf16[304,128]{1,0:T(8,128)(2,1)S(1)}, u32[]{:S(2)}, u32[]{:S(2)}) collective-permute-start(bf16[304,128]{1,0:T(8,128)(2,1)S(1)} %get-tuple-element.67), channel_id=1, source_target_pairs={{0,2},{1,3},{2,0},{3,1},{4,6},{5,7},{6,4},{7,5},{8,10},{9,11},{10,... | collective-permute-start | bytes 233480 | tf_op jit(solution)/shard_map/ppermute | solution.py:26
  59.8 5.7 %collective-permute-start.17 = (bf16[304,128]{1,0:T(8,128)(2,1)S(1)}, bf16[304,128]{1,0:T(8,128)(2,1)S(1)}, u32[]{:S(2)}, u32[]{:S(2)}) collective-permute-start(bf16[304,128]{1,0:T(8,128)(2,1)S(1)} %get-tuple-element.68), channel_id=1, source_target_pairs={{0,3},{1,0},{2,1},{3,2},{4,7},{5,4},{6,5},{7,6},{8,11},{9,8},{10,9... | collective-permute-start | bytes 233480 | tf_op jit(solution)/shard_map/ppermute | solution.py:26

commit v18 on v17

--- a/solution.py
+++ b/solution.py
@@ -301,14 +301,24 @@
 
 
 def second_output_kernel(split, partial, first, second, *refs):
-    *blocks, out = refs
+    *blocks, out, held, sems = refs
     rows, _, features = partial.shape
     blocks = [block[...].astype(jnp.float32) for block in blocks]
-    tokens = partial[...]
     count, shape = rows * split, (rows, split, features)
-    left = tokens[:, :split] + projected(blocks, 0, count, first, shape)
+    left = projected(blocks, 0, count, first, shape)
     left += projected(blocks, packed_rows(count)[0], count, second, shape)
-    out[...] = jnp.concatenate([left, tokens[:, split:]], axis=1).astype(jnp.bfloat16)
+    copies = []
+    for start, size in ((0, rows // 2), (rows // 2, rows - rows // 2)):
+        end = start + size
+        tokens = partial[start:end]
+        held[start:end] = jnp.concatenate(
+            [tokens[:, :split] + left[start:end], tokens[:, split:]], axis=1
+        ).astype(jnp.bfloat16)
+        part = pl.ds(start, size)
+        copies.append(pltpu.make_async_copy(held.at[part], out.at[part], sems.at[len(copies)]))
+        copies[-1].start()
+    for copy in copies:
+        copy.wait()
 
 
 def whole(count):
@@ -450,7 +460,11 @@
         functools.partial(second_output_kernel, split),
         out_shape=jax.ShapeDtypeStruct(field.shape, jnp.bfloat16),
         in_specs=whole(3 + groups),
-        out_specs=pl.BlockSpec(memory_space=pltpu.VMEM),
+        out_specs=hbm,
+        scratch_shapes=[
+            pltpu.VMEM(field.shape, jnp.bfloat16),
+            pltpu.SemaphoreType.DMA((2,)),
+        ],
         compiler_params=limit(24),
         cost_estimate=cost,
     )(partial, *weights, *second)

time: 67.6 us -> 67.7 us (level)
  no operation moved by 1% of the time
where the time goes in v18:
time: 67.7 us; the launch traced here: 67.5 us
  starting transfers between devices  34.1 us (50%)
  Pallas kernels  20.4 us (30%)
  waiting for transfers between devices  11.6 us (17%)
  local copies, waits for them, and re-layouts  1.14 us (2%)
    ppermute x18, starting transfers between devices, shifted(): lax.ppermute(block, axis, [(i, (i + distance) % count) for i in range(cou...  34.1 us
    ppermute x18, waiting for transfers between devices, shifted(): lax.ppermute(block, axis, [(i, (i + distance) % count) for i in range(cou...  11.6 us
    pallas_call x2, Pallas kernels, projection(): pl.pallas_call(functools.partial(kernel, split), out_shape=[block] * (par...  9.09 us
    pallas_call x2, Pallas kernels, attention(): pl.pallas_call(functools.partial(attention_kernel, head, groups, kept_cou...  8.08 us
    pallas_call x1, Pallas kernels, shards(): pl.pallas_call(functools.partial(second_output_kernel, split), out_shape=...  1.82 us
  transfers between devices with their start and end apart: 18, of which 7 were waited for; matrix products, arithmetic and copies ran while one was open for 0% of the time, Pallas kernels for 28%

profile of v18, /device:TPU:0, one launch (start us, length us, event | category | flops | bytes accessed | tf_op | source)
XLA Modules:
  0.0 67.5 jit_solution(18087477526942130711)
XLA Ops:
  0.0 1.1 %slice.4 = bf16[10,24,1280]{2,1,0:T(8,128)(2,1)S(1)} slice(bf16[10,40,1280]{2,1,0:T(8,128)(2,1)} %bitcast.2), slice={[0:10], [0:24], [0:1280]} | slice | bytes 1228800 | tf_op jit(solution)/shard_map/slice | solution.py:368
  1.1 0.0 copy-start
  1.1 0.0 copy-start.2
  1.1 0.0 copy-start.3
  1.2 3.0 %collective-permute-start.3 = (bf16[10,24,1280]{2,1,0:T(8,128)(2,1)S(1)}, bf16[10,24,1280]{2,1,0:T(8,128)(2,1)S(1)}, u32[]{:S(2)}, u32[]{:S(2)}) collective-permute-start(bf16[10,24,1280]{2,1,0:T(8,128)(2,1)S(1)} %slice.4), channel_id=1, source_target_pairs={{0,16},{4,20},{8,24},{12,28},{16,0},{20,4},{24,8},{28,12},{1,17},{... | collective-permute-start | bytes 1843208 | tf_op jit(solution)/shard_map/ppermute | solution.py:26
  4.2 4.6 %shard_map.55 = (bf16[608,128]{1,0:T(8,128)(2,1)}, bf16[608,128]{1,0:T(8,128)(2,1)}, bf16[608,128]{1,0:T(8,128)(2,1)}, bf16[608,128]{1,0:T(8,128)(2,1)}) custom-call(bf16[10,40,1280]{2,1,0:T(8,128)(2,1)} %bitcast.3, f32[1280]{0:T(1024)} %gain.3, bf16[1280,1920]{1,0:T(8,128)(2,1)} %weight.4), custom_call_target="tpu_custom_call" | custom-call | flops 786432000 | bytes 5734400 | tf_op jit(solution)/shard_map/pallas_call | solution.py:345
  8.8 1.6 %collective-permute-start.2 = (bf16[608,128]{1,0:T(8,128)(2,1)}, bf16[608,128]{1,0:T(8,128)(2,1)S(1)}, u32[]{:S(2)}, u32[]{:S(2)}) collective-permute-start(bf16[608,128]{1,0:T(8,128)(2,1)} %get-tuple-element.40), channel_id=1, source_target_pairs={{0,1},{1,2},{2,3},{3,0},{4,5},{5,6},{6,7},{7,4},{8,9},{9,10},{10,1... | collective-permute-start | bytes 466952 | tf_op jit(solution)/shard_map/ppermute | solution.py:26
  10.4 2.6 %collective-permute-start.1 = (bf16[608,128]{1,0:T(8,128)(2,1)}, bf16[608,128]{1,0:T(8,128)(2,1)S(1)}, u32[]{:S(2)}, u32[]{:S(2)}) collective-permute-start(bf16[608,128]{1,0:T(8,128)(2,1)} %get-tuple-element.39), channel_id=1, source_target_pairs={{0,2},{1,3},{2,0},{3,1},{4,6},{5,7},{6,4},{7,5},{8,10},{9,11},{10,... | collective-permute-start | bytes 466952 | tf_op jit(solution)/shard_map/ppermute | solution.py:26
  13.0 0.0 copy-start.4
  13.0 1.3 %collective-permute-start = (bf16[608,128]{1,0:T(8,128)(2,1)}, bf16[608,128]{1,0:T(8,128)(2,1)S(1)}, u32[]{:S(2)}, u32[]{:S(2)}) collective-permute-start(bf16[608,128]{1,0:T(8,128)(2,1)} %get-tuple-element.38), channel_id=1, source_target_pairs={{0,3},{1,0},{2,1},{3,2},{4,7},{5,4},{6,5},{7,6},{8,11},{9,8},{10,9... | collective-permute-start | bytes 466952 | tf_op jit(solution)/shard_map/ppermute | solution.py:26
  14.4 3.7 %collective-permute-done.3.eastern = bf16[10,24,1280]{2,1,0:T(8,128)(2,1)S(1)} collective-permute-done((bf16[10,24,1280]{2,1,0:T(8,128)(2,1)S(1)}, bf16[10,24,1280]{2,1,0:T(8,128)(2,1)S(1)}, u32[]{:S(2)}, u32[]{:S(2)}) %collective-permute-start.3) | collective-permute-done | bytes 614432 | tf_op jit(solution)/shard_map/ppermute | solution.py:26
  18.0 0.0 copy-done
  18.0 0.0 copy-done.2
  18.0 0.0 copy-done.3
  18.1 4.5 %shard_map.56 = (bf16[464,128]{1,0:T(8,128)(2,1)S(1)}, bf16[464,128]{1,0:T(8,128)(2,1)S(1)}, bf16[464,128]{1,0:T(8,128)(2,1)S(1)}, bf16[464,128]{1,0:T(8,128)(2,...) custom-call(bf16[10,40,1280]{2,1,0:T(8,128)(2,1)S(1)} %bitcast.4, ...), custom_call_target="tpu_custom_call" | custom-call | flops 1179648000 | bytes 6144000 | tf_op jit(solution)/shard_map/pallas_call | solution.py:345
  22.5 0.0 collective-permute-done.2.refs_3_
  22.6 1.8 %collective-permute-start.8 = (bf16[464,128]{1,0:T(8,128)(2,1)S(1)}, bf16[464,128]{1,0:T(8,128)(2,1)S(1)}, u32[]{:S(2)}, u32[]{:S(2)}) collective-permute-start(bf16[464,128]{1,0:T(8,128)(2,1)S(1)} %get-tuple-element.52), channel_id=1, source_target_pairs={{0,1},{1,2},{2,3},{3,0},{4,5},{5,6},{6,7},{7,4},{8,9},{9,10},{10,1... | collective-permute-start | bytes 356360 | tf_op jit(solution)/shard_map/ppermute | solution.py:26
  24.4 0.0 collective-permute-done.1.refs_2_
  24.4 2.6 %collective-permute-start.6 = (bf16[464,128]{1,0:T(8,128)(2,1)S(1)}, bf16[464,128]{1,0:T(8,128)(2,1)S(1)}, u32[]{:S(2)}, u32[]{:S(2)}) collective-permute-start(bf16[464,128]{1,0:T(8,128)(2,1)S(1)} %get-tuple-element.48), channel_id=1, source_target_pairs={{0,2},{1,3},{2,0},{3,1},{4,6},{5,7},{6,4},{7,5},{8,10},{9,11},{10,... | collective-permute-start | bytes 356360 | tf_op jit(solution)/shard_map/ppermute | solution.py:26
  27.0 0.0 collective-permute-done.refs_1_
  27.0 1.3 %collective-permute-start.4 = (bf16[464,128]{1,0:T(8,128)(2,1)S(1)}, bf16[464,128]{1,0:T(8,128)(2,1)S(1)}, u32[]{:S(2)}, u32[]{:S(2)}) collective-permute-start(bf16[464,128]{1,0:T(8,128)(2,1)S(1)} %get-tuple-element.44), channel_id=1, source_target_pairs={{0,3},{1,0},{2,1},{3,2},{4,7},{5,4},{6,5},{7,6},{8,11},{9,8},{10,9... | collective-permute-start | bytes 356360 | tf_op jit(solution)/shard_map/ppermute | solution.py:26
  28.4 2.3 %collective-permute-done.8.refs_7_ = bf16[464,128]{1,0:T(8,128)(2,1)S(1)} collective-permute-done((bf16[464,128]{1,0:T(8,128)(2,1)S(1)}, bf16[464,128]{1,0:T(8,128)(2,1)S(1)}, u32[]{:S(2)}, u32[]{:S(2)}) %collective-permute-start.8) | collective-permute-done | bytes 118816 | tf_op jit(solution)/shard_map/ppermute | solution.py:26
  30.7 3.0 %collective-permute-start.9 = (bf16[464,128]{1,0:T(8,128)(2,1)S(1)}, bf16[464,128]{1,0:T(8,128)(2,1)S(1)}, u32[]{:S(2)}, u32[]{:S(2)}) collective-permute-start(bf16[464,128]{1,0:T(8,128)(2,1)S(1)} %get-tuple-element.53), channel_id=1, source_target_pairs={{0,1},{1,2},{2,3},{3,0},{4,5},{5,6},{6,7},{7,4},{8,9},{9,10},{10,1... | collective-permute-start | bytes 356360 | tf_op jit(solution)/shard_map/ppermute | solution.py:26
  33.6 1.7 %collective-permute-done.6.refs_6_ = bf16[464,128]{1,0:T(8,128)(2,1)S(1)} collective-permute-done((bf16[464,128]{1,0:T(8,128)(2,1)S(1)}, bf16[464,128]{1,0:T(8,128)(2,1)S(1)}, u32[]{:S(2)}, u32[]{:S(2)}) %collective-permute-start.6) | collective-permute-done | bytes 118816 | tf_op jit(solution)/shard_map/ppermute | solution.py:26
  35.3 0.7 %collective-permute-start.7 = (bf16[464,128]{1,0:T(8,128)(2,1)S(1)}, bf16[464,128]{1,0:T(8,128)(2,1)S(1)}, u32[]{:S(2)}, u32[]{:S(2)}) collective-permute-start(bf16[464,128]{1,0:T(8,128)(2,1)S(1)} %get-tuple-element.49), channel_id=1, source_target_pairs={{0,2},{1,3},{2,0},{3,1},{4,6},{5,7},{6,4},{7,5},{8,10},{9,11},{10,... | collective-permute-start | bytes 356360 | tf_op jit(solution)/shard_map/ppermute | solution.py:26
  36.1 0.0 collective-permute-done.4.refs_5_
  36.1 3.7 %collective-permute-start.5 = (bf16[464,128]{1,0:T(8,128)(2,1)S(1)}, bf16[464,128]{1,0:T(8,128)(2,1)S(1)}, u32[]{:S(2)}, u32[]{:S(2)}) collective-permute-start(bf16[464,128]{1,0:T(8,128)(2,1)S(1)} %get-tuple-element.45), channel_id=1, source_target_pairs={{0,3},{1,0},{2,1},{3,2},{4,7},{5,4},{6,5},{7,6},{8,11},{9,8},{10,9... | collective-permute-start | bytes 356360 | tf_op jit(solution)/shard_map/ppermute | solution.py:26
  39.8 0.0 copy-done.4
  39.8 4.0 %shard_map.57 = (bf16[608,128]{1,0:T(8,128)(2,1)S(1)}, bf16[416,128]{1,0:T(8,128)(2,1)S(1)}) custom-call(bf16[608,128]{1,0:T(8,128)(2,1)S(1)} %copy-done.4, bf16[608,128]{1,0:T(8,128)(2,1)S(1)} %collective-permute-done.refs_1_, bf16[608,128]{1,0:T(8,128)(2,1)S(1)} %collective-permute-done.1.refs_2_, bf16[608,128]{1,0:T(8,128)(2,1)S(1)} %collective-permute-done.2.refs_3_, ...), custom_call_target="tpu_custom_call" | custom-call | flops 2621440000 | bytes 1228800 | tf_op jit(solution)/shard_map/pallas_call | solution.py:397
  43.9 1.8 %collective-permute-start.13 = (bf16[608,128]{1,0:T(8,128)(2,1)S(1)}, bf16[608,128]{1,0:T(8,128)(2,1)S(1)}, u32[]{:S(2)}, u32[]{:S(2)}) collective-permute-start(bf16[608,128]{1,0:T(8,128)(2,1)S(1)} %get-tuple-element.63.refs_0_), channel_id=1, source_target_pairs={{0,16},{4,20},{8,24},{12,28},{16,0},{20,4},{24,8},{28,12},{1,17},{... | collective-permute-start | bytes 466952 | tf_op jit(solution)/shard_map/ppermute | solution.py:26
  45.7 0.0 collective-permute-done.9.refs_7_
  45.7 0.0 collective-permute-done.7.refs_6_
  45.7 0.1 collective-permute-done.5.refs_5_
  45.8 0.0 copy-start.1
  45.8 4.0 %shard_map.58 = (bf16[608,128]{1,0:T(8,128)(2,1)S(1)}, bf16[208,128]{1,0:T(8,128)(2,1)S(1)}, bf16[208,128]{1,0:T(8,128)(2,1)S(1)}, bf16[208,128]{1,0:T(8,128)(2,1)S(1)}, bf16[208,128]{1,0:T(8,128)(2,1)S(1)}) custom-call(bf16[608,128]{1,0:T(8,128)(2,1)S(1)} %copy-done.4, bf16[608,128]{1,0:T(8,128)(2,1)S(1)} %collective-permute-done.refs_1_, ...), custom_call_target="tpu_custom_call" | custom-call | flops 2621440000 | bytes 1228800 | tf_op jit(solution)/shard_map/pallas_call | solution.py:397
  49.8 1.3 %collective-permute-start.14 = (bf16[608,128]{1,0:T(8,128)(2,1)S(1)}, bf16[608,128]{1,0:T(8,128)(2,1)S(1)}, u32[]{:S(2)}, u32[]{:S(2)}) collective-permute-start(bf16[608,128]{1,0:T(8,128)(2,1)S(1)} %get-tuple-element.64.refs_2_), channel_id=1, source_target_pairs={{0,16},{4,20},{8,24},{12,28},{16,0},{20,4},{24,8},{28,12},{1,17},{... | collective-permute-start | bytes 466952 | tf_op jit(solution)/shard_map/ppermute | solution.py:26
  51.1 2.0 %collective-permute-start.10 = (bf16[208,128]{1,0:T(8,128)(2,1)S(1)}, bf16[208,128]{1,0:T(8,128)(2,1)S(1)}, u32[]{:S(2)}, u32[]{:S(2)}) collective-permute-start(bf16[208,128]{1,0:T(8,128)(2,1)S(1)} %get-tuple-element.57), channel_id=1, source_target_pairs={{0,1},{1,2},{2,3},{3,0},{4,5},{5,6},{6,7},{7,4},{8,9},{9,10},{10,1... | collective-permute-start | bytes 159752 | tf_op jit(solution)/shard_map/ppermute | solution.py:26
  53.1 1.4 %collective-permute-start.11 = (bf16[208,128]{1,0:T(8,128)(2,1)S(1)}, bf16[208,128]{1,0:T(8,128)(2,1)S(1)}, u32[]{:S(2)}, u32[]{:S(2)}) collective-permute-start(bf16[208,128]{1,0:T(8,128)(2,1)S(1)} %get-tuple-element.58), channel_id=1, source_target_pairs={{0,2},{1,3},{2,0},{3,1},{4,6},{5,7},{6,4},{7,5},{8,10},{9,11},{10,... | collective-permute-start | bytes 159752 | tf_op jit(solution)/shard_map/ppermute | solution.py:26
  54.5 1.1 %collective-permute-start.12 = (bf16[208,128]{1,0:T(8,128)(2,1)S(1)}, bf16[208,128]{1,0:T(8,128)(2,1)S(1)}, u32[]{:S(2)}, u32[]{:S(2)}) collective-permute-start(bf16[208,128]{1,0:T(8,128)(2,1)S(1)} %get-tuple-element.59), channel_id=1, source_target_pairs={{0,3},{1,0},{2,1},{3,2},{4,7},{5,4},{6,5},{7,6},{8,11},{9,8},{10,9... | collective-permute-start | bytes 159752 | tf_op jit(solution)/shard_map/ppermute | solution.py:26
  55.6 0.0 collective-permute-done.13.refs_1_
  55.6 0.1 collective-permute-done.14.refs_3_
  55.7 0.6 shard_map.60
  56.3 1.8 %collective-permute-start.15 = (bf16[304,128]{1,0:T(8,128)(2,1)S(1)}, bf16[304,128]{1,0:T(8,128)(2,1)S(1)}, u32[]{:S(2)}, u32[]{:S(2)}) collective-permute-start(bf16[304,128]{1,0:T(8,128)(2,1)S(1)} %get-tuple-element.66), channel_id=1, source_target_pairs={{0,1},{1,2},{2,3},{3,0},{4,5},{5,6},{6,7},{7,4},{8,9},{9,10},{10,1... | collective-permute-start | bytes 233480 | tf_op jit(solution)/shard_map/ppermute | solution.py:26
  58.1 1.7 %collective-permute-start.16 = (bf16[304,128]{1,0:T(8,128)(2,1)S(1)}, bf16[304,128]{1,0:T(8,128)(2,1)S(1)}, u32[]{:S(2)}, u32[]{:S(2)}) collective-permute-start(bf16[304,128]{1,0:T(8,128)(2,1)S(1)} %get-tuple-element.67), channel_id=1, source_target_pairs={{0,2},{1,3},{2,0},{3,1},{4,6},{5,7},{6,4},{7,5},{8,10},{9,11},{10,... | collective-permute-start | bytes 233480 | tf_op jit(solution)/shard_map/ppermute | solution.py:26
  59.8 0.0 collective-permute-done.10.refs_1_
  59.8 1.2 %collective-permute-start.17 = (bf16[304,128]{1,0:T(8,128)(2,1)S(1)}, bf16[304,128]{1,0:T(8,128)(2,1)S(1)}, u32[]{:S(2)}, u32[]{:S(2)}) collective-permute-start(bf16[304,128]{1,0:T(8,128)(2,1)S(1)} %get-tuple-element.68), channel_id=1, source_target_pairs={{0,3},{1,0},{2,1},{3,2},{4,7},{5,4},{6,5},{7,6},{8,11},{9,8},{10,9... | collective-permute-start | bytes 233480 | tf_op jit(solution)/shard_map/ppermute | solution.py:26
  61.0 0.0 collective-permute-done.11.refs_2_
  61.0 0.0 collective-permute-done.12.refs_3_
  61.1 0.0 copy-done.1
  61.1 0.8 %shard_map.59 = (f32[10,40,1280]{2,1,0:T(8,128)S(1)}, bf16[512,1280]{1,0:T(8,128)(2,1)S(1)}, bf16[512,1280]{1,0:T(8,128)(2,1)S(1)}) custom-call(bf16[10,40,1280]{2,1,0:T(8,128)(2,1)S(1)} %bitcast.5, bf16[640,1280]{1,0:T(8,128)(2,1)S(1)} %copy-done.1, bf16[208,128]{1,0:T(8,128)(2,1)S(1)} %get-tuple-element.56.refs_0_, ...), custom_call_target="tpu_custom_call" | custom-call | flops 524288000 | bytes 3891200 | tf_op jit(solution)/shard_map/pallas_call | solution.py:447
  61.9 1.4 %collective-permute-done.15.refs_1_ = bf16[304,128]{1,0:T(8,128)(2,1)S(1)} collective-permute-done((bf16[304,128]{1,0:T(8,128)(2,1)S(1)}, bf16[304,128]{1,0:T(8,128)(2,1)S(1)}, u32[]{:S(2)}, u32[]{:S(2)}) %collective-permute-start.15) | collective-permute-done | bytes 77856 | tf_op jit(solution)/shard_map/ppermute | solution.py:26
  63.3 2.2 %collective-permute-done.16.refs_2_ = bf16[304,128]{1,0:T(8,128)(2,1)S(1)} collective-permute-done((bf16[304,128]{1,0:T(8,128)(2,1)S(1)}, bf16[304,128]{1,0:T(8,128)(2,1)S(1)}, u32[]{:S(2)}, u32[]{:S(2)}) %collective-permute-start.16) | collective-permute-done | bytes 77856 | tf_op jit(solution)/shard_map/ppermute | solution.py:26
  65.5 0.0 collective-permute-done.17.refs_3_
  65.5 1.8 %shard_map.61 = bf16[10,40,1280]{2,1,0:T(8,128)(2,1)} custom-call(f32[10,40,1280]{2,1,0:T(8,128)S(1)} %get-tuple-element.60.partial, bf16[512,1280]{1,0:T(8,128)(2,1)S(1)} %get-tuple-element.61.first, bf16[512,1280]{1,0:T(8,128)(2,1)S(1)} %get-tuple-element.62.second, bf16[304,128]{1,0:T(8,128)(2,1)S(1)} %get-tuple-element.65.refs_0_, ...), custom_call_target="tpu_custom_call" | custom-call | flops 524288000 | bytes 3891200 | tf_op jit(solution)/shard_map/pallas_call | solution.py:459
Async XLA Ops:
  1.1 16.9 %copy-start = (bf16[1,10,40,1280]{3,2,1,0:T(8,128)(2,1)S(1)}, bf16[1,10,40,1280]{3,2,1,0:T(8,128)(2,1)}, u32[]{:S(2)}) copy-start(bf16[1,10,40,1280]{3,2,1,0:T(8,128)(2,1)} %param.5) | copy-start | bytes 3072004
  1.1 16.9 %copy-start.2 = (f32[1280]{0:T(1024)S(1)}, f32[1280]{0:T(1024)}, u32[]{:S(2)}) copy-start(f32[1280]{0:T(1024)} %gain.3) | copy-start | bytes 15364
  1.1 16.9 %copy-start.3 = (s32[4]{0:T(128)S(1)}, s32[4]{0:T(128)}, u32[]{:S(2)}) copy-start(s32[4]{0:T(128)} %lon_shift.3) | copy-start | bytes 52
  1.2 16.9 %collective-permute-start.3 = (bf16[10,24,1280]{2,1,0:T(8,128)(2,1)S(1)}, bf16[10,24,1280]{2,1,0:T(8,128)(2,1)S(1)}, u32[]{:S(2)}, u32[]{:S(2)}) collective-permute-start(bf16[10,24,1280]{2,1,0:T(8,128)(2,1)S(1)} %slice.4), channel_id=1, source_target_pairs={{0,16},{4,20},{8,24},{12,28},{16,0},{20,4},{24,8},{28,12},{1,17},{... | collective-permute-start | bytes 1843208 | tf_op jit(solution)/shard_map/ppermute | solution.py:26
  8.8 13.8 %collective-permute-start.2 = (bf16[608,128]{1,0:T(8,128)(2,1)}, bf16[608,128]{1,0:T(8,128)(2,1)S(1)}, u32[]{:S(2)}, u32[]{:S(2)}) collective-permute-start(bf16[608,128]{1,0:T(8,128)(2,1)} %get-tuple-element.40), channel_id=1, source_target_pairs={{0,1},{1,2},{2,3},{3,0},{4,5},{5,6},{6,7},{7,4},{8,9},{9,10},{10,1... | collective-permute-start | bytes 466952 | tf_op jit(solution)/shard_map/ppermute | solution.py:26
  10.4 14.0 %collective-permute-start.1 = (bf16[608,128]{1,0:T(8,128)(2,1)}, bf16[608,128]{1,0:T(8,128)(2,1)S(1)}, u32[]{:S(2)}, u32[]{:S(2)}) collective-permute-start(bf16[608,128]{1,0:T(8,128)(2,1)} %get-tuple-element.39), channel_id=1, source_target_pairs={{0,2},{1,3},{2,0},{3,1},{4,6},{5,7},{6,4},{7,5},{8,10},{9,11},{10,... | collective-permute-start | bytes 466952 | tf_op jit(solution)/shard_map/ppermute | solution.py:26
  13.0 26.8 %copy-start.4 = (bf16[608,128]{1,0:T(8,128)(2,1)S(1)}, bf16[608,128]{1,0:T(8,128)(2,1)}, u32[]{:S(2)}) copy-start(bf16[608,128]{1,0:T(8,128)(2,1)} %get-tuple-element.37.refs_0_) | copy-start | bytes 466948
  13.0 14.0 %collective-permute-start = (bf16[608,128]{1,0:T(8,128)(2,1)}, bf16[608,128]{1,0:T(8,128)(2,1)S(1)}, u32[]{:S(2)}, u32[]{:S(2)}) collective-permute-start(bf16[608,128]{1,0:T(8,128)(2,1)} %get-tuple-element.38), channel_id=1, source_target_pairs={{0,3},{1,0},{2,1},{3,2},{4,7},{5,4},{6,5},{7,6},{8,11},{9,8},{10,9... | collective-permute-start | bytes 466952 | tf_op jit(solution)/shard_map/ppermute | solution.py:26
  22.6 8.1 %collective-permute-start.8 = (bf16[464,128]{1,0:T(8,128)(2,1)S(1)}, bf16[464,128]{1,0:T(8,128)(2,1)S(1)}, u32[]{:S(2)}, u32[]{:S(2)}) collective-permute-start(bf16[464,128]{1,0:T(8,128)(2,1)S(1)} %get-tuple-element.52), channel_id=1, source_target_pairs={{0,1},{1,2},{2,3},{3,0},{4,5},{5,6},{6,7},{7,4},{8,9},{9,10},{10,1... | collective-permute-start | bytes 356360 | tf_op jit(solution)/shard_map/ppermute | solution.py:26
  24.4 10.9 %collective-permute-start.6 = (bf16[464,128]{1,0:T(8,128)(2,1)S(1)}, bf16[464,128]{1,0:T(8,128)(2,1)S(1)}, u32[]{:S(2)}, u32[]{:S(2)}) collective-permute-start(bf16[464,128]{1,0:T(8,128)(2,1)S(1)} %get-tuple-element.48), channel_id=1, source_target_pairs={{0,2},{1,3},{2,0},{3,1},{4,6},{5,7},{6,4},{7,5},{8,10},{9,11},{10,... | collective-permute-start | bytes 356360 | tf_op jit(solution)/shard_map/ppermute | solution.py:26
  27.0 9.1 %collective-permute-start.4 = (bf16[464,128]{1,0:T(8,128)(2,1)S(1)}, bf16[464,128]{1,0:T(8,128)(2,1)S(1)}, u32[]{:S(2)}, u32[]{:S(2)}) collective-permute-start(bf16[464,128]{1,0:T(8,128)(2,1)S(1)} %get-tuple-element.44), channel_id=1, source_target_pairs={{0,3},{1,0},{2,1},{3,2},{4,7},{5,4},{6,5},{7,6},{8,11},{9,8},{10,9... | collective-permute-start | bytes 356360 | tf_op jit(solution)/shard_map/ppermute | solution.py:26
  30.7 15.0 %collective-permute-start.9 = (bf16[464,128]{1,0:T(8,128)(2,1)S(1)}, bf16[464,128]{1,0:T(8,128)(2,1)S(1)}, u32[]{:S(2)}, u32[]{:S(2)}) collective-permute-start(bf16[464,128]{1,0:T(8,128)(2,1)S(1)} %get-tuple-element.53), channel_id=1, source_target_pairs={{0,1},{1,2},{2,3},{3,0},{4,5},{5,6},{6,7},{7,4},{8,9},{9,10},{10,1... | collective-permute-start | bytes 356360 | tf_op jit(solution)/shard_map/ppermute | solution.py:26
  35.3 10.4 %collective-permute-start.7 = (bf16[464,128]{1,0:T(8,128)(2,1)S(1)}, bf16[464,128]{1,0:T(8,128)(2,1)S(1)}, u32[]{:S(2)}, u32[]{:S(2)}) collective-permute-start(bf16[464,128]{1,0:T(8,128)(2,1)S(1)} %get-tuple-element.49), channel_id=1, source_target_pairs={{0,2},{1,3},{2,0},{3,1},{4,6},{5,7},{6,4},{7,5},{8,10},{9,11},{10,... | collective-permute-start | bytes 356360 | tf_op jit(solution)/shard_map/ppermute | solution.py:26
  36.1 9.7 %collective-permute-start.5 = (bf16[464,128]{1,0:T(8,128)(2,1)S(1)}, bf16[464,128]{1,0:T(8,128)(2,1)S(1)}, u32[]{:S(2)}, u32[]{:S(2)}) collective-permute-start(bf16[464,128]{1,0:T(8,128)(2,1)S(1)} %get-tuple-element.45), channel_id=1, source_target_pairs={{0,3},{1,0},{2,1},{3,2},{4,7},{5,4},{6,5},{7,6},{8,11},{9,8},{10,9... | collective-permute-start | bytes 356360 | tf_op jit(solution)/shard_map/ppermute | solution.py:26
  43.9 11.7 %collective-permute-start.13 = (bf16[608,128]{1,0:T(8,128)(2,1)S(1)}, bf16[608,128]{1,0:T(8,128)(2,1)S(1)}, u32[]{:S(2)}, u32[]{:S(2)}) collective-permute-start(bf16[608,128]{1,0:T(8,128)(2,1)S(1)} %get-tuple-element.63.refs_0_), channel_id=1, source_target_pairs={{0,16},{4,20},{8,24},{12,28},{16,0},{20,4},{24,8},{28,12},{1,17},{... | collective-permute-start | bytes 466952 | tf_op jit(solution)/shard_map/ppermute | solution.py:26
  45.8 15.3 %copy-start.1 = (bf16[640,1280]{1,0:T(8,128)(2,1)S(1)}, bf16[640,1280]{1,0:T(8,128)(2,1)}, u32[]{:S(2)}) copy-start(bf16[640,1280]{1,0:T(8,128)(2,1)} %weight.5) | copy-start | bytes 4915204
  49.8 5.8 %collective-permute-start.14 = (bf16[608,128]{1,0:T(8,128)(2,1)S(1)}, bf16[608,128]{1,0:T(8,128)(2,1)S(1)}, u32[]{:S(2)}, u32[]{:S(2)}) collective-permute-start(bf16[608,128]{1,0:T(8,128)(2,1)S(1)} %get-tuple-element.64.refs_2_), channel_id=1, source_target_pairs={{0,16},{4,20},{8,24},{12,28},{16,0},{20,4},{24,8},{28,12},{1,17},{... | collective-permute-start | bytes 466952 | tf_op jit(solution)/shard_map/ppermute | solution.py:26
  51.1 8.7 %collective-permute-start.10 = (bf16[208,128]{1,0:T(8,128)(2,1)S(1)}, bf16[208,128]{1,0:T(8,128)(2,1)S(1)}, u32[]{:S(2)}, u32[]{:S(2)}) collective-permute-start(bf16[208,128]{1,0:T(8,128)(2,1)S(1)} %get-tuple-element.57), channel_id=1, source_target_pairs={{0,1},{1,2},{2,3},{3,0},{4,5},{5,6},{6,7},{7,4},{8,9},{9,10},{10,1... | collective-permute-start | bytes 159752 | tf_op jit(solution)/shard_map/ppermute | solution.py:26
  53.1 8.0 %collective-permute-start.11 = (bf16[208,128]{1,0:T(8,128)(2,1)S(1)}, bf16[208,128]{1,0:T(8,128)(2,1)S(1)}, u32[]{:S(2)}, u32[]{:S(2)}) collective-permute-start(bf16[208,128]{1,0:T(8,128)(2,1)S(1)} %get-tuple-element.58), channel_id=1, source_target_pairs={{0,2},{1,3},{2,0},{3,1},{4,6},{5,7},{6,4},{7,5},{8,10},{9,11},{10,... | collective-permute-start | bytes 159752 | tf_op jit(solution)/shard_map/ppermute | solution.py:26
  54.5 6.6 %collective-permute-start.12 = (bf16[208,128]{1,0:T(8,128)(2,1)S(1)}, bf16[208,128]{1,0:T(8,128)(2,1)S(1)}, u32[]{:S(2)}, u32[]{:S(2)}) collective-permute-start(bf16[208,128]{1,0:T(8,128)(2,1)S(1)} %get-tuple-element.59), channel_id=1, source_target_pairs={{0,3},{1,0},{2,1},{3,2},{4,7},{5,4},{6,5},{7,6},{8,11},{9,8},{10,9... | collective-permute-start | bytes 159752 | tf_op jit(solution)/shard_map/ppermute | solution.py:26
  56.3 7.0 %collective-permute-start.15 = (bf16[304,128]{1,0:T(8,128)(2,1)S(1)}, bf16[304,128]{1,0:T(8,128)(2,1)S(1)}, u32[]{:S(2)}, u32[]{:S(2)}) collective-permute-start(bf16[304,128]{1,0:T(8,128)(2,1)S(1)} %get-tuple-element.66), channel_id=1, source_target_pairs={{0,1},{1,2},{2,3},{3,0},{4,5},{5,6},{6,7},{7,4},{8,9},{9,10},{10,1... | collective-permute-start | bytes 233480 | tf_op jit(solution)/shard_map/ppermute | solution.py:26
  58.1 7.4 %collective-permute-start.16 = (bf16[304,128]{1,0:T(8,128)(2,1)S(1)}, bf16[304,128]{1,0:T(8,128)(2,1)S(1)}, u32[]{:S(2)}, u32[]{:S(2)}) collective-permute-start(bf16[304,128]{1,0:T(8,128)(2,1)S(1)} %get-tuple-element.67), channel_id=1, source_target_pairs={{0,2},{1,3},{2,0},{3,1},{4,6},{5,7},{6,4},{7,5},{8,10},{9,11},{10,... | collective-permute-start | bytes 233480 | tf_op jit(solution)/shard_map/ppermute | solution.py:26
  59.8 5.7 %collective-permute-start.17 = (bf16[304,128]{1,0:T(8,128)(2,1)S(1)}, bf16[304,128]{1,0:T(8,128)(2,1)S(1)}, u32[]{:S(2)}, u32[]{:S(2)}) collective-permute-start(bf16[304,128]{1,0:T(8,128)(2,1)S(1)} %get-tuple-element.68), channel_id=1, source_target_pairs={{0,3},{1,0},{2,1},{3,2},{4,7},{5,4},{6,5},{7,6},{8,11},{9,8},{10,9... | collective-permute-start | bytes 233480 | tf_op jit(solution)/shard_map/ppermute | solution.py:26
